TPU v7x, 32 devices: a whole 2x2x4 slice. The times are simulated.
32 devices in a mesh: fsdp: 8 (over z, x), tensor: 4 (over y, core).
Axes of the slice: x: 2, y: 2, z: 4, core: 2. Of those that a mesh axis runs over, the one named last changes fastest.
Arguments:
- layer_input: bfloat16 [8192, 1024], P(('fsdp', 'tensor')), may hold values from -6 to 6
- segment_ids: int32 [8, 1024], P('fsdp'), may hold values from 0 to 3, never falling along the last dimension, each value on 1 to 512 neighbouring positions
- pad_mask: int32 [8, 1024], P('fsdp'), may hold values 0 or 1
- attn_gain: float32 [1, 1024], replicated, may hold values from 0.1 to 1.9
- ffn_gain: float32 [1, 1024], replicated, may hold values from 0.1 to 1.9
- out_gain: float32 [1, 128], replicated, may hold values from 0.1 to 1.9
- qkv_weight: bfloat16 [1, 3, 1024, 1024], P(None, None, 'fsdp', 'tensor'), may hold values from -0.1875 to 0.1875
- beta_weight: bfloat16 [1, 1024, 8], P(None, 'fsdp', 'tensor'), may hold values from -0.1875 to 0.1875
- conv_weight: float32 [1, 3, 4, 1024], P(None, None, None, 'tensor'), may hold values from -3 to 3
- out_weight: bfloat16 [1, 1024, 1024], P(None, 'tensor', 'fsdp'), may hold values from -0.1875 to 0.1875
- expand_weight: bfloat16 [1, 2, 1024, 2816], P(None, None, 'fsdp', 'tensor'), may hold values from -0.1875 to 0.1875
- down_weight: bfloat16 [1, 2816, 1024], P(None, 'tensor', 'fsdp'), may hold values from -0.15625 to 0.15625
- cotangent: bfloat16 [8192, 1024], P(('fsdp', 'tensor')), may hold values from -6 to 6
Outputs:
- block_outs: bfloat16 [1, 8192, 1024], P(None, ('fsdp', 'tensor'))
- input_grad: float32 [8192, 1024], P(('fsdp', 'tensor'))
- attn_gain_grad: float32 [1, 1024], replicated
- ffn_gain_grad: float32 [1, 1024], replicated
- out_gain_grad: float32 [1, 128], replicated
- qkv_grad: float32 [1, 3, 1024, 1024], P(None, None, 'fsdp', 'tensor')
- beta_grad: float32 [1, 1024, 8], P(None, 'fsdp', 'tensor')
- conv_grad: float32 [1, 3, 4, 1024], P(None, None, None, 'tensor')
- out_grad: float32 [1, 1024, 1024], P(None, 'tensor', 'fsdp')
- expand_grad: float32 [1, 2, 1024, 2816], P(None, None, 'fsdp', 'tensor')
- down_grad: float32 [1, 2816, 1024], P(None, 'tensor', 'fsdp')
Inputs may be any that keep to these rules, and one draw needn't show every extreme that they name: `segment_ids`: along each sequence the ids never fall; every id from 0 to 3 occurs on 1 to 512 consecutive tokens.
All inputs are finite; a program needn't handle non-finite values. No bound on the sum of `pad_mask` on one device may be relied on, other than what follows from the above.
Results may differ from a plain program's by a relative error of at most 0.012.
Values may be sent and summed in bfloat16 or wider, within the bound.
No kernel may reach another device: no remote copies, remote signals or barrier semaphores. Data moves between devices by JAX's collectives and lax.ppermute only.
A program may use at most 128 MiB of HBM per device.

v0:
```python
import jax
import jax.numpy as jnp
from jax import lax
from jax.sharding import PartitionSpec as P

HEAD = 128
SPAN = 64


highest_precision = lax.Precision.HIGHEST


def rms_norm(value_rows, gain):
    return (
        value_rows
        * lax.rsqrt(jnp.mean(value_rows * value_rows, axis=-1, keepdims=True) + 1e-06)
        * gain
    )


def conv_silu(value_rows, kernel, segments):
    tap_count = kernel.shape[0]
    seq_len = value_rows.shape[1]
    padded = jnp.pad(value_rows, ((0, 0), (tap_count - 1, 0), (0, 0)))
    seg_pad = jnp.concatenate(
        [jnp.full((segments.shape[0], tap_count - 1), -1, jnp.int32), segments], axis=1
    )
    summed = jnp.zeros_like(value_rows)
    for offset in range(tap_count):
        start_at = tap_count - 1 - offset
        same_doc = (seg_pad[:, start_at : start_at + seq_len] == segments).astype(value_rows.dtype)
        summed = (
            summed
            + kernel[offset] * padded[:, start_at : start_at + seq_len] * same_doc[:, :, None]
        )
    return jax.nn.silu(summed)


def unit_rows(value_rows):
    return value_rows * lax.rsqrt(jnp.sum(value_rows * value_rows, axis=-1, keepdims=True) + 1e-06)


def delta_spans(queries, key_vecs, value_vecs, beta_vals, segments):
    members, seq_len, head_dim = key_vecs.shape
    block_count = seq_len // SPAN

    def blocked(value_rows):
        return jnp.moveaxis(
            value_rows.reshape((members, block_count, SPAN) + value_rows.shape[2:]), 1, 0
        )

    identity = jnp.eye(SPAN, dtype=key_vecs.dtype)
    causal = jnp.tril(jnp.ones((SPAN, SPAN), key_vecs.dtype))

    def advance(carried, block):
        memory_state, previous = carried
        query_block, key_block, value_blk, beta_blk, seg_blk = block
        same_doc = (seg_blk[:, :, None] == seg_blk[:, None, :]).astype(key_block.dtype)
        leading_shape = (seg_blk == previous[:, None]).astype(key_block.dtype)
        trailing_shape = (seg_blk == seg_blk[:, -1:]).astype(key_block.dtype)
        products = jnp.einsum("nid,njd->nij", key_block, key_block, precision=highest_precision)
        system = identity + jnp.tril(beta_blk[:, :, None] * products * same_doc, -1)
        recalled_values = jnp.einsum(
            "vhr,vcr->vch", memory_state, key_block, precision=highest_precision
        )
        right_side = beta_blk[:, :, None] * (
            value_blk - leading_shape[:, :, None] * recalled_values
        )
        state_update = jax.scipy.linalg.solve_triangular(
            system, right_side, lower=True, unit_diagonal=True
        )
        score_matrix = (
            jnp.einsum("nid,njd->nij", query_block, key_block, precision=highest_precision)
            * same_doc
            * causal
        )
        output_rows = leading_shape[:, :, None] * jnp.einsum(
            "vhr,vcr->vch", memory_state, query_block, precision=highest_precision
        ) + jnp.einsum("fwu,fug->fwg", score_matrix, state_update, precision=highest_precision)
        memory_state = leading_shape[:, -1][:, None, None] * memory_state + jnp.einsum(
            "ytz,ytv->yzv",
            state_update * trailing_shape[:, :, None],
            key_block,
            precision=highest_precision,
        )
        return ((memory_state, seg_blk[:, -1]), output_rows)

    start_mem = jnp.zeros((members, head_dim, head_dim), key_vecs.dtype)
    start_seg = jnp.full((members,), -1, jnp.int32)
    carried, outputs = lax.scan(
        jax.checkpoint(advance),
        (start_mem, start_seg),
        (
            blocked(queries),
            blocked(key_vecs),
            blocked(value_vecs),
            blocked(beta_vals),
            blocked(segments),
        ),
    )
    return jnp.moveaxis(outputs, 0, 1).reshape(members, seq_len, head_dim)


def mixer(query_pre, key_pre, value_pre, logits, kernels, gain_out, segments, pad_mask):
    batch_size, seq_len, channels = query_pre.shape
    head_count = channels // HEAD

    def heads_first(value_rows):
        return (
            value_rows.reshape(batch_size, seq_len, head_count, HEAD)
            .transpose(0, 2, 1, 3)
            .reshape(batch_size * head_count, seq_len, HEAD)
        )

    queries = unit_rows(heads_first(conv_silu(query_pre, kernels[0], segments)))
    key_vecs = unit_rows(heads_first(conv_silu(key_pre, kernels[1], segments)))
    value_vecs = heads_first(conv_silu(value_pre, kernels[2], segments))
    beta_vals = (
        (jax.nn.sigmoid(logits) * pad_mask.astype(logits.dtype)[:, :, None])
        .transpose(0, 2, 1)
        .reshape(batch_size * head_count, seq_len)
    )
    seg_rep = jnp.repeat(segments, head_count, axis=0)
    output_rows = delta_spans(queries, key_vecs, value_vecs, beta_vals, seg_rep)
    output_rows = (
        output_rows
        * lax.rsqrt(jnp.mean(output_rows * output_rows, axis=-1, keepdims=True) + 1e-05)
        * gain_out
    )
    return (
        output_rows.reshape(batch_size, head_count, seq_len, HEAD)
        .transpose(0, 2, 1, 3)
        .reshape(batch_size, seq_len, channels)
    )


def spread_rows(normed):
    return lax.all_gather(normed, "tensor", axis=0, tiled=True)


def collect_rows(term_fn, row_count):
    return lax.psum_scatter(
        term_fn(jnp.int32(0), lax.axis_size("tensor") * row_count),
        "tensor",
        scatter_dimension=0,
        tiled=True,
    )


def spread_grad(gradient):
    return lax.all_gather(gradient, "tensor", axis=0, tiled=True)


def collect_grad(term_fn, row_count):
    return lax.psum_scatter(
        term_fn(jnp.int32(0), lax.axis_size("tensor") * row_count),
        "tensor",
        scatter_dimension=0,
        tiled=True,
    )


def on_device(
    layer_input,
    segment_ids,
    pad_mask,
    attn_gain,
    ffn_gain,
    out_gain,
    qkv_weight,
    beta_weight,
    conv_weight,
    out_weight,
    expand_weight,
    down_weight,
    cotangent,
):
    layer_count = qkv_weight.shape[0]
    row_count = layer_input.shape[0]
    resid = layer_input.astype(jnp.float32)
    layer_index = 0
    matrices = (
        lax.all_gather(qkv_weight[layer_index], "fsdp", axis=1, tiled=True),
        lax.all_gather(beta_weight[layer_index], "fsdp", axis=0, tiled=True),
        lax.all_gather(expand_weight[layer_index], "fsdp", axis=1, tiled=True),
        lax.all_gather(out_weight[layer_index], "fsdp", axis=1, tiled=True),
        lax.all_gather(down_weight[layer_index], "fsdp", axis=1, tiled=True),
    )
    qkv_full, beta_full, expand_full, out_full, down_full = matrices
    normed = rms_norm(resid, attn_gain[layer_index]).astype(jnp.bfloat16)
    gathered = spread_rows(normed)
    projected = jnp.einsum("ld,sdc->slc", gathered, qkv_full, preferred_element_type=jnp.float32)
    logits = jnp.dot(gathered, beta_full, preferred_element_type=jnp.float32)

    def local_mix(query_pre, key_pre, value_pre, logit_vals, kernels, gain_out):
        return mixer(
            query_pre[None],
            key_pre[None],
            value_pre[None],
            logit_vals[None],
            kernels,
            gain_out,
            segment_ids,
            pad_mask,
        )[0]

    mixed_tokens, pullback = jax.vjp(
        local_mix,
        projected[0],
        projected[1],
        projected[2],
        logits,
        conv_weight[layer_index],
        out_gain[layer_index],
    )
    mixed_low = mixed_tokens.astype(jnp.bfloat16)

    def attn_term(start, count):
        return jnp.dot(mixed_low, out_full, preferred_element_type=jnp.float32)

    resid_mid = resid + collect_rows(attn_term, row_count)
    token_mixed = mixed_low
    out_entire = out_full
    normed_ffn = rms_norm(resid_mid, ffn_gain[layer_index]).astype(jnp.bfloat16)
    gathered_ffn = spread_rows(normed_ffn)
    expanded = jnp.einsum(
        "ld,sdf->slf", gathered_ffn, expand_full, preferred_element_type=jnp.float32
    )
    hidden = (jax.nn.silu(expanded[0]) * expanded[1]).astype(jnp.bfloat16)

    def ffn_term(start, count):
        return jnp.dot(hidden, down_full, preferred_element_type=jnp.float32)

    resid_out = resid_mid + collect_rows(ffn_term, row_count)
    stored = [
        (
            resid,
            gathered,
            pullback,
            mixed_low,
            resid_mid,
            gathered_ffn,
            expanded,
            hidden,
            matrices,
            token_mixed,
            out_entire,
        )
    ]
    block_outs = [resid_out.astype(jnp.bfloat16)]
    gradient = cotangent.astype(jnp.float32)
    weight_parts = [None] * layer_count
    conv_parts = [None] * layer_count
    attn_parts = [None] * layer_count
    ffn_parts = [None] * layer_count
    head_parts = [None] * layer_count
    layer_index = 0
    (
        resid,
        gathered,
        pullback,
        mixed_low,
        resid_mid,
        gathered_ffn,
        expanded,
        hidden,
        matrices,
        token_mixed,
        out_entire,
    ) = stored[layer_index]
    matrices = (
        lax.all_gather(qkv_weight[layer_index], "fsdp", axis=1, tiled=True),
        lax.all_gather(beta_weight[layer_index], "fsdp", axis=0, tiled=True),
        lax.all_gather(expand_weight[layer_index], "fsdp", axis=1, tiled=True),
        lax.all_gather(out_weight[layer_index], "fsdp", axis=1, tiled=True),
        lax.all_gather(down_weight[layer_index], "fsdp", axis=1, tiled=True),
    )
    qkv_full, beta_full, expand_full, out_full, down_full = matrices
    grad_full = spread_grad(gradient.astype(jnp.bfloat16))
    d_hidden = lax.dot_general(
        grad_full, down_full, (((1,), (1,)), ((), ())), preferred_element_type=jnp.float32
    )
    d_down = lax.dot_general(
        hidden, grad_full, (((0,), (0,)), ((), ())), preferred_element_type=jnp.float32
    )
    gate_vals = expanded[0]
    up_vals = expanded[1]
    sig_gate = jax.nn.sigmoid(gate_vals)
    d_gate = d_hidden * up_vals * sig_gate * (1.0 + gate_vals * (1.0 - sig_gate))
    d_up = d_hidden * gate_vals * sig_gate
    d_expanded = jnp.stack([d_gate, d_up]).astype(jnp.bfloat16)
    d_expand = jnp.einsum(
        "ld,slf->sdf", gathered_ffn, d_expanded, preferred_element_type=jnp.float32
    )

    def ffn_back(start, count):
        return jnp.einsum(
            "slf,sdf->ld", d_expanded, expand_full, preferred_element_type=jnp.float32
        )

    d_normed_ffn = collect_grad(ffn_back, row_count)
    unused, norm_back = jax.vjp(rms_norm, resid_mid, ffn_gain[layer_index])
    d_resid_mid, d_ffn_gain = norm_back(d_normed_ffn)
    gradient = gradient + d_resid_mid
    grad_low = gradient.astype(jnp.bfloat16)
    grad_full = spread_grad(grad_low)
    d_mixed = lax.dot_general(
        grad_full, out_full, (((1,), (1,)), ((), ())), preferred_element_type=jnp.float32
    )
    d_out = lax.dot_general(
        mixed_low, grad_full, (((0,), (0,)), ((), ())), preferred_element_type=jnp.float32
    )
    d_query, d_key, d_value, d_logits, d_kernels, d_head_gain = pullback(d_mixed)
    d_projected = jnp.stack([d_query, d_key, d_value]).astype(jnp.bfloat16)
    d_logit_low = d_logits.astype(jnp.bfloat16)
    d_qkv = jnp.einsum("ld,slc->sdc", gathered, d_projected, preferred_element_type=jnp.float32)
    d_beta = lax.dot_general(
        gathered, d_logit_low, (((0,), (0,)), ((), ())), preferred_element_type=jnp.float32
    )

    def attn_back(start, count):
        part_qkv = jnp.einsum(
            "slc,sdc->ld", d_projected, qkv_full, preferred_element_type=jnp.float32
        )
        part_beta = lax.dot_general(
            d_logit_low, beta_full, (((1,), (1,)), ((), ())), preferred_element_type=jnp.float32
        )
        return part_qkv + part_beta

    d_normed = collect_grad(attn_back, row_count)
    unused, norm_back = jax.vjp(rms_norm, resid, attn_gain[layer_index])
    d_resid, d_attn_gain = norm_back(d_normed)
    gradient = gradient + d_resid
    weight_parts[layer_index] = (
        lax.psum_scatter(d_qkv, "fsdp", scatter_dimension=1, tiled=True),
        lax.psum_scatter(d_beta, "fsdp", scatter_dimension=0, tiled=True),
        lax.psum_scatter(d_expand, "fsdp", scatter_dimension=1, tiled=True),
        lax.psum_scatter(d_out, "fsdp", scatter_dimension=1, tiled=True),
        lax.psum_scatter(d_down, "fsdp", scatter_dimension=1, tiled=True),
    )
    conv_parts[layer_index] = d_kernels
    attn_parts[layer_index] = d_attn_gain
    ffn_parts[layer_index] = d_ffn_gain
    head_parts[layer_index] = d_head_gain
    conv_total = lax.psum(jnp.stack(conv_parts), "fsdp")
    attn_total, ffn_total, head_total = lax.psum(
        (jnp.stack(attn_parts), jnp.stack(ffn_parts), jnp.stack(head_parts)), ("fsdp", "tensor")
    )
    qkv_total = jnp.stack([parts[0] for parts in weight_parts])
    beta_total = jnp.stack([parts[1] for parts in weight_parts])
    expand_total = jnp.stack([parts[2] for parts in weight_parts])
    out_total = jnp.stack([parts[3] for parts in weight_parts])
    down_total = jnp.stack([parts[4] for parts in weight_parts])
    return (
        jnp.stack(block_outs),
        gradient,
        attn_total,
        ffn_total,
        head_total,
        qkv_total,
        beta_total,
        conv_total,
        out_total,
        expand_total,
        down_total,
    )


def solution(mesh):
    in_specs = (
        P(("fsdp", "tensor"), None),
        P("fsdp", None),
        P("fsdp", None),
        P(),
        P(),
        P(),
        P(None, None, "fsdp", "tensor"),
        P(None, "fsdp", "tensor"),
        P(None, None, None, "tensor"),
        P(None, "tensor", "fsdp"),
        P(None, None, "fsdp", "tensor"),
        P(None, "tensor", "fsdp"),
        P(("fsdp", "tensor"), None),
    )
    out_specs = (
        P(None, ("fsdp", "tensor"), None),
        P(("fsdp", "tensor"), None),
        P(),
        P(),
        P(),
        P(None, None, "fsdp", "tensor"),
        P(None, "fsdp", "tensor"),
        P(None, None, None, "tensor"),
        P(None, "tensor", "fsdp"),
        P(None, None, "fsdp", "tensor"),
        P(None, "tensor", "fsdp"),
    )
    return jax.shard_map(
        on_device, mesh=mesh, in_specs=in_specs, out_specs=out_specs, check_vma=False
    )
```

profile of v0, /device:TPU:0, one launch (start us, length us, event | category | flops | bytes accessed | tf_op | source)
XLA Modules:
  0.0 1515.9 jit_solution(4596001099387857349)
XLA Ops:
  12.7 22.1 %all-gather = bf16[1,1024,2]{1,2,0:T(2,128)(2,1)S(1)} all-gather(bf16[1,128,2]{1,2,0:T(2,128)(2,1)S(1)} %copy-done.35), channel_id=2, replica_groups=mesh['fsdp'=8,'tensor'=4] {'fsdp'}, dimensions={1}, use_global_device_ids=true | all-gather | bytes 4608 | tf_op jit(solution)/shard_map/all_gather | solution.py:184
  35.0 29.6 %all-gather.2 = bf16[1,256,1024]{2,1,0:T(8,128)(2,1)S(1)} all-gather(bf16[1,256,128]{2,1,0:T(8,128)(2,1)S(1)} %copy-done.29), channel_id=4, replica_groups=mesh['fsdp'=8,'tensor'=4] {'fsdp'}, dimensions={2}, use_global_device_ids=true | all-gather | bytes 589824 | tf_op jit(solution)/shard_map/all_gather | solution.py:186
  64.7 22.7 %all-gather.13.cloned.1.call-done = bf16[1024,1024]{1,0:T(8,128)(2,1)} async-done(((bf16[256,1024]{1,0:T(8,128)(2,1)}), bf16[1024,1024]{1,0:T(8,128)(2,1)}) %all-gather.13.cloned.1.call-update) | async-done | bytes 2097168 | tf_op jit(solution)/shard_map/all_gather | solution.py:138
  87.4 3.8 fusion.113
  104.5 255.6 %while.43 = (s32[]{:T(128)}, f32[2,128,128]{2,1,0:T(8,128)S(1)}, s32[2]{0:T(128)S(1)}, f32[16,2,64,128]{3,2,0,1:T(8,128)S(1)}, f32[16,2,128,128]{3,2,1,0:T(8,128...) while((s32[]{:T(128)}, f32[2,128,128]{2,1,0:T(8,128)S(1)}, ...), condition=%wide.region_4.6_spmd.clone, body=%wide.region_3.5_spmd.clone.sunk | while | flops 126235200 | bytes 2117866 | solution.py:90
  104.9 9.8 custom-call.26
  120.9 9.8 custom-call.26
  136.9 9.8 custom-call.26
  152.9 9.8 custom-call.26
  168.8 9.8 custom-call.26
  184.8 9.8 custom-call.26
  200.8 9.8 custom-call.26
  216.8 9.8 custom-call.26
  232.8 9.8 custom-call.26
  248.7 9.8 custom-call.26
  264.7 9.8 custom-call.26
  280.7 9.8 custom-call.26
  296.7 9.8 custom-call.26
  312.6 9.8 custom-call.26
  328.6 9.8 custom-call.26
  344.6 9.8 custom-call.26
  366.5 44.0 %reduce-scatter.12.cloned.1.call-done = f32[256,1024]{1,0:T(8,128)} async-done(((f32[1024,1024]{1,0:T(8,128)}), f32[256,1024]{1,0:T(8,128)}) %reduce-scatter.12.cloned.1.call-update) | async-done | bytes 1048592 | tf_op jit(solution)/shard_map/reduce_scatter | solution.py:142
  414.8 57.8 %all-gather.23.cloned.1.call-done = bf16[1,2,1024,704]{2,3,1,0:T(8,128)(2,1)} async-done(((bf16[1,2,128,704]{2,3,1,0:T(8,128)(2,1)}), bf16[1,2,1024,704]{2,3,1,0:T(8,128)(2,1)}) %all-gather.23.cloned.1.call-update) | async-done | bytes 2883600 | tf_op jit(solution)/shard_map/all_gather | solution.py:185
  472.6 22.9 %all-gather.15.cloned.1.call-done = bf16[1024,1024]{1,0:T(8,128)(2,1)} async-done(((bf16[256,1024]{1,0:T(8,128)(2,1)}), bf16[1024,1024]{1,0:T(8,128)(2,1)}) %all-gather.15.cloned.1.call-update) | async-done | bytes 2097168 | tf_op jit(solution)/shard_map/all_gather | solution.py:138
  495.5 8.1 fusion.101
  503.6 37.9 %all-gather.25.cloned.1.call-done = bf16[1,704,1024]{2,1,0:T(8,128)(2,1)} async-done(((bf16[1,704,128]{2,1,0:T(8,128)(2,1)}), bf16[1,704,1024]{2,1,0:T(8,128)(2,1)}) %all-gather.25.cloned.1.call-update) | async-done | bytes 1441808 | tf_op jit(solution)/shard_map/all_gather | solution.py:187
  541.5 22.6 %all-gather.17.cloned.1.call-done = bf16[1024,1024]{1,0:T(8,128)(2,1)} async-done(((bf16[256,1024]{1,0:T(8,128)(2,1)}), bf16[1024,1024]{1,0:T(8,128)(2,1)}) %all-gather.17.cloned.1.call-update) | async-done | bytes 2097168 | tf_op jit(solution)/shard_map/all_gather | solution.py:151
  564.1 7.7 fusion.126
  573.4 5.0 fusion.104
  578.5 44.6 %reduce-scatter.16.cloned.1.call-done = f32[256,1024]{1,0:T(8,128)} async-done(((f32[1024,1024]{1,0:T(8,128)}), f32[256,1024]{1,0:T(8,128)}) %reduce-scatter.16.cloned.1.call-update) | async-done | bytes 1048592 | tf_op jit(solution)/shard_map/reduce_scatter | solution.py:155
  626.1 22.5 %all-gather.19.cloned.1.call-done = bf16[1024,1024]{1,0:T(8,128)(2,1)} async-done(((bf16[256,1024]{1,0:T(8,128)(2,1)}), bf16[1024,1024]{1,0:T(8,128)(2,1)}) %all-gather.19.cloned.1.call-update) | async-done | bytes 2097168 | tf_op jit(solution)/shard_map/all_gather | solution.py:151
  658.6 350.7 %while.44 = (s32[]{:T(128)}, f32[2,128,128]{2,1,0:T(8,128)S(1)}, f32[16,2,64,128]{3,2,0,1:T(8,128)}, f32[16,2,64,128]{3,2,0,1:T(8,128)}, f32[16,2,64,128]{3,2,0,...) while((s32[]{:T(128)}, f32[2,128,128]{2,1,0:T(8,128)S(1)}, ...), condition=%wide.region_15.17_spmd.clone, body=%wide.region_12.16_spmd.clone.sunk | while | flops 321565120 | bytes 5879079 | solution.py:90
  663.3 9.8 custom-call.27
  685.2 9.8 custom-call.27
  707.1 9.8 custom-call.27
  729.0 9.8 custom-call.27
  751.0 9.8 custom-call.27
  772.9 9.8 custom-call.27
  794.8 9.8 custom-call.27
  816.7 9.8 custom-call.27
  838.6 9.8 custom-call.27
  860.5 9.8 custom-call.27
  882.5 9.8 custom-call.27
  904.4 9.8 custom-call.27
  926.3 9.8 custom-call.27
  948.2 9.8 custom-call.27
  970.1 9.8 custom-call.27
  992.1 9.8 custom-call.27
  1016.7 4.1 fusion.136
  1020.9 5.0 multiply_reduce_fusion.10
  1029.6 3.5 fusion.116
  1034.8 3.9 bitcast_add_fusion
  1038.8 5.6 fusion.123
  1044.5 5.3 fusion.198
  1050.1 8.1 convolution_bitcast_fusion
  1058.2 3.6 fusion.197
  1061.9 37.6 %psum.31 = f32[1,3,4,256]{3,2,1,0:T(4,128)} all-reduce(f32[1,3,4,256]{3,2,1,0:T(4,128)S(1)} %add_bitcast_fusion), channel_id=1, replica_groups=mesh['fsdp'=8,'tensor'=4] {'fsdp'}, use_global_device_ids=true, to_apply=%region_40.42 | all-reduce | flops 3072 | bytes 24576 | tf_op jit(solution)/shard_map/psum | solution.py:345
  1101.5 54.9 %reduce-scatter.20.cloned.1.call-done = f32[3,128,256]{1,2,0:T(8,128)} async-done(((f32[3,1024,256]{1,2,0:T(8,128)}), f32[3,128,256]{1,2,0:T(8,128)}) %reduce-scatter.20.cloned.1.call-update) | async-done | bytes 393232 | tf_op jit(solution)/shard_map/reduce_scatter | solution.py:335
  1158.4 44.2 %reduce-scatter.18.cloned.1.call-done = f32[256,1024]{1,0:T(8,128)} async-done(((f32[1024,1024]{1,0:T(8,128)}), f32[256,1024]{1,0:T(8,128)}) %reduce-scatter.18.cloned.1.call-update) | async-done | bytes 1048592 | tf_op jit(solution)/shard_map/reduce_scatter | solution.py:155
  1204.3 39.8 %all-reduce.31 = (f32[1,1024]{1,0:T(1,128)}, f32[1,1024]{1,0:T(1,128)}, f32[1,128]{1,0:T(1,128)}) all-reduce(f32[1,1024]{1,0:T(1,128)S(1)} %bitcast.553, f32[1,1024]{1,0:T(1,128)S(1)} %bitcast.552, f32[1,128]{1,0:T(1,128)S(1)} %bitcast.593), channel_id=1, replica_groups=mesh['fsdp'=8,'tensor'=4] {'fsdp','tensor'}, use_global_device_ids=true, to_apply=%region_21.23 | all-reduce | flops 2176 | bytes 17408 | tf_op jit(solution)/shard_map/psum | solution.py:346
  1244.1 6.3 reduce-scatter.14.cloned.1.call-done
  1253.5 73.5 %reduce-scatter.26.cloned.1.call-done = f32[704,128]{1,0:T(8,128)} async-done(((f32[704,1024]{1,0:T(8,128)}), f32[704,128]{1,0:T(8,128)}) %reduce-scatter.26.cloned.1.call-update) | async-done | bytes 360464 | tf_op jit(solution)/shard_map/reduce_scatter | solution.py:339
  1327.1 114.0 %reduce-scatter.24.cloned.1.call-done = f32[2,128,704]{1,2,0:T(8,128)} async-done(((f32[2,1024,704]{1,2,0:T(8,128)}), f32[2,128,704]{1,2,0:T(8,128)}) %reduce-scatter.24.cloned.1.call-update) | async-done | bytes 720912 | tf_op jit(solution)/shard_map/reduce_scatter | solution.py:337
  1441.1 67.9 %reduce-scatter.22.cloned.1.call-done = f32[256,128]{1,0:T(8,128)} async-done(((f32[256,1024]{1,0:T(8,128)}), f32[256,128]{1,0:T(8,128)}) %reduce-scatter.22.cloned.1.call-update) | async-done | bytes 131088 | tf_op jit(solution)/shard_map/reduce_scatter | solution.py:338
  (1081 shorter events, 352.9 us)
Async XLA Ops:
  7.2 4.2 copy-start.34
  7.2 4.7 copy-start.31
  7.2 5.5 copy-start.35
  7.2 27.8 %copy-start.32 = (f32[1,3,4,256]{3,2,1,0:T(4,128)S(1)}, f32[1,3,4,256]{3,2,1,0:T(4,128)}, u32[]{:S(2)}) copy-start(f32[1,3,4,256]{3,2,1,0:T(4,128)} %param.27) | copy-start | bytes 36868
  7.2 27.8 %copy-start.29 = (bf16[1,256,128]{2,1,0:T(8,128)(2,1)S(1)}, bf16[1,256,128]{2,1,0:T(8,128)(2,1)}, u32[]{:S(2)}) copy-start(bf16[1,256,128]{2,1,0:T(8,128)(2,1)} %param.28) | copy-start | bytes 196612
  7.2 57.4 %all-gather.21.cloned.1.call-start = ((), (), s32[]{:S(2)}) async-start(), calls=%async_computation.21 | async-start | bytes 1769472 | tf_op jit(solution)/shard_map/all_gather | solution.py:183
  8.0 79.4 %all-gather.13.cloned.1.call-start = ((), (), s32[]{:S(2)}) async-start(), calls=%async_computation.9 | async-start | bytes 2621440 | tf_op jit(solution)/shard_map/all_gather | solution.py:138
  11.3 399.2 %reduce-scatter.12.cloned.1.call-start = ((), (), s32[]{:S(2)}) async-start(), calls=%async_computation.10 | async-start | bytes 5242880 | tf_op jit(solution)/shard_map/reduce_scatter | solution.py:142
  64.7 298.3 %copy-start.21 = (bf16[1,256,1024]{2,1,0:T(8,128)(2,1)}, bf16[1,256,1024]{2,1,0:T(8,128)(2,1)S(1)}, u32[]{:S(2)}) copy-start(bf16[1,256,1024]{2,1,0:T(8,128)(2,1)S(1)} %all-gather.2) | copy-start | bytes 1572868
  91.2 1.7 copy-start.7
  92.9 2.9 copy-start.11
  92.9 2.9 copy-start.13
  92.9 4.8 copy-start.9
  96.2 1.5 copy-start.2
  100.0 1.0 copy-start.4
  100.1 1.5 copy-start.25
  101.6 2.0 copy-start.17
  104.5 256.1 %copy-start.33 = (f32[1,128]{1,0:T(1,128)S(1)}, f32[1,128]{1,0:T(1,128)}, u32[]{:S(2)}) copy-start(f32[1,128]{1,0:T(1,128)} %param.24) | copy-start | bytes 1540
  360.1 5.7 copy-start.20
  363.0 2.8 copy-start.19
  365.8 44.7 %copy-start.5 = (bf16[256,1024]{1,0:T(8,128)(2,1)S(1)}, bf16[256,1024]{1,0:T(8,128)(2,1)}, u32[]{:S(2)}) copy-start(bf16[256,1024]{1,0:T(8,128)(2,1)} %param.19) | copy-start | bytes 1572868
  365.8 46.1 %copy-start.28 = (f32[1,1024]{1,0:T(1,128)S(1)}, f32[1,1024]{1,0:T(1,128)}, u32[]{:S(2)}) copy-start(f32[1,1024]{1,0:T(1,128)} %param.23) | copy-start | bytes 12292
  365.8 106.8 %all-gather.23.cloned.1.call-start = ((), (), s32[]{:S(2)}) async-start(), calls=%async_computation.22 | async-start | bytes 3244032 | tf_op jit(solution)/shard_map/all_gather | solution.py:185
  366.4 129.1 %all-gather.15.cloned.1.call-start = ((), (), s32[]{:S(2)}) async-start(), calls=%async_computation.11 | async-start | bytes 2621440 | tf_op jit(solution)/shard_map/all_gather | solution.py:138
  412.9 128.5 %all-gather.25.cloned.1.call-start = ((), (), s32[]{:S(2)}) async-start(), calls=%async_computation.23 | async-start | bytes 1622016 | tf_op jit(solution)/shard_map/all_gather | solution.py:187
  413.5 150.6 %all-gather.17.cloned.1.call-start = ((), (), s32[]{:S(2)}) async-start(), calls=%async_computation.13 | async-start | bytes 2621440 | tf_op jit(solution)/shard_map/all_gather | solution.py:151
  414.2 208.8 %reduce-scatter.16.cloned.1.call-start = ((), (), s32[]{:S(2)}) async-start(), calls=%async_computation.14 | async-start | bytes 5242880 | tf_op jit(solution)/shard_map/reduce_scatter | solution.py:155
  564.1 9.3 copy-start.36
  571.8 1.1 copy-start.38
  571.8 1.6 copy-start.39
  578.4 46.2 %copy-start.23 = (bf16[256,1024]{1,0:T(8,128)(2,1)S(1)}, bf16[256,1024]{1,0:T(8,128)(2,1)}, u32[]{:S(2)}) copy-start(bf16[256,1024]{1,0:T(8,128)(2,1)} %param.31) | copy-start | bytes 1572868
  578.4 70.1 %all-gather.19.cloned.1.call-start = ((), (), s32[]{:S(2)}) async-start(), calls=%async_computation.15 | async-start | bytes 2621440 | tf_op jit(solution)/shard_map/all_gather | solution.py:151
  623.0 1.6 copy-start.15
  624.6 23.9 %copy-start.22 = (bf16[1,256,1024]{2,1,0:T(8,128)(2,1)S(1)}, bf16[1,256,1024]{2,1,0:T(8,128)(2,1)}, u32[]{:S(2)}) copy-start(bf16[1,256,1024]{2,1,0:T(8,128)(2,1)} %copy-done.21) | copy-start | bytes 1572868
  625.8 474.1 %reduce-scatter.28.cloned.1.call-start = ((), (), s32[]{:S(2)}) async-start(), calls=%async_computation.24 | async-start | bytes 589824
  653.4 1.9 copy-start
  1009.3 2.1 copy-start.3
  1016.4 140.1 %reduce-scatter.20.cloned.1.call-start = ((), (), s32[]{:S(2)}) async-start(), calls=%async_computation.17 | async-start | bytes 3538944 | tf_op jit(solution)/shard_map/reduce_scatter | solution.py:335
  1016.7 4.2 copy-start.8
  1016.7 4.2 copy-start.10
  1016.7 4.2 copy-start.12
  1016.7 4.2 copy-start.14
  1027.8 1.8 copy-start.18
  1028.2 0.8 copy-start.26
  1033.2 169.4 %reduce-scatter.18.cloned.1.call-start = ((), (), s32[]{:S(2)}) async-start(), calls=%async_computation.16 | async-start | bytes 5242880 | tf_op jit(solution)/shard_map/reduce_scatter | solution.py:155
  1033.2 1.0 copy-start.27
  1033.2 1.6 copy-start.37
  1038.7 211.6 %reduce-scatter.14.cloned.1.call-start = ((), (), s32[]{:S(2)}) async-start(), calls=%async_computation.12 | async-start | bytes 5242880 | tf_op jit(solution)/shard_map/reduce_scatter | solution.py:142
  1044.4 282.7 %reduce-scatter.26.cloned.1.call-start = ((), (), s32[]{:S(2)}) async-start(), calls=%async_computation.20 | async-start | bytes 3244032 | tf_op jit(solution)/shard_map/reduce_scatter | solution.py:339
  1049.8 391.3 %reduce-scatter.24.cloned.1.call-start = ((), (), s32[]{:S(2)}) async-start(), calls=%async_computation.19 | async-start | bytes 6488064 | tf_op jit(solution)/shard_map/reduce_scatter | solution.py:337
  1058.2 41.3 %copy-start.1 = (f32[1,1024,2,128]{3,1,2,0:T(8,128)S(1)}, f32[1,1024,2,128]{3,1,2,0:T(8,128)}, u32[]{:S(2)}) copy-start(f32[1,1024,2,128]{3,1,2,0:T(8,128)} %copy-done) | copy-start | bytes 3145732
  1058.2 450.9 %reduce-scatter.22.cloned.1.call-start = ((), (), s32[]{:S(2)}) async-start(), calls=%async_computation.18 | async-start | bytes 1179648 | tf_op jit(solution)/shard_map/reduce_scatter | solution.py:338
  1061.8 140.8 %copy-start.30 = (f32[1,1024]{1,0:T(1,128)S(1)}, f32[1,1024]{1,0:T(1,128)}, u32[]{:S(2)}) copy-start(f32[1,1024]{1,0:T(1,128)} %param.22) | copy-start | bytes 12292
  1099.9 150.5 %copy-start.6 = (bf16[256,1024]{1,0:T(8,128)(2,1)S(1)}, bf16[256,1024]{1,0:T(8,128)(2,1)}, u32[]{:S(2)}) copy-start(bf16[256,1024]{1,0:T(8,128)(2,1)} %param.19) | copy-start | bytes 1572868
  1099.9 150.5 %copy-start.16 = (f32[256,1024]{1,0:T(8,128)S(1)}, f32[256,1024]{1,0:T(8,128)}, u32[]{:S(2)}) copy-start(f32[256,1024]{1,0:T(8,128)} %reduce-scatter.16.cloned.1.call-done) | copy-start | bytes 3145732
  1099.9 150.5 %copy-start.24 = (bf16[256,1024]{1,0:T(8,128)(2,1)S(1)}, bf16[256,1024]{1,0:T(8,128)(2,1)}, u32[]{:S(2)}) copy-start(bf16[256,1024]{1,0:T(8,128)(2,1)} %param.31) | copy-start | bytes 1572868
Sparse Core Ops, SparseCore 0:
  10.2 50.5 all-gather.20
  62.9 24.3 all-gather.12
  365.9 44.4 reduce-scatter.11
  412.6 60.0 all-gather.22
  474.7 20.7 all-gather.14
  497.6 43.8 all-gather.24
  543.1 20.9 all-gather.16
  578.5 44.4 reduce-scatter.15
  625.9 22.5 all-gather.18
  1016.5 61.8 reduce-scatter.27
  1082.4 73.9 reduce-scatter.19
  1159.0 43.5 reduce-scatter.17
  1205.1 45.1 reduce-scatter.13
  1254.8 72.2 reduce-scatter.25
  1331.6 109.4 reduce-scatter.23
  1445.3 63.6 reduce-scatter.21
where the time goes:
time: 1530 us; the launch traced here: 1520 us
  waiting for transfers between devices  639 us (42%)
  other arithmetic  374 us (24%)
  matrix products  263 us (17%)
  blocking collectives  129 us (8%)
  local copies, waits for them, and re-layouts  89.5 us (6%)
    another operation x112, other arithmetic, advance(): jax.scipy.linalg.solve_triangular(system, right_side, lower=True, unit_di...  319 us
    reduce_scatter x1, waiting for transfers between devices, on_device(): lax.psum_scatter(d_expand, 'fsdp', scatter_dimension=1, tiled=True)  114 us
    reduce_scatter x2, waiting for transfers between devices, collect_grad(): lax.psum_scatter(term_fn(jnp.int32(0), lax.axis_size('tensor') * row_coun...  88.8 us
    reduce_scatter x1, waiting for transfers between devices, on_device(): lax.psum_scatter(d_down, 'fsdp', scatter_dimension=1, tiled=True)  73.5 us
    reduce_scatter x1, waiting for transfers between devices, on_device(): lax.psum_scatter(d_out, 'fsdp', scatter_dimension=1, tiled=True)  67.9 us
    all_gather x1, waiting for transfers between devices, on_device(): lax.all_gather(expand_weight[layer_index], 'fsdp', axis=1, tiled=True)  57.8 us
    squeeze x112, local copies, waits for them, and re-layouts, delta_spans(): lax.scan(jax.checkpoint(advance), (start_mem, start_seg), (blocked(querie...  56.3 us
    reduce_scatter x1, waiting for transfers between devices, on_device(): lax.psum_scatter(d_qkv, 'fsdp', scatter_dimension=1, tiled=True)  54.9 us
  transfers between devices with their start and end apart: 16, of which 14 were waited for; matrix products, arithmetic and copies ran while one was open for 4% of the time, Pallas kernels for 0%

commit v1 on v0

v1 whole, which is shorter than its diff:
```python
import functools
import jax
import jax.numpy as jnp
from jax import lax
from jax.experimental import pallas as pl
from jax.experimental.pallas import tpu as pltpu
from jax.sharding import PartitionSpec as P

HEAD = 128
C = 128
F32 = jnp.float32
BF = jnp.bfloat16

NN = (((1,), (0,)), ((), ()))
NT = (((1,), (1,)), ((), ()))
TN = (((0,), (0,)), ((), ()))


def dot1(a, b, dims=NN):
    return lax.dot_general(a.astype(BF), b.astype(BF), dims, preferred_element_type=F32)


def split(x):
    hi = x.astype(BF)
    return hi, (x - hi.astype(F32)).astype(BF)


def dot3(a, b, dims=NN):
    a1, a2 = split(a) if not isinstance(a, tuple) else a
    b1, b2 = split(b) if not isinstance(b, tuple) else b
    d = functools.partial(lax.dot_general, dimension_numbers=dims, preferred_element_type=F32)
    return d(a1, b1) + (d(a1, b2) + d(a2, b1))


def block_masks():
    r = lax.broadcasted_iota(jnp.int32, (C, C), 0)
    c = lax.broadcasted_iota(jnp.int32, (C, C), 1)
    return r, c


def invert(systems, dot):
    r, c = block_masks()
    eye = (r == c).astype(F32)
    x = r ^ c
    out = [eye - jnp.where((x == 1), low, 0.0) for low in systems]
    size = 2
    while size < C:
        here = (x >= size) & (x < 2 * size)
        mids = [dot(jnp.where(here, low, 0.0), t) for low, t in zip(systems, out)]
        out = [t - dot(t, m) for t, m in zip(out, mids)]
        size *= 2
    return out


def sigmoid(x):
    return 1.0 / (1.0 + jnp.exp(-x))


def taps_down(ext, rows, j):
    return lax.slice_in_dim(ext, 8 - j, 8 - j + rows, axis=0)


def fwd_kernel(heads, cb, seg_s, pre_ref, cols_ref, segr_ref, taps_ref, gain_ref,
               mixed_ref, conv_ref, o_ref, t_ref, a_ref, p_ref, n_ref, z_ref, s_ref, u_ref, g_ref,
               tail, state):
    step = pl.program_id(0)
    width = heads * HEAD
    rows = cb * C
    taps = taps_ref.shape[1]

    @pl.when(step == 0)
    def _():
        tail[...] = jnp.zeros_like(tail)
        state[...] = jnp.zeros_like(state)

    r, c = block_masks()
    parts = []
    for i in range(3):
        cur = pre_ref[:, i * width:(i + 1) * width]
        ext = jnp.concatenate([tail[:, i * width:(i + 1) * width], cur], axis=0)
        tot = cur * taps_ref[i, 0:1, :]
        for j in range(1, taps):
            tot = tot + taps_down(ext, rows, j) * taps_ref[i, j:j + 1, :] * cols_ref[:, j - 1:j]
        tail[:, i * width:(i + 1) * width] = cur[rows - 8:, :]
        conv_ref[:, i * width:(i + 1) * width] = tot
        parts.append(tot * sigmoid(tot))
    eye = (r == c).astype(F32)
    items = []
    for b in range(cb):
        sl = slice(b * C, (b + 1) * C)
        chunk = step * cb + b
        first = chunk * C
        prev = jnp.where(first > 0, seg_s[jnp.maximum(first - 1, 0)], -1)
        last = seg_s[first + C - 1]
        keep = (prev == last).astype(F32)
        segc = cols_ref[sl, 4:5]
        segr = segr_ref[0:1, sl]
        same = segc == segr
        lead = (segc == prev.astype(F32)).astype(F32)
        trail = (segc == last.astype(F32)).astype(F32)
        for h in range(heads):
            hs = slice(h * HEAD, (h + 1) * HEAD)
            q, k, v = (part[sl, hs] for part in parts)
            q = q * lax.rsqrt(jnp.sum(q * q, axis=-1, keepdims=True) + 1e-6)
            k = k * lax.rsqrt(jnp.sum(k * k, axis=-1, keepdims=True) + 1e-6)
            beta = sigmoid(pre_ref[sl, 3 * width + h:3 * width + h + 1]) * cols_ref[sl, 3:4]
            items.append(dict(b=b, h=h, q=q, k=k, v=v, beta=beta, same=same, lead=lead, trail=trail, keep=keep, sl=sl, hs=hs))
    for it in items:
        it["kk"] = split(it["k"])
        p = jnp.where(it["same"] & (r > c), dot3(it["kk"], it["kk"], NT), 0.0)
        it["p"] = p
        it["low"] = p * it["beta"]
        it["a"] = jnp.where(it["same"] & (r >= c), dot3(it["q"], it["kk"], NT), 0.0)
    inv = invert([it["low"] for it in items], dot3)
    for it, t in zip(items, inv):
        rhs = jnp.concatenate([it["beta"] * it["v"], (it["beta"] * it["lead"]) * it["k"]], axis=1)
        tw = dot3(t, rhs)
        tws = split(tw)
        aw = dot3(it["a"], tws)
        bz = dot3(it["trail"] * it["k"], tws, TN)
        it["tv"], it["w"] = tw[:, :HEAD], tw[:, HEAD:]
        it["o0"], it["n"] = aw[:, :HEAD], it["lead"] * it["q"] - aw[:, HEAD:]
        it["bk"], it["z"] = bz[:, :HEAD], it["keep"] * eye - bz[:, HEAD:]
        it["t"] = t
    for it in items:
        b, h = it["b"], it["h"]
        s = state[h]
        ss = split(s)
        u = it["tv"] - dot3(it["w"], ss)
        o = it["o0"] + dot3(it["n"], ss)
        g = it["v"] - it["lead"] * dot3(it["kk"], ss)
        state[h] = it["bk"] + dot3(it["z"], ss)
        s_ref[b, h] = s
        u_ref[b, h] = u
        g_ref[b, h] = g
        t_ref[b, h] = it["t"]
        a_ref[b, h] = it["a"]
        p_ref[b, h] = it["p"]
        n_ref[b, h] = it["n"]
        z_ref[b, h] = it["z"]
        o_ref[it["sl"], it["hs"]] = o
        mixed_ref[it["sl"], it["hs"]] = (o * lax.rsqrt(jnp.mean(o * o, axis=-1, keepdims=True) + 1e-5) * gain_ref[0:1, :]).astype(BF)


def bwd_kernel(heads, cb, seg_s, dmix_ref, pre_ref, conv_ref, o_ref, cols_ref, segr_ref, taps_ref, gain_ref,
               t_ref, a_ref, p_ref, n_ref, z_ref, s_ref, u_ref, g_ref,
               dpre_ref, dtap_ref, dgain_ref,
               head_rows, dstate):
    step = pl.program_id(0)
    steps = pl.num_programs(0)
    width = heads * HEAD
    rows = cb * C
    taps = taps_ref.shape[1]
    back = steps - 1 - step

    @pl.when(step == 0)
    def _():
        head_rows[...] = jnp.zeros_like(head_rows)
        dstate[...] = jnp.zeros_like(dstate)
        dtap_ref[...] = jnp.zeros_like(dtap_ref)
        dgain_ref[...] = jnp.zeros_like(dgain_ref)

    r, c = block_masks()
    dcs = [[[None] * heads for _ in range(cb)] for _ in range(3)]
    dgain = jnp.zeros((1, HEAD), F32)
    dlog = [None] * cb
    for b in reversed(range(cb)):
        sl = slice(b * C, (b + 1) * C)
        chunk = back * cb + b
        first = chunk * C
        prev = jnp.where(first > 0, seg_s[jnp.maximum(first - 1, 0)], -1)
        last = seg_s[first + C - 1]
        segc = cols_ref[sl, 4:5]
        segr = segr_ref[0:1, sl]
        same = segc == segr
        lead = (segc == prev.astype(F32)).astype(F32)
        trail = (segc == last.astype(F32)).astype(F32)
        lane = lax.broadcasted_iota(jnp.int32, (C, HEAD), 1)
        dl = jnp.zeros((C, HEAD), F32)
        for h in range(heads):
            hs = slice(h * HEAD, (h + 1) * HEAD)
            cq, ck, cv = (conv_ref[sl, i * width + h * HEAD:i * width + (h + 1) * HEAD] for i in range(3))
            gq, gk, gv = sigmoid(cq), sigmoid(ck), sigmoid(cv)
            q, k = cq * gq, ck * gk
            rq = lax.rsqrt(jnp.sum(q * q, axis=-1, keepdims=True) + 1e-6)
            rk = lax.rsqrt(jnp.sum(k * k, axis=-1, keepdims=True) + 1e-6)
            q, k = q * rq, k * rk
            gb = sigmoid(pre_ref[sl, 3 * width + h:3 * width + h + 1])
            pad = cols_ref[sl, 3:4]
            beta = gb * pad
            o = o_ref[sl, hs]
            dm = dmix_ref[sl, hs]
            ro = lax.rsqrt(jnp.mean(o * o, axis=-1, keepdims=True) + 1e-5)
            oh = o * ro
            dgain = dgain + jnp.sum(dm * oh, axis=0, keepdims=True)
            du0 = dm * gain_ref[0:1, :]
            do = ro * (du0 - oh * jnp.mean(du0 * oh, axis=-1, keepdims=True))
            ds1 = dstate[h]
            u = u_ref[b, h]
            s = s_ref[b, h]
            a = a_ref[b, h]
            p = p_ref[b, h]
            ks = split(k)
            ds1s = split(ds1)
            dos = split(do)
            us = split(u)
            dstate[h] = dot3(z_ref[b, h], ds1s, TN) + dot3(n_ref[b, h], dos, TN)
            du = dot3(a, dos, TN) + trail * dot3(ks, ds1s)
            dr = dot3(t_ref[b, h], du, TN)
            drs = split(dr)
            ss = split(s)
            dlow = jnp.where(same & (r > c), -dot3(drs, us, NT), 0.0)
            da = jnp.where(same & (r >= c), dot3(dos, us, NT), 0.0)
            dv = beta * dr
            dbeta = jnp.sum(dr * g_ref[b, h] , axis=-1, keepdims=True) + jnp.sum(dlow * p, axis=-1, keepdims=True)
            dp = split(beta * dlow)
            das = split(da)
            dq = lead * dot3(dos, ss, NT) + dot3(das, ks)
            dk = (dot3(das, q, TN) + trail * dot3(us, ds1s, NT) - (beta * lead) * dot3(drs, ss, NT)
                  + dot3(dp, ks) + dot3(dp, ks, TN))
            dsq = rq * (dq - q * jnp.sum(q * dq, axis=-1, keepdims=True))
            dsk = rk * (dk - k * jnp.sum(k * dk, axis=-1, keepdims=True))
            dcs[0][b][h] = dsq * gq * (1.0 + cq * (1.0 - gq))
            dcs[1][b][h] = dsk * gk * (1.0 + ck * (1.0 - gk))
            dcs[2][b][h] = dv * gv * (1.0 + cv * (1.0 - gv))
            dl = jnp.where(lane == h, dbeta * pad * gb * (1.0 - gb), dl)
        dlog[b] = dl
    dgain_ref[...] += dgain
    for b in range(cb):
        dpre_ref[b * C:(b + 1) * C, 3 * width:] = dlog[b].astype(BF)
    for i in range(3):
        dc = jnp.concatenate([jnp.concatenate(dcs[i][b], axis=1) for b in range(cb)], axis=0)
        pre = pre_ref[:, i * width:(i + 1) * width]
        tot = dc * taps_ref[i, 0:1, :]
        grads = [jnp.sum(dc * pre, axis=0, keepdims=True)]
        for j in range(1, taps):
            e = dc * cols_ref[:, j - 1:j]
            ext = jnp.concatenate([e, head_rows[j - 1, :, i * width:(i + 1) * width]], axis=0)
            head_rows[j - 1, :, i * width:(i + 1) * width] = e[:8]
            e = lax.slice_in_dim(ext, j, j + rows, axis=0)
            tot = tot + e * taps_ref[i, j:j + 1, :]
            grads.append(jnp.sum(e * pre, axis=0, keepdims=True))
        dpre_ref[:, i * width:(i + 1) * width] = tot.astype(BF)
        dtap_ref[i] += jnp.concatenate(grads, axis=0)


def mixer_fwd(pre, cols, segr, seg, taps, gain, cb=2):
    n, wide = pre.shape
    width = taps.shape[2]
    heads = width // HEAD
    rows = cb * C
    chunks = n // C
    sq = jax.ShapeDtypeStruct((chunks, heads, C, HEAD), F32)
    sqspec = pl.BlockSpec((cb, heads, C, HEAD), lambda i, s: (i, 0, 0, 0))
    row = lambda w: pl.BlockSpec((rows, w), lambda i, s: (i, 0))
    return pl.pallas_call(
        functools.partial(fwd_kernel, heads, cb),
        grid_spec=pltpu.PrefetchScalarGridSpec(
            num_scalar_prefetch=1, grid=(n // rows,),
            in_specs=[row(wide), row(cols.shape[1]), pl.BlockSpec((1, rows), lambda i, s: (0, i)),
                      pl.BlockSpec(taps.shape, lambda i, s: (0, 0, 0)), pl.BlockSpec((1, HEAD), lambda i, s: (0, 0))],
            out_specs=[row(width), row(3 * width), row(width)] + [sqspec] * 8,
            scratch_shapes=[pltpu.VMEM((8, 3 * width), F32), pltpu.VMEM((heads, HEAD, HEAD), F32)]),
        out_shape=[jax.ShapeDtypeStruct((n, width), BF), jax.ShapeDtypeStruct((n, 3 * width), F32),
                   jax.ShapeDtypeStruct((n, width), F32)] + [sq] * 8,
        compiler_params=pltpu.CompilerParams(dimension_semantics=("arbitrary",), vmem_limit_bytes=48 * 2**20),
        name="mixer_fwd",
    )(seg, pre, cols, segr, taps, gain)


def mixer_bwd(dmix, pre, cols, segr, seg, taps, gain, kept, cb=2):
    conv, o, *rest = kept
    n, wide = pre.shape
    width = taps.shape[2]
    heads = width // HEAD
    rows = cb * C
    steps = n // rows
    sqspec = pl.BlockSpec((cb, heads, C, HEAD), lambda i, s: (steps - 1 - i, 0, 0, 0))
    row = lambda w: pl.BlockSpec((rows, w), lambda i, s: (steps - 1 - i, 0))
    ntap = taps.shape[1]
    return pl.pallas_call(
        functools.partial(bwd_kernel, heads, cb),
        grid_spec=pltpu.PrefetchScalarGridSpec(
            num_scalar_prefetch=1, grid=(steps,),
            in_specs=[row(width), row(wide), row(3 * width), row(width), row(cols.shape[1]),
                      pl.BlockSpec((1, rows), lambda i, s: (0, steps - 1 - i)),
                      pl.BlockSpec(taps.shape, lambda i, s: (0, 0, 0)), pl.BlockSpec((1, HEAD), lambda i, s: (0, 0))] + [sqspec] * 8,
            out_specs=[row(wide), pl.BlockSpec(taps.shape, lambda i, s: (0, 0, 0)), pl.BlockSpec((1, HEAD), lambda i, s: (0, 0))],
            scratch_shapes=[pltpu.VMEM((ntap - 1, 8, 3 * width), F32), pltpu.VMEM((heads, HEAD, HEAD), F32)]),
        out_shape=[jax.ShapeDtypeStruct((n, wide), BF), jax.ShapeDtypeStruct(taps.shape, F32), jax.ShapeDtypeStruct((1, HEAD), F32)],
        compiler_params=pltpu.CompilerParams(dimension_semantics=("arbitrary",), vmem_limit_bytes=48 * 2**20),
        name="mixer_bwd",
    )(seg, dmix, pre, conv, o, cols, segr, taps, gain, *rest)


def columns(seg, pad):
    n = seg.shape[0]
    cols = []
    for j in range(1, 4):
        before = jnp.concatenate([jnp.full((j,), -1, seg.dtype), seg[:n - j]])
        cols.append((before == seg).astype(F32))
    cols += [pad.astype(F32), seg.astype(F32)]
    cols += [jnp.zeros((n,), F32)] * 3
    return jnp.stack(cols, axis=1)


def rms_norm(value_rows, gain):
    return (
        value_rows
        * lax.rsqrt(jnp.mean(value_rows * value_rows, axis=-1, keepdims=True) + 1e-06)
        * gain
    )


def gather_t(value):
    return lax.all_gather(value, "tensor", axis=0, tiled=True)


def scatter_t(value):
    return lax.psum_scatter(value, "tensor", scatter_dimension=0, tiled=True)


def on_device(
    layer_input, segment_ids, pad_mask, attn_gain, ffn_gain, out_gain,
    qkv_weight, beta_weight, conv_weight, out_weight, expand_weight, down_weight, cotangent,
):
    resid = layer_input.astype(F32)
    width = qkv_weight.shape[3]
    heads = beta_weight.shape[2]
    qkv_full = lax.all_gather(qkv_weight[0], "fsdp", axis=1, tiled=True)
    beta_full = lax.all_gather(beta_weight[0], "fsdp", axis=0, tiled=True)
    expand_full = lax.all_gather(expand_weight[0], "fsdp", axis=1, tiled=True)
    out_full = lax.all_gather(out_weight[0], "fsdp", axis=1, tiled=True)
    down_full = lax.all_gather(down_weight[0], "fsdp", axis=1, tiled=True)
    wide = jnp.concatenate(
        [qkv_full[0], qkv_full[1], qkv_full[2], jnp.pad(beta_full, ((0, 0), (0, HEAD - heads)))], axis=1
    )
    normed = rms_norm(resid, attn_gain[0]).astype(BF)
    gathered = gather_t(normed)
    pre = jnp.dot(gathered, wide, preferred_element_type=F32)
    seg = segment_ids[0]
    cols = columns(seg, pad_mask[0])
    segr = seg.astype(F32)[None]
    mixed, *kept = mixer_fwd(pre, cols, segr, seg, conv_weight[0], out_gain)
    resid_mid = resid + scatter_t(jnp.dot(mixed, out_full, preferred_element_type=F32))
    normed_ffn = rms_norm(resid_mid, ffn_gain[0]).astype(BF)
    gathered_ffn = gather_t(normed_ffn)
    expanded = jnp.einsum("ld,sdf->slf", gathered_ffn, expand_full, preferred_element_type=F32)
    gate, up = expanded[0], expanded[1]
    sig = jax.nn.sigmoid(gate)
    hidden = (gate * sig * up).astype(BF)
    resid_out = resid_mid + scatter_t(jnp.dot(hidden, down_full, preferred_element_type=F32))
    block_outs = resid_out.astype(BF)[None]

    grad = cotangent.astype(F32)
    grad_full = gather_t(cotangent)
    d_hidden = lax.dot_general(grad_full, down_full, NT, preferred_element_type=F32)
    d_down = lax.dot_general(hidden, grad_full, TN, preferred_element_type=F32)
    d_gate = d_hidden * up * sig * (1.0 + gate * (1.0 - sig))
    d_up = d_hidden * gate * sig
    d_expanded = jnp.stack([d_gate, d_up]).astype(BF)
    d_expand = jnp.einsum("ld,slf->sdf", gathered_ffn, d_expanded, preferred_element_type=F32)
    d_normed_ffn = scatter_t(jnp.einsum("slf,sdf->ld", d_expanded, expand_full, preferred_element_type=F32))
    unused, norm_back = jax.vjp(rms_norm, resid_mid, ffn_gain[0])
    d_mid, d_ffn_gain = norm_back(d_normed_ffn)
    grad = grad + d_mid
    grad_full = gather_t(grad.astype(BF))
    d_mixed = lax.dot_general(grad_full, out_full, NT, preferred_element_type=F32)
    d_out = lax.dot_general(mixed, grad_full, TN, preferred_element_type=F32)
    d_wide, d_taps, d_head = mixer_bwd(d_mixed, pre, cols, segr, seg, conv_weight[0], out_gain, kept)
    d_all = lax.dot_general(gathered, d_wide, TN, preferred_element_type=F32)
    d_qkv = jnp.stack([d_all[:, i * width:(i + 1) * width] for i in range(3)])
    d_beta = d_all[:, 3 * width:3 * width + heads]
    d_normed = scatter_t(lax.dot_general(d_wide, wide, NT, preferred_element_type=F32))
    unused, norm_back = jax.vjp(rms_norm, resid, attn_gain[0])
    d_resid, d_attn_gain = norm_back(d_normed)
    grad = grad + d_resid
    qkv_grad = lax.psum_scatter(d_qkv, "fsdp", scatter_dimension=1, tiled=True)
    beta_grad = lax.psum_scatter(d_beta, "fsdp", scatter_dimension=0, tiled=True)
    expand_grad = lax.psum_scatter(d_expand, "fsdp", scatter_dimension=1, tiled=True)
    out_grad = lax.psum_scatter(d_out, "fsdp", scatter_dimension=1, tiled=True)
    down_grad = lax.psum_scatter(d_down, "fsdp", scatter_dimension=1, tiled=True)
    conv_grad = lax.psum(d_taps, "fsdp")
    attn_total, ffn_total, head_total = lax.psum((d_attn_gain[None], d_ffn_gain[None], d_head), ("fsdp", "tensor"))
    return (
        block_outs, grad, attn_total, ffn_total, head_total, qkv_grad[None], beta_grad[None],
        conv_grad[None], out_grad[None], expand_grad[None], down_grad[None],
    )


def solution(mesh):
    in_specs = (
        P(("fsdp", "tensor"), None),
        P("fsdp", None),
        P("fsdp", None),
        P(),
        P(),
        P(),
        P(None, None, "fsdp", "tensor"),
        P(None, "fsdp", "tensor"),
        P(None, None, None, "tensor"),
        P(None, "tensor", "fsdp"),
        P(None, None, "fsdp", "tensor"),
        P(None, "tensor", "fsdp"),
        P(("fsdp", "tensor"), None),
    )
    out_specs = (
        P(None, ("fsdp", "tensor"), None),
        P(("fsdp", "tensor"), None),
        P(),
        P(),
        P(),
        P(None, None, "fsdp", "tensor"),
        P(None, "fsdp", "tensor"),
        P(None, None, None, "tensor"),
        P(None, "tensor", "fsdp"),
        P(None, None, "fsdp", "tensor"),
        P(None, "tensor", "fsdp"),
    )
    return jax.shard_map(
        on_device, mesh=mesh, in_specs=in_specs, out_specs=out_specs, check_vma=False
    )
```

time: 1530 us -> 939 us (0.61)
  other arithmetic: 374 us -> 18.2 us
  matrix products: 263 us -> 59.9 us
  local copies, waits for them, and re-layouts: 89.5 us -> 19.4 us
  Pallas kernels: 0 us -> 48 us
    another operation x132 -> x2, other arithmetic: 320 us -> 3.36 us  [the longest x1 3.28 us: on_device(): d_qkv = jnp.stack([d_all[:, i * width:(i + 1) * width] for i in range(3)])]
    dot_general x364 -> x10, matrix products: 215 us -> 44.9 us  [the longest x1 7.69 us: on_device(): lax.dot_general(grad_full, down_full, NT, preferred_element_type=F32)]
    squeeze x112 -> x1, local copies, waits for them, and re-layouts: 56.3 us -> 1.46 us  [on_device(): qkv_full[0]]
    pallas_call x0 -> x2, Pallas kernels: none -> 48 us  [the longest x1 24.5 us: mixer_fwd(): pl.pallas_call(functools.partial(fwd_kernel, heads, cb), grid_spec=pltpu....]
    another operation x64 -> x0, matrix products: 28.2 us -> none  [advance(): jax.scipy.linalg.solve_triangular(system, right_side, lower=True, unit_di...]
  transfers between devices with their start and end apart: 16 -> 16, of which waited for: 14 -> 14; matrix products, arithmetic and copies ran while one was open for 4% -> 6% of each run, Pallas kernels for 0% -> 0%
where the time goes in v1:
time: 939 us; the launch traced here: 938 us
  waiting for transfers between devices  647 us (69%)
  blocking collectives  130 us (14%)
  matrix products  59.9 us (6%)
  Pallas kernels  48 us (5%)
  local copies, waits for them, and re-layouts  19.4 us (2%)
  other arithmetic  18.2 us (2%)
  between operations  14.2 us (2%)
    reduce_scatter x4, waiting for transfers between devices, scatter_t(): return lax.psum_scatter(value, 'tensor', scatter_dimension=0, tiled=True)  139 us
    reduce_scatter x1, waiting for transfers between devices, on_device(): lax.psum_scatter(d_expand, 'fsdp', scatter_dimension=1, tiled=True)  114 us
    all_gather x4, waiting for transfers between devices, gather_t(): return lax.all_gather(value, 'tensor', axis=0, tiled=True)  88.4 us
    reduce_scatter x1, waiting for transfers between devices, on_device(): lax.psum_scatter(d_down, 'fsdp', scatter_dimension=1, tiled=True)  73.5 us
    reduce_scatter x1, waiting for transfers between devices, on_device(): out_grad = lax.psum_scatter(d_out, 'fsdp', scatter_dimension=1, tiled=True)  67.9 us
    reduce_scatter x1, waiting for transfers between devices, on_device(): qkv_grad = lax.psum_scatter(d_qkv, 'fsdp', scatter_dimension=1, tiled=True)  66 us
    all_gather x1, waiting for transfers between devices, on_device(): expand_full = lax.all_gather(expand_weight[0], 'fsdp', axis=1, tiled=True)  57.1 us
    psum x1, blocking collectives, on_device(): lax.psum((d_attn_gain[None], d_ffn_gain[None], d_head), ('fsdp', 'tensor'))  39.8 us
  transfers between devices with their start and end apart: 16, of which 14 were waited for; matrix products, arithmetic and copies ran while one was open for 6% of the time, Pallas kernels for 0%

profile of v1, /device:TPU:0, one launch (start us, length us, event | category | flops | bytes accessed | tf_op | source)
XLA Modules:
  0.0 937.6 jit_solution(5505654835126991521)
XLA Ops:
  7.3 0.7 all-gather.21.cloned.1.call-update
  8.0 1.2 fusion.26
  9.2 2.0 fusion.22
  11.3 22.3 %all-gather.1 = bf16[1,1024,2]{1,2,0:T(2,128)(2,1)S(1)} all-gather(bf16[1,128,2]{1,2,0:T(2,128)(2,1)S(1)} %copy-done.26), channel_id=3, replica_groups=mesh['fsdp'=8,'tensor'=4] {'fsdp'}, dimensions={1}, use_global_device_ids=true | all-gather | bytes 4608 | tf_op jit(solution)/shard_map/all_gather | solution.py:331
  33.6 0.2 copy.40
  34.4 30.4 %all-gather.2 = bf16[1,256,1024]{2,1,0:T(8,128)(2,1)} all-gather(bf16[1,256,128]{2,1,0:T(8,128)(2,1)S(1)} %copy-done.23), channel_id=4, replica_groups=mesh['fsdp'=8,'tensor'=4] {'fsdp'}, dimensions={2}, use_global_device_ids=true | all-gather | bytes 589824 | tf_op jit(solution)/shard_map/all_gather | solution.py:333
  64.8 1.5 slice_bitcast_fusion.7
  66.3 20.4 %all-gather.13.cloned.1.call-done = bf16[1024,1024]{1,0:T(8,128)(2,1)} async-done(((bf16[256,1024]{1,0:T(8,128)(2,1)}), bf16[1024,1024]{1,0:T(8,128)(2,1)}) %all-gather.13.cloned.1.call-update) | async-done | bytes 2097168 | tf_op jit(solution)/shard_map/all_gather | solution.py:316
  86.7 5.8 fusion.41.pre_ref
  92.5 24.5 %mixer_fwd.1 = (bf16[1024,256]{1,0:T(8,128)(2,1)S(1)}, f32[1024,768]{1,0:T(8,128)}, f32[1024,256]{1,0:T(8,128)S(1)}, f32[8,2,128,128]{3,2,1,0:T(8,128)S(1)}, f32...) custom-call(s32[1024]{0:T(1024)S(1)} %bitcast.112, ...), custom_call_target="tpu_custom_call" | custom-call | tf_op jit(solution)/shard_map/mixer_fwd/pallas_call | solution.py:256
  117.0 1.0 copy-done
  118.0 1.0 copy-done.2
  119.1 2.7 fusion.31
  121.8 0.5 all-gather.23.cloned.1.call-update
  122.4 44.0 %reduce-scatter.12.cloned.1.call-done = f32[256,1024]{1,0:T(8,128)} async-done(((f32[1024,1024]{1,0:T(8,128)}), f32[256,1024]{1,0:T(8,128)}) %reduce-scatter.12.cloned.1.call-update) | async-done | bytes 1048592 | tf_op jit(solution)/shard_map/reduce_scatter | solution.py:320
  166.4 1.6 multiply_reduce_fusion.2
  168.0 1.0 copy-done.7
  169.0 0.9 multiply_convert_fusion.3
  170.0 0.5 all-gather.25.cloned.1.call-update
  170.6 0.7 all-gather.17.cloned.1.call-update
  171.3 0.2 reduce-scatter.16.cloned.1.call-start
  171.5 57.1 %all-gather.23.cloned.1.call-done = bf16[1,2,1024,704]{2,3,1,0:T(8,128)(2,1)} async-done(((bf16[1,2,128,704]{2,3,1,0:T(8,128)(2,1)}), bf16[1,2,1024,704]{2,3,1,0:T(8,128)(2,1)}) %all-gather.23.cloned.1.call-update) | async-done | bytes 2883600 | tf_op jit(solution)/shard_map/all_gather | solution.py:332
  228.6 22.9 %all-gather.15.cloned.1.call-done = bf16[1024,1024]{1,0:T(8,128)(2,1)} async-done(((bf16[256,1024]{1,0:T(8,128)(2,1)}), bf16[1024,1024]{1,0:T(8,128)(2,1)}) %all-gather.15.cloned.1.call-update) | async-done | bytes 2097168 | tf_op jit(solution)/shard_map/all_gather | solution.py:316
  251.5 8.1 fusion.5
  259.6 37.8 %all-gather.25.cloned.1.call-done = bf16[1,704,1024]{2,1,0:T(8,128)(2,1)} async-done(((bf16[1,704,128]{2,1,0:T(8,128)(2,1)}), bf16[1,704,1024]{2,1,0:T(8,128)(2,1)}) %all-gather.25.cloned.1.call-update) | async-done | bytes 1441808 | tf_op jit(solution)/shard_map/all_gather | solution.py:334
  297.4 22.6 %all-gather.17.cloned.1.call-done = bf16[1024,1024]{1,0:T(8,128)(2,1)} async-done(((bf16[256,1024]{1,0:T(8,128)(2,1)}), bf16[1024,1024]{1,0:T(8,128)(2,1)}) %all-gather.17.cloned.1.call-update) | async-done | bytes 2097168 | tf_op jit(solution)/shard_map/all_gather | solution.py:316
  320.1 7.7 fusion.19
  327.8 1.1 copy-done.32
  328.9 0.6 copy-done.33
  329.4 5.0 fusion.8
  334.5 44.6 %reduce-scatter.16.cloned.1.call-done = f32[256,1024]{1,0:T(8,128)} async-done(((f32[1024,1024]{1,0:T(8,128)}), f32[256,1024]{1,0:T(8,128)}) %reduce-scatter.16.cloned.1.call-update) | async-done | bytes 1048592 | tf_op jit(solution)/shard_map/reduce_scatter | solution.py:320
  379.1 1.9 multiply_reduce_fusion
  381.3 2.1 fusion.43
  383.5 0.3 reduce-scatter.28.cloned.1.call-start
  383.7 22.5 %all-gather.19.cloned.1.call-done = bf16[1024,1024]{1,0:T(8,128)(2,1)} async-done(((bf16[256,1024]{1,0:T(8,128)(2,1)}), bf16[1024,1024]{1,0:T(8,128)(2,1)}) %all-gather.19.cloned.1.call-update) | async-done | bytes 2097168 | tf_op jit(solution)/shard_map/all_gather | solution.py:316
  406.2 2.6 fusion.29.dmix_ref
  408.8 23.5 %mixer_bwd.1 = (bf16[1024,896]{1,0:T(8,128)(2,1)}, f32[3,4,256]{2,1,0:T(4,128)S(1)}, f32[1,128]{1,0:T(1,128)S(1)}) custom-call(s32[1024]{0:T(1024)S(1)} %bitcast.113, f32[1024,256]{1,0:T(8,128)S(1)} %fusion.29.dmix_ref, f32[1024,896]{1,0:T(8,128)} %fusion.41.pre_ref, f32[1024,768]{1,0:T(8,128)} %get-tuple-element.26.conv_ref, ...), custom_call_target="tpu_custom_call" | custom-call | tf_op jit(solution)/shard_map/mixer_bwd/pallas_call | solution.py:281
  432.3 3.7 fusion.47
  436.0 1.2 slice_bitcast_fusion.4
  437.2 1.0 copy.38
  438.3 3.3 pad_maximum_fusion
  441.7 1.0 copy-done.17
  442.9 5.9 fusion.39
  448.9 1.3 copy-done.31
  450.2 5.3 fusion.16
  455.5 0.3 reduce-scatter.26.cloned.1.call-start
  455.8 1.3 copy-done.30
  457.1 4.6 fusion.49
  461.8 1.5 copy-done.29
  463.3 6.8 convolution_bitcast_fusion
  470.3 1.5 copy-done.14
  471.8 1.7 fusion.48
  473.5 37.5 %psum.31 = f32[1,3,4,256]{3,2,1,0:T(4,128)} all-reduce(f32[1,3,4,256]{3,2,1,0:T(4,128)S(1)} %bitcast.116), channel_id=1, replica_groups=mesh['fsdp'=8,'tensor'=4] {'fsdp'}, use_global_device_ids=true, to_apply=%region_15.16 | all-reduce | flops 3072 | bytes 24576 | tf_op jit(solution)/shard_map/psum | solution.py:383
  510.9 1.5 copy.39
  512.4 66.0 %reduce-scatter.20.cloned.1.call-done = f32[3,128,256]{1,2,0:T(8,128)} async-done(((f32[3,1024,256]{1,2,0:T(8,128)}), f32[3,128,256]{1,2,0:T(8,128)}) %reduce-scatter.20.cloned.1.call-update) | async-done | bytes 393232 | tf_op jit(solution)/shard_map/reduce_scatter | solution.py:378
  578.4 1.9 copy.37
  580.3 44.2 %reduce-scatter.18.cloned.1.call-done = f32[256,1024]{1,0:T(8,128)} async-done(((f32[1024,1024]{1,0:T(8,128)}), f32[256,1024]{1,0:T(8,128)}) %reduce-scatter.18.cloned.1.call-update) | async-done | bytes 1048592 | tf_op jit(solution)/shard_map/reduce_scatter | solution.py:320
  624.5 1.6 fusion.23
  626.1 39.8 %all-reduce.3 = (f32[1,1024]{1,0:T(1,128)}, f32[1,1024]{1,0:T(1,128)}, f32[1,128]{1,0:T(1,128)}) all-reduce(f32[1,1024]{1,0:T(1,128)S(1)} %bitcast.126, f32[1,1024]{1,0:T(1,128)S(1)} %bitcast.125, f32[1,128]{1,0:T(1,128)S(1)} %get-tuple-element.37), channel_id=1, replica_groups=mesh['fsdp'=8,'tensor'=4] {'fsdp','tensor'}, use_global_device_ids=true, to_apply=%region_9.10 | all-reduce | flops 2176 | bytes 17408 | tf_op jit(solution)/shard_map/psum | solution.py:384
  665.9 6.4 reduce-scatter.14.cloned.1.call-done
  672.3 3.2 fusion.25
  675.5 73.5 %reduce-scatter.26.cloned.1.call-done = f32[704,128]{1,0:T(8,128)} async-done(((f32[704,1024]{1,0:T(8,128)}), f32[704,128]{1,0:T(8,128)}) %reduce-scatter.26.cloned.1.call-update) | async-done | bytes 360464 | tf_op jit(solution)/shard_map/reduce_scatter | solution.py:382
  749.0 114.1 %reduce-scatter.24.cloned.1.call-done = f32[2,128,704]{1,2,0:T(8,128)} async-done(((f32[2,1024,704]{1,2,0:T(8,128)}), f32[2,128,704]{1,2,0:T(8,128)}) %reduce-scatter.24.cloned.1.call-update) | async-done | bytes 720912 | tf_op jit(solution)/shard_map/reduce_scatter | solution.py:380
  863.2 67.9 %reduce-scatter.22.cloned.1.call-done = f32[256,128]{1,0:T(8,128)} async-done(((f32[256,1024]{1,0:T(8,128)}), f32[256,128]{1,0:T(8,128)}) %reduce-scatter.22.cloned.1.call-update) | async-done | bytes 131088 | tf_op jit(solution)/shard_map/reduce_scatter | solution.py:381
  (99 shorter events, 1.8 us)
Async XLA Ops:
  7.2 4.2 copy-start.26
  7.2 26.7 %copy-start.25 = (s32[1,1024]{1,0:T(1,128)S(1)}, s32[1,1024]{1,0:T(1,128)}, u32[]{:S(2)}) copy-start(s32[1,1024]{1,0:T(1,128)} %param.15) | copy-start | bytes 12292
  7.2 26.7 %copy-start.4 = (s32[1,1024]{1,0:T(1,128)S(1)}, s32[1,1024]{1,0:T(1,128)}, u32[]{:S(2)}) copy-start(s32[1,1024]{1,0:T(1,128)} %param.14) | copy-start | bytes 12292
  7.2 27.1 %copy-start.23 = (bf16[1,256,128]{2,1,0:T(8,128)(2,1)S(1)}, bf16[1,256,128]{2,1,0:T(8,128)(2,1)}, u32[]{:S(2)}) copy-start(bf16[1,256,128]{2,1,0:T(8,128)(2,1)} %param.22) | copy-start | bytes 196612
  7.2 57.5 %all-gather.21.cloned.1.call-start = ((), (), s32[]{:S(2)}) async-start(), calls=%async_computation.21 | async-start | bytes 1769472 | tf_op jit(solution)/shard_map/all_gather | solution.py:330
  8.0 78.7 %all-gather.13.cloned.1.call-start = ((), (), s32[]{:S(2)}) async-start(), calls=%async_computation.9 | async-start | bytes 2621440 | tf_op jit(solution)/shard_map/all_gather | solution.py:316
  11.3 155.1 %reduce-scatter.12.cloned.1.call-start = ((), (), s32[]{:S(2)}) async-start(), calls=%async_computation.10 | async-start | bytes 5242880 | tf_op jit(solution)/shard_map/reduce_scatter | solution.py:320
  66.2 26.2 %copy-start.16 = (bf16[1024,256]{1,0:T(8,128)(2,1)}, bf16[1024,256]{1,0:T(8,128)(2,1)S(1)}, u32[]{:S(2)}) copy-start(bf16[1024,256]{1,0:T(8,128)(2,1)S(1)} %get-tuple-element.87) | copy-start | bytes 1572868
  66.2 26.2 %copy-start.18 = (bf16[1024,256]{1,0:T(8,128)(2,1)}, bf16[1024,256]{1,0:T(8,128)(2,1)S(1)}, u32[]{:S(2)}) copy-start(bf16[1024,256]{1,0:T(8,128)(2,1)S(1)} %get-tuple-element.88) | copy-start | bytes 1572868
  66.3 26.2 %copy-start.20 = (bf16[1024,256]{1,0:T(8,128)(2,1)}, bf16[1024,256]{1,0:T(8,128)(2,1)S(1)}, u32[]{:S(2)}) copy-start(bf16[1024,256]{1,0:T(8,128)(2,1)S(1)} %get-tuple-element.89) | copy-start | bytes 1572868
  86.7 5.8 copy-start.5
  86.7 5.8 copy-start.6
  92.5 26.6 %copy-start.15 = (bf16[1,256,1024]{2,1,0:T(8,128)(2,1)S(1)}, bf16[1,256,1024]{2,1,0:T(8,128)(2,1)}, u32[]{:S(2)}) copy-start(bf16[1,256,1024]{2,1,0:T(8,128)(2,1)} %all-gather.2) | copy-start | bytes 1572868
  117.0 1.0 copy-start
  118.0 1.0 copy-start.2
  121.8 47.2 %copy-start.22 = (f32[1,1024]{1,0:T(1,128)S(1)}, f32[1,1024]{1,0:T(1,128)}, u32[]{:S(2)}) copy-start(f32[1,1024]{1,0:T(1,128)} %param.17) | copy-start | bytes 12292
  121.8 106.8 %all-gather.23.cloned.1.call-start = ((), (), s32[]{:S(2)}) async-start(), calls=%async_computation.22 | async-start | bytes 3244032 | tf_op jit(solution)/shard_map/all_gather | solution.py:332
  122.4 129.1 %all-gather.15.cloned.1.call-start = ((), (), s32[]{:S(2)}) async-start(), calls=%async_computation.11 | async-start | bytes 2621440 | tf_op jit(solution)/shard_map/all_gather | solution.py:316
  168.0 1.0 copy-start.7
  170.0 127.4 %all-gather.25.cloned.1.call-start = ((), (), s32[]{:S(2)}) async-start(), calls=%async_computation.23 | async-start | bytes 1622016 | tf_op jit(solution)/shard_map/all_gather | solution.py:334
  170.5 149.5 %all-gather.17.cloned.1.call-start = ((), (), s32[]{:S(2)}) async-start(), calls=%async_computation.13 | async-start | bytes 2621440 | tf_op jit(solution)/shard_map/all_gather | solution.py:316
  171.3 207.8 %reduce-scatter.16.cloned.1.call-start = ((), (), s32[]{:S(2)}) async-start(), calls=%async_computation.14 | async-start | bytes 5242880 | tf_op jit(solution)/shard_map/reduce_scatter | solution.py:320
  320.1 9.4 %copy-start.27 = (bf16[1,2,1024,704]{2,3,1,0:T(8,128)(2,1)S(1)}, bf16[1,2,1024,704]{2,3,1,0:T(8,128)(2,1)}, u32[]{:S(2)}) copy-start(bf16[1,2,1024,704]{2,3,1,0:T(8,128)(2,1)} %all-gather.23.cloned.1.call-done) | copy-start | bytes 8650756
  327.8 1.1 copy-start.32
  327.8 1.7 copy-start.33
  334.5 71.7 %all-gather.19.cloned.1.call-start = ((), (), s32[]{:S(2)}) async-start(), calls=%async_computation.15 | async-start | bytes 2621440 | tf_op jit(solution)/shard_map/all_gather | solution.py:316
  379.1 2.0 copy-start.8
  379.1 2.2 copy-start.11
  383.5 127.5 %reduce-scatter.28.cloned.1.call-start = ((), (), s32[]{:S(2)}) async-start(), calls=%async_computation.24 | async-start | bytes 589824
  406.2 2.6 copy-start.1
  406.2 2.6 copy-start.3
  408.8 23.5 %copy-start.28 = (bf16[1024,1024]{1,0:T(8,128)(2,1)S(1)}, bf16[1024,1024]{1,0:T(8,128)(2,1)}, u32[]{:S(2)}) copy-start(bf16[1024,1024]{1,0:T(8,128)(2,1)} %all-gather.13.cloned.1.call-done) | copy-start | bytes 6291460
  438.3 140.1 %reduce-scatter.20.cloned.1.call-start = ((), (), s32[]{:S(2)}) async-start(), calls=%async_computation.17 | async-start | bytes 3538944 | tf_op jit(solution)/shard_map/reduce_scatter | solution.py:378
  441.6 1.0 copy-start.17
  441.6 1.2 copy-start.19
  441.6 1.4 copy-start.21
  441.6 182.9 %reduce-scatter.18.cloned.1.call-start = ((), (), s32[]{:S(2)}) async-start(), calls=%async_computation.16 | async-start | bytes 5242880 | tf_op jit(solution)/shard_map/reduce_scatter | solution.py:320
  448.8 1.4 copy-start.31
  448.9 223.4 %reduce-scatter.14.cloned.1.call-start = ((), (), s32[]{:S(2)}) async-start(), calls=%async_computation.12 | async-start | bytes 5242880 | tf_op jit(solution)/shard_map/reduce_scatter | solution.py:320
  455.5 1.6 copy-start.30
  455.5 293.5 %reduce-scatter.26.cloned.1.call-start = ((), (), s32[]{:S(2)}) async-start(), calls=%async_computation.20 | async-start | bytes 3244032 | tf_op jit(solution)/shard_map/reduce_scatter | solution.py:382
  461.7 1.6 copy-start.29
  461.7 401.4 %reduce-scatter.24.cloned.1.call-start = ((), (), s32[]{:S(2)}) async-start(), calls=%async_computation.19 | async-start | bytes 6488064 | tf_op jit(solution)/shard_map/reduce_scatter | solution.py:380
  470.2 1.6 copy-start.14
  470.2 154.3 %copy-start.10 = (bf16[256,1024]{1,0:T(8,128)(2,1)S(1)}, bf16[256,1024]{1,0:T(8,128)(2,1)}, u32[]{:S(2)}) copy-start(bf16[256,1024]{1,0:T(8,128)(2,1)} %param.13) | copy-start | bytes 1572868
  470.2 154.3 %copy-start.24 = (f32[1,1024]{1,0:T(1,128)S(1)}, f32[1,1024]{1,0:T(1,128)}, u32[]{:S(2)}) copy-start(f32[1,1024]{1,0:T(1,128)} %param.16) | copy-start | bytes 12292
  470.2 460.8 %reduce-scatter.22.cloned.1.call-start = ((), (), s32[]{:S(2)}) async-start(), calls=%async_computation.18 | async-start | bytes 1179648 | tf_op jit(solution)/shard_map/reduce_scatter | solution.py:381
  473.4 198.8 %copy-start.9 = (f32[256,1024]{1,0:T(8,128)S(1)}, f32[256,1024]{1,0:T(8,128)}, u32[]{:S(2)}) copy-start(f32[256,1024]{1,0:T(8,128)} %copy-done.7) | copy-start | bytes 3145732
  473.4 198.8 %copy-start.12 = (f32[256,1024]{1,0:T(8,128)S(1)}, f32[256,1024]{1,0:T(8,128)}, u32[]{:S(2)}) copy-start(f32[256,1024]{1,0:T(8,128)} %reduce-scatter.16.cloned.1.call-done) | copy-start | bytes 3145732
  473.4 198.8 %copy-start.13 = (bf16[256,1024]{1,0:T(8,128)(2,1)S(1)}, bf16[256,1024]{1,0:T(8,128)(2,1)}, u32[]{:S(2)}) copy-start(bf16[256,1024]{1,0:T(8,128)(2,1)} %param.25) | copy-start | bytes 1572868
Sparse Core Ops, SparseCore 0:
  10.2 50.4 all-gather.20
  62.9 23.7 all-gather.12
  121.9 44.4 reduce-scatter.11
  168.5 60.0 all-gather.22
  230.6 20.7 all-gather.14
  253.6 43.8 all-gather.24
  299.0 20.9 all-gather.16
  334.6 44.4 reduce-scatter.15
  383.6 22.5 all-gather.18
  438.4 61.8 reduce-scatter.27
  504.3 73.9 reduce-scatter.19
  580.9 43.5 reduce-scatter.17
  627.0 45.1 reduce-scatter.13
  676.7 72.2 reduce-scatter.25
  753.6 109.5 reduce-scatter.23
  867.4 63.6 reduce-scatter.21

commit v2 on v1

--- a/solution.py
+++ b/solution.py
@@ -304,86 +304,253 @@
     return jnp.stack(cols, axis=1)
 
 
-def rms_norm(value_rows, gain):
-    return (
-        value_rows
-        * lax.rsqrt(jnp.mean(value_rows * value_rows, axis=-1, keepdims=True) + 1e-06)
-        * gain
-    )
-
-
-def gather_t(value):
-    return lax.all_gather(value, "tensor", axis=0, tiled=True)
-
-
-def scatter_t(value):
-    return lax.psum_scatter(value, "tensor", scatter_dimension=0, tiled=True)
+def hop(value, axis, bit):
+    n = lax.axis_size(axis)
+    return lax.ppermute(value, axis, [(i, i ^ bit) for i in range(n)])
+
+
+def tensor_bits():
+    n = lax.axis_size("tensor")
+    bits = []
+    while n > 1:
+        n //= 2
+        bits.append(n)
+    return bits
+
+
+def gather_relative(value):
+    blocks = value[None]
+    for bit in tensor_bits():
+        blocks = jnp.concatenate([blocks, hop(blocks, "tensor", bit)], axis=0)
+    return blocks
+
+
+def relative_order():
+    order = [0]
+    for bit in tensor_bits():
+        order = order + [k ^ bit for k in order]
+    return order
+
+
+def gather_rows(value):
+    n = lax.axis_size("tensor")
+    me = lax.axis_index("tensor")
+    blocks = [(0, value)]
+    for bit in tensor_bits():
+        sent = jnp.stack([b for _, b in blocks])
+        got = hop(sent, "tensor", bit)
+        blocks = blocks + [(k ^ bit, got[i]) for i, (k, _) in enumerate(blocks)]
+    full = jnp.zeros((n,) + value.shape, value.dtype)
+    for k, b in blocks:
+        full = lax.dynamic_update_slice(full, b[None], (me ^ k,) + (0,) * value.ndim)
+    return full.reshape((n * value.shape[0],) + value.shape[1:])
+
+
+def ring_order(n):
+    return [i for i in range(0, n, 2)] + [i for i in reversed(range(1, n, 2))]
+
+
+def ring_gather(value):
+    n = lax.axis_size("fsdp")
+    order = ring_order(n)
+    place = jnp.array([order.index(i) for i in range(n)], jnp.int32)
+    there = jnp.array(order, jnp.int32)
+    me = place[lax.axis_index("fsdp")]
+    right = [(order[i], order[(i + 1) % n]) for i in range(n)]
+    left = [(b, a) for a, b in right]
+    rows = value.shape[0]
+    full = jnp.zeros((n * rows,) + value.shape[1:], value.dtype)
+
+    def put(full, part, steps, start):
+        owner = there[lax.rem(me + steps + n, n)]
+        return lax.dynamic_update_slice(full, part, (owner * rows + start,) + (0,) * (value.ndim - 1))
+
+    full = put(full, value, 0, 0)
+    a = b = value
+    for k in range(1, n // 2 + 1):
+        if 2 * k == n and rows % 32 == 0:
+            half = rows // 2
+            a = lax.ppermute(a[:half], "fsdp", right)
+            b = lax.ppermute(b[half:], "fsdp", left)
+            full = put(put(full, a, -k, 0), b, k, half)
+        else:
+            a = lax.ppermute(a, "fsdp", right)
+            full = put(full, a, -k, 0)
+            if 2 * k < n:
+                b = lax.ppermute(b, "fsdp", left)
+                full = put(full, b, k, 0)
+    return full
+
+
+def owner_sum(parts):
+    n = lax.axis_size("fsdp")
+    me = lax.axis_index("fsdp")
+    total = lax.dynamic_index_in_dim(parts, me, 0, keepdims=False).astype(F32)
+    got = []
+    for k in range(1, n):
+        block = lax.dynamic_index_in_dim(parts, me ^ k, 0, keepdims=False)
+        got.append(hop(block, "fsdp", k))
+    for g in got:
+        total = total + g.astype(F32)
+    return total
+
+
+def all_sum(value, axis):
+    n = lax.axis_size(axis)
+    bit = 1
+    while bit < n:
+        value = value + hop(value, axis, bit)
+        bit *= 2
+    return value
+
+
+def core_scatter(parts):
+    core = lax.axis_index("tensor") % 2
+    mine = lax.dynamic_index_in_dim(parts, core, 1, keepdims=False)
+    theirs = lax.dynamic_index_in_dim(parts, 1 - core, 1, keepdims=False).astype(BF)
+    return mine + hop(theirs, "tensor", 1).astype(F32)
+
+
+def scatter_rows(parts):
+    n = lax.axis_size("tensor")
+    rows = parts.shape[0] // n
+    blocks = core_scatter(parts.reshape(n // 2, 2, rows, parts.shape[1]))
+    chip = lax.axis_index("tensor") // 2
+    total = lax.dynamic_index_in_dim(blocks, chip, 0, keepdims=False)
+    for k in range(1, n // 2):
+        sent = lax.dynamic_index_in_dim(blocks, chip ^ k, 0, keepdims=False).astype(BF)
+        total = total + hop(sent, "tensor", 2 * k).astype(F32)
+    return total
+
+
+def norm_factor(rows):
+    return lax.rsqrt(jnp.mean(rows * rows, axis=-1, keepdims=True) + 1e-06)
+
+
+def norm_grad(rows, factor, gain, d_normed):
+    u = d_normed * gain
+    return factor * u - rows * (factor * factor * factor) * jnp.mean(u * rows, axis=-1, keepdims=True)
 
 
 def on_device(
     layer_input, segment_ids, pad_mask, attn_gain, ffn_gain, out_gain,
     qkv_weight, beta_weight, conv_weight, out_weight, expand_weight, down_weight, cotangent,
 ):
-    resid = layer_input.astype(F32)
+    n_t = lax.axis_size("tensor")
+    n_f = lax.axis_size("fsdp")
+    me_t = lax.axis_index("tensor")
+    core = me_t % 2
+    rows, d_model = layer_input.shape
+    tokens = n_t * rows
     width = qkv_weight.shape[3]
     heads = beta_weight.shape[2]
-    qkv_full = lax.all_gather(qkv_weight[0], "fsdp", axis=1, tiled=True)
-    beta_full = lax.all_gather(beta_weight[0], "fsdp", axis=0, tiled=True)
-    expand_full = lax.all_gather(expand_weight[0], "fsdp", axis=1, tiled=True)
-    out_full = lax.all_gather(out_weight[0], "fsdp", axis=1, tiled=True)
-    down_full = lax.all_gather(down_weight[0], "fsdp", axis=1, tiled=True)
-    wide = jnp.concatenate(
-        [qkv_full[0], qkv_full[1], qkv_full[2], jnp.pad(beta_full, ((0, 0), (0, HEAD - heads)))], axis=1
-    )
-    normed = rms_norm(resid, attn_gain[0]).astype(BF)
-    gathered = gather_t(normed)
-    pre = jnp.dot(gathered, wide, preferred_element_type=F32)
+    ff = down_weight.shape[1]
+    shard = qkv_weight.shape[2]
+
+    w = qkv_weight[0]
+    wide_own = jnp.concatenate(
+        [w[0], w[1], w[2], jnp.pad(beta_weight[0], ((0, 0), (0, HEAD - heads)))], axis=1
+    )
+    ffn_own = jnp.concatenate(
+        [expand_weight[0, 0].T, expand_weight[0, 1].T, down_weight[0], out_weight[0]], axis=0
+    )
+    wide = ring_gather(wide_own)
+    x_full = gather_rows(layer_input)
+    ffn_all = lax.all_gather(ffn_own, "fsdp", axis=1, tiled=True)
+    g_f = gather_rows(cotangent)
+
     seg = segment_ids[0]
     cols = columns(seg, pad_mask[0])
     segr = seg.astype(F32)[None]
+
+    x_rows = x_full.astype(F32)
+    factor_a = norm_factor(x_rows)
+    normed_a = (x_rows * factor_a * attn_gain).astype(BF)
+    pre = jnp.dot(normed_a, wide, preferred_element_type=F32)
     mixed, *kept = mixer_fwd(pre, cols, segr, seg, conv_weight[0], out_gain)
-    resid_mid = resid + scatter_t(jnp.dot(mixed, out_full, preferred_element_type=F32))
-    normed_ffn = rms_norm(resid_mid, ffn_gain[0]).astype(BF)
-    gathered_ffn = gather_t(normed_ffn)
-    expanded = jnp.einsum("ld,sdf->slf", gathered_ffn, expand_full, preferred_element_type=F32)
-    gate, up = expanded[0], expanded[1]
+
+    expand_t = ffn_all[:2 * ff]
+    down = ffn_all[2 * ff:3 * ff]
+    out_own = ffn_all[3 * ff:]
+    out_rel = gather_relative(out_own).reshape(n_t * width, d_model)
+    mixed_rel = gather_relative(mixed)
+    mixed_rel = jnp.concatenate([mixed_rel[i] for i in range(n_t)], axis=1)
+    x_mid = x_rows + jnp.dot(mixed_rel, out_rel, preferred_element_type=F32)
+    factor_f = norm_factor(x_mid)
+    normed_f = (x_mid * factor_f * ffn_gain).astype(BF)
+
+    expanded = lax.dot_general(expand_t, normed_f, NT, preferred_element_type=F32)
+    gate, up = expanded[:ff], expanded[ff:]
+    d_hidden = lax.dot_general(down, g_f, NT, preferred_element_type=F32)
     sig = jax.nn.sigmoid(gate)
     hidden = (gate * sig * up).astype(BF)
-    resid_out = resid_mid + scatter_t(jnp.dot(hidden, down_full, preferred_element_type=F32))
-    block_outs = resid_out.astype(BF)[None]
-
-    grad = cotangent.astype(F32)
-    grad_full = gather_t(cotangent)
-    d_hidden = lax.dot_general(grad_full, down_full, NT, preferred_element_type=F32)
-    d_down = lax.dot_general(hidden, grad_full, TN, preferred_element_type=F32)
     d_gate = d_hidden * up * sig * (1.0 + gate * (1.0 - sig))
     d_up = d_hidden * gate * sig
-    d_expanded = jnp.stack([d_gate, d_up]).astype(BF)
-    d_expand = jnp.einsum("ld,slf->sdf", gathered_ffn, d_expanded, preferred_element_type=F32)
-    d_normed_ffn = scatter_t(jnp.einsum("slf,sdf->ld", d_expanded, expand_full, preferred_element_type=F32))
-    unused, norm_back = jax.vjp(rms_norm, resid_mid, ffn_gain[0])
-    d_mid, d_ffn_gain = norm_back(d_normed_ffn)
-    grad = grad + d_mid
-    grad_full = gather_t(grad.astype(BF))
-    d_mixed = lax.dot_general(grad_full, out_full, NT, preferred_element_type=F32)
-    d_out = lax.dot_general(mixed, grad_full, TN, preferred_element_type=F32)
+    d_expanded = jnp.concatenate([d_gate.astype(BF), d_up.astype(BF)], axis=0)
+
+    d_nf = lax.dot_general(d_expanded, expand_t, TN, preferred_element_type=F32)
+    d_ffn_gain = jnp.sum(d_nf * (x_mid * factor_f), axis=0)
+    d_nf = core_scatter(d_nf.reshape(n_t // 2, 2, rows, d_model))
+    low = d_nf.astype(BF)
+    d_nf = low.astype(F32)
+    for k in range(1, n_t // 2):
+        d_nf = d_nf + hop(low, "tensor", 2 * k).astype(F32)
+
+    def of_core(full):
+        return lax.dynamic_index_in_dim(full.reshape(n_t // 2, 2, rows, full.shape[1]), core, 1, keepdims=False)
+
+    grad = of_core(g_f).astype(F32) + norm_grad(of_core(x_mid), of_core(factor_f), ffn_gain, d_nf)
+    g_low = grad.astype(BF)
+    other = hop(g_low, "tensor", 1)
+    g_a = jnp.zeros((n_t // 2, 2, rows, d_model), BF)
+    g_a = lax.dynamic_update_slice(g_a, g_low[:, None], (0, core, 0, 0))
+    g_a = lax.dynamic_update_slice(g_a, other[:, None], (0, 1 - core, 0, 0))
+    g_a = g_a.reshape(tokens, d_model)
+    grad_own = lax.dynamic_index_in_dim(grad, me_t // 2, 0, keepdims=False)
+
+    d_down = jnp.dot(hidden, g_f, preferred_element_type=BF)
+    d_expand = jnp.dot(d_expanded, normed_f, preferred_element_type=BF)
+    d_ffn = lax.psum_scatter(
+        jnp.concatenate([d_expand, d_down], axis=0), "fsdp", scatter_dimension=1, tiled=True
+    )
+
+    d_mixed = lax.dot_general(g_a, out_own, NT, preferred_element_type=F32)
     d_wide, d_taps, d_head = mixer_bwd(d_mixed, pre, cols, segr, seg, conv_weight[0], out_gain, kept)
-    d_all = lax.dot_general(gathered, d_wide, TN, preferred_element_type=F32)
-    d_qkv = jnp.stack([d_all[:, i * width:(i + 1) * width] for i in range(3)])
-    d_beta = d_all[:, 3 * width:3 * width + heads]
-    d_normed = scatter_t(lax.dot_general(d_wide, wide, NT, preferred_element_type=F32))
-    unused, norm_back = jax.vjp(rms_norm, resid, attn_gain[0])
-    d_resid, d_attn_gain = norm_back(d_normed)
-    grad = grad + d_resid
-    qkv_grad = lax.psum_scatter(d_qkv, "fsdp", scatter_dimension=1, tiled=True)
-    beta_grad = lax.psum_scatter(d_beta, "fsdp", scatter_dimension=0, tiled=True)
-    expand_grad = lax.psum_scatter(d_expand, "fsdp", scatter_dimension=1, tiled=True)
-    out_grad = lax.psum_scatter(d_out, "fsdp", scatter_dimension=1, tiled=True)
-    down_grad = lax.psum_scatter(d_down, "fsdp", scatter_dimension=1, tiled=True)
-    conv_grad = lax.psum(d_taps, "fsdp")
-    attn_total, ffn_total, head_total = lax.psum((d_attn_gain[None], d_ffn_gain[None], d_head), ("fsdp", "tensor"))
+    d_out = lax.dot_general(mixed, g_a, TN, preferred_element_type=F32).astype(BF)
+    out_grad = owner_sum(d_out.reshape(width, n_f, shard).transpose(1, 0, 2))
+
+    ffn_part = lax.dot_general(hidden, down, TN, preferred_element_type=F32)
+    own_mid = lax.dynamic_slice(x_mid, (me_t * rows, 0), (rows, d_model))
+    block_outs = (own_mid + scatter_rows(ffn_part)).astype(BF)[None]
+
+    d_all = lax.dot_general(normed_a, d_wide, TN, preferred_element_type=F32)
+    qkv_sum = owner_sum(d_all[:, :3 * width].astype(BF).reshape(n_f, shard, 3 * width))
+    qkv_grad = jnp.stack([qkv_sum[:, i * width:(i + 1) * width] for i in range(3)])
+    d_na = lax.dot_general(d_wide, wide, NT, preferred_element_type=F32)
+    d_attn_gain = jnp.sum(d_na * (x_rows * factor_a), axis=0)
+    d_na = scatter_rows(d_na)
+    own_x = layer_input.astype(F32)
+    input_grad = grad_own + norm_grad(own_x, norm_factor(own_x), attn_gain, d_na)
+
+    gains = jnp.concatenate([d_attn_gain, d_ffn_gain, d_head[0]]).reshape(-1, HEAD)
+    gains = all_sum(gains, "tensor")
+    d_beta = d_all[:, 3 * width:3 * width + heads].T.reshape(-1, HEAD)
+    taps = d_taps.reshape(-1, HEAD)
+    small = all_sum(jnp.concatenate([taps, d_beta, gains], axis=0), "fsdp")
+    n1 = taps.shape[0]
+    n2 = n1 + d_beta.shape[0]
+    conv_grad = small[:n1].reshape(d_taps.shape)
+    beta_all = small[n1:n2].reshape(heads, d_model)
+    beta_grad = lax.dynamic_slice(beta_all, (0, lax.axis_index("fsdp") * shard), (heads, shard)).T
+    gains = small[n2:].reshape(-1)
+    attn_total = gains[:d_model][None]
+    ffn_total = gains[d_model:2 * d_model][None]
+    head_total = gains[2 * d_model:][None]
+
+    expand_grad = jnp.stack([d_ffn[:ff].T, d_ffn[ff:2 * ff].T]).astype(F32)
+    down_grad = d_ffn[2 * ff:].astype(F32)
     return (
-        block_outs, grad, attn_total, ffn_total, head_total, qkv_grad[None], beta_grad[None],
+        block_outs, input_grad, attn_total, ffn_total, head_total, qkv_grad[None], beta_grad[None],
         conv_grad[None], out_grad[None], expand_grad[None], down_grad[None],
     )
 

time: 939 us -> 337 us (0.36)
  the two profiles are of different devices: /device:TPU:0 before, /device:TPU:9 now
where the time goes in v2:
time: 337 us; the launch traced here: 331 us
  waiting for transfers between devices  68.5 us (20%)
  starting transfers between devices  66 us (20%)
  Pallas kernels  48.7 us (14%)
  matrix products  44.3 us (13%)
  local copies, waits for them, and re-layouts  41.7 us (12%)
  other arithmetic  34.6 us (10%)
  between operations  27.2 us (8%)
    ppermute x34, starting transfers between devices, hop(): return lax.ppermute(value, axis, [(i, i ^ bit) for i in range(n)])  53.4 us
    ppermute x34, waiting for transfers between devices, hop(): return lax.ppermute(value, axis, [(i, i ^ bit) for i in range(n)])  44.7 us
    pallas_call x1, Pallas kernels, mixer_fwd(): pl.pallas_call(functools.partial(fwd_kernel, heads, cb), grid_spec=pltpu....  24.7 us
    pallas_call x1, Pallas kernels, mixer_bwd(): pl.pallas_call(functools.partial(bwd_kernel, heads, cb), grid_spec=pltpu....  24 us
    unnamed x109, local copies, waits for them, and re-layouts  13.6 us
    ppermute x3, waiting for transfers between devices, ring_gather(): a = lax.ppermute(a, 'fsdp', right)  10.9 us
    ppermute x3, starting transfers between devices, ring_gather(): a = lax.ppermute(a, 'fsdp', right)  9.02 us
    all_gather x1, waiting for transfers between devices, on_device(): ffn_all = lax.all_gather(ffn_own, 'fsdp', axis=1, tiled=True)  8.85 us
  transfers between devices with their start and end apart: 44, of which 16 were waited for; matrix products, arithmetic and copies ran while one was open for 28% of the time, Pallas kernels for 15%

profile of v2, /device:TPU:9, one launch (start us, length us, event | category | flops | bytes accessed | tf_op | source)
XLA Modules:
  0.0 331.0 jit_solution(11421725709517161321)
XLA Ops:
  8.4 1.8 pad_maximum_fusion.9
  18.5 1.3 collective-permute-start.2
  27.6 3.0 collective-permute-done.2
  30.6 2.3 collective-permute-start.4
  33.0 3.2 collective-permute-start.1
  36.3 7.6 %collective-permute-done.4 = bf16[128,896]{1,0:T(8,128)(2,1)S(1)} collective-permute-done((bf16[128,896]{1,0:T(8,128)(2,1)S(1)}, bf16[128,896]{1,0:T(8,128)(2,1)S(1)}, u32[]{:S(2)}, u32[]{:S(2)}) %collective-permute-start.4) | collective-permute-done | bytes 229408 | tf_op jit(solution)/shard_map/ppermute | solution.py:377
  43.9 5.4 %collective-permute-start.6 = (bf16[128,896]{1,0:T(8,128)(2,1)S(1)}, bf16[128,896]{1,0:T(8,128)(2,1)S(1)}, u32[]{:S(2)}, u32[]{:S(2)}) collective-permute-start(bf16[128,896]{1,0:T(8,128)(2,1)S(1)} %collective-permute-done.4), channel_id=1, source_target_pairs={{0,8},{8,16},{16,24},{24,28},{28,20},{20,12},{12,4},{4,0},{1,9},{9... | collective-permute-start | bytes 688136 | tf_op jit(solution)/shard_map/ppermute | solution.py:377
  50.5 3.3 collective-permute-start.17
  54.2 2.4 collective-permute-start.8
  59.0 2.6 collective-permute-done.9
  63.3 4.2 %fusion.72.pre_ref = f32[1024,896]{1,0:T(8,128)} fusion(bf16[1024,1024]{1,0:T(8,128)(2,1)S(1)} %fusion.2, bf16[1024,896]{1,0:T(8,128)(2,1)S(1)} %constant_dynamic-update-slice_fusion.2), kind=kOutput, calls=%fused_computation.185 | convolution fusion | flops 1879048192 | bytes 7602176 | tf_op jit(solution)/shard_map/dot_general | solution.py:469
  67.5 24.7 %mixer_fwd.1 = (bf16[1024,256]{1,0:T(8,128)(2,1)S(1)}, f32[1024,768]{1,0:T(8,128)}, f32[1024,256]{1,0:T(8,128)S(1)}, f32[8,2,128,128]{3,2,1,0:T(8,128)S(1)}, f32...) custom-call(s32[1024]{0:T(1024)S(1)} %bitcast.268, ...), custom_call_target="tpu_custom_call" | custom-call | tf_op jit(solution)/shard_map/mixer_fwd/pallas_call | solution.py:256
  95.2 8.9 %all-gather.2.cloned.1.call-done = bf16[2368,1024]{1,0:T(8,128)(2,1)} async-done(((bf16[2368,128]{1,0:T(8,128)(2,1)}), bf16[2368,1024]{1,0:T(8,128)(2,1)}) %all-gather.2.cloned.1.call-update) | async-done | bytes 4849680 | tf_op jit(solution)/shard_map/all_gather | solution.py:459
  104.1 1.9 slice_bitcast_fusion.3
  107.1 2.1 pad_maximum_fusion.6
  109.2 12.8 %collective-permute-start.11 = (bf16[2,1024,256]{2,1,0:T(8,128)(2,1)}, bf16[2,1024,256]{2,1,0:T(8,128)(2,1)}, u32[]{:S(2)}, u32[]{:S(2)}) collective-permute-start(bf16[2,1024,256]{2,1,0:T(8,128)(2,1)} %pad_maximum_fusion.6), channel_id=1, source_target_pairs={{0,1},{1,0},{2,3},{3,2},{4,5},{5,4},{6,7},{7,6},{8,9},{9,8},{10,11... | collective-permute-start | bytes 3145736 | tf_op jit(solution)/shard_map/ppermute | solution.py:309
  122.1 1.4 pad_maximum_fusion.7
  123.4 3.8 %collective-permute-start.13 = (bf16[2,256,1024]{2,1,0:T(8,128)(2,1)S(1)}, bf16[2,256,1024]{2,1,0:T(8,128)(2,1)S(1)}, u32[]{:S(2)}, u32[]{:S(2)}) collective-permute-start(bf16[2,256,1024]{2,1,0:T(8,128)(2,1)S(1)} %pad_maximum_fusion.7), channel_id=1, source_target_pairs={{0,1},{1,0},{2,3},{3,2},{4,5},{5,4},{6,7},{7,6},{8,9},{9,8},{10,11... | collective-permute-start | bytes 3145736 | tf_op jit(solution)/shard_map/ppermute | solution.py:309
  129.8 2.0 slice_bitcast_fusion.2
  131.8 1.6 pad_maximum_fusion.2
  133.7 3.8 %multiply_reduce_fusion.1 = (f32[1024]{0:T(1024)S(1)}, f32[1024,1024]{1,0:T(8,128)S(1)}) fusion(bf16[1024,1024]{1,0:T(8,128)(2,1)S(1)} %bitcast.290, bf16[1024,256]{1,0:T(8,128)(2,1)S(1)} %get-tuple-element.55, bf16[1024,256]{1,0:T(8,128)(2,1)S(1)} %get-tuple-element.54, bf16[1024,256]{1,0:T(8,128)(2,1)} %bitcast.36, ...), kind=kOutput, calls=%fused_computation.11 | convolution fusion | flops 2160065536 | bytes 10489856 | tf_op jit(solution)/shard_map/dot_general | solution.py:478
  137.6 3.4 %fusion.7 = f32[1408,1024]{1,0:T(8,128)S(1)} fusion(bf16[2368,1024]{1,0:T(8,128)(2,1)S(1)} %bitcast.303, f32[1024,1024]{1,0:T(8,128)S(1)} %get-tuple-element.95, f32[1024]{0:T(1024)S(1)} %bitcast.307, f32[1024]{0:T(1024)S(1)} %add_rsqrt_fusion), kind=kOutput, calls=%fused_computation.20 | convolution fusion | flops 2955935744 | bytes 12853248 | tf_op jit(solution)/shard_map/dot_general | solution.py:482
  141.0 3.2 multiply_convert_fusion.2
  144.2 3.7 %multiply_reduce_fusion = (f32[1024]{0:T(1024)S(1)}, f32[1024,1024]{1,0:T(8,128)S(1)}) fusion(f32[1024,1024]{1,0:T(8,128)S(1)} %get-tuple-element.95, f32[1024]{0:T(1024)S(1)} %add_rsqrt_fusion, bf16[2368,1024]{1,0:T(8,128)(2,1)S(1)} %bitcast.303, bf16[704,1024]{1,0:T(8,128)(2,1)S(1)} %get-tuple-element.45, bf16[704,1024]{1,0:T(8,128)(2,1)S(1)} %get-tuple-element.44), kind=kOutput, calls=%fused_computation.9 | convolution fusion | flops 2961701888 | bytes 14163968 | tf_op jit(solution)/shard_map/dot_general | solution.py:491
  148.8 1.7 fusion.74
  150.5 5.0 %fusion.23 = bf16[1408,1024]{1,0:T(8,128)(2,1)S(1)} fusion(bf16[704,1024]{1,0:T(8,128)(2,1)S(1)} %get-tuple-element.45, bf16[704,1024]{1,0:T(8,128)(2,1)S(1)} %get-tuple-element.44, f32[1024,1024]{1,0:T(8,128)S(1)} %get-tuple-element.95, f32[1024]{0:T(1024)S(1)} %bitcast.308, f32[1024]{0:T(1024)S(1)} %add_rsqrt_fusion), kind=kOutput, calls=%fused_computation.45 | convolution fusion | flops 2961702912 | bytes 9969664 | tf_op jit(solution)/shard_map/dot_general | solution.py:512
  155.5 1.4 fusion.20
  157.0 1.5 collective-permute-start.19
  158.5 2.5 pad_maximum_fusion
  161.1 6.7 %copy.88 = bf16[2112,1024]{0,1:T(8,128)(2,1)} copy(bf16[2112,1024]{1,0:T(8,128)(2,1)} %pad_maximum_fusion) | data formatting | bytes 8650752
  167.8 5.9 %fusion.26 = f32[1024,1024]{1,0:T(8,128)} fusion(bf16[704,1024]{1,0:T(8,128)(2,1)} %copy-done.44, bf16[2368,1024]{1,0:T(8,128)(2,1)} %all-gather.2.cloned.1.call-done), kind=kOutput, calls=%fused_computation.52 | convolution fusion | flops 1476395008 | bytes 7077888 | tf_op jit(solution)/shard_map/dot_general | solution.py:522
  173.7 2.8 fusion.35
  176.8 5.4 %collective-permute-done.19 = bf16[2,256,1024]{2,1,0:T(8,128)(2,1)} collective-permute-done((bf16[2,256,1024]{2,1,0:T(8,128)(2,1)}, bf16[2,256,1024]{2,1,0:T(8,128)(2,1)}, u32[]{:S(2)}, u32[]{:S(2)}) %collective-permute-start.19) | collective-permute-done | bytes 1048608 | tf_op jit(solution)/shard_map/ppermute | solution.py:309
  182.2 2.1 fusion.19
  184.3 1.6 broadcast_in_dim.63
  186.7 4.3 %bitcast_dynamic-update-slice_fusion.1 = (bf16[2,2,256,1024]{3,2,1,0:T(8,128)(2,1)}, bf16[2,256,1024]{2,1,0:T(8,128)(2,1)}, f32[2,256,1024]{2,1,0:T(8,128)}) fusion(bf16[2,2,256,1024]{3,2,1,0:T(8,128)(2,1)} %broadcast_in_dim.63, s32[]{:T(128)S(6)} %select_n.183, f32[2,256]{1,0:T(2,128)S(1)} %broadcast_multiply_fusion, ...), kind=kLoop, calls=%fused_computation.68 | loop fusion | flops 5767168 | bytes 9447428 | tf_op jit(solution)/shard_map/dynamic_update_slice | solution.py:506
  191.7 2.3 bitcast_add_fusion.3
  195.0 1.5 collective-permute-start.15
  196.4 2.3 bitcast_dynamic-update-slice_fusion
  198.7 2.3 fusion.28
  201.2 2.6 fusion.43.dmix_ref
  203.9 24.0 %mixer_bwd.1 = (bf16[1024,896]{1,0:T(8,128)(2,1)}, f32[3,4,256]{2,1,0:T(4,128)S(1)}, f32[1,128]{1,0:T(1,128)S(1)}) custom-call(s32[1024]{0:T(1024)S(1)} %bitcast.269, f32[1024,256]{1,0:T(8,128)S(1)} %fusion.43.dmix_ref, f32[1024,896]{1,0:T(8,128)} %fusion.72.pre_ref, f32[1024,768]{1,0:T(8,128)} %get-tuple-element.26.conv_ref, ...), custom_call_target="tpu_custom_call" | custom-call | tf_op jit(solution)/shard_map/mixer_bwd/pallas_call | solution.py:281
  227.9 6.1 %fusion.3 = (f32[1024]{0:T(1024)S(1)}, f32[1024,1024]{1,0:T(8,128)}) fusion(bf16[4,256,1024]{2,1,0:T(8,128)(2,1)S(1)} %copy-done.9, f32[1024]{0:T(1024)S(1)} %bitcast.314, bf16[1024,896]{1,0:T(8,128)(2,1)} %get-tuple-element.36, bf16[1024,896]{1,0:T(8,128)(2,1)S(1)} %copy-done.28), kind=kOutput, calls=%fused_computation.7 | convolution fusion | flops 1883241472 | bytes 9969664 | tf_op jit(solution)/shard_map/dot_general | solution.py:529
  234.3 2.4 fusion.73
  236.8 1.9 constant_dynamic-slice_fusion.7
  240.6 2.6 collective-permute-start.37
  243.7 2.6 collective-permute-done.24
  247.1 1.8 fusion.36
  248.8 1.5 collective-permute-done.25
  250.4 2.3 collective-permute-start.21
  252.8 2.5 fusion.42
  255.3 2.1 slice.215
  258.3 1.6 collective-permute-start.39
  260.3 2.1 collective-permute-start.41
  263.5 1.8 collective-permute-done.39
  265.3 4.9 %collective-permute-start.29 = (bf16[128,768]{1,0:T(8,128)(2,1)}, bf16[128,768]{1,0:T(8,128)(2,1)}, u32[]{:S(2)}, u32[]{:S(2)}) collective-permute-start(bf16[128,768]{1,0:T(8,128)(2,1)} %get-tuple-element.53), channel_id=1, source_target_pairs={{0,8},{4,12},{8,0},{12,4},{16,24},{20,28},{24,16},{28,20},{1,9},{5... | collective-permute-start | bytes 589832 | tf_op jit(solution)/shard_map/ppermute | solution.py:309
  271.8 1.6 fusion.59
  273.4 5.8 %collective-permute-done.27 = f32[57,128]{1,0:T(8,128)S(1)} collective-permute-done((f32[57,128]{1,0:T(8,128)S(1)}, f32[57,128]{1,0:T(8,128)S(1)}, u32[]{:S(2)}, u32[]{:S(2)}) %collective-permute-start.27) | collective-permute-done | bytes 29216 | tf_op jit(solution)/shard_map/ppermute | solution.py:309
  281.5 1.9 collective-permute-start.32
  283.4 3.7 %collective-permute-start.33 = (bf16[128,768]{1,0:T(8,128)(2,1)S(1)}, bf16[128,768]{1,0:T(8,128)(2,1)S(1)}, u32[]{:S(2)}, u32[]{:S(2)}) collective-permute-start(bf16[128,768]{1,0:T(8,128)(2,1)S(1)} %get-tuple-element.49), channel_id=1, source_target_pairs={{0,24},{4,28},{8,16},{12,20},{16,8},{20,12},{24,0},{28,4},{1,25},{... | collective-permute-start | bytes 589832 | tf_op jit(solution)/shard_map/ppermute | solution.py:309
  287.1 2.2 bitcast_add_fusion.1
  289.6 13.6 %collective-permute-done.32 = bf16[128,768]{1,0:T(8,128)(2,1)S(1)} collective-permute-done((bf16[128,768]{1,0:T(8,128)(2,1)S(1)}, bf16[128,768]{1,0:T(8,128)(2,1)S(1)}, u32[]{:S(2)}, u32[]{:S(2)}) %collective-permute-start.32) | collective-permute-done | bytes 196640 | tf_op jit(solution)/shard_map/ppermute | solution.py:309
  303.2 6.9 %collective-permute-done.33 = bf16[128,768]{1,0:T(8,128)(2,1)S(1)} collective-permute-done((bf16[128,768]{1,0:T(8,128)(2,1)S(1)}, bf16[128,768]{1,0:T(8,128)(2,1)S(1)}, u32[]{:S(2)}, u32[]{:S(2)}) %collective-permute-start.33) | collective-permute-done | bytes 196640 | tf_op jit(solution)/shard_map/ppermute | solution.py:309
  310.1 6.1 %collective-permute-done.34 = bf16[128,768]{1,0:T(8,128)(2,1)S(1)} collective-permute-done((bf16[128,768]{1,0:T(8,128)(2,1)S(1)}, bf16[128,768]{1,0:T(8,128)(2,1)S(1)}, u32[]{:S(2)}, u32[]{:S(2)}) %collective-permute-start.34) | collective-permute-done | bytes 196640 | tf_op jit(solution)/shard_map/ppermute | solution.py:309
  (247 shorter events, 39.8 us)
Async XLA Ops:
  7.2 9.6 %copy-start.35 = (s32[8]{0:T(128)S(1)}, s32[8]{0:T(128)}, u32[]{:S(2)}) copy-start(s32[8]{0:T(128)} %constant.233.clone) | copy-start | bytes 100
  7.2 10.9 %copy-start.41 = (bf16[1,128,2]{1,2,0:T(2,128)(2,1)S(1)}, bf16[1,128,2]{1,2,0:T(2,128)(2,1)}, u32[]{:S(2)}) copy-start(bf16[1,128,2]{1,2,0:T(2,128)(2,1)} %param.22) | copy-start | bytes 1540
  7.2 11.0 %copy-start.32 = (bf16[1,3,128,256]{3,2,1,0:T(8,128)(2,1)S(1)}, bf16[1,3,128,256]{3,2,1,0:T(8,128)(2,1)}, u32[]{:S(2)}) copy-start(bf16[1,3,128,256]{3,2,1,0:T(8,128)(2,1)} %param.21) | copy-start | bytes 589828
  7.2 96.8 %all-gather.2.cloned.1.call-start = ((), (), s32[]{:S(2)}) async-start(), calls=%async_computation.1 | async-start | bytes 5455872 | tf_op jit(solution)/shard_map/all_gather | solution.py:459
  10.2 9.8 %copy-start.10 = (bf16[256,1024]{1,0:T(8,128)(2,1)S(1)}, bf16[256,1024]{1,0:T(8,128)(2,1)}, u32[]{:S(2)}) copy-start(bf16[256,1024]{1,0:T(8,128)(2,1)} %param.15) | copy-start | bytes 1572868
  10.2 11.1 %copy-start.21 = (bf16[256,1024]{1,0:T(8,128)(2,1)S(1)}, bf16[256,1024]{1,0:T(8,128)(2,1)}, u32[]{:S(2)}) copy-start(bf16[256,1024]{1,0:T(8,128)(2,1)} %param.27) | copy-start | bytes 1572868
  10.2 16.5 %copy-start.4 = (s32[1,1024]{1,0:T(1,128)S(1)}, s32[1,1024]{1,0:T(1,128)}, u32[]{:S(2)}) copy-start(s32[1,1024]{1,0:T(1,128)} %param.16) | copy-start | bytes 12292
  10.2 16.5 %copy-start.40 = (s32[1,1024]{1,0:T(1,128)S(1)}, s32[1,1024]{1,0:T(1,128)}, u32[]{:S(2)}) copy-start(s32[1,1024]{1,0:T(1,128)} %param.17) | copy-start | bytes 12292
  10.2 310.3 %reduce-scatter.4.cloned.1.call-start = ((), (), s32[]{:S(2)}) async-start(), calls=%async_computation.2 | async-start | bytes 5013504
  18.5 12.1 %collective-permute-start.2 = (bf16[128,896]{1,0:T(8,128)(2,1)S(1)}, bf16[128,896]{1,0:T(8,128)(2,1)S(1)}, u32[]{:S(2)}, u32[]{:S(2)}) collective-permute-start(bf16[128,896]{1,0:T(8,128)(2,1)S(1)} %get-tuple-element.72), channel_id=1, source_target_pairs={{0,8},{8,16},{16,24},{24,28},{28,20},{20,12},{12,4},{4,0},{1,9},{9... | collective-permute-start | bytes 688136 | tf_op jit(solution)/shard_map/ppermute | solution.py:377
  19.8 13.0 %collective-permute-start.3 = (bf16[128,896]{1,0:T(8,128)(2,1)S(1)}, bf16[128,896]{1,0:T(8,128)(2,1)S(1)}, u32[]{:S(2)}, u32[]{:S(2)}) collective-permute-start(bf16[128,896]{1,0:T(8,128)(2,1)S(1)} %get-tuple-element.72), channel_id=1, source_target_pairs={{8,0},{16,8},{24,16},{28,24},{20,28},{12,20},{4,12},{0,4},{9,1},{1... | collective-permute-start | bytes 688136 | tf_op jit(solution)/shard_map/ppermute | solution.py:380
  20.0 12.9 %collective-permute-start = (bf16[1,256,1024]{2,1,0:T(8,128)(2,1)S(1)}, bf16[1,256,1024]{2,1,0:T(8,128)(2,1)S(1)}, u32[]{:S(2)}, u32[]{:S(2)}) collective-permute-start(bf16[1,256,1024]{2,1,0:T(8,128)(2,1)S(1)} %bitcast.276), channel_id=1, source_target_pairs={{0,2},{1,3},{2,0},{3,1},{4,6},{5,7},{6,4},{7,5},{8,10},{9,11},{10,... | collective-permute-start | bytes 1572872 | tf_op jit(solution)/shard_map/ppermute | solution.py:309
  21.2 28.1 %collective-permute-start.16 = (bf16[1,256,1024]{2,1,0:T(8,128)(2,1)S(1)}, bf16[1,256,1024]{2,1,0:T(8,128)(2,1)S(1)}, u32[]{:S(2)}, u32[]{:S(2)}) collective-permute-start(bf16[1,256,1024]{2,1,0:T(8,128)(2,1)S(1)} %bitcast.291), channel_id=1, source_target_pairs={{0,2},{1,3},{2,0},{3,1},{4,6},{5,7},{6,4},{7,5},{8,10},{9,11},{10,... | collective-permute-start | bytes 1572872 | tf_op jit(solution)/shard_map/ppermute | solution.py:309
  30.6 13.3 %collective-permute-start.4 = (bf16[128,896]{1,0:T(8,128)(2,1)S(1)}, bf16[128,896]{1,0:T(8,128)(2,1)S(1)}, u32[]{:S(2)}, u32[]{:S(2)}) collective-permute-start(bf16[128,896]{1,0:T(8,128)(2,1)S(1)} %collective-permute-done.2), channel_id=1, source_target_pairs={{0,8},{8,16},{16,24},{24,28},{28,20},{20,12},{12,4},{4,0},{1,9},{9... | collective-permute-start | bytes 688136 | tf_op jit(solution)/shard_map/ppermute | solution.py:377
  32.9 16.4 %collective-permute-start.5 = (bf16[128,896]{1,0:T(8,128)(2,1)S(1)}, bf16[128,896]{1,0:T(8,128)(2,1)S(1)}, u32[]{:S(2)}, u32[]{:S(2)}) collective-permute-start(bf16[128,896]{1,0:T(8,128)(2,1)S(1)} %collective-permute-done.3), channel_id=1, source_target_pairs={{8,0},{16,8},{24,16},{28,24},{20,28},{12,20},{4,12},{0,4},{9,1},{1... | collective-permute-start | bytes 688136 | tf_op jit(solution)/shard_map/ppermute | solution.py:380
  33.0 28.6 %collective-permute-start.1 = (bf16[2,256,1024]{2,1,0:T(8,128)(2,1)S(1)}, bf16[2,256,1024]{2,1,0:T(8,128)(2,1)S(1)}, u32[]{:S(2)}, u32[]{:S(2)}) collective-permute-start(bf16[2,256,1024]{2,1,0:T(8,128)(2,1)S(1)} %pad_maximum_fusion.5), channel_id=1, source_target_pairs={{0,1},{1,0},{2,3},{3,2},{4,5},{5,4},{6,7},{7,6},{8,9},{9,8},{10,11... | collective-permute-start | bytes 3145736 | tf_op jit(solution)/shard_map/ppermute | solution.py:309
  43.9 10.3 %collective-permute-start.6 = (bf16[128,896]{1,0:T(8,128)(2,1)S(1)}, bf16[128,896]{1,0:T(8,128)(2,1)S(1)}, u32[]{:S(2)}, u32[]{:S(2)}) collective-permute-start(bf16[128,896]{1,0:T(8,128)(2,1)S(1)} %collective-permute-done.4), channel_id=1, source_target_pairs={{0,8},{8,16},{16,24},{24,28},{28,20},{20,12},{12,4},{4,0},{1,9},{9... | collective-permute-start | bytes 688136 | tf_op jit(solution)/shard_map/ppermute | solution.py:377
  49.3 8.6 %collective-permute-start.7 = (bf16[128,896]{1,0:T(8,128)(2,1)S(1)}, bf16[128,896]{1,0:T(8,128)(2,1)S(1)}, u32[]{:S(2)}, u32[]{:S(2)}) collective-permute-start(bf16[128,896]{1,0:T(8,128)(2,1)S(1)} %collective-permute-done.5), channel_id=1, source_target_pairs={{8,0},{16,8},{24,16},{28,24},{20,28},{12,20},{4,12},{0,4},{9,1},{1... | collective-permute-start | bytes 688136 | tf_op jit(solution)/shard_map/ppermute | solution.py:380
  49.3 9.6 %copy-start.23 = (bf16[1,256,1024]{2,1,0:T(8,128)(2,1)}, bf16[1,256,1024]{2,1,0:T(8,128)(2,1)S(1)}, u32[]{:S(2)}) copy-start(bf16[1,256,1024]{2,1,0:T(8,128)(2,1)S(1)} %collective-permute-done.16) | copy-start | bytes 1572868
  50.5 77.1 %collective-permute-start.17 = (bf16[2,256,1024]{2,1,0:T(8,128)(2,1)}, bf16[2,256,1024]{2,1,0:T(8,128)(2,1)}, u32[]{:S(2)}, u32[]{:S(2)}) collective-permute-start(bf16[2,256,1024]{2,1,0:T(8,128)(2,1)} %pad_maximum_fusion.8), channel_id=1, source_target_pairs={{0,1},{1,0},{2,3},{3,2},{4,5},{5,4},{6,7},{7,6},{8,9},{9,8},{10,11... | collective-permute-start | bytes 3145736 | tf_op jit(solution)/shard_map/ppermute | solution.py:309
  54.2 4.8 %collective-permute-start.8 = (bf16[64,896]{1,0:T(8,128)(2,1)S(1)}, bf16[64,896]{1,0:T(8,128)(2,1)S(1)}, u32[]{:S(2)}, u32[]{:S(2)}) collective-permute-start(bf16[64,896]{1,0:T(8,128)(2,1)S(1)} %slice.158), channel_id=1, source_target_pairs={{0,8},{8,16},{16,24},{24,28},{28,20},{20,12},{12,4},{4,0},{1,9},{9... | collective-permute-start | bytes 344072 | tf_op jit(solution)/shard_map/ppermute | solution.py:373
  57.9 3.7 %collective-permute-start.9 = (bf16[64,896]{1,0:T(8,128)(2,1)S(1)}, bf16[64,896]{1,0:T(8,128)(2,1)S(1)}, u32[]{:S(2)}, u32[]{:S(2)}) collective-permute-start(bf16[64,896]{1,0:T(8,128)(2,1)S(1)} %slice.159), channel_id=1, source_target_pairs={{8,0},{16,8},{24,16},{28,24},{20,28},{12,20},{4,12},{0,4},{9,1},{1... | collective-permute-start | bytes 344072 | tf_op jit(solution)/shard_map/ppermute | solution.py:374
  94.2 12.9 %collective-permute-start.10 = (bf16[1,1024,256]{2,1,0:T(8,128)(2,1)S(1)}, bf16[1,1024,256]{2,1,0:T(8,128)(2,1)}, u32[]{:S(2)}, u32[]{:S(2)}) collective-permute-start(bf16[1,1024,256]{2,1,0:T(8,128)(2,1)S(1)} %bitcast.263), channel_id=1, source_target_pairs={{0,2},{1,3},{2,0},{3,1},{4,6},{5,7},{6,4},{7,5},{8,10},{9,11},{10,... | collective-permute-start | bytes 1572872 | tf_op jit(solution)/shard_map/ppermute | solution.py:309
  105.9 16.1 %collective-permute-start.12 = (bf16[1,256,1024]{2,1,0:T(8,128)(2,1)}, bf16[1,256,1024]{2,1,0:T(8,128)(2,1)}, u32[]{:S(2)}, u32[]{:S(2)}) collective-permute-start(bf16[1,256,1024]{2,1,0:T(8,128)(2,1)} %slice_bitcast_fusion.3), channel_id=1, source_target_pairs={{0,2},{1,3},{2,0},{3,1},{4,6},{5,7},{6,4},{7,5},{8,10},{9,11},{10,... | collective-permute-start | bytes 1572872 | tf_op jit(solution)/shard_map/ppermute | solution.py:309
  109.2 20.5 %collective-permute-start.11 = (bf16[2,1024,256]{2,1,0:T(8,128)(2,1)}, bf16[2,1024,256]{2,1,0:T(8,128)(2,1)}, u32[]{:S(2)}, u32[]{:S(2)}) collective-permute-start(bf16[2,1024,256]{2,1,0:T(8,128)(2,1)} %pad_maximum_fusion.6), channel_id=1, source_target_pairs={{0,1},{1,0},{2,3},{3,2},{4,5},{5,4},{6,7},{7,6},{8,9},{9,8},{10,11... | collective-permute-start | bytes 3145736 | tf_op jit(solution)/shard_map/ppermute | solution.py:309
  123.4 8.4 %collective-permute-start.13 = (bf16[2,256,1024]{2,1,0:T(8,128)(2,1)S(1)}, bf16[2,256,1024]{2,1,0:T(8,128)(2,1)S(1)}, u32[]{:S(2)}, u32[]{:S(2)}) collective-permute-start(bf16[2,256,1024]{2,1,0:T(8,128)(2,1)S(1)} %pad_maximum_fusion.7), channel_id=1, source_target_pairs={{0,1},{1,0},{2,3},{3,2},{4,5},{5,4},{6,7},{7,6},{8,9},{9,8},{10,11... | collective-permute-start | bytes 3145736 | tf_op jit(solution)/shard_map/ppermute | solution.py:309
  129.8 19.1 %copy-start.16 = (bf16[4,256,1024]{2,1,0:T(8,128)(2,1)}, bf16[4,256,1024]{2,1,0:T(8,128)(2,1)S(1)}, u32[]{:S(2)}) copy-start(bf16[4,256,1024]{2,1,0:T(8,128)(2,1)S(1)} %slice_dynamic-update-slice_fusion) | copy-start | bytes 6291460
  137.5 13.0 %copy-start.12 = (f32[1024,1024]{1,0:T(8,128)}, f32[1024,1024]{1,0:T(8,128)S(1)}, u32[]{:S(2)}) copy-start(f32[1024,1024]{1,0:T(8,128)S(1)} %get-tuple-element.95) | copy-start | bytes 12582916
  147.9 95.3 %copy-start.36 = (f32[1024]{0:T(1024)}, f32[1024]{0:T(1024)S(1)}, u32[]{:S(2)}) copy-start(f32[1024]{0:T(1024)S(1)} %get-tuple-element.96) | copy-start | bytes 12292
  148.1 7.4 %collective-permute-start.18 = (bf16[2,256,1024]{2,1,0:T(8,128)(2,1)S(1)}, bf16[2,256,1024]{2,1,0:T(8,128)(2,1)S(1)}, u32[]{:S(2)}, u32[]{:S(2)}) collective-permute-start(bf16[2,256,1024]{2,1,0:T(8,128)(2,1)S(1)} %fusion.34), channel_id=1, source_target_pairs={{0,1},{1,0},{2,3},{3,2},{4,5},{5,4},{6,7},{7,6},{8,9},{9,8},{10,11... | collective-permute-start | bytes 3145736 | tf_op jit(solution)/shard_map/ppermute | solution.py:309
  157.0 25.2 %collective-permute-start.19 = (bf16[2,256,1024]{2,1,0:T(8,128)(2,1)}, bf16[2,256,1024]{2,1,0:T(8,128)(2,1)}, u32[]{:S(2)}, u32[]{:S(2)}) collective-permute-start(bf16[2,256,1024]{2,1,0:T(8,128)(2,1)} %fusion.20), channel_id=1, source_target_pairs={{0,2},{1,3},{2,0},{3,1},{4,6},{5,7},{6,4},{7,5},{8,10},{9,11},{10,... | collective-permute-start | bytes 3145736 | tf_op jit(solution)/shard_map/ppermute | solution.py:309
  167.8 14.4 %copy-start.13 = (f32[1024,1024]{1,0:T(8,128)S(1)}, f32[1024,1024]{1,0:T(8,128)}, u32[]{:S(2)}) copy-start(f32[1024,1024]{1,0:T(8,128)} %copy-done.12) | copy-start | bytes 12582916
  176.5 15.3 %collective-permute-start.14 = (bf16[2,256,1024]{2,1,0:T(8,128)(2,1)}, bf16[2,256,1024]{2,1,0:T(8,128)(2,1)}, u32[]{:S(2)}, u32[]{:S(2)}) collective-permute-start(bf16[2,256,1024]{2,1,0:T(8,128)(2,1)} %fusion.35), channel_id=1, source_target_pairs={{0,1},{1,0},{2,3},{3,2},{4,5},{5,4},{6,7},{7,6},{8,9},{9,8},{10,11... | collective-permute-start | bytes 3145736 | tf_op jit(solution)/shard_map/ppermute | solution.py:309
  191.0 5.5 %collective-permute-start.20 = (bf16[2,256,1024]{2,1,0:T(8,128)(2,1)}, bf16[2,256,1024]{2,1,0:T(8,128)(2,1)}, u32[]{:S(2)}, u32[]{:S(2)}) collective-permute-start(bf16[2,256,1024]{2,1,0:T(8,128)(2,1)} %get-tuple-element.42), channel_id=1, source_target_pairs={{0,1},{1,0},{2,3},{3,2},{4,5},{5,4},{6,7},{7,6},{8,9},{9,8},{10,11... | collective-permute-start | bytes 3145736 | tf_op jit(solution)/shard_map/ppermute | solution.py:309
  194.0 7.1 %copy-start.14 = (f32[2,256,1024]{2,1,0:T(8,128)}, f32[2,256,1024]{2,1,0:T(8,128)S(1)}, u32[]{:S(2)}) copy-start(f32[2,256,1024]{2,1,0:T(8,128)S(1)} %bitcast_add_fusion.3) | copy-start | bytes 6291460
  195.0 57.7 %collective-permute-start.15 = (bf16[256,1024]{1,0:T(8,128)(2,1)}, bf16[256,1024]{1,0:T(8,128)(2,1)}, u32[]{:S(2)}, u32[]{:S(2)}) collective-permute-start(bf16[256,1024]{1,0:T(8,128)(2,1)} %fusion.40), channel_id=1, source_target_pairs={{0,2},{1,3},{2,0},{3,1},{4,6},{5,7},{6,4},{7,5},{8,10},{9,11},{10,... | collective-permute-start | bytes 1572872 | tf_op jit(solution)/shard_map/ppermute | solution.py:309
  203.8 24.0 %copy-start.9 = (bf16[4,256,1024]{2,1,0:T(8,128)(2,1)S(1)}, bf16[4,256,1024]{2,1,0:T(8,128)(2,1)}, u32[]{:S(2)}) copy-start(bf16[4,256,1024]{2,1,0:T(8,128)(2,1)} %copy-done.7) | copy-start | bytes 6291460
  203.8 24.0 %copy-start.28 = (bf16[1024,896]{1,0:T(8,128)(2,1)S(1)}, bf16[1024,896]{1,0:T(8,128)(2,1)}, u32[]{:S(2)}) copy-start(bf16[1024,896]{1,0:T(8,128)(2,1)} %copy-done.27) | copy-start | bytes 5505028
  234.0 9.2 %collective-permute-start.23 = (f32[17,128]{1,0:T(8,128)S(1)}, f32[17,128]{1,0:T(8,128)S(1)}, u32[]{:S(2)}, u32[]{:S(2)}) collective-permute-start(f32[17,128]{1,0:T(8,128)S(1)} %maximum_bitcast_fusion.1), channel_id=1, source_target_pairs={{0,1},{1,0},{2,3},{3,2},{4,5},{5,4},{6,7},{7,6},{8,9},{9,8},{10,11... | collective-permute-start | bytes 26120 | tf_op jit(solution)/shard_map/ppermute | solution.py:309
  236.8 6.6 %copy-start.29 = (f32[1024,896]{1,0:T(8,128)}, f32[1024,896]{1,0:T(8,128)S(1)}, u32[]{:S(2)}) copy-start(f32[1024,896]{1,0:T(8,128)S(1)} %fusion.73) | copy-start | bytes 11010052
  239.3 18.2 %collective-permute-start.35 = (bf16[256,128]{1,0:T(8,128)(2,1)}, bf16[256,128]{1,0:T(8,128)(2,1)}, u32[]{:S(2)}, u32[]{:S(2)}) collective-permute-start(bf16[256,128]{1,0:T(8,128)(2,1)} %bitcast.259), channel_id=1, source_target_pairs={{0,4},{4,0},{8,12},{12,8},{16,20},{20,16},{24,28},{28,24},{1,5},{5... | collective-permute-start | bytes 196616 | tf_op jit(solution)/shard_map/ppermute | solution.py:309
  239.9 12.9 %copy-start.15 = (f32[2,256,1024]{2,1,0:T(8,128)S(1)}, f32[2,256,1024]{2,1,0:T(8,128)}, u32[]{:S(2)}) copy-start(f32[2,256,1024]{2,1,0:T(8,128)} %copy-done.14) | copy-start | bytes 6291460
  239.9 18.3 %collective-permute-start.36 = (bf16[256,128]{1,0:T(8,128)(2,1)}, bf16[256,128]{1,0:T(8,128)(2,1)}, u32[]{:S(2)}, u32[]{:S(2)}) collective-permute-start(bf16[256,128]{1,0:T(8,128)(2,1)} %bitcast.258), channel_id=1, source_target_pairs={{0,8},{4,12},{8,0},{12,4},{16,24},{20,28},{24,16},{28,20},{1,9},{5... | collective-permute-start | bytes 196616 | tf_op jit(solution)/shard_map/ppermute | solution.py:309
  240.6 19.3 %collective-permute-start.37 = (bf16[256,128]{1,0:T(8,128)(2,1)}, bf16[256,128]{1,0:T(8,128)(2,1)}, u32[]{:S(2)}, u32[]{:S(2)}) collective-permute-start(bf16[256,128]{1,0:T(8,128)(2,1)} %bitcast.257), channel_id=1, source_target_pairs={{0,12},{4,8},{8,4},{12,0},{16,28},{20,24},{24,20},{28,16},{1,13},{... | collective-permute-start | bytes 196616 | tf_op jit(solution)/shard_map/ppermute | solution.py:309
  243.2 3.0 collective-permute-start.24
  247.0 3.4 %collective-permute-start.25 = (f32[57,128]{1,0:T(8,128)S(1)}, f32[57,128]{1,0:T(8,128)S(1)}, u32[]{:S(2)}, u32[]{:S(2)}) collective-permute-start(f32[57,128]{1,0:T(8,128)S(1)} %pad_maximum_fusion.10), channel_id=1, source_target_pairs={{0,4},{4,0},{8,12},{12,8},{16,20},{20,16},{24,28},{28,24},{1,5},{5... | collective-permute-start | bytes 87560 | tf_op jit(solution)/shard_map/ppermute | solution.py:309
  250.4 36.8 %collective-permute-start.21 = (bf16[2,256,1024]{2,1,0:T(8,128)(2,1)S(1)}, bf16[2,256,1024]{2,1,0:T(8,128)(2,1)}, u32[]{:S(2)}, u32[]{:S(2)}) collective-permute-start(bf16[2,256,1024]{2,1,0:T(8,128)(2,1)S(1)} %fusion.36), channel_id=1, source_target_pairs={{0,1},{1,0},{2,3},{3,2},{4,5},{5,4},{6,7},{7,6},{8,9},{9,8},{10,11... | collective-permute-start | bytes 3145736 | tf_op jit(solution)/shard_map/ppermute | solution.py:309
  252.7 7.6 %collective-permute-start.26 = (f32[57,128]{1,0:T(8,128)S(1)}, f32[57,128]{1,0:T(8,128)S(1)}, u32[]{:S(2)}, u32[]{:S(2)}) collective-permute-start(f32[57,128]{1,0:T(8,128)S(1)} %fusion.67), channel_id=1, source_target_pairs={{0,8},{4,12},{8,0},{12,4},{16,24},{20,28},{24,16},{28,20},{1,9},{5... | collective-permute-start | bytes 87560 | tf_op jit(solution)/shard_map/ppermute | solution.py:309
  257.4 14.4 %copy-start.31 = (bf16[256,1,128]{2,1,0:T(2,128)(2,1)S(1)}, bf16[256,1,128]{2,1,0:T(2,128)(2,1)}, u32[]{:S(2)}) copy-start(bf16[256,1,128]{2,1,0:T(2,128)(2,1)} %get-tuple-element.59) | copy-start | bytes 196612
  257.5 5.7 %collective-permute-start.38 = (bf16[256,128]{1,0:T(8,128)(2,1)S(1)}, bf16[256,128]{1,0:T(8,128)(2,1)S(1)}, u32[]{:S(2)}, u32[]{:S(2)}) collective-permute-start(bf16[256,128]{1,0:T(8,128)(2,1)S(1)} %bitcast.301), channel_id=1, source_target_pairs={{0,16},{4,20},{8,24},{12,28},{16,0},{20,4},{24,8},{28,12},{1,17},{... | collective-permute-start | bytes 196616 | tf_op jit(solution)/shard_map/ppermute | solution.py:309
  258.3 7.0 %collective-permute-start.39 = (bf16[256,128]{1,0:T(8,128)(2,1)S(1)}, bf16[256,128]{1,0:T(8,128)(2,1)S(1)}, u32[]{:S(2)}, u32[]{:S(2)}) collective-permute-start(bf16[256,128]{1,0:T(8,128)(2,1)S(1)} %bitcast.300), channel_id=1, source_target_pairs={{0,20},{4,16},{8,28},{12,24},{16,4},{20,0},{24,12},{28,8},{1,21},{... | collective-permute-start | bytes 196616 | tf_op jit(solution)/shard_map/ppermute | solution.py:309
  259.9 11.2 %collective-permute-start.40 = (bf16[256,128]{1,0:T(8,128)(2,1)S(1)}, bf16[256,128]{1,0:T(8,128)(2,1)S(1)}, u32[]{:S(2)}, u32[]{:S(2)}) collective-permute-start(bf16[256,128]{1,0:T(8,128)(2,1)S(1)} %bitcast.299), channel_id=1, source_target_pairs={{0,24},{4,28},{8,16},{12,20},{16,8},{20,12},{24,0},{28,4},{1,25},{... | collective-permute-start | bytes 196616 | tf_op jit(solution)/shard_map/ppermute | solution.py:309
  260.3 11.5 %collective-permute-start.41 = (bf16[256,128]{1,0:T(8,128)(2,1)S(1)}, bf16[256,128]{1,0:T(8,128)(2,1)S(1)}, u32[]{:S(2)}, u32[]{:S(2)}) collective-permute-start(bf16[256,128]{1,0:T(8,128)(2,1)S(1)} %bitcast.298), channel_id=1, source_target_pairs={{0,28},{4,24},{8,20},{12,16},{16,12},{20,8},{24,4},{28,0},{1,29},{... | collective-permute-start | bytes 196616 | tf_op jit(solution)/shard_map/ppermute | solution.py:309
  263.3 18.3 %collective-permute-start.28 = (bf16[128,768]{1,0:T(8,128)(2,1)}, bf16[128,768]{1,0:T(8,128)(2,1)}, u32[]{:S(2)}, u32[]{:S(2)}) collective-permute-start(bf16[128,768]{1,0:T(8,128)(2,1)} %get-tuple-element.47), channel_id=1, source_target_pairs={{0,4},{4,0},{8,12},{12,8},{16,20},{20,16},{24,28},{28,24},{1,5},{5... | collective-permute-start | bytes 589832 | tf_op jit(solution)/shard_map/ppermute | solution.py:309
  265.3 18.1 %collective-permute-start.29 = (bf16[128,768]{1,0:T(8,128)(2,1)}, bf16[128,768]{1,0:T(8,128)(2,1)}, u32[]{:S(2)}, u32[]{:S(2)}) collective-permute-start(bf16[128,768]{1,0:T(8,128)(2,1)} %get-tuple-element.53), channel_id=1, source_target_pairs={{0,8},{4,12},{8,0},{12,4},{16,24},{20,28},{24,16},{28,20},{1,9},{5... | collective-permute-start | bytes 589832 | tf_op jit(solution)/shard_map/ppermute | solution.py:309
  271.1 18.4 %collective-permute-start.30 = (bf16[128,768]{1,0:T(8,128)(2,1)}, bf16[128,768]{1,0:T(8,128)(2,1)}, u32[]{:S(2)}, u32[]{:S(2)}) collective-permute-start(bf16[128,768]{1,0:T(8,128)(2,1)} %get-tuple-element.52), channel_id=1, source_target_pairs={{0,12},{4,8},{8,4},{12,0},{16,28},{20,24},{24,20},{28,16},{1,13},{... | collective-permute-start | bytes 589832 | tf_op jit(solution)/shard_map/ppermute | solution.py:309
  271.8 7.4 %collective-permute-start.27 = (f32[57,128]{1,0:T(8,128)S(1)}, f32[57,128]{1,0:T(8,128)S(1)}, u32[]{:S(2)}, u32[]{:S(2)}) collective-permute-start(f32[57,128]{1,0:T(8,128)S(1)} %add.446), channel_id=1, source_target_pairs={{0,16},{4,20},{8,24},{12,28},{16,0},{20,4},{24,8},{28,12},{1,17},{... | collective-permute-start | bytes 87560 | tf_op jit(solution)/shard_map/ppermute | solution.py:309
  279.2 10.4 %collective-permute-start.31 = (bf16[128,768]{1,0:T(8,128)(2,1)}, bf16[128,768]{1,0:T(8,128)(2,1)S(1)}, u32[]{:S(2)}, u32[]{:S(2)}) collective-permute-start(bf16[128,768]{1,0:T(8,128)(2,1)} %get-tuple-element.51), channel_id=1, source_target_pairs={{0,16},{4,20},{8,24},{12,28},{16,0},{20,4},{24,8},{28,12},{1,17},{... | collective-permute-start | bytes 589832 | tf_op jit(solution)/shard_map/ppermute | solution.py:309
  281.5 21.7 %collective-permute-start.32 = (bf16[128,768]{1,0:T(8,128)(2,1)S(1)}, bf16[128,768]{1,0:T(8,128)(2,1)S(1)}, u32[]{:S(2)}, u32[]{:S(2)}) collective-permute-start(bf16[128,768]{1,0:T(8,128)(2,1)S(1)} %get-tuple-element.50), channel_id=1, source_target_pairs={{0,20},{4,16},{8,28},{12,24},{16,4},{20,0},{24,12},{28,8},{1,21},{... | collective-permute-start | bytes 589832 | tf_op jit(solution)/shard_map/ppermute | solution.py:309
  283.4 26.7 %collective-permute-start.33 = (bf16[128,768]{1,0:T(8,128)(2,1)S(1)}, bf16[128,768]{1,0:T(8,128)(2,1)S(1)}, u32[]{:S(2)}, u32[]{:S(2)}) collective-permute-start(bf16[128,768]{1,0:T(8,128)(2,1)S(1)} %get-tuple-element.49), channel_id=1, source_target_pairs={{0,24},{4,28},{8,16},{12,20},{16,8},{20,12},{24,0},{28,4},{1,25},{... | collective-permute-start | bytes 589832 | tf_op jit(solution)/shard_map/ppermute | solution.py:309
  287.1 29.0 %collective-permute-start.34 = (bf16[128,768]{1,0:T(8,128)(2,1)S(1)}, bf16[128,768]{1,0:T(8,128)(2,1)S(1)}, u32[]{:S(2)}, u32[]{:S(2)}) collective-permute-start(bf16[128,768]{1,0:T(8,128)(2,1)S(1)} %get-tuple-element.48), channel_id=1, source_target_pairs={{0,28},{4,24},{8,20},{12,16},{16,12},{20,8},{24,4},{28,0},{1,29},{... | collective-permute-start | bytes 589832 | tf_op jit(solution)/shard_map/ppermute | solution.py:309
  289.4 28.9 %copy-start.11 = (bf16[256,1024]{1,0:T(8,128)(2,1)S(1)}, bf16[256,1024]{1,0:T(8,128)(2,1)}, u32[]{:S(2)}) copy-start(bf16[256,1024]{1,0:T(8,128)(2,1)} %param.15) | copy-start | bytes 1572868
  289.4 28.9 %copy-start.38 = (f32[1,1024]{1,0:T(1,128)S(1)}, f32[1,1024]{1,0:T(1,128)}, u32[]{:S(2)}) copy-start(f32[1,1024]{1,0:T(1,128)} %param.18) | copy-start | bytes 12292
  289.5 28.8 %collective-permute-start.22 = (bf16[256,1024]{1,0:T(8,128)(2,1)S(1)}, bf16[256,1024]{1,0:T(8,128)(2,1)S(1)}, u32[]{:S(2)}, u32[]{:S(2)}) collective-permute-start(bf16[256,1024]{1,0:T(8,128)(2,1)S(1)} %fusion.41), channel_id=1, source_target_pairs={{0,2},{1,3},{2,0},{3,1},{4,6},{5,7},{6,4},{7,5},{8,10},{9,11},{10,... | collective-permute-start | bytes 1572872 | tf_op jit(solution)/shard_map/ppermute | solution.py:309
  (27 other events, 97.1 us)
Sparse Core Ops, SparseCore 0:
  10.7 93.3 all-gather.1
  168.0 92.1 reduce-scatter.3

commit v3 on v1

v3 whole, which is shorter than its diff:
```python
import functools
import jax
import jax.numpy as jnp
from jax import lax
from jax.experimental import pallas as pl
from jax.experimental.pallas import tpu as pltpu
from jax.sharding import PartitionSpec as P

HEAD = 128
C = 128
F32 = jnp.float32
BF = jnp.bfloat16

NN = (((1,), (0,)), ((), ()))
NT = (((1,), (1,)), ((), ()))
TN = (((0,), (0,)), ((), ()))


def dot1(a, b, dims=NN):
    return lax.dot_general(a.astype(BF), b.astype(BF), dims, preferred_element_type=F32)


def split(x):
    hi = x.astype(BF)
    return hi, (x - hi.astype(F32)).astype(BF)


def dot3(a, b, dims=NN):
    a1, a2 = split(a) if not isinstance(a, tuple) else a
    b1, b2 = split(b) if not isinstance(b, tuple) else b
    ka, kb = dims[0][0][0], dims[0][1][0]
    left = jnp.concatenate([a1, a2], axis=ka)
    n = b1.shape[1 - kb]
    if n == 128:
        right = jnp.concatenate([jnp.concatenate([b1, b2], axis=1 - kb), jnp.concatenate([b1, jnp.zeros_like(b1)], axis=1 - kb)], axis=kb)
        r = lax.dot_general(left, right, dims, preferred_element_type=F32)
        return r[:, :128] + r[:, 128:]
    r = lax.dot_general(left, jnp.concatenate([b1, b1], axis=kb), dims, preferred_element_type=F32)
    return r + lax.dot_general(a1, b2, dims, preferred_element_type=F32)


def dot3_old(a, b, dims=NN):
    a1, a2 = split(a) if not isinstance(a, tuple) else a
    b1, b2 = split(b) if not isinstance(b, tuple) else b
    d = functools.partial(lax.dot_general, dimension_numbers=dims, preferred_element_type=F32)
    return d(a1, b1) + (d(a1, b2) + d(a2, b1))


def block_masks():
    r = lax.broadcasted_iota(jnp.int32, (C, C), 0)
    c = lax.broadcasted_iota(jnp.int32, (C, C), 1)
    return r, c


def invert(systems, dot):
    r, c = block_masks()
    eye = (r == c).astype(F32)
    x = r ^ c
    lows = [low.astype(BF) for low in systems]
    out = [eye - jnp.where((x == 1), low, 0.0) for low in systems]
    size = 2
    while size < C:
        here = (x >= size) & (x < 2 * size)
        short = [t.astype(BF) for t in out]
        mids = [dot1(jnp.where(here, low, 0.0).astype(BF), t) for low, t in zip(lows, short)]
        out = [t - dot1(b, m) for t, b, m in zip(out, short, mids)]
        size *= 2
    splits = [split(t) for t in out]
    errors = [eye - t - dot(low, p) for low, t, p in zip(systems, out, splits)]
    return [t + dot1(p[0], e) for t, p, e in zip(out, splits, errors)]


def sigmoid(x):
    return 1.0 / (1.0 + jnp.exp(-x))


def taps_down(ext, rows, j):
    return lax.slice_in_dim(ext, 8 - j, 8 - j + rows, axis=0)


def row_sum(x):
    return jnp.dot(x.astype(BF), jnp.ones((HEAD, HEAD), BF), preferred_element_type=F32)


def head_norm(x):
    return x * lax.rsqrt(row_sum(x * x) + 1e-6)


def segment_parts(seg_s, cols_ref, segr_ref, first, sl):
    prev = jnp.where(first > 0, seg_s[jnp.maximum(first - 1, 0)], -1)
    last = seg_s[first + C - 1]
    segc = cols_ref[sl, 4:5]
    same = segc == segr_ref[0:1, sl]
    lead = (segc == prev.astype(F32)).astype(F32)
    trail = (segc == last.astype(F32)).astype(F32)
    return same, lead, trail, (prev == last).astype(F32)


def fwd_kernel(heads, cb, base, seg_s, x_ref, wide_ref, again_ref, cols_ref, segr_ref, taps_ref, gain_ref, tail_in, state_in,
               mixed_ref, kept_ref, na_ref, pre_ref, conv_ref, o_ref, t_ref, a_ref, p_ref, n_ref, z_ref, s_ref, u_ref, g_ref,
               tail, state, line):
    step = pl.program_id(0)
    width = heads * HEAD
    rows = cb * C
    taps = taps_ref.shape[1]

    @pl.when(step == 0)
    def _():
        tail[...] = tail_in[...]
        state[...] = state_in[...]

    r, c = block_masks()
    x = x_ref[...].astype(F32)
    na = (x * lax.rsqrt(jnp.mean(x * x, axis=-1, keepdims=True) + 1e-6) * again_ref[0:1, :]).astype(BF)
    na_ref[...] = na
    pre_ref[...] = jnp.dot(na, wide_ref[...], preferred_element_type=F32)
    tap = lambda j: jnp.concatenate([taps_ref[i, j:j + 1, :] for i in range(3)], axis=1)
    cur = pre_ref[:, :3 * width]
    line[:8, :] = tail[...]
    line[8:, :] = cur
    tot = cur * tap(0)
    for j in range(1, taps):
        tot = tot + line[8 - j:8 - j + rows, :] * tap(j) * cols_ref[:, j - 1:j]
    tail[...] = line[rows:, :]
    conv_ref[...] = tot
    tot = tot * sigmoid(tot)
    parts = [tot[:, i * width:(i + 1) * width] for i in range(3)]
    eye = (r == c).astype(F32)
    items = []
    for b in range(cb):
        sl = slice(b * C, (b + 1) * C)
        same, lead, trail, keep = segment_parts(seg_s, cols_ref, segr_ref, ((base + step) * cb + b) * C, sl)
        for h in range(heads):
            hs = slice(h * HEAD, (h + 1) * HEAD)
            q, k, v = (part[sl, hs] for part in parts)
            beta = sigmoid(pre_ref[sl, 3 * width + h:3 * width + h + 1]) * cols_ref[sl, 3:4]
            items.append(dict(b=b, h=h, q=head_norm(q), k=head_norm(k), v=v, beta=beta, same=same, lead=lead,
                              trail=trail, keep=keep, sl=sl, hs=hs))
    for it in items:
        it["kk"] = split(it["k"])
        p = jnp.where(it["same"] & (r > c), dot3(it["kk"], it["kk"], NT), 0.0)
        it["p"] = p
        it["low"] = p * it["beta"]
        it["a"] = jnp.where(it["same"] & (r >= c), dot3(it["q"], it["kk"], NT), 0.0)
    inv = invert([it["low"] for it in items], dot3)
    for it, t in zip(items, inv):
        rhs = jnp.concatenate([it["beta"] * it["v"], (it["beta"] * it["lead"]) * it["k"]], axis=1)
        tw = dot3(t, rhs)
        tws = split(tw)
        aw = dot3(it["a"], tws)
        bz = dot3(it["trail"] * it["k"], tws, TN)
        it["tv"], it["w"] = tw[:, :HEAD], tw[:, HEAD:]
        it["o0"], it["n"] = aw[:, :HEAD], it["lead"] * it["q"] - aw[:, HEAD:]
        it["bk"], it["z"] = bz[:, :HEAD], it["keep"] * eye - bz[:, HEAD:]
        it["t"] = t
    for it in items:
        b, h = it["b"], it["h"]
        s = state[h]
        ss = split(s)
        u = it["tv"] - dot3(it["w"], ss)
        o = it["o0"] + dot3(it["n"], ss)
        g = it["v"] - it["lead"] * dot3(it["kk"], ss)
        state[h] = it["bk"] + dot3(it["z"], ss)
        s_ref[b, h] = s
        u_ref[b, h] = u
        g_ref[b, h] = g
        t_ref[b, h] = it["t"]
        a_ref[b, h] = it["a"]
        p_ref[b, h] = it["p"]
        n_ref[b, h] = it["n"]
        z_ref[b, h] = it["z"]
        o_ref[it["sl"], it["hs"]] = o
        mixed = (o * lax.rsqrt(row_sum(o * o) * (1.0 / HEAD) + 1e-5) * gain_ref[0:1, :]).astype(BF)
        mixed_ref[it["sl"], it["hs"]] = mixed
        kept_ref[it["sl"], it["hs"]] = mixed


def stage_bits(n):
    bits = [1 << i for i in range(n.bit_length() - 1)]
    return bits, bits[1:] + bits[:1]


def bwd_kernel(heads, cb, n_f, shard, seg_s, ga0_ref, ga0c_ref, ga1_ref, ga1c_ref, mix_ref, na_ref, out_ref, wide_ref, x_ref, dffn0_ref, dffn1_ref,
               pre_ref, conv_ref, o_ref, cols_ref, segr_ref, taps_ref, gain_ref,
               t_ref, a_ref, p_ref, n_ref, z_ref, s_ref, u_ref, g_ref,
               away1_ref, keep1_ref, away2_ref, keep2_ref, sna_ref, kna_ref, gains_ref, small_ref,
               head_rows, dstate, acc, dpre):
    step = pl.program_id(0)
    steps = pl.num_programs(0)
    width = heads * HEAD
    rows = cb * C
    taps = taps_ref.shape[1]
    back = steps - 1 - step
    core = lax.axis_index("tensor") % 2

    @pl.when(step == 0)
    def _():
        head_rows[...] = jnp.zeros_like(head_rows)
        dstate[...] = jnp.zeros_like(dstate)
        acc[...] = jnp.zeros_like(acc)
        gains_ref[...] = jnp.zeros_like(gains_ref)
        gains_ref[1:2, :] = dffn0_ref[...] + dffn1_ref[...]
        small_ref[...] = jnp.zeros_like(small_ref)

    r, c = block_masks()
    dcs = [[[None] * heads for _ in range(cb)] for _ in range(3)]
    dgain = jnp.zeros((1, HEAD), F32)
    dlog = [None] * cb
    ga = jnp.where(back % 2 == core, jnp.where(back >= 2, ga1_ref[...], ga0_ref[...]),
                   jnp.where(back >= 2, ga1c_ref[...], ga0c_ref[...]))
    dmix = jnp.dot(ga, out_ref[...], preferred_element_type=F32)
    acc[:, 3 * width:4 * width] += lax.dot_general(ga, mix_ref[...], TN, preferred_element_type=F32)
    for b in reversed(range(cb)):
        sl = slice(b * C, (b + 1) * C)
        same, lead, trail, keep = segment_parts(seg_s, cols_ref, segr_ref, (back * cb + b) * C, sl)
        lane = lax.broadcasted_iota(jnp.int32, (C, HEAD), 1)
        dl = jnp.zeros((C, HEAD), F32)
        for h in range(heads):
            hs = slice(h * HEAD, (h + 1) * HEAD)
            cq, ck, cv = (conv_ref[sl, i * width + h * HEAD:i * width + (h + 1) * HEAD] for i in range(3))
            gq, gk, gv = sigmoid(cq), sigmoid(ck), sigmoid(cv)
            q, k = cq * gq, ck * gk
            rq = lax.rsqrt(jnp.sum(q * q, axis=-1, keepdims=True) + 1e-6)
            rk = lax.rsqrt(jnp.sum(k * k, axis=-1, keepdims=True) + 1e-6)
            q, k = q * rq, k * rk
            gb = sigmoid(pre_ref[sl, 3 * width + h:3 * width + h + 1])
            pad = cols_ref[sl, 3:4]
            beta = gb * pad
            o = o_ref[sl, hs]
            dm = dmix[sl, hs]
            ro = lax.rsqrt(jnp.mean(o * o, axis=-1, keepdims=True) + 1e-5)
            oh = o * ro
            dgain = dgain + jnp.sum(dm * oh, axis=0, keepdims=True)
            du0 = dm * gain_ref[0:1, :]
            do = ro * (du0 - oh * jnp.mean(du0 * oh, axis=-1, keepdims=True))
            ds1 = dstate[h]
            u = u_ref[b, h]
            s = s_ref[b, h]
            a = a_ref[b, h]
            p = p_ref[b, h]
            ks = split(k)
            ds1s = split(ds1)
            dos = split(do)
            us = split(u)
            dstate[h] = dot3(z_ref[b, h], ds1s, TN) + dot3(n_ref[b, h], dos, TN)
            du = dot3(a, dos, TN) + trail * dot3(ks, ds1s)
            dr = dot3(t_ref[b, h], du, TN)
            drs = split(dr)
            ss = split(s)
            dlow = jnp.where(same & (r > c), -dot3(drs, us, NT), 0.0)
            da = jnp.where(same & (r >= c), dot3(dos, us, NT), 0.0)
            dv = beta * dr
            dbeta = jnp.sum(dr * g_ref[b, h] , axis=-1, keepdims=True) + jnp.sum(dlow * p, axis=-1, keepdims=True)
            dp = split(beta * dlow)
            das = split(da)
            dq = lead * dot3(dos, ss, NT) + dot3(das, ks)
            dk = (dot3(das, q, TN) + trail * dot3(us, ds1s, NT) - (beta * lead) * dot3(drs, ss, NT)
                  + dot3(dp, ks) + dot3(dp, ks, TN))
            dsq = rq * (dq - q * jnp.sum(q * dq, axis=-1, keepdims=True))
            dsk = rk * (dk - k * jnp.sum(k * dk, axis=-1, keepdims=True))
            dcs[0][b][h] = dsq * gq * (1.0 + cq * (1.0 - gq))
            dcs[1][b][h] = dsk * gk * (1.0 + ck * (1.0 - gk))
            dcs[2][b][h] = dv * gv * (1.0 + cv * (1.0 - gv))
            dl = jnp.where(lane == h, dbeta * pad * gb * (1.0 - gb), dl)
        dlog[b] = dl
    gains_ref[2:3, :HEAD] += dgain
    for b in range(cb):
        dpre[b * C:(b + 1) * C, 3 * width:] = dlog[b].astype(BF)
    for i in range(3):
        dc = jnp.concatenate([jnp.concatenate(dcs[i][b], axis=1) for b in range(cb)], axis=0)
        pre = pre_ref[:, i * width:(i + 1) * width]
        tot = dc * taps_ref[i, 0:1, :]
        grads = [jnp.sum(dc * pre, axis=0, keepdims=True)]
        for j in range(1, taps):
            e = dc * cols_ref[:, j - 1:j]
            ext = jnp.concatenate([e, head_rows[j - 1, :, i * width:(i + 1) * width]], axis=0)
            head_rows[j - 1, :, i * width:(i + 1) * width] = e[:8]
            e = lax.slice_in_dim(ext, j, j + rows, axis=0)
            tot = tot + e * taps_ref[i, j:j + 1, :]
            grads.append(jnp.sum(e * pre, axis=0, keepdims=True))
        dpre[:, i * width:(i + 1) * width] = tot.astype(BF)
        small_ref[taps * i:taps * (i + 1), :width] += jnp.concatenate(grads, axis=0)
    low = dpre[...]
    acc[:, :3 * width] += lax.dot_general(na_ref[...], low[:, :3 * width], TN, preferred_element_type=F32)
    acc[:, 4 * width:] += lax.dot_general(na_ref[...], low[:, 3 * width:], TN, preferred_element_type=F32)
    dna = lax.dot_general(low, wide_ref[...], NT, preferred_element_type=F32)
    x = x_ref[...].astype(F32)
    gains_ref[0:1, :] += jnp.sum(dna * (x * lax.rsqrt(jnp.mean(x * x, axis=-1, keepdims=True) + 1e-6)), axis=0, keepdims=True)

    @pl.when(back % 2 == core)
    def _():
        kna_ref[back // 2] = dna

    @pl.when(back % 2 != core)
    def _():
        sna_ref[back // 2] = dna.astype(BF)

    @pl.when(step == steps - 1)
    def _():
        small_ref[3 * taps:3 * taps + heads, :] = acc[:, 4 * width:].T[:heads, :]
        me = lax.axis_index("fsdp")
        first, second = stage_bits(n_f)
        half = 2 * width
        for ref, other, bit, lanes in ((away1_ref, keep1_ref, first[0], slice(0, half)), (away2_ref, keep2_ref, second[0], slice(half, 2 * half))):
            mine = (me // bit) % 2
            for j in range(n_f // 2):
                low_bits = j % bit
                there = (j - low_bits) * 2 + low_bits
                ref[j] = acc[pl.ds(pl.multiple_of((there + (1 - mine) * bit) * shard, 16), shard), lanes].astype(BF)
                other[j] = acc[pl.ds(pl.multiple_of((there + mine * bit) * shard, 16), shard), lanes].astype(other.dtype)


def whole(shape):
    return pl.BlockSpec(shape, lambda i, *_: (0,) * len(shape), pipeline_mode=pl.Buffered(1))


def shaped(shape, dtype=F32):
    return jax.ShapeDtypeStruct(shape, dtype)


def params(limit=60):
    return pltpu.CompilerParams(dimension_semantics=("arbitrary",), vmem_limit_bytes=limit * 2**20)


COST = pl.CostEstimate(flops=10**10, bytes_accessed=10**7, transcendentals=0)
TINY = pl.CostEstimate(flops=1, bytes_accessed=1, transcendentals=0)


def fwd_call_kernel(heads, cb, base, n_old, *refs):
    ins, rest = refs[:10], refs[10 + n_old:]
    outs, tail_out, state_out, tail, state, line = rest[:14], rest[14], rest[15], rest[16], rest[17], rest[18]
    fwd_kernel(heads, cb, base, *ins, *outs, tail, state, line)

    @pl.when(pl.program_id(0) == pl.num_programs(0) - 1)
    def _():
        tail_out[...] = tail[...]
        state_out[...] = state[...]


def mixer_fwd(part, parts, x, wide, again, cols, segr, seg, taps, gain, tail, state, old, cb=4):
    n, d = x.shape
    width = taps.shape[2]
    heads = width // HEAD
    wide_cols = 3 * width + HEAD
    rows = cb * C
    steps = n // parts // rows
    base = part * steps
    sq = shaped((n // C, heads, C, HEAD))
    sqspec = pl.BlockSpec((cb, heads, C, HEAD), lambda i, s: (i + base, 0, 0, 0))
    here = lambda w: pl.BlockSpec((rows, w), lambda i, s: (i + base, 0))
    ins = [x, wide, again, cols, segr, taps, gain, tail, state]
    kept = [shaped((n, width), BF), shaped((n, d), BF), shaped((n, wide_cols)), shaped((n, 3 * width)), shaped((n, width))] + [sq] * 8
    return pl.pallas_call(
        functools.partial(fwd_call_kernel, heads, cb, base, len(old)),
        grid_spec=pltpu.PrefetchScalarGridSpec(
            num_scalar_prefetch=1, grid=(steps,),
            in_specs=[here(d), whole((d, wide_cols)), whole((1, d)), here(cols.shape[1]),
                      pl.BlockSpec((1, rows), lambda i, s: (0, i + base)),
                      whole(taps.shape), whole((1, HEAD)), whole(tail.shape), whole(state.shape)]
            + [pl.BlockSpec(memory_space=pl.ANY)] * len(old),
            out_specs=[pl.BlockSpec((rows, width), lambda i, s: (i, 0)), here(width), here(d), here(wide_cols), here(3 * width), here(width)]
            + [sqspec] * 8 + [whole(tail.shape), whole(state.shape)],
            scratch_shapes=[pltpu.VMEM(tail.shape, F32), pltpu.VMEM(state.shape, F32), pltpu.VMEM((rows + 8, 3 * width), F32)]),
        out_shape=[shaped((n // parts, width), BF)] + kept + [shaped(tail.shape), shaped(state.shape)],
        input_output_aliases={1 + len(ins) + i: 1 + i for i in range(len(old))},
        compiler_params=params(),
        cost_estimate=COST,
        name="mixer_fwd",
    )(seg, *ins, *old)


def mixer_bwd(n_f, shard, ga, out, wide, x, dffn, cols, segr, seg, taps, gain, kept, cb=2):
    mix, na, pre, conv, o, *rest = kept
    n, wide_cols = pre.shape
    d = x.shape[1]
    width = taps.shape[2]
    heads = width // HEAD
    rows = cb * C
    steps = n // rows
    ntap = taps.shape[1]
    sqspec = pl.BlockSpec((cb, heads, C, HEAD), lambda i, s: (steps - 1 - i, 0, 0, 0))
    row = lambda w: pl.BlockSpec((rows, w), lambda i, s: (steps - 1 - i, 0))
    outs = [shaped((n_f // 2, shard, 2 * width), BF)] * 4 + [
            shaped((2, rows, d), BF), shaped((2, rows, d)), shaped((8, d)), shaped((16, d))]
    return pl.pallas_call(
        functools.partial(bwd_kernel, heads, cb, n_f, shard),
        grid_spec=pltpu.PrefetchScalarGridSpec(
            num_scalar_prefetch=1, grid=(steps,),
            in_specs=[whole((rows, d))] * 4 + [row(width), row(d), whole(out.shape), whole((d, wide_cols)), row(d), whole((1, d)), whole((1, d)),
                      row(wide_cols), row(3 * width), row(width),
                      row(cols.shape[1]), pl.BlockSpec((1, rows), lambda i, s: (0, steps - 1 - i)),
                      whole(taps.shape), whole((1, HEAD))] + [sqspec] * 8,
            out_specs=[whole(v.shape) for v in outs],
            scratch_shapes=[pltpu.VMEM((ntap - 1, 8, 3 * width), F32), pltpu.VMEM((heads, HEAD, HEAD), F32),
                            pltpu.VMEM((d, 4 * width + HEAD), F32), pltpu.VMEM((rows, wide_cols), BF)]),
        out_shape=outs,
        compiler_params=params(),
        cost_estimate=COST,
        name="mixer_bwd",
    )(seg, *ga, mix, na, out, wide, x, *dffn, pre, conv, o, cols, segr, taps, gain, *rest)


def fold_kernel(n_f, stage, k1_ref, g1_ref, k2_ref, g2_ref, a1_out, k1_out, a2_out, k2_out):
    me = lax.axis_index("fsdp")
    for order, keep, got, away_out, keep_out in ((0, k1_ref, g1_ref, a1_out, k1_out), (1, k2_ref, g2_ref, a2_out, k2_out)):
        bits = stage_bits(n_f)[order]
        bit = bits[stage]
        left = sorted(b for b in bits[stage:])
        place = 1 << left.index(bit)
        mine = (me // bit) % 2
        for j in range(keep.shape[0] // 2):
            low = j % place
            there = (j - low) * 2 + low
            theirs = there + (1 - mine) * place
            away_out[j] = (keep[theirs].astype(F32) + got[theirs].astype(F32)).astype(BF)
            ours = there + mine * place
            keep_out[j] = (keep[ours].astype(F32) + got[ours].astype(F32)).astype(keep_out.dtype)


def fold(n_f, stage, k1, g1, k2, g2):
    m, shard, w = k1.shape
    outs = [shaped((m // 2, shard, w), BF)] * 4
    return pl.pallas_call(
        functools.partial(fold_kernel, n_f, stage),
        out_shape=outs,
        compiler_params=pltpu.CompilerParams(vmem_limit_bytes=60 * 2**20),
        cost_estimate=TINY,
        name="fold",
    )(k1, g1, k2, g2)


def finish_kernel(heads, ntap, k1_ref, g1_ref, k2_ref, g2_ref, s_ref, *refs):
    got, (qkv_ref, out_ref, taps_ref, beta_ref, attn_ref, ffn_ref, head_ref, hold) = refs[:-8], refs[-8:]
    width = qkv_ref.shape[2]
    shard = qkv_ref.shape[1]
    a = k1_ref[0].astype(F32) + g1_ref[0].astype(F32)
    b = k2_ref[0].astype(F32) + g2_ref[0].astype(F32)
    qkv_ref[0] = a[:, :width]
    qkv_ref[1] = a[:, width:]
    qkv_ref[2] = b[:, :width]
    out_ref[...] = b[:, width:].T
    small = s_ref[...]
    for g in got:
        small = small + g[...]
    for i in range(3):
        taps_ref[i] = small[ntap * i:ntap * (i + 1), :width]
    attn_ref[...] = small[16:17]
    ffn_ref[...] = small[17:18]
    head_ref[...] = small[18:19, :HEAD]
    if shard == 128:
        hold[...] = small[8:16]
        me = lax.axis_index("fsdp")
        beta_ref[...] = hold[3 * ntap - 8:3 * ntap - 8 + heads, pl.ds(pl.multiple_of(me * shard, 128), shard)]
    else:
        beta_ref[...] = small[3 * ntap:3 * ntap + heads]


def finish(heads, ntap, k1, g1, k2, g2, small, got):
    m, shard, w = k1.shape
    d = small.shape[1]
    return pl.pallas_call(
        functools.partial(finish_kernel, heads, ntap),
        out_shape=[shaped((3, shard, w // 2)), shaped((w // 2, shard)), shaped((3, ntap, w // 2)),
                   shaped((heads, 128 if shard == 128 else d)), shaped((1, d)), shaped((1, d)), shaped((1, HEAD))],
        scratch_shapes=[pltpu.VMEM((8, d), F32)],
        compiler_params=pltpu.CompilerParams(vmem_limit_bytes=60 * 2**20),
        cost_estimate=TINY,
        name="finish",
    )(k1, g1, k2, g2, small, *got)


def ffn_kernel(ff, *refs):
    m, out, (x_ref, w_ref, gf_ref, gain_ref), rest = refs[:4], refs[4:8], refs[8:12], refs[12:]
    mid_ref, nf_ref, hid_ref, dgu_ref, keep_ref, send_ref, dgain_ref, hold = rest
    rows = keep_ref.shape[0]
    core = lax.axis_index("tensor") % 2
    mid = x_ref[...].astype(F32)
    for k in range(4):
        mid = mid + lax.dot_general(m[k][...], out[k][...], NT, preferred_element_type=F32)
    hold[...] = mid
    unit = mid * lax.rsqrt(jnp.mean(mid * mid, axis=-1, keepdims=True) + 1e-6)
    nf = (unit * gain_ref[0:1, :]).astype(BF)
    nf_ref[...] = nf
    mid_ref[...] = hold[pl.ds(pl.multiple_of(core * rows, 16), rows), :]
    gate = lax.dot_general(w_ref[:ff, :], nf, NT, preferred_element_type=F32)
    up = lax.dot_general(w_ref[ff:2 * ff, :], nf, NT, preferred_element_type=F32)
    dh = lax.dot_general(w_ref[2 * ff:, :], gf_ref[...], NT, preferred_element_type=F32)
    sig = sigmoid(gate)
    act = gate * sig
    hid_ref[...] = (act * up).astype(BF)
    dgu_ref[:ff, :] = (dh * up * sig * (1.0 + gate * (1.0 - sig))).astype(BF)
    dgu_ref[ff:, :] = (dh * act).astype(BF)
    dnf = lax.dot_general(dgu_ref[...], w_ref[:2 * ff, :], TN, preferred_element_type=F32)
    dgain_ref[...] = jnp.sum(dnf * unit, axis=0, keepdims=True)
    hold[...] = dnf
    keep_ref[...] = hold[pl.ds(pl.multiple_of(core * rows, 16), rows), :]
    send_ref[...] = hold[pl.ds(pl.multiple_of((1 - core) * rows, 16), rows), :].astype(BF)


def ffn(part, m, out, x, weights, gf, gain):
    n, width = m[0].shape
    d = x.shape[1]
    ff = weights.shape[0] // 3
    here = pl.BlockSpec((n, d), lambda i: (part, 0))
    outs = [shaped((n // 2, d)), shaped((n, d), BF), shaped((ff, n), BF), shaped((2 * ff, n), BF),
            shaped((n // 2, d)), shaped((n // 2, d), BF), shaped((1, d))]
    return pl.pallas_call(
        functools.partial(ffn_kernel, ff),
        grid=(1,),
        in_specs=[whole(v.shape) for v in (*m, *out)] + [here, whole(weights.shape), here, whole((1, d))],
        out_specs=[whole(v.shape) for v in outs],
        out_shape=outs,
        scratch_shapes=[pltpu.VMEM((n, d), F32)],
        compiler_params=params(),
        cost_estimate=COST,
        name="ffn",
    )(*m, *out, x, weights, gf, gain)


def grad_kernel(part, low_ref, other_ref, mid_ref, cot_ref, coty_ref, gain_ref, grad_ref, low_out):
    chip = lax.axis_index("tensor") // 2
    mid = mid_ref[...]
    factor = lax.rsqrt(jnp.mean(mid * mid, axis=-1, keepdims=True) + 1e-6)
    u = (low_ref[...].astype(F32) + other_ref[...].astype(F32)) * gain_ref[0:1, :]
    cot = jnp.where(chip == part, cot_ref[...], coty_ref[...]).astype(F32)
    grad = cot + factor * u - mid * (factor * factor * factor) * jnp.mean(u * mid, axis=-1, keepdims=True)
    grad_ref[...] = grad
    low_out[...] = grad.astype(BF)


def grad_rows(part, low, other, mid, cot, cot_y, gain):
    return pl.pallas_call(
        functools.partial(grad_kernel, part),
        out_shape=[shaped(mid.shape), shaped(mid.shape, BF)],
        compiler_params=pltpu.CompilerParams(vmem_limit_bytes=24 * 2**20),
        cost_estimate=TINY,
        name="grad_rows",
    )(low, other, mid, cot, cot_y, gain)


def down_kernel(hid0_ref, hid1_ref, w_ref, send_ref, keep_ref, hold):
    core = lax.axis_index("tensor") % 2
    rows = send_ref.shape[1]
    for i, hid in enumerate((hid0_ref, hid1_ref)):
        hold[...] = lax.dot_general(hid[...], w_ref[...], TN, preferred_element_type=F32)
        keep_ref[i] = hold[pl.ds(pl.multiple_of(core * rows, 16), rows), :]
        send_ref[i] = hold[pl.ds(pl.multiple_of((1 - core) * rows, 16), rows), :].astype(BF)


def down(hid0, hid1, weights, wait_for):
    ff, n = hid0.shape
    d = weights.shape[1]
    outs = [shaped((2, n // 2, d), BF), shaped((2, n // 2, d))]

    def body(*refs):
        down_kernel(*refs[:3], *refs[3 + len(wait_for):])

    return pl.pallas_call(
        body,
        grid=(1,),
        in_specs=[whole(hid0.shape)] * 2 + [pl.BlockSpec((ff, d), lambda i: (2, 0))] + [pl.BlockSpec(memory_space=pl.ANY)] * len(wait_for),
        out_specs=[whole(v.shape) for v in outs],
        out_shape=outs,
        scratch_shapes=[pltpu.VMEM((n, d), F32)],
        compiler_params=params(),
        cost_estimate=TINY,
        name="down",
    )(hid0, hid1, weights, *wait_for)


def ffn_grads_kernel(ff, parts, *refs):
    gf_ref, o_ref = refs[3 * parts], refs[-1]
    n = refs[0].shape[1]
    up = down = None
    for i in range(parts):
        dgu, hid, nf = refs[3 * i:3 * i + 3]
        a = jnp.dot(dgu[...], nf[...], preferred_element_type=F32)
        b = jnp.dot(hid[...], gf_ref[i * n:(i + 1) * n, :], preferred_element_type=F32)
        up = a if up is None else up + a
        down = b if down is None else down + b
    for k in range(o_ref.shape[0]):
        lanes = slice(k * 128, (k + 1) * 128)
        o_ref[k, :2 * ff, :] = up[:, lanes].astype(BF)
        o_ref[k, 2 * ff:, :] = down[:, lanes].astype(BF)


def ffn_grads(pieces, gf, wait_for, step=256):
    ff = pieces[0][1].shape[0]
    n, d = gf.shape
    flat, specs = [], []
    for dgu, hid, nf in pieces:
        flat += [dgu, hid, nf]
        specs += [whole(dgu.shape), whole(hid.shape), pl.BlockSpec((nf.shape[0], step), lambda i: (0, i))]
    return pl.pallas_call(
        functools.partial(ffn_grads_kernel, ff, len(pieces)),
        grid=(d // step,),
        in_specs=specs + [pl.BlockSpec((n, step), lambda i: (0, i))] + [pl.BlockSpec(memory_space=pl.ANY)] * len(wait_for),
        out_specs=pl.BlockSpec((step // 128, 3 * ff, 128), lambda i: (i, 0, 0)),
        out_shape=shaped((d // 128, 3 * ff, 128), BF),
        compiler_params=params(),
        cost_estimate=pl.CostEstimate(flops=5 * 10**9, bytes_accessed=10**7, transcendentals=0),
        name="ffn_grads",
    )(*flat, gf, *wait_for)


def to_chips_kernel(keep, got, wait_for, mine_ref, away_ref):
    chip = lax.axis_index("tensor") // 2
    mine_ref[...] = keep[chip] + got[chip].astype(F32)
    away_ref[...] = (keep[1 - chip] + got[1 - chip].astype(F32)).astype(BF)


def to_chips(keep, got, wait_for):
    spec = pl.BlockSpec(memory_space=pltpu.VMEM)
    return pl.pallas_call(
        to_chips_kernel,
        in_specs=[spec] * 2 + [pl.BlockSpec(memory_space=pl.ANY)],
        out_shape=[shaped(keep.shape[1:]), shaped(keep.shape[1:], BF)],
        compiler_params=pltpu.CompilerParams(vmem_limit_bytes=60 * 2**20),
        cost_estimate=TINY,
        name="to_chips",
    )(keep, got, wait_for)


def last_kernel(g0, g1, na, na_y, x_ref, gain_ref, mid0, mid1, out, out_y, in_ref, block_ref):
    first = lax.axis_index("tensor") // 2 == 0
    x = x_ref[...].astype(F32)
    factor = lax.rsqrt(jnp.mean(x * x, axis=-1, keepdims=True) + 1e-6)
    u = (na[...] + na_y[...].astype(F32)) * gain_ref[0:1, :]
    in_ref[...] = jnp.where(first, g0[...], g1[...]) + (factor * u - x * (factor * factor * factor) * jnp.mean(u * x, axis=-1, keepdims=True))
    block_ref[...] = (jnp.where(first, mid0[...], mid1[...]) + out[...] + out_y[...].astype(F32)).astype(BF)


def last_rows(g0, g1, na, na_y, x, gain, mid0, mid1, out, out_y):
    return pl.pallas_call(
        last_kernel,
        out_shape=[shaped(g0.shape), shaped(g0.shape, BF)],
        compiler_params=pltpu.CompilerParams(vmem_limit_bytes=60 * 2**20),
        cost_estimate=TINY,
        name="last_rows",
    )(g0, g1, na, na_y, x, gain, mid0, mid1, out, out_y)


def ffn_cast_kernel(d_ref, expand_ref, down_ref):
    ff = down_ref.shape[0]
    expand_ref[0] = d_ref[:ff, :].astype(F32)
    expand_ref[1] = d_ref[ff:2 * ff, :].astype(F32)
    down_ref[...] = d_ref[2 * ff:, :].astype(F32)


def ffn_cast(d):
    ff, w = d.shape[0] // 3, d.shape[1]
    return pl.pallas_call(
        ffn_cast_kernel,
        out_shape=[shaped((2, ff, w)), shaped((ff, w))],
        compiler_params=pltpu.CompilerParams(vmem_limit_bytes=60 * 2**20),
        cost_estimate=TINY,
        name="ffn_cast",
    )(d)


def pack_kernel(qkv_ref, beta_ref, out_ref, o_ref):
    width = qkv_ref.shape[2]
    n = o_ref.shape[0]
    for i in range(3):
        o_ref[:, i * width:(i + 1) * width] = qkv_ref[i]
    beta = beta_ref[...].astype(F32)
    heads = beta.shape[1]
    o_ref[:, 3 * width:3 * width + 128] = jnp.concatenate([beta, jnp.zeros((n, 128 - heads), F32)], axis=1).astype(BF)
    o_ref[:, 3 * width + 128:] = out_ref[...].astype(F32).T.astype(BF)


def pack(qkv, beta, out):
    n, width = qkv.shape[1:]
    return pl.pallas_call(
        pack_kernel,
        out_shape=shaped((n, 4 * width + 128), BF),
        compiler_params=pltpu.CompilerParams(vmem_limit_bytes=60 * 2**20),
        name="pack",
    )(qkv, beta, out)


def columns(seg, pad):
    n = seg.shape[0]
    cols = []
    for j in range(1, 4):
        before = jnp.concatenate([jnp.full((j,), -1, seg.dtype), seg[:n - j]])
        cols.append((before == seg).astype(F32))
    cols += [pad.astype(F32), seg.astype(F32)]
    cols += [jnp.zeros((n,), F32)] * 3
    return jnp.stack(cols, axis=1)


def hop(value, axis, bit):
    n = lax.axis_size(axis)
    return lax.ppermute(value, axis, [(i, i ^ bit) for i in range(n)])


def fence(*values):
    return lax.optimization_barrier(values)


def y_hop(value):
    return hop(value, "tensor", 2)


def core_hop(value):
    return hop(value, "tensor", 1)


def in_order(own, other_chip, pair):
    me = lax.axis_index("tensor")
    full = jnp.zeros((4,) + own.shape, own.dtype)
    for k, block in ((0, own), (2, other_chip), (1, pair[0]), (3, pair[1])):
        full = lax.dynamic_update_slice(full, block[None], (me ^ k,) + (0,) * own.ndim)
    return full.reshape((4 * own.shape[0],) + own.shape[1:])


class Ring:
    def __init__(self, value):
        n = lax.axis_size("fsdp")
        order = [i for i in range(0, n, 2)] + [i for i in reversed(range(1, n, 2))]
        me = lax.axis_index("fsdp")
        self.n = n
        self.me = jnp.where(me % 2 == 0, me // 2, n - 1 - me // 2)
        self.right = [(order[i], order[(i + 1) % n]) for i in range(n)]
        self.left = [(b, a) for a, b in self.right]
        self.rows = value.shape[0]
        self.full = jnp.zeros((n * self.rows,) + value.shape[1:], value.dtype)
        self.a = self.b = value
        self.k = 0
        self.put(value, 0, 0)

    def put(self, part, steps, start):
        place = lax.rem(self.me + steps + self.n, self.n)
        owner = jnp.where(place < self.n // 2, 2 * place, 2 * (self.n - 1 - place) + 1)
        self.full = lax.dynamic_update_slice(self.full, part, (owner * self.rows + start, 0))

    def step(self):
        self.k += 1
        k, half = self.k, self.rows // 2
        self.split = 2 * k == self.n and half % 16 == 0
        if self.split:
            self.a = lax.ppermute(self.a[:half], "fsdp", self.right)
            self.b = lax.ppermute(self.b[half:], "fsdp", self.left)
            return
        self.a = lax.ppermute(self.a, "fsdp", self.right)
        if 2 * k < self.n:
            self.b = lax.ppermute(self.b, "fsdp", self.left)

    def keep(self):
        self.put(self.a, -self.k, 0)
        if self.split or 2 * self.k < self.n:
            self.put(self.b, self.k, self.rows // 2 if self.split else 0)


def hop_sum(value, axis, bit):
    return value + hop(value, axis, bit)


def on_device(
    layer_input, segment_ids, pad_mask, attn_gain, ffn_gain, out_gain,
    qkv_weight, beta_weight, conv_weight, out_weight, expand_weight, down_weight, cotangent,
):
    n_f = lax.axis_size("fsdp")
    me_t = lax.axis_index("tensor")
    chip = me_t // 2
    rows, d_model = layer_input.shape
    width = qkv_weight.shape[3]
    heads = beta_weight.shape[2]
    ff = down_weight.shape[1]
    shard = qkv_weight.shape[2]
    taps = conv_weight[0]
    ntap = taps.shape[1]
    first_bits, second_bits = stage_bits(n_f)

    packed = pack(qkv_weight[0], beta_weight[0], out_weight[0])
    packed, expand_own, down_own = fence(packed, expand_weight[0], down_weight[0])
    ring = Ring(packed)
    ring.step()
    x_y = y_hop(layer_input)
    x_c = core_hop(layer_input)
    ffn_own = jnp.concatenate([expand_own[0].T, expand_own[1].T, down_own], axis=0)
    weights = lax.all_gather(ffn_own, "fsdp", axis=1, tiled=True)
    seg = segment_ids[0]
    cols = columns(seg, pad_mask[0])
    segr = seg.astype(F32)[None]
    ring.a, ring.b, x_y, x_c = fence(ring.a, ring.b, x_y, x_c)
    ring.keep()
    ring.step()
    x_cy = core_hop(x_y)
    c_y = y_hop(cotangent)
    c_c = core_hop(cotangent)
    ring.a, ring.b, x_cy = fence(ring.a, ring.b, x_cy)
    ring.keep()
    ring.step()
    x_full = in_order(layer_input, x_y, (x_c, x_cy))
    ring.a, ring.b, x_full, cols, c_y = fence(ring.a, ring.b, x_full, cols, c_y)
    ring.keep()
    while 2 * ring.k < n_f:
        ring.step()
        ring.keep()
    c_cy = core_hop(c_y)
    g_f = in_order(cotangent, c_y, (c_c, c_cy))
    wide, g_f = fence(ring.full, g_f)

    out_own = wide[:, 3 * width + HEAD:]
    tail = jnp.zeros((8, 3 * width), F32)
    state = jnp.zeros((heads, HEAD, HEAD), F32)

    def mix(i, tail, state, old):
        m, *kept, tail, state = mixer_fwd(i, 2, x_full, wide, attn_gain, cols, segr, seg, taps, out_gain, tail, state, old)
        return m, kept, tail, state

    ow_y = y_hop(out_own)
    ow_c = core_hop(out_own)
    m0, kept, tail, state = mix(0, tail, state, [])
    ow_y, ow_c, m0, tail, state = fence(ow_y, ow_c, m0, tail, state)
    m0_y = y_hop(m0)
    m0_c = core_hop(m0)
    ow_cy = core_hop(ow_y)
    m1, kept, tail, state = mix(1, tail, state, kept)
    m0_y, m0_c, ow_cy, m1 = fence(m0_y, m0_c, ow_cy, m1)

    def feed(i, *m):
        return ffn(i, m, (out_own, ow_y, ow_c, ow_cy), x_full, weights, g_f, ffn_gain)

    m1_y = y_hop(m1)
    m1_c = core_hop(m1)
    m0_cy = core_hop(m0_y)
    mid0, nf0, hid0, dgu0, keep0, send0, dgain0 = feed(0, m0, m0_y, m0_c, m0_cy)
    m1_y, m1_c, send0 = fence(m1_y, m1_c, send0)
    m1_cy = core_hop(m1_y)
    low0 = (keep0 + core_hop(send0).astype(F32)).astype(BF)
    m1_cy, low0 = fence(m1_cy, low0)
    low0_y = y_hop(low0)
    mid1, nf1, hid1, dgu1, keep1, send1, dgain1 = feed(1, m1, m1_y, m1_c, m1_cy)
    low0_y, send1 = fence(low0_y, send1)
    low1 = (keep1 + core_hop(send1).astype(F32)).astype(BF)
    grad0, ga0 = grad_rows(0, low0, low0_y, mid0, cotangent, c_y, ffn_gain)
    low1, ga0 = fence(low1, ga0)
    low1_y = y_hop(low1)
    ga0_c = core_hop(ga0)
    blocks = ffn_grads([(dgu0, hid0, nf0), (dgu1, hid1, nf1)], g_f, [low1])
    q = d_model // 128
    if q != n_f:
        blocks = blocks.reshape(q, 3 * ff, n_f // q, shard).transpose(0, 2, 1, 3).reshape(n_f, 3 * ff, shard)
    send_out, keep_out = down(hid0, hid1, weights, [blocks])
    low1_y, ga0_c, send_out, done_blocks = fence(low1_y, ga0_c, send_out, blocks)
    d_ffn = lax.psum_scatter(blocks, "fsdp", scatter_dimension=0, tiled=False)
    grad1, ga1 = grad_rows(1, low1, low1_y, mid1, cotangent, c_y, ffn_gain)
    ga1_c = core_hop(ga1)
    ga1, ga1_c = fence(ga1, ga1_c)

    out_c = core_hop(send_out)
    made = mixer_bwd(
        n_f, shard, (ga0, ga0_c, ga1, ga1_c), out_own, wide, x_full, (dgain0, dgain1), cols, segr, seg, taps, out_gain, kept)
    away1, k1, away2, k2, send_na, keep_na, gains, small, out_c = fence(*made, out_c)

    g1 = hop(away1, "fsdp", first_bits[0])
    g2 = hop(away2, "fsdp", second_bits[0])
    na_c = core_hop(send_na)
    gains_got = [hop(gains, "tensor", k) for k in range(1, 4)]
    out, out_away = to_chips(keep_out, out_c, done_blocks)
    na, na_away = to_chips(keep_na, na_c, gains)
    g1, g2, na_away, out_away, *gains_got = fence(g1, g2, na_away, out_away, *gains_got)
    count = len(first_bits)
    small = jnp.concatenate([small, gains + gains_got[0] + (gains_got[1] + gains_got[2])], axis=0)
    for stage in range(1, count):
        away1, k1, away2, k2 = fold(n_f, stage, k1, g1, k2, g2)
        if stage == 1:
            na_y, out_y = y_hop(na_away), y_hop(out_away)
        g1 = hop(away1, "fsdp", first_bits[stage])
        g2 = hop(away2, "fsdp", second_bits[stage])
        if stage < count - 1:
            small = hop_sum(small, "fsdp", first_bits[stage - 1])
            g1, g2, small, na_y = fence(g1, g2, small, na_y)
    if n_f == 8:
        got = [hop(small, "fsdp", k) for k in (2, 4, 6)]
    else:
        small = hop_sum(small, "fsdp", first_bits[count - 2])
        got = [hop(small, "fsdp", first_bits[count - 1])]
    input_grad, block_outs = last_rows(grad0, grad1, na, na_y, layer_input, attn_gain, mid0, mid1, out, out_y)
    block_outs = block_outs[None]
    qkv_grad, out_grad, conv_grad, beta_grad, attn_total, ffn_total, head_total = finish(heads, ntap, k1, g1, k2, g2, small, got)
    if shard != 128:
        beta_grad = lax.dynamic_slice(beta_grad, (0, lax.axis_index("fsdp") * shard), (heads, shard))
    beta_grad = beta_grad.T
    expand_grad, down_grad = ffn_cast(d_ffn)
    expand_grad = expand_grad.transpose(0, 2, 1)
    return (
        block_outs, input_grad, attn_total, ffn_total, head_total, qkv_grad[None], beta_grad[None],
        conv_grad[None], out_grad[None], expand_grad[None], down_grad[None],
    )


def solution(mesh):
    in_specs = (
        P(("fsdp", "tensor"), None),
        P("fsdp", None),
        P("fsdp", None),
        P(),
        P(),
        P(),
        P(None, None, "fsdp", "tensor"),
        P(None, "fsdp", "tensor"),
        P(None, None, None, "tensor"),
        P(None, "tensor", "fsdp"),
        P(None, None, "fsdp", "tensor"),
        P(None, "tensor", "fsdp"),
        P(("fsdp", "tensor"), None),
    )
    out_specs = (
        P(None, ("fsdp", "tensor"), None),
        P(("fsdp", "tensor"), None),
        P(),
        P(),
        P(),
        P(None, None, "fsdp", "tensor"),
        P(None, "fsdp", "tensor"),
        P(None, None, None, "tensor"),
        P(None, "tensor", "fsdp"),
        P(None, None, "fsdp", "tensor"),
        P(None, "tensor", "fsdp"),
    )
    return jax.shard_map(
        on_device, mesh=mesh, in_specs=in_specs, out_specs=out_specs, check_vma=False
    )
```

time: 939 us -> 298 us (0.32)
  waiting for transfers between devices: 647 us -> 75.9 us
  blocking collectives: 130 us -> 0 us
  Pallas kernels: 48 us -> 123 us
  matrix products: 59.9 us -> 0 us
  starting transfers between devices: 1.31 us -> 43.4 us
  other arithmetic: 18.2 us -> 4.85 us
  local copies, waits for them, and re-layouts: 19.4 us -> 32.5 us
    reduce_scatter x8 -> x1, waiting for transfers between devices: 461 us -> 0.01 us  [on_device(): d_ffn = lax.psum_scatter(blocks, 'fsdp', scatter_dimension=0, tiled=False)]
    all_gather x7 -> x1, waiting for transfers between devices: 183 us -> 0.01 us  [on_device(): weights = lax.all_gather(ffn_own, 'fsdp', axis=1, tiled=True)]
    psum x2 -> x0, blocking collectives: 77.2 us -> none  [the longest x1 39.8 us: on_device(): lax.psum((d_attn_gain[None], d_ffn_gain[None], d_head), ('fsdp', 'tensor'))]
    ppermute x0 -> x46, waiting for transfers between devices: none -> 75.9 us  [the longest x38 47.3 us: hop(): return lax.ppermute(value, axis, [(i, i ^ bit) for i in range(n)])]
    pallas_call x2 -> x17, Pallas kernels: 48 us -> 123 us  [the longest x1 34.7 us: mixer_bwd(): pl.pallas_call(functools.partial(bwd_kernel, heads, cb, n_f, shard), grid...]
    dot_general x12 -> x0, matrix products: 59.9 us -> none  [the longest x1 8.14 us: on_device(): jnp.einsum('ld,sdf->slf', gathered_ffn, expand_full, preferred_element_ty...]
    all_gather x2 -> x0, blocking collectives: 52.7 us -> none  [the longest x1 30.4 us: on_device(): out_full = lax.all_gather(out_weight[0], 'fsdp', axis=1, tiled=True)]
    ppermute x0 -> x46, starting transfers between devices: none -> 43.3 us  [the longest x38 34 us: hop(): return lax.ppermute(value, axis, [(i, i ^ bit) for i in range(n)])]
  transfers between devices with their start and end apart: 16 -> 48, of which waited for: 14 -> 17; matrix products, arithmetic and copies ran while one was open for 6% -> 9% of each run, Pallas kernels for 0% -> 37%
where the time goes in v3:
time: 298 us; the launch traced here: 295 us
  Pallas kernels  123 us (41%)
  waiting for transfers between devices  75.9 us (25%)
  starting transfers between devices  43.4 us (15%)
  local copies, waits for them, and re-layouts  32.5 us (11%)
  between operations  14.9 us (5%)
  other arithmetic  4.85 us (2%)
    ppermute x38, waiting for transfers between devices, hop(): return lax.ppermute(value, axis, [(i, i ^ bit) for i in range(n)])  47.3 us
    pallas_call x1, Pallas kernels, mixer_bwd(): pl.pallas_call(functools.partial(bwd_kernel, heads, cb, n_f, shard), grid...  34.7 us
    ppermute x38, starting transfers between devices, hop(): return lax.ppermute(value, axis, [(i, i ^ bit) for i in range(n)])  34 us
    pallas_call x2, Pallas kernels, mixer_fwd(): pl.pallas_call(functools.partial(fwd_call_kernel, heads, cb, base, len(ol...  28 us
    pallas_call x2, Pallas kernels, ffn(): pl.pallas_call(functools.partial(ffn_kernel, ff), grid=(1,), in_specs=[wh...  22.4 us
    ppermute x3, waiting for transfers between devices, step(): self.a = lax.ppermute(self.a, 'fsdp', self.right)  15.2 us
    dynamic_update_slice x8, local copies, waits for them, and re-layouts, in_order(): lax.dynamic_update_slice(full, block[None], (me ^ k,) + (0,) * own.ndim)  11.4 us
    pallas_call x1, Pallas kernels, ffn_grads(): pl.pallas_call(functools.partial(ffn_grads_kernel, ff, len(pieces)), grid...  9.18 us
  transfers between devices with their start and end apart: 48, of which 17 were waited for; matrix products, arithmetic and copies ran while one was open for 9% of the time, Pallas kernels for 37%

profile of v3, /device:TPU:0, one launch (start us, length us, event | category | flops | bytes accessed | tf_op | source)
XLA Modules:
  0.0 294.6 jit_solution(12945610990551903719)
XLA Ops:
  7.2 1.4 copy.45
  8.7 1.8 pack.1
  10.4 1.0 slice_bitcast_fusion.1
  11.5 1.8 pad_maximum_fusion
  13.3 3.1 %collective-permute-start = (bf16[128,1152]{1,0:T(8,128)(2,1)}, bf16[128,1152]{1,0:T(8,128)(2,1)}, u32[]{:S(2)}, u32[]{:S(2)}) collective-permute-start(bf16[128,1152]{1,0:T(8,128)(2,1)} %pack.1), channel_id=1, source_target_pairs={{0,8},{8,16},{16,24},{24,28},{28,20},{20,12},{12,4},{4,0},{1,9},{9... | collective-permute-start | bytes 884744 | tf_op jit(solution)/shard_map/ppermute | solution.py:746
  16.4 2.0 collective-permute-start.2
  19.3 1.0 constant_dynamic-update-slice_fusion.8
  20.3 1.7 broadcast.20.clone
  22.0 1.9 bitcast_dynamic-update-slice_fusion.7
  24.8 1.6 broadcast.20.clone.1
  27.7 3.9 %collective-permute-done.2 = bf16[256,1024]{1,0:T(8,128)(2,1)} collective-permute-done((bf16[256,1024]{1,0:T(8,128)(2,1)}, bf16[256,1024]{1,0:T(8,128)(2,1)}, u32[]{:S(2)}, u32[]{:S(2)}) %collective-permute-start.2) | collective-permute-done | bytes 524320 | tf_op jit(solution)/shard_map/ppermute | solution.py:695
  31.6 2.0 collective-permute-start.4
  33.6 1.9 bitcast_dynamic-update-slice_fusion.6
  35.5 1.0 constant_dynamic-update-slice_fusion.7
  36.5 1.0 constant_dynamic-update-slice_fusion.6
  37.5 1.9 bitcast_dynamic-update-slice_fusion.5
  39.4 7.7 %collective-permute-done.4 = bf16[128,1152]{1,0:T(8,128)(2,1)S(1)} collective-permute-done((bf16[128,1152]{1,0:T(8,128)(2,1)}, bf16[128,1152]{1,0:T(8,128)(2,1)S(1)}, u32[]{:S(2)}, u32[]{:S(2)}) %collective-permute-start.4) | collective-permute-done | bytes 294944 | tf_op jit(solution)/shard_map/ppermute | solution.py:746
  47.1 3.7 %collective-permute-done.5 = bf16[128,1152]{1,0:T(8,128)(2,1)S(1)} collective-permute-done((bf16[128,1152]{1,0:T(8,128)(2,1)}, bf16[128,1152]{1,0:T(8,128)(2,1)S(1)}, u32[]{:S(2)}, u32[]{:S(2)}) %collective-permute-start.5) | collective-permute-done | bytes 294944 | tf_op jit(solution)/shard_map/ppermute | solution.py:748
  50.8 1.8 collective-permute-start.7
  53.8 7.5 %collective-permute-done.7 = bf16[128,1152]{1,0:T(8,128)(2,1)S(1)} collective-permute-done((bf16[128,1152]{1,0:T(8,128)(2,1)S(1)}, bf16[128,1152]{1,0:T(8,128)(2,1)S(1)}, u32[]{:S(2)}, u32[]{:S(2)}) %collective-permute-start.7) | collective-permute-done | bytes 294944 | tf_op jit(solution)/shard_map/ppermute | solution.py:746
  61.2 3.6 %collective-permute-done.8 = bf16[128,1152]{1,0:T(8,128)(2,1)S(1)} collective-permute-done((bf16[128,1152]{1,0:T(8,128)(2,1)S(1)}, bf16[128,1152]{1,0:T(8,128)(2,1)S(1)}, u32[]{:S(2)}, u32[]{:S(2)}) %collective-permute-start.8) | collective-permute-done | bytes 294944 | tf_op jit(solution)/shard_map/ppermute | solution.py:748
  66.2 2.2 collective-permute-start.11
  70.1 1.8 copy.46.refs_4_.cols_ref
  71.8 2.2 collective-permute-done.10
  75.0 3.9 %collective-permute-done.11 = bf16[64,1152]{1,0:T(8,128)(2,1)S(1)} collective-permute-done((bf16[64,1152]{1,0:T(8,128)(2,1)}, bf16[64,1152]{1,0:T(8,128)(2,1)S(1)}, u32[]{:S(2)}, u32[]{:S(2)}) %collective-permute-start.11) | collective-permute-done | bytes 147488 | tf_op jit(solution)/shard_map/ppermute | solution.py:744
  78.9 2.3 bitcast_dynamic-update-slice_fusion
  81.3 1.3 collective-permute-start.14
  83.9 14.0 %mixer_fwd.2 = (bf16[512,256]{1,0:T(8,128)(2,1)}, bf16[1024,256]{1,0:T(8,128)(2,1)}, bf16[1024,1024]{1,0:T(8,128)(2,1)}, f32[1024,896]{1,0:T(8,128)}, f32[1024,7...) custom-call(s32[1024]{0:T(1024)} %bitcast.62, ...), custom_call_target="tpu_custom_call" | custom-call | flops 10000000000 | bytes 10000000 | tf_op jit(solution)/shard_map/mixer_fwd/pallas_call | solution.py:353
  99.2 14.0 %mixer_fwd.3 = (bf16[512,256]{1,0:T(8,128)(2,1)}, bf16[1024,256]{1,0:T(8,128)(2,1)}, bf16[1024,1024]{1,0:T(8,128)(2,1)}, f32[1024,896]{1,0:T(8,128)}, f32[1024,7...) custom-call(s32[1024]{0:T(1024)} %bitcast.63, ...), custom_call_target="tpu_custom_call", output_to_operand_aliasing={{1}: (10, {}), {2}: (11, {}), {3}: (12, {}), {4}: (13, {}),... | custom-call | flops 10000000000 | bytes 10000000 | tf_op jit(solution)/shard_map/mixer_fwd/pallas_call | solution.py:353
  113.6 1.2 collective-permute-start.19
  115.6 11.1 %ffn.2 = (f32[256,1024]{1,0:T(8,128)}, bf16[512,1024]{1,0:T(8,128)(2,1)}, bf16[704,512]{1,0:T(8,128)(2,1)}, bf16[1408,512]{1,0:T(8,128)(2,1)}, f32[256,1024]{1,0...) custom-call(bf16[512,256]{1,0:T(8,128)(2,1)} %get-tuple-element.170.refs_0_, bf16[512,256]{1,0:T(8,128)(2,1)} %copy-done.33, ...), custom_call_target="tpu_custom_call" | custom-call | flops 10000000000 | bytes 10000000 | tf_op jit(solution)/shard_map/ffn/pallas_call | solution.py:507
  127.4 1.7 collective-permute-done.23
  129.0 1.4 add_convert_fusion.1.low_ref
  130.5 1.2 collective-permute-start.24
  131.7 11.3 %ffn.3 = (f32[256,1024]{1,0:T(8,128)}, bf16[512,1024]{1,0:T(8,128)(2,1)}, bf16[704,512]{1,0:T(8,128)(2,1)}, bf16[1408,512]{1,0:T(8,128)(2,1)}, f32[256,1024]{1,0...) custom-call(bf16[512,256]{1,0:T(8,128)(2,1)} %get-tuple-element.188.refs_0_, bf16[512,256]{1,0:T(8,128)(2,1)} %copy-done.35, ...), custom_call_target="tpu_custom_call" | custom-call | flops 10000000000 | bytes 10000000 | tf_op jit(solution)/shard_map/ffn/pallas_call | solution.py:507
  143.0 1.8 collective-permute-done.24.other_ref
  147.8 9.2 %ffn_grads.1.refs_3_.wait_for = bf16[8,2112,128]{2,1,0:T(8,128)(2,1)} custom-call(bf16[1408,512]{1,0:T(8,128)(2,1)} %get-tuple-element.214.refs_0_, bf16[704,512]{1,0:T(8,128)(2,1)} %get-tuple-element.212.refs_1_.refs_0_, bf16[512,1024]{1,0:T(8,128)(2,1)} %get-tuple-element.215.refs_2_, bf16[1408,512]{1,0:T(8,128)(2,1)} %get-tuple-element.216.refs_3_, ...), custom_call_target="tpu_custom_call" | custom-call | flops 5000000000 | bytes 10000000 | tf_op jit(solution)/shard_map/ffn_grads/pallas_call | solution.py:594
  157.0 1.0 copy-done.3
  158.0 1.0 collective-permute-start.26
  159.1 5.8 %down.1 = (bf16[2,256,1024]{2,1,0:T(8,128)(2,1)}, f32[2,256,1024]{2,1,0:T(8,128)}) custom-call(bf16[704,512]{1,0:T(8,128)(2,1)} %get-tuple-element.212.refs_1_.refs_0_, bf16[704,512]{1,0:T(8,128)(2,1)} %get-tuple-element.213.refs_4_.refs_1_, bf16[2112,1024]{1,0:T(8,128)(2,1)} %all-gather.2.cloned.1.call-done.refs_9_.refs_2_, ...), custom_call_target="tpu_custom_call" | custom-call | flops 1 | bytes 1 | tf_op jit(solution)/shard_map/down/pallas_call | solution.py:558
  164.8 7.2 %collective-permute-done.26.other_ref = bf16[256,1024]{1,0:T(8,128)(2,1)S(1)} collective-permute-done((bf16[256,1024]{1,0:T(8,128)(2,1)S(1)}, bf16[256,1024]{1,0:T(8,128)(2,1)S(1)}, u32[]{:S(2)}, u32[]{:S(2)}) %collective-permute-start.26) | collective-permute-done | bytes 524320 | tf_op jit(solution)/shard_map/ppermute | solution.py:695
  174.1 2.1 collective-permute-done.28.ga1c_ref
  177.0 34.7 %mixer_bwd.1 = (bf16[4,128,512]{2,1,0:T(8,128)(2,1)}, bf16[4,128,512]{2,1,0:T(8,128)(2,1)}, bf16[4,128,512]{2,1,0:T(8,128)(2,1)}, bf16[4,128,512]{2,1,0:T(8,128)...) custom-call(s32[1024]{0:T(1024)} %bitcast.64, ...), custom_call_target="tpu_custom_call" | custom-call | flops 10000000000 | bytes 10000000 | tf_op jit(solution)/shard_map/mixer_bwd/pallas_call | solution.py:385
  212.0 3.7 %collective-permute-start.31 = (bf16[4,128,512]{2,1,0:T(8,128)(2,1)}, bf16[4,128,512]{2,1,0:T(8,128)(2,1)S(1)}, u32[]{:S(2)}, u32[]{:S(2)}) collective-permute-start(bf16[4,128,512]{2,1,0:T(8,128)(2,1)} %get-tuple-element.255), channel_id=1, source_target_pairs={{0,4},{4,0},{8,12},{12,8},{16,20},{20,16},{24,28},{28,24},{1,5},{5... | collective-permute-start | bytes 1572872 | tf_op jit(solution)/shard_map/ppermute | solution.py:695
  215.7 4.5 %collective-permute-start.32 = (bf16[4,128,512]{2,1,0:T(8,128)(2,1)}, bf16[4,128,512]{2,1,0:T(8,128)(2,1)S(1)}, u32[]{:S(2)}, u32[]{:S(2)}) collective-permute-start(bf16[4,128,512]{2,1,0:T(8,128)(2,1)} %get-tuple-element.256), channel_id=1, source_target_pairs={{0,8},{4,12},{8,0},{12,4},{16,24},{20,28},{24,16},{28,20},{1,9},{5... | collective-permute-start | bytes 1572872 | tf_op jit(solution)/shard_map/ppermute | solution.py:695
  220.1 1.1 collective-permute-start.34
  222.0 3.1 %to_chips.3 = (f32[256,1024]{1,0:T(8,128)}, bf16[256,1024]{1,0:T(8,128)(2,1)}) custom-call(f32[2,256,1024]{2,1,0:T(8,128)} %get-tuple-element.258.keep, bf16[2,256,1024]{2,1,0:T(8,128)(2,1)} %copy-done.10, bf16[8,2112,128]{2,1,0:T(8,128)(2,1)} %ffn_grads.1.refs_3_.wait_for), custom_call_target="tpu_custom_call" | custom-call | flops 1 | bytes 1 | tf_op jit(solution)/shard_map/to_chips/pallas_call | solution.py:614
  225.2 3.2 %to_chips.2 = (f32[256,1024]{1,0:T(8,128)}, bf16[256,1024]{1,0:T(8,128)(2,1)}) custom-call(f32[2,256,1024]{2,1,0:T(8,128)} %get-tuple-element.250.keep, bf16[2,256,1024]{2,1,0:T(8,128)(2,1)} %copy-done.11, f32[8,1024]{1,0:T(8,128)} %get-tuple-element.252.wait_for), custom_call_target="tpu_custom_call" | custom-call | flops 1 | bytes 1 | tf_op jit(solution)/shard_map/to_chips/pallas_call | solution.py:614
  228.4 3.9 %collective-permute-done.31.g1_ref = bf16[4,128,512]{2,1,0:T(8,128)(2,1)S(1)} collective-permute-done((bf16[4,128,512]{2,1,0:T(8,128)(2,1)}, bf16[4,128,512]{2,1,0:T(8,128)(2,1)S(1)}, u32[]{:S(2)}, u32[]{:S(2)}) %collective-permute-start.31) | collective-permute-done | bytes 524320 | tf_op jit(solution)/shard_map/ppermute | solution.py:695
  232.6 1.3 collective-permute-start.39
  234.7 1.3 collective-permute-start.38
  236.0 2.6 fold.2
  239.5 2.2 collective-permute-start.37
  241.7 22.8 %collective-permute-done.36.g1_ref = bf16[2,128,512]{2,1,0:T(8,128)(2,1)S(1)} collective-permute-done((bf16[2,128,512]{2,1,0:T(8,128)(2,1)}, bf16[2,128,512]{2,1,0:T(8,128)(2,1)S(1)}, u32[]{:S(2)}, u32[]{:S(2)}) %collective-permute-start.36) | collective-permute-done | bytes 262176 | tf_op jit(solution)/shard_map/ppermute | solution.py:695
  265.3 2.0 fold.3
  267.3 1.1 collective-permute-start.41
  268.5 1.7 collective-permute-start.42
  270.2 1.9 collective-permute-start.43
  272.1 1.3 collective-permute-start.44
  273.4 1.2 collective-permute-start.45
  274.6 5.0 %last_rows.1 = (f32[256,1024]{1,0:T(8,128)}, bf16[256,1024]{1,0:T(8,128)(2,1)}) custom-call(f32[256,1024]{1,0:T(8,128)} %copy-done.4, f32[256,1024]{1,0:T(8,128)} %copy-done.5, f32[256,1024]{1,0:T(8,128)} %get-tuple-element.253.na, bf16[256,1024]{1,0:T(8,128)(2,1)} %copy-done.13, bf16[256,1024]{1,0:T(8,128)(2,1)} %x_ref.1, f32[1,1024]{1,0:T(1,128)} %gain_ref.7, ...), custom_call_target="tpu_custom_call" | custom-call | flops 1 | bytes 1 | tf_op jit(solution)/shard_map/last_rows/pallas_call | solution.py:634
  279.6 3.0 %collective-permute-done.44.refs_1_ = f32[24,1024]{1,0:T(8,128)S(1)} collective-permute-done((f32[24,1024]{1,0:T(8,128)S(1)}, f32[24,1024]{1,0:T(8,128)S(1)}, u32[]{:S(2)}, u32[]{:S(2)}) %collective-permute-start.44) | collective-permute-done | bytes 98336 | tf_op jit(solution)/shard_map/ppermute | solution.py:695
  283.4 2.1 finish.1
  285.5 2.1 ffn_cast.1
  (171 shorter events, 23.2 us)
Async XLA Ops:
  7.2 11.2 %copy-start = (bf16[256,1024]{1,0:T(8,128)(2,1)S(1)}, bf16[256,1024]{1,0:T(8,128)(2,1)}, u32[]{:S(2)}) copy-start(bf16[256,1024]{1,0:T(8,128)(2,1)} %cot_ref.3) | copy-start | bytes 1572868
  7.2 11.3 %copy-start.22 = (s32[1,1024]{1,0:T(1,128)S(1)}, s32[1,1024]{1,0:T(1,128)}, u32[]{:S(2)}) copy-start(s32[1,1024]{1,0:T(1,128)} %param.14) | copy-start | bytes 12292
  7.2 107.7 %all-gather.2.cloned.1.call-start = ((), (), s32[]{:S(2)}) async-start(), calls=%async_computation.1 | async-start | bytes 4866048 | tf_op jit(solution)/shard_map/all_gather | solution.py:783
  13.3 272.2 %reduce-scatter.2.cloned.1.call-start = ((), (), s32[]{:S(2)}) async-start(), calls=%async_computation.2 | async-start | bytes 4866048 | tf_op jit(solution)/shard_map/reduce_scatter | solution.py:849
  13.3 13.9 %collective-permute-start = (bf16[128,1152]{1,0:T(8,128)(2,1)}, bf16[128,1152]{1,0:T(8,128)(2,1)}, u32[]{:S(2)}, u32[]{:S(2)}) collective-permute-start(bf16[128,1152]{1,0:T(8,128)(2,1)} %pack.1), channel_id=1, source_target_pairs={{0,8},{8,16},{16,24},{24,28},{28,20},{20,12},{12,4},{4,0},{1,9},{9... | collective-permute-start | bytes 884744 | tf_op jit(solution)/shard_map/ppermute | solution.py:746
  16.4 11.3 %collective-permute-start.1 = (bf16[128,1152]{1,0:T(8,128)(2,1)}, bf16[128,1152]{1,0:T(8,128)(2,1)}, u32[]{:S(2)}, u32[]{:S(2)}) collective-permute-start(bf16[128,1152]{1,0:T(8,128)(2,1)} %pack.1), channel_id=1, source_target_pairs={{8,0},{16,8},{24,16},{28,24},{20,28},{12,20},{4,12},{0,4},{9,1},{1... | collective-permute-start | bytes 884744 | tf_op jit(solution)/shard_map/ppermute | solution.py:748
  16.4 15.2 %collective-permute-start.2 = (bf16[256,1024]{1,0:T(8,128)(2,1)}, bf16[256,1024]{1,0:T(8,128)(2,1)}, u32[]{:S(2)}, u32[]{:S(2)}) collective-permute-start(bf16[256,1024]{1,0:T(8,128)(2,1)} %x_ref.1), channel_id=1, source_target_pairs={{0,2},{1,3},{2,0},{3,1},{4,6},{5,7},{6,4},{7,5},{8,10},{9,11},{10,... | collective-permute-start | bytes 1572872 | tf_op jit(solution)/shard_map/ppermute | solution.py:695
  18.4 13.2 %collective-permute-start.3 = (bf16[256,1024]{1,0:T(8,128)(2,1)}, bf16[256,1024]{1,0:T(8,128)(2,1)}, u32[]{:S(2)}, u32[]{:S(2)}) collective-permute-start(bf16[256,1024]{1,0:T(8,128)(2,1)} %x_ref.1), channel_id=1, source_target_pairs={{0,1},{1,0},{2,3},{3,2},{4,5},{5,4},{6,7},{7,6},{8,9},{9,8},{10,11... | collective-permute-start | bytes 1572872 | tf_op jit(solution)/shard_map/ppermute | solution.py:695
  18.4 35.4 %collective-permute-start.9 = (bf16[256,1024]{1,0:T(8,128)(2,1)S(1)}, bf16[256,1024]{1,0:T(8,128)(2,1)S(1)}, u32[]{:S(2)}, u32[]{:S(2)}) collective-permute-start(bf16[256,1024]{1,0:T(8,128)(2,1)S(1)} %copy-done), channel_id=1, source_target_pairs={{0,2},{1,3},{2,0},{3,1},{4,6},{5,7},{6,4},{7,5},{8,10},{9,11},{10,... | collective-permute-start | bytes 1572872 | tf_op jit(solution)/shard_map/ppermute | solution.py:695
  19.3 4.6 %copy-start.29 = (s32[1,1024]{1,0:T(1,128)S(1)}, s32[1,1024]{1,0:T(1,128)}, u32[]{:S(2)}) copy-start(s32[1,1024]{1,0:T(1,128)} %param.15) | copy-start | bytes 12292
  27.2 42.0 %collective-permute-start.12 = (bf16[256,1024]{1,0:T(8,128)(2,1)S(1)}, bf16[256,1024]{1,0:T(8,128)(2,1)S(1)}, u32[]{:S(2)}, u32[]{:S(2)}) collective-permute-start(bf16[256,1024]{1,0:T(8,128)(2,1)S(1)} %copy-done), channel_id=1, source_target_pairs={{0,1},{1,0},{2,3},{3,2},{4,5},{5,4},{6,7},{7,6},{8,9},{9,8},{10,11... | collective-permute-start | bytes 1572872 | tf_op jit(solution)/shard_map/ppermute | solution.py:695
  31.6 19.2 %collective-permute-start.6 = (bf16[256,1024]{1,0:T(8,128)(2,1)}, bf16[256,1024]{1,0:T(8,128)(2,1)S(1)}, u32[]{:S(2)}, u32[]{:S(2)}) collective-permute-start(bf16[256,1024]{1,0:T(8,128)(2,1)} %collective-permute-done.2), channel_id=1, source_target_pairs={{0,1},{1,0},{2,3},{3,2},{4,5},{5,4},{6,7},{7,6},{8,9},{9,8},{10,11... | collective-permute-start | bytes 1572872 | tf_op jit(solution)/shard_map/ppermute | solution.py:695
  31.6 15.5 %collective-permute-start.4 = (bf16[128,1152]{1,0:T(8,128)(2,1)}, bf16[128,1152]{1,0:T(8,128)(2,1)S(1)}, u32[]{:S(2)}, u32[]{:S(2)}) collective-permute-start(bf16[128,1152]{1,0:T(8,128)(2,1)} %collective-permute-done), channel_id=1, source_target_pairs={{0,8},{8,16},{16,24},{24,28},{28,20},{20,12},{12,4},{4,0},{1,9},{9... | collective-permute-start | bytes 884744 | tf_op jit(solution)/shard_map/ppermute | solution.py:746
  33.6 17.2 %collective-permute-start.5 = (bf16[128,1152]{1,0:T(8,128)(2,1)}, bf16[128,1152]{1,0:T(8,128)(2,1)S(1)}, u32[]{:S(2)}, u32[]{:S(2)}) collective-permute-start(bf16[128,1152]{1,0:T(8,128)(2,1)} %collective-permute-done.1), channel_id=1, source_target_pairs={{8,0},{16,8},{24,16},{28,24},{20,28},{12,20},{4,12},{0,4},{9,1},{1... | collective-permute-start | bytes 884744 | tf_op jit(solution)/shard_map/ppermute | solution.py:748
  50.8 10.4 %collective-permute-start.7 = (bf16[128,1152]{1,0:T(8,128)(2,1)S(1)}, bf16[128,1152]{1,0:T(8,128)(2,1)S(1)}, u32[]{:S(2)}, u32[]{:S(2)}) collective-permute-start(bf16[128,1152]{1,0:T(8,128)(2,1)S(1)} %collective-permute-done.4), channel_id=1, source_target_pairs={{0,8},{8,16},{16,24},{24,28},{28,20},{20,12},{12,4},{4,0},{1,9},{9... | collective-permute-start | bytes 884744 | tf_op jit(solution)/shard_map/ppermute | solution.py:746
  52.5 12.3 %collective-permute-start.8 = (bf16[128,1152]{1,0:T(8,128)(2,1)S(1)}, bf16[128,1152]{1,0:T(8,128)(2,1)S(1)}, u32[]{:S(2)}, u32[]{:S(2)}) collective-permute-start(bf16[128,1152]{1,0:T(8,128)(2,1)S(1)} %collective-permute-done.5), channel_id=1, source_target_pairs={{8,0},{16,8},{24,16},{28,24},{20,28},{12,20},{4,12},{0,4},{9,1},{1... | collective-permute-start | bytes 884744 | tf_op jit(solution)/shard_map/ppermute | solution.py:748
  65.5 8.6 %collective-permute-start.10 = (bf16[64,1152]{1,0:T(8,128)(2,1)}, bf16[64,1152]{1,0:T(8,128)(2,1)}, u32[]{:S(2)}, u32[]{:S(2)}) collective-permute-start(bf16[64,1152]{1,0:T(8,128)(2,1)} %slice.36), channel_id=1, source_target_pairs={{0,8},{8,16},{16,24},{24,28},{28,20},{20,12},{12,4},{4,0},{1,9},{9... | collective-permute-start | bytes 442376 | tf_op jit(solution)/shard_map/ppermute | solution.py:743
  66.2 12.7 %collective-permute-start.11 = (bf16[64,1152]{1,0:T(8,128)(2,1)}, bf16[64,1152]{1,0:T(8,128)(2,1)S(1)}, u32[]{:S(2)}, u32[]{:S(2)}) collective-permute-start(bf16[64,1152]{1,0:T(8,128)(2,1)} %slice.37), channel_id=1, source_target_pairs={{8,0},{16,8},{24,16},{28,24},{20,28},{12,20},{4,12},{0,4},{9,1},{1... | collective-permute-start | bytes 442376 | tf_op jit(solution)/shard_map/ppermute | solution.py:744
  68.3 10.6 %collective-permute-start.13 = (bf16[256,1024]{1,0:T(8,128)(2,1)S(1)}, bf16[256,1024]{1,0:T(8,128)(2,1)}, u32[]{:S(2)}, u32[]{:S(2)}) collective-permute-start(bf16[256,1024]{1,0:T(8,128)(2,1)S(1)} %collective-permute-done.9.coty_ref), channel_id=1, source_target_pairs={{0,1},{1,0},{2,3},{3,2},{4,5},{5,4},{6,7},{7,6},{8,9},{9,8},{10,11... | collective-permute-start | bytes 1572872 | tf_op jit(solution)/shard_map/ppermute | solution.py:695
  78.9 4.9 %copy-start.9 = (bf16[1024,1152]{1,0:T(8,128)(2,1)}, bf16[1024,1152]{1,0:T(8,128)(2,1)S(1)}, u32[]{:S(2)}) copy-start(bf16[1024,1152]{1,0:T(8,128)(2,1)S(1)} %constant_dynamic-update-slice_fusion.refs_2_.wide_ref) | copy-start | bytes 7077892
  81.3 16.6 %copy-start.15 = (bf16[1024,256]{1,0:T(8,128)(2,1)}, bf16[1024,256]{1,0:T(8,128)(2,1)S(1)}, u32[]{:S(2)}) copy-start(bf16[1024,256]{1,0:T(8,128)(2,1)S(1)} %slice.38.refs_4_.out_ref) | copy-start | bytes 1572868
  81.3 16.6 %collective-permute-start.14 = (bf16[1024,256]{1,0:T(8,128)(2,1)S(1)}, bf16[1024,256]{1,0:T(8,128)(2,1)}, u32[]{:S(2)}, u32[]{:S(2)}) collective-permute-start(bf16[1024,256]{1,0:T(8,128)(2,1)S(1)} %slice.38.refs_4_.out_ref), channel_id=1, source_target_pairs={{0,2},{1,3},{2,0},{3,1},{4,6},{5,7},{6,4},{7,5},{8,10},{9,11},{10,... | collective-permute-start | bytes 1572872 | tf_op jit(solution)/shard_map/ppermute | solution.py:695
  82.6 15.3 %collective-permute-start.15 = (bf16[1024,256]{1,0:T(8,128)(2,1)S(1)}, bf16[1024,256]{1,0:T(8,128)(2,1)}, u32[]{:S(2)}, u32[]{:S(2)}) collective-permute-start(bf16[1024,256]{1,0:T(8,128)(2,1)S(1)} %slice.38.refs_4_.out_ref), channel_id=1, source_target_pairs={{0,1},{1,0},{2,3},{3,2},{4,5},{5,4},{6,7},{7,6},{8,9},{9,8},{10,11... | collective-permute-start | bytes 1572872 | tf_op jit(solution)/shard_map/ppermute | solution.py:695
  97.9 15.4 %collective-permute-start.16 = (bf16[512,256]{1,0:T(8,128)(2,1)}, bf16[512,256]{1,0:T(8,128)(2,1)S(1)}, u32[]{:S(2)}, u32[]{:S(2)}) collective-permute-start(bf16[512,256]{1,0:T(8,128)(2,1)} %get-tuple-element.170.refs_0_), channel_id=1, source_target_pairs={{0,2},{1,3},{2,0},{3,1},{4,6},{5,7},{6,4},{7,5},{8,10},{9,11},{10,... | collective-permute-start | bytes 786440 | tf_op jit(solution)/shard_map/ppermute | solution.py:695
  98.7 14.5 %collective-permute-start.17 = (bf16[512,256]{1,0:T(8,128)(2,1)}, bf16[512,256]{1,0:T(8,128)(2,1)S(1)}, u32[]{:S(2)}, u32[]{:S(2)}) collective-permute-start(bf16[512,256]{1,0:T(8,128)(2,1)} %get-tuple-element.170.refs_0_), channel_id=1, source_target_pairs={{0,1},{1,0},{2,3},{3,2},{4,5},{5,4},{6,7},{7,6},{8,9},{9,8},{10,11... | collective-permute-start | bytes 786440 | tf_op jit(solution)/shard_map/ppermute | solution.py:695
  99.0 14.3 %collective-permute-start.18 = (bf16[1024,256]{1,0:T(8,128)(2,1)}, bf16[1024,256]{1,0:T(8,128)(2,1)S(1)}, u32[]{:S(2)}, u32[]{:S(2)}) collective-permute-start(bf16[1024,256]{1,0:T(8,128)(2,1)} %collective-permute-done.14.refs_5_), channel_id=1, source_target_pairs={{0,1},{1,0},{2,3},{3,2},{4,5},{5,4},{6,7},{7,6},{8,9},{9,8},{10,11... | collective-permute-start | bytes 1572872 | tf_op jit(solution)/shard_map/ppermute | solution.py:695
  113.3 1.6 collective-permute-start.21
  113.6 13.1 %collective-permute-start.19 = (bf16[512,256]{1,0:T(8,128)(2,1)}, bf16[512,256]{1,0:T(8,128)(2,1)S(1)}, u32[]{:S(2)}, u32[]{:S(2)}) collective-permute-start(bf16[512,256]{1,0:T(8,128)(2,1)} %get-tuple-element.188.refs_0_), channel_id=1, source_target_pairs={{0,2},{1,3},{2,0},{3,1},{4,6},{5,7},{6,4},{7,5},{8,10},{9,11},{10,... | collective-permute-start | bytes 786440 | tf_op jit(solution)/shard_map/ppermute | solution.py:695
  114.9 11.9 %collective-permute-start.20 = (bf16[512,256]{1,0:T(8,128)(2,1)}, bf16[512,256]{1,0:T(8,128)(2,1)S(1)}, u32[]{:S(2)}, u32[]{:S(2)}) collective-permute-start(bf16[512,256]{1,0:T(8,128)(2,1)} %get-tuple-element.188.refs_0_), channel_id=1, source_target_pairs={{0,1},{1,0},{2,3},{3,2},{4,5},{5,4},{6,7},{7,6},{8,9},{9,8},{10,11... | collective-permute-start | bytes 786440 | tf_op jit(solution)/shard_map/ppermute | solution.py:695
  126.7 5.0 %copy-start.35 = (bf16[512,256]{1,0:T(8,128)(2,1)}, bf16[512,256]{1,0:T(8,128)(2,1)S(1)}, u32[]{:S(2)}) copy-start(bf16[512,256]{1,0:T(8,128)(2,1)S(1)} %collective-permute-done.19.refs_1_) | copy-start | bytes 786436
  126.8 2.3 collective-permute-start.23
  127.3 3.1 %collective-permute-start.22 = (bf16[512,256]{1,0:T(8,128)(2,1)S(1)}, bf16[512,256]{1,0:T(8,128)(2,1)S(1)}, u32[]{:S(2)}, u32[]{:S(2)}) collective-permute-start(bf16[512,256]{1,0:T(8,128)(2,1)S(1)} %collective-permute-done.19.refs_1_), channel_id=1, source_target_pairs={{0,1},{1,0},{2,3},{3,2},{4,5},{5,4},{6,7},{7,6},{8,9},{9,8},{10,11... | collective-permute-start | bytes 786440 | tf_op jit(solution)/shard_map/ppermute | solution.py:695
  130.4 14.3 %copy-start.1 = (f32[256,1024]{1,0:T(8,128)S(1)}, f32[256,1024]{1,0:T(8,128)}, u32[]{:S(2)}) copy-start(f32[256,1024]{1,0:T(8,128)} %get-tuple-element.205.mid_ref.mid0) | copy-start | bytes 3145732
  130.4 14.3 %copy-start.6 = (f32[1,1024]{1,0:T(1,128)S(1)}, f32[1,1024]{1,0:T(1,128)}, u32[]{:S(2)}) copy-start(f32[1,1024]{1,0:T(1,128)} %gain_ref.5) | copy-start | bytes 12292
  130.5 14.3 %collective-permute-start.24 = (bf16[256,1024]{1,0:T(8,128)(2,1)S(1)}, bf16[256,1024]{1,0:T(8,128)(2,1)S(1)}, u32[]{:S(2)}, u32[]{:S(2)}) collective-permute-start(bf16[256,1024]{1,0:T(8,128)(2,1)S(1)} %add_convert_fusion.1.low_ref), channel_id=1, source_target_pairs={{0,2},{1,3},{2,0},{3,1},{4,6},{5,7},{6,4},{7,5},{8,10},{9,11},{10,... | collective-permute-start | bytes 1572872 | tf_op jit(solution)/shard_map/ppermute | solution.py:695
  144.7 2.1 collective-permute-start.25
  146.3 12.8 %copy-start.7 = (bf16[256,1024]{1,0:T(8,128)(2,1)}, bf16[256,1024]{1,0:T(8,128)(2,1)S(1)}, u32[]{:S(2)}) copy-start(bf16[256,1024]{1,0:T(8,128)(2,1)S(1)} %get-tuple-element.211.ga0_ref) | copy-start | bytes 1572868
  158.0 14.0 %copy-start.2 = (f32[256,1024]{1,0:T(8,128)S(1)}, f32[256,1024]{1,0:T(8,128)}, u32[]{:S(2)}) copy-start(f32[256,1024]{1,0:T(8,128)} %get-tuple-element.220.mid_ref.mid1) | copy-start | bytes 3145732
  158.0 14.0 %collective-permute-start.26 = (bf16[256,1024]{1,0:T(8,128)(2,1)S(1)}, bf16[256,1024]{1,0:T(8,128)(2,1)S(1)}, u32[]{:S(2)}, u32[]{:S(2)}) collective-permute-start(bf16[256,1024]{1,0:T(8,128)(2,1)S(1)} %copy-done.3), channel_id=1, source_target_pairs={{0,2},{1,3},{2,0},{3,1},{4,6},{5,7},{6,4},{7,5},{8,10},{9,11},{10,... | collective-permute-start | bytes 1572872 | tf_op jit(solution)/shard_map/ppermute | solution.py:695
  159.1 12.9 %collective-permute-start.27 = (bf16[256,1024]{1,0:T(8,128)(2,1)S(1)}, bf16[256,1024]{1,0:T(8,128)(2,1)}, u32[]{:S(2)}, u32[]{:S(2)}) collective-permute-start(bf16[256,1024]{1,0:T(8,128)(2,1)S(1)} %get-tuple-element.211.ga0_ref), channel_id=1, source_target_pairs={{0,1},{1,0},{2,3},{3,2},{4,5},{5,4},{6,7},{7,6},{8,9},{9,8},{10,11... | collective-permute-start | bytes 1572872 | tf_op jit(solution)/shard_map/ppermute | solution.py:695
  173.6 2.6 collective-permute-start.28
  173.6 38.2 %collective-permute-start.29 = (bf16[2,256,1024]{2,1,0:T(8,128)(2,1)}, bf16[2,256,1024]{2,1,0:T(8,128)(2,1)S(1)}, u32[]{:S(2)}, u32[]{:S(2)}) collective-permute-start(bf16[2,256,1024]{2,1,0:T(8,128)(2,1)} %get-tuple-element.249), channel_id=1, source_target_pairs={{0,1},{1,0},{2,3},{3,2},{4,5},{5,4},{6,7},{7,6},{8,9},{9,8},{10,11... | collective-permute-start | bytes 3145736 | tf_op jit(solution)/shard_map/ppermute | solution.py:695
  211.7 10.3 %copy-start.10 = (bf16[2,256,1024]{2,1,0:T(8,128)(2,1)}, bf16[2,256,1024]{2,1,0:T(8,128)(2,1)S(1)}, u32[]{:S(2)}) copy-start(bf16[2,256,1024]{2,1,0:T(8,128)(2,1)S(1)} %collective-permute-done.29.got) | copy-start | bytes 3145732
  211.8 9.5 %collective-permute-start.30 = (bf16[2,256,1024]{2,1,0:T(8,128)(2,1)}, bf16[2,256,1024]{2,1,0:T(8,128)(2,1)S(1)}, u32[]{:S(2)}, u32[]{:S(2)}) collective-permute-start(bf16[2,256,1024]{2,1,0:T(8,128)(2,1)} %get-tuple-element.251), channel_id=1, source_target_pairs={{0,1},{1,0},{2,3},{3,2},{4,5},{5,4},{6,7},{7,6},{8,9},{9,8},{10,11... | collective-permute-start | bytes 3145736 | tf_op jit(solution)/shard_map/ppermute | solution.py:695
  212.0 20.4 %collective-permute-start.31 = (bf16[4,128,512]{2,1,0:T(8,128)(2,1)}, bf16[4,128,512]{2,1,0:T(8,128)(2,1)S(1)}, u32[]{:S(2)}, u32[]{:S(2)}) collective-permute-start(bf16[4,128,512]{2,1,0:T(8,128)(2,1)} %get-tuple-element.255), channel_id=1, source_target_pairs={{0,4},{4,0},{8,12},{12,8},{16,20},{20,16},{24,28},{28,24},{1,5},{5... | collective-permute-start | bytes 1572872 | tf_op jit(solution)/shard_map/ppermute | solution.py:695
  215.7 16.9 %collective-permute-start.32 = (bf16[4,128,512]{2,1,0:T(8,128)(2,1)}, bf16[4,128,512]{2,1,0:T(8,128)(2,1)S(1)}, u32[]{:S(2)}, u32[]{:S(2)}) collective-permute-start(bf16[4,128,512]{2,1,0:T(8,128)(2,1)} %get-tuple-element.256), channel_id=1, source_target_pairs={{0,8},{4,12},{8,0},{12,4},{16,24},{20,28},{24,16},{28,20},{1,9},{5... | collective-permute-start | bytes 1572872 | tf_op jit(solution)/shard_map/ppermute | solution.py:695
  220.1 8.2 %collective-permute-start.33 = (f32[8,1024]{1,0:T(8,128)}, f32[8,1024]{1,0:T(8,128)S(1)}, u32[]{:S(2)}, u32[]{:S(2)}) collective-permute-start(f32[8,1024]{1,0:T(8,128)} %get-tuple-element.252.wait_for), channel_id=1, source_target_pairs={{0,1},{1,0},{2,3},{3,2},{4,5},{5,4},{6,7},{7,6},{8,9},{9,8},{10,11... | collective-permute-start | bytes 98312 | tf_op jit(solution)/shard_map/ppermute | solution.py:695
  220.1 8.2 %collective-permute-start.34 = (f32[8,1024]{1,0:T(8,128)}, f32[8,1024]{1,0:T(8,128)S(1)}, u32[]{:S(2)}, u32[]{:S(2)}) collective-permute-start(f32[8,1024]{1,0:T(8,128)} %get-tuple-element.252.wait_for), channel_id=1, source_target_pairs={{0,2},{1,3},{2,0},{3,1},{4,6},{5,7},{6,4},{7,5},{8,10},{9,11},{10,... | collective-permute-start | bytes 98312 | tf_op jit(solution)/shard_map/ppermute | solution.py:695
  221.2 7.2 %collective-permute-start.35 = (f32[8,1024]{1,0:T(8,128)}, f32[8,1024]{1,0:T(8,128)S(1)}, u32[]{:S(2)}, u32[]{:S(2)}) collective-permute-start(f32[8,1024]{1,0:T(8,128)} %get-tuple-element.252.wait_for), channel_id=1, source_target_pairs={{0,3},{1,2},{2,1},{3,0},{4,7},{5,6},{6,5},{7,4},{8,11},{9,10},{10,... | collective-permute-start | bytes 98312 | tf_op jit(solution)/shard_map/ppermute | solution.py:695
  225.2 8.7 %copy-start.31 = (bf16[256,1024]{1,0:T(8,128)(2,1)S(1)}, bf16[256,1024]{1,0:T(8,128)(2,1)}, u32[]{:S(2)}) copy-start(bf16[256,1024]{1,0:T(8,128)(2,1)} %get-tuple-element.274) | copy-start | bytes 1572868
  225.2 9.5 %copy-start.23 = (f32[8,1024]{1,0:T(8,128)S(1)}, f32[8,1024]{1,0:T(8,128)}, u32[]{:S(2)}) copy-start(f32[8,1024]{1,0:T(8,128)} %get-tuple-element.252.wait_for) | copy-start | bytes 98308
  225.2 9.5 %copy-start.19 = (f32[16,1024]{1,0:T(8,128)S(1)}, f32[16,1024]{1,0:T(8,128)}, u32[]{:S(2)}) copy-start(f32[16,1024]{1,0:T(8,128)} %get-tuple-element.267) | copy-start | bytes 196612
  232.6 31.9 %collective-permute-start.39 = (bf16[256,1024]{1,0:T(8,128)(2,1)}, bf16[256,1024]{1,0:T(8,128)(2,1)S(1)}, u32[]{:S(2)}, u32[]{:S(2)}) collective-permute-start(bf16[256,1024]{1,0:T(8,128)(2,1)} %get-tuple-element.271), channel_id=1, source_target_pairs={{0,2},{1,3},{2,0},{3,1},{4,6},{5,7},{6,4},{7,5},{8,10},{9,11},{10,... | collective-permute-start | bytes 1572872 | tf_op jit(solution)/shard_map/ppermute | solution.py:695
  233.9 39.5 %collective-permute-start.40 = (bf16[256,1024]{1,0:T(8,128)(2,1)S(1)}, bf16[256,1024]{1,0:T(8,128)(2,1)S(1)}, u32[]{:S(2)}, u32[]{:S(2)}) collective-permute-start(bf16[256,1024]{1,0:T(8,128)(2,1)S(1)} %copy-done.31), channel_id=1, source_target_pairs={{0,2},{1,3},{2,0},{3,1},{4,6},{5,7},{6,4},{7,5},{8,10},{9,11},{10,... | collective-permute-start | bytes 1572872 | tf_op jit(solution)/shard_map/ppermute | solution.py:695
  234.7 7.0 %collective-permute-start.38 = (f32[24,1024]{1,0:T(8,128)S(1)}, f32[24,1024]{1,0:T(8,128)S(1)}, u32[]{:S(2)}, u32[]{:S(2)}) collective-permute-start(f32[24,1024]{1,0:T(8,128)S(1)} %pad_maximum_fusion.1), channel_id=1, source_target_pairs={{0,4},{4,0},{8,12},{12,8},{16,20},{20,16},{24,28},{28,24},{1,5},{5... | collective-permute-start | bytes 294920 | tf_op jit(solution)/shard_map/ppermute | solution.py:695
  238.6 25.9 %collective-permute-start.36 = (bf16[2,128,512]{2,1,0:T(8,128)(2,1)}, bf16[2,128,512]{2,1,0:T(8,128)(2,1)S(1)}, u32[]{:S(2)}, u32[]{:S(2)}) collective-permute-start(bf16[2,128,512]{2,1,0:T(8,128)(2,1)} %get-tuple-element.265), channel_id=1, source_target_pairs={{0,8},{4,12},{8,0},{12,4},{16,24},{20,28},{24,16},{28,20},{1,9},{5... | collective-permute-start | bytes 786440 | tf_op jit(solution)/shard_map/ppermute | solution.py:695
  239.5 25.0 %collective-permute-start.37 = (bf16[2,128,512]{2,1,0:T(8,128)(2,1)}, bf16[2,128,512]{2,1,0:T(8,128)(2,1)S(1)}, u32[]{:S(2)}, u32[]{:S(2)}) collective-permute-start(bf16[2,128,512]{2,1,0:T(8,128)(2,1)} %get-tuple-element.266), channel_id=1, source_target_pairs={{0,16},{4,20},{8,24},{12,28},{16,0},{20,4},{24,8},{28,12},{1,17},{... | collective-permute-start | bytes 786440 | tf_op jit(solution)/shard_map/ppermute | solution.py:695
  241.7 37.8 %copy-start.18 = (f32[24,1024]{1,0:T(8,128)}, f32[24,1024]{1,0:T(8,128)S(1)}, u32[]{:S(2)}) copy-start(f32[24,1024]{1,0:T(8,128)S(1)} %fusion.2.s_ref) | copy-start | bytes 294916
  264.5 10.0 %copy-start.13 = (bf16[256,1024]{1,0:T(8,128)(2,1)}, bf16[256,1024]{1,0:T(8,128)(2,1)S(1)}, u32[]{:S(2)}) copy-start(bf16[256,1024]{1,0:T(8,128)(2,1)S(1)} %collective-permute-done.39.na_y) | copy-start | bytes 1572868
  267.3 15.3 %collective-permute-start.41 = (bf16[1,128,512]{2,1,0:T(8,128)(2,1)}, bf16[1,128,512]{2,1,0:T(8,128)(2,1)S(1)}, u32[]{:S(2)}, u32[]{:S(2)}) collective-permute-start(bf16[1,128,512]{2,1,0:T(8,128)(2,1)} %get-tuple-element.282), channel_id=1, source_target_pairs={{0,16},{4,20},{8,24},{12,28},{16,0},{20,4},{24,8},{28,12},{1,17},{... | collective-permute-start | bytes 393224 | tf_op jit(solution)/shard_map/ppermute | solution.py:695
  268.5 14.2 %collective-permute-start.42 = (bf16[1,128,512]{2,1,0:T(8,128)(2,1)}, bf16[1,128,512]{2,1,0:T(8,128)(2,1)S(1)}, u32[]{:S(2)}, u32[]{:S(2)}) collective-permute-start(bf16[1,128,512]{2,1,0:T(8,128)(2,1)} %get-tuple-element.284), channel_id=1, source_target_pairs={{0,4},{4,0},{8,12},{12,8},{16,20},{20,16},{24,28},{28,24},{1,5},{5... | collective-permute-start | bytes 393224 | tf_op jit(solution)/shard_map/ppermute | solution.py:695
  270.2 9.4 %collective-permute-start.43 = (f32[24,1024]{1,0:T(8,128)S(1)}, f32[24,1024]{1,0:T(8,128)S(1)}, u32[]{:S(2)}, u32[]{:S(2)}) collective-permute-start(f32[24,1024]{1,0:T(8,128)S(1)} %fusion.2.s_ref), channel_id=1, source_target_pairs={{0,8},{4,12},{8,0},{12,4},{16,24},{20,28},{24,16},{28,20},{1,9},{5... | collective-permute-start | bytes 294920 | tf_op jit(solution)/shard_map/ppermute | solution.py:695
  272.1 10.5 %collective-permute-start.44 = (f32[24,1024]{1,0:T(8,128)S(1)}, f32[24,1024]{1,0:T(8,128)S(1)}, u32[]{:S(2)}, u32[]{:S(2)}) collective-permute-start(f32[24,1024]{1,0:T(8,128)S(1)} %fusion.2.s_ref), channel_id=1, source_target_pairs={{0,16},{4,20},{8,24},{12,28},{16,0},{20,4},{24,8},{28,12},{1,17},{... | collective-permute-start | bytes 294920 | tf_op jit(solution)/shard_map/ppermute | solution.py:695
  273.4 9.3 %collective-permute-start.45 = (f32[24,1024]{1,0:T(8,128)S(1)}, f32[24,1024]{1,0:T(8,128)S(1)}, u32[]{:S(2)}, u32[]{:S(2)}) collective-permute-start(f32[24,1024]{1,0:T(8,128)S(1)} %fusion.2.s_ref), channel_id=1, source_target_pairs={{0,24},{4,28},{8,16},{12,20},{16,8},{20,12},{24,0},{28,4},{1,25},{... | collective-permute-start | bytes 294920 | tf_op jit(solution)/shard_map/ppermute | solution.py:695
  (23 other events, 39.1 us)
Sparse Core Ops, SparseCore 0:
  13.4 88.9 all-gather.1
  157.1 109.9 reduce-scatter.1

commit v4 on v3

--- a/solution.py
+++ b/solution.py
@@ -106,8 +106,8 @@
 
     @pl.when(step == 0)
     def _():
-        tail[...] = tail_in[...]
-        state[...] = state_in[...]
+        tail[...] = jnp.zeros_like(tail) if tail_in is None else tail_in[...]
+        state[...] = jnp.zeros_like(state) if state_in is None else state_in[...]
 
     r, c = block_masks()
     x = x_ref[...].astype(F32)
@@ -177,7 +177,7 @@
 
 def stage_bits(n):
     bits = [1 << i for i in range(n.bit_length() - 1)]
-    return bits, bits[1:] + bits[:1]
+    return bits, [bits[1], bits[0]] + bits[2:]
 
 
 def bwd_kernel(heads, cb, n_f, shard, seg_s, ga0_ref, ga0c_ref, ga1_ref, ga1c_ref, mix_ref, na_ref, out_ref, wide_ref, x_ref, dffn0_ref, dffn1_ref,
@@ -199,7 +199,7 @@
         dstate[...] = jnp.zeros_like(dstate)
         acc[...] = jnp.zeros_like(acc)
         gains_ref[...] = jnp.zeros_like(gains_ref)
-        gains_ref[1:2, :] = dffn0_ref[...] + dffn1_ref[...]
+        gains_ref[6:7, :] = dffn0_ref[...] + dffn1_ref[...]
         small_ref[...] = jnp.zeros_like(small_ref)
 
     r, c = block_masks()
@@ -263,7 +263,7 @@
             dcs[2][b][h] = dv * gv * (1.0 + cv * (1.0 - gv))
             dl = jnp.where(lane == h, dbeta * pad * gb * (1.0 - gb), dl)
         dlog[b] = dl
-    gains_ref[2:3, :HEAD] += dgain
+    gains_ref[7:8, :HEAD] += dgain
     for b in range(cb):
         dpre[b * C:(b + 1) * C, 3 * width:] = dlog[b].astype(BF)
     for i in range(3):
@@ -279,13 +279,13 @@
             tot = tot + e * taps_ref[i, j:j + 1, :]
             grads.append(jnp.sum(e * pre, axis=0, keepdims=True))
         dpre[:, i * width:(i + 1) * width] = tot.astype(BF)
-        small_ref[taps * i:taps * (i + 1), :width] += jnp.concatenate(grads, axis=0)
+        small_ref[i:i + 1, :taps * width] += jnp.concatenate(grads, axis=1)
     low = dpre[...]
     acc[:, :3 * width] += lax.dot_general(na_ref[...], low[:, :3 * width], TN, preferred_element_type=F32)
     acc[:, 4 * width:] += lax.dot_general(na_ref[...], low[:, 3 * width:], TN, preferred_element_type=F32)
     dna = lax.dot_general(low, wide_ref[...], NT, preferred_element_type=F32)
     x = x_ref[...].astype(F32)
-    gains_ref[0:1, :] += jnp.sum(dna * (x * lax.rsqrt(jnp.mean(x * x, axis=-1, keepdims=True) + 1e-6)), axis=0, keepdims=True)
+    gains_ref[5:6, :] += jnp.sum(dna * (x * lax.rsqrt(jnp.mean(x * x, axis=-1, keepdims=True) + 1e-6)), axis=0, keepdims=True)
 
     @pl.when(back % 2 == core)
     def _():
@@ -297,7 +297,7 @@
 
     @pl.when(step == steps - 1)
     def _():
-        small_ref[3 * taps:3 * taps + heads, :] = acc[:, 4 * width:].T[:heads, :]
+        small_ref[3:3 + heads, :] = acc[:, 4 * width:].T[:heads, :]
         me = lax.axis_index("fsdp")
         first, second = stage_bits(n_f)
         half = 2 * width
@@ -327,7 +327,7 @@
 
 
 def fwd_call_kernel(heads, cb, base, n_old, *refs):
-    ins, rest = refs[:10], refs[10 + n_old:]
+    ins, rest = ((*refs[:8], None, None), refs[8:]) if n_old == 0 else (refs[:10], refs[10 + n_old:])
     outs, tail_out, state_out, tail, state, line = rest[:14], rest[14], rest[15], rest[16], rest[17], rest[18]
     fwd_kernel(heads, cb, base, *ins, *outs, tail, state, line)
 
@@ -348,7 +348,8 @@
     sq = shaped((n // C, heads, C, HEAD))
     sqspec = pl.BlockSpec((cb, heads, C, HEAD), lambda i, s: (i + base, 0, 0, 0))
     here = lambda w: pl.BlockSpec((rows, w), lambda i, s: (i + base, 0))
-    ins = [x, wide, again, cols, segr, taps, gain, tail, state]
+    ins = [x, wide, again, cols, segr, taps, gain] + ([tail, state] if old else [])
+    tail, state = shaped((8, 3 * width)), shaped((heads, HEAD, HEAD))
     kept = [shaped((n, width), BF), shaped((n, d), BF), shaped((n, wide_cols)), shaped((n, 3 * width)), shaped((n, width))] + [sq] * 8
     return pl.pallas_call(
         functools.partial(fwd_call_kernel, heads, cb, base, len(old)),
@@ -356,7 +357,7 @@
             num_scalar_prefetch=1, grid=(steps,),
             in_specs=[here(d), whole((d, wide_cols)), whole((1, d)), here(cols.shape[1]),
                       pl.BlockSpec((1, rows), lambda i, s: (0, i + base)),
-                      whole(taps.shape), whole((1, HEAD)), whole(tail.shape), whole(state.shape)]
+                      whole(taps.shape), whole((1, HEAD))] + ([whole(tail.shape), whole(state.shape)] if old else [])
             + [pl.BlockSpec(memory_space=pl.ANY)] * len(old),
             out_specs=[pl.BlockSpec((rows, width), lambda i, s: (i, 0)), here(width), here(d), here(wide_cols), here(3 * width), here(width)]
             + [sqspec] * 8 + [whole(tail.shape), whole(state.shape)],
@@ -381,7 +382,7 @@
     sqspec = pl.BlockSpec((cb, heads, C, HEAD), lambda i, s: (steps - 1 - i, 0, 0, 0))
     row = lambda w: pl.BlockSpec((rows, w), lambda i, s: (steps - 1 - i, 0))
     outs = [shaped((n_f // 2, shard, 2 * width), BF)] * 4 + [
-            shaped((2, rows, d), BF), shaped((2, rows, d)), shaped((8, d)), shaped((16, d))]
+            shaped((2, rows, d), BF), shaped((2, rows, d)), shaped((8, d)), shaped((8, d))]
     return pl.pallas_call(
         functools.partial(bwd_kernel, heads, cb, n_f, shard),
         grid_spec=pltpu.PrefetchScalarGridSpec(
@@ -430,7 +431,7 @@
 
 
 def finish_kernel(heads, ntap, k1_ref, g1_ref, k2_ref, g2_ref, s_ref, *refs):
-    got, (qkv_ref, out_ref, taps_ref, beta_ref, attn_ref, ffn_ref, head_ref, hold) = refs[:-8], refs[-8:]
+    got, (qkv_ref, out_ref, taps_ref, beta_ref, attn_ref, ffn_ref, head_ref, hold) = refs[:-9], refs[-8:]
     width = qkv_ref.shape[2]
     shard = qkv_ref.shape[1]
     a = k1_ref[0].astype(F32) + g1_ref[0].astype(F32)
@@ -442,31 +443,34 @@
     small = s_ref[...]
     for g in got:
         small = small + g[...]
+    width = taps_ref.shape[2]
     for i in range(3):
-        taps_ref[i] = small[ntap * i:ntap * (i + 1), :width]
-    attn_ref[...] = small[16:17]
-    ffn_ref[...] = small[17:18]
-    head_ref[...] = small[18:19, :HEAD]
+        for k in range(ntap):
+            taps_ref[i, k:k + 1, :] = small[i:i + 1, k * width:(k + 1) * width]
+    attn_ref[...] = small[5:6]
+    ffn_ref[...] = small[6:7]
+    head_ref[...] = small[7:8, :HEAD]
     if shard == 128:
-        hold[...] = small[8:16]
+        hold[...] = small
         me = lax.axis_index("fsdp")
-        beta_ref[...] = hold[3 * ntap - 8:3 * ntap - 8 + heads, pl.ds(pl.multiple_of(me * shard, 128), shard)]
+        beta_ref[...] = hold[3:3 + heads, pl.ds(pl.multiple_of(me * shard, 128), shard)]
     else:
-        beta_ref[...] = small[3 * ntap:3 * ntap + heads]
-
-
-def finish(heads, ntap, k1, g1, k2, g2, small, got):
+        beta_ref[...] = small[3:3 + heads]
+
+
+def finish(heads, ntap, k1, g1, k2, g2, small, got, wait_for):
     m, shard, w = k1.shape
     d = small.shape[1]
     return pl.pallas_call(
         functools.partial(finish_kernel, heads, ntap),
+        in_specs=[pl.BlockSpec(memory_space=pltpu.VMEM)] * (5 + len(got)) + [pl.BlockSpec(memory_space=pl.ANY)],
         out_shape=[shaped((3, shard, w // 2)), shaped((w // 2, shard)), shaped((3, ntap, w // 2)),
                    shaped((heads, 128 if shard == 128 else d)), shaped((1, d)), shaped((1, d)), shaped((1, HEAD))],
         scratch_shapes=[pltpu.VMEM((8, d), F32)],
         compiler_params=pltpu.CompilerParams(vmem_limit_bytes=60 * 2**20),
         cost_estimate=TINY,
         name="finish",
-    )(k1, g1, k2, g2, small, *got)
+    )(k1, g1, k2, g2, small, *got, wait_for)
 
 
 def ffn_kernel(ff, *refs):
@@ -517,25 +521,27 @@
     )(*m, *out, x, weights, gf, gain)
 
 
-def grad_kernel(part, low_ref, other_ref, mid_ref, cot_ref, coty_ref, gain_ref, grad_ref, low_out):
+def grad_kernel(part, n, *refs):
+    lows, others, (mid_ref, cot_ref, coty_ref, gain_ref, grad_ref, low_out) = refs[:n], refs[n:2 * n], refs[2 * n:]
     chip = lax.axis_index("tensor") // 2
     mid = mid_ref[...]
     factor = lax.rsqrt(jnp.mean(mid * mid, axis=-1, keepdims=True) + 1e-6)
-    u = (low_ref[...].astype(F32) + other_ref[...].astype(F32)) * gain_ref[0:1, :]
+    d_nf = jnp.concatenate([a[...].astype(F32) + b[...].astype(F32) for a, b in zip(lows, others)], axis=0)
+    u = d_nf * gain_ref[0:1, :]
     cot = jnp.where(chip == part, cot_ref[...], coty_ref[...]).astype(F32)
     grad = cot + factor * u - mid * (factor * factor * factor) * jnp.mean(u * mid, axis=-1, keepdims=True)
     grad_ref[...] = grad
     low_out[...] = grad.astype(BF)
 
 
-def grad_rows(part, low, other, mid, cot, cot_y, gain):
-    return pl.pallas_call(
-        functools.partial(grad_kernel, part),
+def grad_rows(part, lows, others, mid, cot, cot_y, gain):
+    return pl.pallas_call(
+        functools.partial(grad_kernel, part, len(lows)),
         out_shape=[shaped(mid.shape), shaped(mid.shape, BF)],
         compiler_params=pltpu.CompilerParams(vmem_limit_bytes=24 * 2**20),
         cost_estimate=TINY,
         name="grad_rows",
-    )(low, other, mid, cot, cot_y, gain)
+    )(*lows, *others, mid, cot, cot_y, gain)
 
 
 def down_kernel(hid0_ref, hid1_ref, w_ref, send_ref, keep_ref, hold):
@@ -656,6 +662,85 @@
         cost_estimate=TINY,
         name="ffn_cast",
     )(d)
+
+
+def ffn_split_kernel(ff, parts, *refs):
+    blocks, expand, away, keep = refs[-1], refs[-4], refs[-3], refs[-2]
+    ffn_grads_kernel(ff, parts, *refs[:3 * parts + 1], blocks)
+    me = lax.axis_index("fsdp")
+    for k in range(blocks.shape[0]):
+        expand[k] = blocks[k, :2 * ff, :]
+        block = pl.program_id(0) * blocks.shape[0] + k
+
+        @pl.when(block % 2 == me % 2)
+        def _(k=k, block=block):
+            keep[block // 2] = blocks[k, 2 * ff:, :]
+
+        @pl.when(block % 2 != me % 2)
+        def _(k=k, block=block):
+            away[block // 2] = blocks[k, 2 * ff:, :]
+
+
+def ffn_split_grads(pieces, gf, wait_for, step=256):
+    ff = pieces[0][1].shape[0]
+    n, d = gf.shape
+    flat, specs = [], []
+    for dgu, hid, nf in pieces:
+        flat += [dgu, hid, nf]
+        specs += [whole(dgu.shape), whole(hid.shape), pl.BlockSpec((nf.shape[0], step), lambda i: (0, i))]
+    per = step // 128
+    halves = shaped((d // 256, ff, 128), BF)
+    return pl.pallas_call(
+        functools.partial(ffn_split_kernel, ff, len(pieces)),
+        grid=(d // step,),
+        in_specs=specs + [pl.BlockSpec((n, step), lambda i: (0, i))] + [pl.BlockSpec(memory_space=pl.ANY)] * len(wait_for),
+        out_specs=[pl.BlockSpec((per, 2 * ff, 128), lambda i: (i, 0, 0)), whole(halves.shape), whole(halves.shape)],
+        out_shape=[shaped((d // 128, 2 * ff, 128), BF), halves, halves],
+        scratch_shapes=[pltpu.VMEM((per, 3 * ff, 128), BF)],
+        compiler_params=params(),
+        cost_estimate=COST,
+        name="ffn_grads",
+    )(*flat, gf, *wait_for)
+
+
+def halve_kernel(bit, k_ref, g_ref, wait_for, away, keep):
+    mine = (lax.axis_index("fsdp") // bit) % 2
+    count = k_ref.shape[0] // 2
+    for j in range(count):
+        ours, theirs = (2 * j + mine, 2 * j + 1 - mine) if bit == 2 else (mine, 1 - mine)
+        away[j] = (k_ref[theirs].astype(F32) + g_ref[theirs].astype(F32)).astype(BF)
+        keep[j] = (k_ref[ours].astype(F32) + g_ref[ours].astype(F32)).astype(BF)
+
+
+def halve(bit, k, g, wait_for):
+    m, ff, w = k.shape
+    spec = pl.BlockSpec(memory_space=pltpu.VMEM)
+    return pl.pallas_call(
+        functools.partial(halve_kernel, bit),
+        in_specs=[spec] * 2 + [pl.BlockSpec(memory_space=pl.ANY)],
+        out_shape=[shaped((m // 2, ff, w), BF)] * 2,
+        compiler_params=pltpu.CompilerParams(vmem_limit_bytes=60 * 2**20),
+        cost_estimate=TINY,
+        name="halve",
+    )(k, g, wait_for)
+
+
+def split_cast_kernel(d_ref, k_ref, g_ref, expand_ref, down_ref):
+    ff = down_ref.shape[0]
+    expand_ref[0] = d_ref[:ff, :].astype(F32)
+    expand_ref[1] = d_ref[ff:, :].astype(F32)
+    down_ref[...] = k_ref[0].astype(F32) + g_ref[0].astype(F32)
+
+
+def split_cast(d, k, g):
+    ff, w = d.shape[0] // 2, d.shape[1]
+    return pl.pallas_call(
+        split_cast_kernel,
+        out_shape=[shaped((2, ff, w)), shaped((ff, w))],
+        compiler_params=pltpu.CompilerParams(vmem_limit_bytes=60 * 2**20),
+        cost_estimate=TINY,
+        name="ffn_cast",
+    )(d, k, g)
 
 
 def pack_kernel(qkv_ref, beta_ref, out_ref, o_ref):
@@ -804,8 +889,7 @@
     wide, g_f = fence(ring.full, g_f)
 
     out_own = wide[:, 3 * width + HEAD:]
-    tail = jnp.zeros((8, 3 * width), F32)
-    state = jnp.zeros((heads, HEAD, HEAD), F32)
+    tail = state = None
 
     def mix(i, tail, state, old):
         m, *kept, tail, state = mixer_fwd(i, 2, x_full, wide, attn_gain, cols, segr, seg, taps, out_gain, tail, state, old)
@@ -835,19 +919,23 @@
     low0_y = y_hop(low0)
     mid1, nf1, hid1, dgu1, keep1, send1, dgain1 = feed(1, m1, m1_y, m1_c, m1_cy)
     low0_y, send1 = fence(low0_y, send1)
-    low1 = (keep1 + core_hop(send1).astype(F32)).astype(BF)
-    grad0, ga0 = grad_rows(0, low0, low0_y, mid0, cotangent, c_y, ffn_gain)
-    low1, ga0 = fence(low1, ga0)
-    low1_y = y_hop(low1)
+    cut = rows // 2
+    got1 = core_hop(send1)
+    low1 = (keep1[:cut] + got1[:cut].astype(F32)).astype(BF)
+    low1b = (keep1[cut:] + got1[cut:].astype(F32)).astype(BF)
+    grad0, ga0 = grad_rows(0, [low0], [low0_y], mid0, cotangent, c_y, ffn_gain)
+    low1, low1b, ga0 = fence(low1, low1b, ga0)
+    low1_y, low1b_y = y_hop(low1), y_hop(low1b)
     ga0_c = core_hop(ga0)
     blocks = ffn_grads([(dgu0, hid0, nf0), (dgu1, hid1, nf1)], g_f, [low1])
     q = d_model // 128
     if q != n_f:
         blocks = blocks.reshape(q, 3 * ff, n_f // q, shard).transpose(0, 2, 1, 3).reshape(n_f, 3 * ff, shard)
     send_out, keep_out = down(hid0, hid1, weights, [blocks])
-    low1_y, ga0_c, send_out, done_blocks = fence(low1_y, ga0_c, send_out, blocks)
+    low1_y, ga0_c, blocks = fence(low1_y, ga0_c, blocks)
+    low1b_y, send_out, done_blocks = fence(low1b_y, send_out, blocks)
     d_ffn = lax.psum_scatter(blocks, "fsdp", scatter_dimension=0, tiled=False)
-    grad1, ga1 = grad_rows(1, low1, low1_y, mid1, cotangent, c_y, ffn_gain)
+    grad1, ga1 = grad_rows(1, [low1, low1b], [low1_y, low1b_y], mid1, cotangent, c_y, ffn_gain)
     ga1_c = core_hop(ga1)
     ga1, ga1_c = fence(ga1, ga1_c)
 
@@ -864,7 +952,7 @@
     na, na_away = to_chips(keep_na, na_c, gains)
     g1, g2, na_away, out_away, *gains_got = fence(g1, g2, na_away, out_away, *gains_got)
     count = len(first_bits)
-    small = jnp.concatenate([small, gains + gains_got[0] + (gains_got[1] + gains_got[2])], axis=0)
+    small = small + gains + gains_got[0] + (gains_got[1] + gains_got[2])
     for stage in range(1, count):
         away1, k1, away2, k2 = fold(n_f, stage, k1, g1, k2, g2)
         if stage == 1:
@@ -881,11 +969,11 @@
         got = [hop(small, "fsdp", first_bits[count - 1])]
     input_grad, block_outs = last_rows(grad0, grad1, na, na_y, layer_input, attn_gain, mid0, mid1, out, out_y)
     block_outs = block_outs[None]
-    qkv_grad, out_grad, conv_grad, beta_grad, attn_total, ffn_total, head_total = finish(heads, ntap, k1, g1, k2, g2, small, got)
+    expand_grad, down_grad = ffn_cast(d_ffn)
+    qkv_grad, out_grad, conv_grad, beta_grad, attn_total, ffn_total, head_total = finish(heads, ntap, k1, g1, k2, g2, small, got, down_grad)
     if shard != 128:
         beta_grad = lax.dynamic_slice(beta_grad, (0, lax.axis_index("fsdp") * shard), (heads, shard))
     beta_grad = beta_grad.T
-    expand_grad, down_grad = ffn_cast(d_ffn)
     expand_grad = expand_grad.transpose(0, 2, 1)
     return (
         block_outs, input_grad, attn_total, ffn_total, head_total, qkv_grad[None], beta_grad[None],

time: 298 us -> 288 us (0.966)
  waiting for transfers between devices: 75.9 us -> 64.4 us
  starting transfers between devices: 43.4 us -> 46.6 us
    ppermute x38 -> x39, waiting for transfers between devices: 47.3 us -> 31.9 us  [hop(): return lax.ppermute(value, axis, [(i, i ^ bit) for i in range(n)])]
    reduce_scatter x1, waiting for transfers between devices: 0.01 us -> 4.24 us  [on_device(): d_ffn = lax.psum_scatter(blocks, 'fsdp', scatter_dimension=0, tiled=False)]
    ppermute x38 -> x39, starting transfers between devices: 34 us -> 37.2 us  [hop(): return lax.ppermute(value, axis, [(i, i ^ bit) for i in range(n)])]
    unnamed x79 -> x81, local copies, waits for them, and re-layouts: 7.53 us -> 7.97 us
  transfers between devices with their start and end apart: 48 -> 49, of which waited for: 17 -> 17; matrix products, arithmetic and copies ran while one was open for 9% -> 9% of each run, Pallas kernels for 37% -> 42%
where the time goes in v4:
time: 288 us; the launch traced here: 284 us
  Pallas kernels  122 us (42%)
  waiting for transfers between devices  64.4 us (22%)
  starting transfers between devices  46.6 us (16%)
  local copies, waits for them, and re-layouts  31.6 us (11%)
  between operations  14.9 us (5%)
  other arithmetic  4.04 us (1%)
    ppermute x39, starting transfers between devices, hop(): return lax.ppermute(value, axis, [(i, i ^ bit) for i in range(n)])  37.2 us
    pallas_call x1, Pallas kernels, mixer_bwd(): pl.pallas_call(functools.partial(bwd_kernel, heads, cb, n_f, shard), grid...  34.6 us
    ppermute x39, waiting for transfers between devices, hop(): return lax.ppermute(value, axis, [(i, i ^ bit) for i in range(n)])  31.9 us
    pallas_call x2, Pallas kernels, mixer_fwd(): pl.pallas_call(functools.partial(fwd_call_kernel, heads, cb, base, len(ol...  27.3 us
    pallas_call x2, Pallas kernels, ffn(): pl.pallas_call(functools.partial(ffn_kernel, ff), grid=(1,), in_specs=[wh...  22.4 us
    ppermute x3, waiting for transfers between devices, step(): self.a = lax.ppermute(self.a, 'fsdp', self.right)  14.9 us
    dynamic_update_slice x8, local copies, waits for them, and re-layouts, in_order(): lax.dynamic_update_slice(full, block[None], (me ^ k,) + (0,) * own.ndim)  11.3 us
    pallas_call x1, Pallas kernels, ffn_grads(): pl.pallas_call(functools.partial(ffn_grads_kernel, ff, len(pieces)), grid...  9.19 us
  transfers between devices with their start and end apart: 49, of which 17 were waited for; matrix products, arithmetic and copies ran while one was open for 9% of the time, Pallas kernels for 42%

profile of v4, /device:TPU:0, one launch (start us, length us, event | category | flops | bytes accessed | tf_op | source)
XLA Modules:
  0.0 283.9 jit_solution(6347053839039101564)
XLA Ops:
  7.2 1.4 copy.45
  8.7 1.8 pack.1
  10.4 1.0 slice_bitcast_fusion.1
  11.5 1.8 pad_maximum_fusion
  13.3 3.1 %collective-permute-start = (bf16[128,1152]{1,0:T(8,128)(2,1)}, bf16[128,1152]{1,0:T(8,128)(2,1)}, u32[]{:S(2)}, u32[]{:S(2)}) collective-permute-start(bf16[128,1152]{1,0:T(8,128)(2,1)} %pack.1), channel_id=1, source_target_pairs={{0,8},{8,16},{16,24},{24,28},{28,20},{20,12},{12,4},{4,0},{1,9},{9... | collective-permute-start | bytes 884744 | tf_op jit(solution)/shard_map/ppermute | solution.py:831
  16.4 2.0 collective-permute-start.2
  19.3 1.0 constant_dynamic-update-slice_fusion.8
  20.3 1.7 broadcast.20.clone
  22.0 1.9 bitcast_dynamic-update-slice_fusion.7
  24.7 1.6 broadcast.20.clone.1
  27.6 3.9 %collective-permute-done.2 = bf16[256,1024]{1,0:T(8,128)(2,1)} collective-permute-done((bf16[256,1024]{1,0:T(8,128)(2,1)}, bf16[256,1024]{1,0:T(8,128)(2,1)}, u32[]{:S(2)}, u32[]{:S(2)}) %collective-permute-start.2) | collective-permute-done | bytes 524320 | tf_op jit(solution)/shard_map/ppermute | solution.py:780
  31.6 2.0 collective-permute-start.4
  33.6 1.9 bitcast_dynamic-update-slice_fusion.6
  35.5 1.0 constant_dynamic-update-slice_fusion.7
  36.5 1.0 constant_dynamic-update-slice_fusion.6
  37.5 1.9 bitcast_dynamic-update-slice_fusion.5
  39.4 7.7 %collective-permute-done.4 = bf16[128,1152]{1,0:T(8,128)(2,1)S(1)} collective-permute-done((bf16[128,1152]{1,0:T(8,128)(2,1)}, bf16[128,1152]{1,0:T(8,128)(2,1)S(1)}, u32[]{:S(2)}, u32[]{:S(2)}) %collective-permute-start.4) | collective-permute-done | bytes 294944 | tf_op jit(solution)/shard_map/ppermute | solution.py:831
  47.1 3.7 %collective-permute-done.5 = bf16[128,1152]{1,0:T(8,128)(2,1)S(1)} collective-permute-done((bf16[128,1152]{1,0:T(8,128)(2,1)}, bf16[128,1152]{1,0:T(8,128)(2,1)S(1)}, u32[]{:S(2)}, u32[]{:S(2)}) %collective-permute-start.5) | collective-permute-done | bytes 294944 | tf_op jit(solution)/shard_map/ppermute | solution.py:833
  50.8 1.6 collective-permute-start.7
  53.7 7.2 %collective-permute-done.7 = bf16[128,1152]{1,0:T(8,128)(2,1)S(1)} collective-permute-done((bf16[128,1152]{1,0:T(8,128)(2,1)S(1)}, bf16[128,1152]{1,0:T(8,128)(2,1)S(1)}, u32[]{:S(2)}, u32[]{:S(2)}) %collective-permute-start.7) | collective-permute-done | bytes 294944 | tf_op jit(solution)/shard_map/ppermute | solution.py:831
  60.9 3.6 %collective-permute-done.8 = bf16[128,1152]{1,0:T(8,128)(2,1)S(1)} collective-permute-done((bf16[128,1152]{1,0:T(8,128)(2,1)S(1)}, bf16[128,1152]{1,0:T(8,128)(2,1)S(1)}, u32[]{:S(2)}, u32[]{:S(2)}) %collective-permute-start.8) | collective-permute-done | bytes 294944 | tf_op jit(solution)/shard_map/ppermute | solution.py:833
  65.9 2.2 collective-permute-start.11
  69.8 1.8 copy.46.refs_4_.cols_ref
  71.6 2.2 collective-permute-done.10
  74.7 3.9 %collective-permute-done.11 = bf16[64,1152]{1,0:T(8,128)(2,1)S(1)} collective-permute-done((bf16[64,1152]{1,0:T(8,128)(2,1)}, bf16[64,1152]{1,0:T(8,128)(2,1)S(1)}, u32[]{:S(2)}, u32[]{:S(2)}) %collective-permute-start.11) | collective-permute-done | bytes 147488 | tf_op jit(solution)/shard_map/ppermute | solution.py:829
  78.6 2.3 bitcast_dynamic-update-slice_fusion
  80.9 1.7 collective-permute-start.14
  82.6 13.3 %mixer_fwd.2 = (bf16[512,256]{1,0:T(8,128)(2,1)}, bf16[1024,256]{1,0:T(8,128)(2,1)}, bf16[1024,1024]{1,0:T(8,128)(2,1)}, f32[1024,896]{1,0:T(8,128)}, f32[1024,7...) custom-call(s32[1024]{0:T(1024)} %bitcast.63, ...), custom_call_target="tpu_custom_call" | custom-call | flops 10000000000 | bytes 10000000 | tf_op jit(solution)/shard_map/mixer_fwd/pallas_call | solution.py:354
  96.9 14.0 %mixer_fwd.3 = (bf16[512,256]{1,0:T(8,128)(2,1)}, bf16[1024,256]{1,0:T(8,128)(2,1)}, bf16[1024,1024]{1,0:T(8,128)(2,1)}, f32[1024,896]{1,0:T(8,128)}, f32[1024,7...) custom-call(s32[1024]{0:T(1024)} %bitcast.64, ...), custom_call_target="tpu_custom_call", output_to_operand_aliasing={{1}: (10, {}), {2}: (11, {}), {3}: (12, {}), {4}: (13, {}),... | custom-call | flops 10000000000 | bytes 10000000 | tf_op jit(solution)/shard_map/mixer_fwd/pallas_call | solution.py:354
  111.3 1.6 collective-permute-start.19
  113.6 11.1 %ffn.2 = (f32[256,1024]{1,0:T(8,128)}, bf16[512,1024]{1,0:T(8,128)(2,1)}, bf16[704,512]{1,0:T(8,128)(2,1)}, bf16[1408,512]{1,0:T(8,128)(2,1)}, f32[256,1024]{1,0...) custom-call(bf16[512,256]{1,0:T(8,128)(2,1)} %get-tuple-element.173.refs_0_, bf16[512,256]{1,0:T(8,128)(2,1)} %copy-done.34, ...), custom_call_target="tpu_custom_call" | custom-call | flops 10000000000 | bytes 10000000 | tf_op jit(solution)/shard_map/ffn/pallas_call | solution.py:511
  125.4 1.7 collective-permute-done.23
  127.0 1.4 add_convert_fusion.refs_0_
  128.5 1.2 collective-permute-start.24
  129.7 11.3 %ffn.3 = (f32[256,1024]{1,0:T(8,128)}, bf16[512,1024]{1,0:T(8,128)(2,1)}, bf16[704,512]{1,0:T(8,128)(2,1)}, bf16[1408,512]{1,0:T(8,128)(2,1)}, f32[256,1024]{1,0...) custom-call(bf16[512,256]{1,0:T(8,128)(2,1)} %get-tuple-element.191.refs_0_, bf16[512,256]{1,0:T(8,128)(2,1)} %copy-done.36, ...), custom_call_target="tpu_custom_call" | custom-call | flops 10000000000 | bytes 10000000 | tf_op jit(solution)/shard_map/ffn/pallas_call | solution.py:511
  141.0 1.7 collective-permute-done.24.refs_1_
  143.3 1.0 copy-done.3
  145.2 1.0 collective-permute-start.26
  146.3 9.2 %ffn_grads.1.refs_3_.wait_for = bf16[8,2112,128]{2,1,0:T(8,128)(2,1)} custom-call(bf16[1408,512]{1,0:T(8,128)(2,1)} %get-tuple-element.216.refs_0_, bf16[704,512]{1,0:T(8,128)(2,1)} %get-tuple-element.217.refs_1_.refs_0_, bf16[512,1024]{1,0:T(8,128)(2,1)} %get-tuple-element.218.refs_2_, bf16[1408,512]{1,0:T(8,128)(2,1)} %get-tuple-element.219.refs_3_, ...), custom_call_target="tpu_custom_call" | custom-call | flops 5000000000 | bytes 10000000 | tf_op jit(solution)/shard_map/ffn_grads/pallas_call | solution.py:600
  156.3 1.1 collective-permute-start.28
  157.4 5.8 %down.1 = (bf16[2,256,1024]{2,1,0:T(8,128)(2,1)}, f32[2,256,1024]{2,1,0:T(8,128)}) custom-call(bf16[704,512]{1,0:T(8,128)(2,1)} %get-tuple-element.217.refs_1_.refs_0_, bf16[704,512]{1,0:T(8,128)(2,1)} %get-tuple-element.220.refs_4_.refs_1_, bf16[2112,1024]{1,0:T(8,128)(2,1)} %all-gather.2.cloned.1.call-done.refs_9_.refs_2_, ...), custom_call_target="tpu_custom_call" | custom-call | flops 1 | bytes 1 | tf_op jit(solution)/shard_map/down/pallas_call | solution.py:564
  163.2 1.5 collective-permute-done.28.refs_3_
  165.2 1.0 copy-done.4
  166.7 2.1 collective-permute-done.29.ga1c_ref
  169.7 34.6 %mixer_bwd.1 = (bf16[4,128,512]{2,1,0:T(8,128)(2,1)}, bf16[4,128,512]{2,1,0:T(8,128)(2,1)}, bf16[4,128,512]{2,1,0:T(8,128)(2,1)}, bf16[4,128,512]{2,1,0:T(8,128)...) custom-call(s32[1024]{0:T(1024)} %bitcast.65, ...), custom_call_target="tpu_custom_call" | custom-call | flops 10000000000 | bytes 10000000 | tf_op jit(solution)/shard_map/mixer_bwd/pallas_call | solution.py:386
  204.5 3.6 %collective-permute-start.32 = (bf16[4,128,512]{2,1,0:T(8,128)(2,1)}, bf16[4,128,512]{2,1,0:T(8,128)(2,1)S(1)}, u32[]{:S(2)}, u32[]{:S(2)}) collective-permute-start(bf16[4,128,512]{2,1,0:T(8,128)(2,1)} %get-tuple-element.261), channel_id=1, source_target_pairs={{0,4},{4,0},{8,12},{12,8},{16,20},{20,16},{24,28},{28,24},{1,5},{5... | collective-permute-start | bytes 1572872 | tf_op jit(solution)/shard_map/ppermute | solution.py:780
  208.1 4.5 %collective-permute-start.33 = (bf16[4,128,512]{2,1,0:T(8,128)(2,1)}, bf16[4,128,512]{2,1,0:T(8,128)(2,1)S(1)}, u32[]{:S(2)}, u32[]{:S(2)}) collective-permute-start(bf16[4,128,512]{2,1,0:T(8,128)(2,1)} %get-tuple-element.262), channel_id=1, source_target_pairs={{0,8},{4,12},{8,0},{12,4},{16,24},{20,28},{24,16},{28,20},{1,9},{5... | collective-permute-start | bytes 1572872 | tf_op jit(solution)/shard_map/ppermute | solution.py:780
  212.6 1.0 collective-permute-start.35
  214.5 3.2 %to_chips.3 = (f32[256,1024]{1,0:T(8,128)}, bf16[256,1024]{1,0:T(8,128)(2,1)}) custom-call(f32[2,256,1024]{2,1,0:T(8,128)} %get-tuple-element.264.keep, bf16[2,256,1024]{2,1,0:T(8,128)(2,1)} %copy-done.11, bf16[8,2112,128]{2,1,0:T(8,128)(2,1)} %ffn_grads.1.refs_3_.wait_for), custom_call_target="tpu_custom_call" | custom-call | flops 1 | bytes 1 | tf_op jit(solution)/shard_map/to_chips/pallas_call | solution.py:620
  217.8 3.2 %to_chips.2 = (f32[256,1024]{1,0:T(8,128)}, bf16[256,1024]{1,0:T(8,128)(2,1)}) custom-call(f32[2,256,1024]{2,1,0:T(8,128)} %get-tuple-element.256.keep, bf16[2,256,1024]{2,1,0:T(8,128)(2,1)} %copy-done.12, f32[8,1024]{1,0:T(8,128)} %get-tuple-element.258.wait_for), custom_call_target="tpu_custom_call" | custom-call | flops 1 | bytes 1 | tf_op jit(solution)/shard_map/to_chips/pallas_call | solution.py:620
  221.0 6.7 %collective-permute-done.32.g1_ref = bf16[4,128,512]{2,1,0:T(8,128)(2,1)S(1)} collective-permute-done((bf16[4,128,512]{2,1,0:T(8,128)(2,1)}, bf16[4,128,512]{2,1,0:T(8,128)(2,1)S(1)}, u32[]{:S(2)}, u32[]{:S(2)}) %collective-permute-start.32) | collective-permute-done | bytes 524320 | tf_op jit(solution)/shard_map/ppermute | solution.py:780
  227.7 1.5 collective-permute-start.40
  229.8 2.6 fold.2
  232.4 3.4 %collective-permute-start.37 = (bf16[2,128,512]{2,1,0:T(8,128)(2,1)}, bf16[2,128,512]{2,1,0:T(8,128)(2,1)S(1)}, u32[]{:S(2)}, u32[]{:S(2)}) collective-permute-start(bf16[2,128,512]{2,1,0:T(8,128)(2,1)} %get-tuple-element.271), channel_id=1, source_target_pairs={{0,8},{4,12},{8,0},{12,4},{16,24},{20,28},{24,16},{28,20},{1,9},{5... | collective-permute-start | bytes 786440 | tf_op jit(solution)/shard_map/ppermute | solution.py:780
  235.8 1.7 collective-permute-start.38
  237.9 11.8 %collective-permute-done.39 = f32[8,1024]{1,0:T(8,128)S(1)} collective-permute-done((f32[8,1024]{1,0:T(8,128)S(1)}, f32[8,1024]{1,0:T(8,128)S(1)}, u32[]{:S(2)}, u32[]{:S(2)}) %collective-permute-start.39) | collective-permute-done | bytes 32800 | tf_op jit(solution)/shard_map/ppermute | solution.py:780
  251.5 2.0 fold.3
  253.5 2.0 collective-permute-start.42
  256.4 1.8 collective-permute-start.44
  258.3 2.9 %collective-permute-start.45 = (f32[8,1024]{1,0:T(8,128)S(1)}, f32[8,1024]{1,0:T(8,128)S(1)}, u32[]{:S(2)}, u32[]{:S(2)}) collective-permute-start(f32[8,1024]{1,0:T(8,128)S(1)} %add.201.s_ref), channel_id=1, source_target_pairs={{0,16},{4,20},{8,24},{12,28},{16,0},{20,4},{24,8},{28,12},{1,17},{... | collective-permute-start | bytes 98312 | tf_op jit(solution)/shard_map/ppermute | solution.py:780
  262.0 5.0 %last_rows.1 = (f32[256,1024]{1,0:T(8,128)}, bf16[256,1024]{1,0:T(8,128)(2,1)}) custom-call(f32[256,1024]{1,0:T(8,128)} %copy-done.3, f32[256,1024]{1,0:T(8,128)} %copy-done.4, f32[256,1024]{1,0:T(8,128)} %get-tuple-element.259.na, bf16[256,1024]{1,0:T(8,128)(2,1)} %copy-done.14, bf16[256,1024]{1,0:T(8,128)(2,1)} %x_ref.1, f32[1,1024]{1,0:T(1,128)} %gain_ref.3, ...), custom_call_target="tpu_custom_call" | custom-call | flops 1 | bytes 1 | tf_op jit(solution)/shard_map/last_rows/pallas_call | solution.py:640
  266.9 4.2 %reduce-scatter.2.cloned.1.call-done = bf16[1,2112,128]{2,1,0:T(8,128)(2,1)} async-done(((bf16[8,2112,128]{2,1,0:T(8,128)(2,1)}), bf16[1,2112,128]{2,1,0:T(8,128)(2,1)}) %reduce-scatter.2.cloned.1.call-update) | async-done | bytes 540688 | tf_op jit(solution)/shard_map/reduce_scatter | solution.py:937
  271.2 2.1 ffn_cast.1
  274.8 2.0 finish.1
  (172 shorter events, 22.5 us)
Async XLA Ops:
  7.2 11.2 %copy-start = (bf16[256,1024]{1,0:T(8,128)(2,1)S(1)}, bf16[256,1024]{1,0:T(8,128)(2,1)}, u32[]{:S(2)}) copy-start(bf16[256,1024]{1,0:T(8,128)(2,1)} %refs_5_.3) | copy-start | bytes 1572868
  7.2 11.3 %copy-start.21 = (s32[1,1024]{1,0:T(1,128)S(1)}, s32[1,1024]{1,0:T(1,128)}, u32[]{:S(2)}) copy-start(s32[1,1024]{1,0:T(1,128)} %param.14) | copy-start | bytes 12292
  7.2 105.7 %all-gather.2.cloned.1.call-start = ((), (), s32[]{:S(2)}) async-start(), calls=%async_computation.1 | async-start | bytes 4866048 | tf_op jit(solution)/shard_map/all_gather | solution.py:868
  13.3 257.9 %reduce-scatter.2.cloned.1.call-start = ((), (), s32[]{:S(2)}) async-start(), calls=%async_computation.2 | async-start | bytes 4866048 | tf_op jit(solution)/shard_map/reduce_scatter | solution.py:937
  13.3 13.9 %collective-permute-start = (bf16[128,1152]{1,0:T(8,128)(2,1)}, bf16[128,1152]{1,0:T(8,128)(2,1)}, u32[]{:S(2)}, u32[]{:S(2)}) collective-permute-start(bf16[128,1152]{1,0:T(8,128)(2,1)} %pack.1), channel_id=1, source_target_pairs={{0,8},{8,16},{16,24},{24,28},{28,20},{20,12},{12,4},{4,0},{1,9},{9... | collective-permute-start | bytes 884744 | tf_op jit(solution)/shard_map/ppermute | solution.py:831
  16.4 11.3 %collective-permute-start.1 = (bf16[128,1152]{1,0:T(8,128)(2,1)}, bf16[128,1152]{1,0:T(8,128)(2,1)}, u32[]{:S(2)}, u32[]{:S(2)}) collective-permute-start(bf16[128,1152]{1,0:T(8,128)(2,1)} %pack.1), channel_id=1, source_target_pairs={{8,0},{16,8},{24,16},{28,24},{20,28},{12,20},{4,12},{0,4},{9,1},{1... | collective-permute-start | bytes 884744 | tf_op jit(solution)/shard_map/ppermute | solution.py:833
  16.4 15.2 %collective-permute-start.2 = (bf16[256,1024]{1,0:T(8,128)(2,1)}, bf16[256,1024]{1,0:T(8,128)(2,1)}, u32[]{:S(2)}, u32[]{:S(2)}) collective-permute-start(bf16[256,1024]{1,0:T(8,128)(2,1)} %x_ref.1), channel_id=1, source_target_pairs={{0,2},{1,3},{2,0},{3,1},{4,6},{5,7},{6,4},{7,5},{8,10},{9,11},{10,... | collective-permute-start | bytes 1572872 | tf_op jit(solution)/shard_map/ppermute | solution.py:780
  18.4 13.2 %collective-permute-start.3 = (bf16[256,1024]{1,0:T(8,128)(2,1)}, bf16[256,1024]{1,0:T(8,128)(2,1)}, u32[]{:S(2)}, u32[]{:S(2)}) collective-permute-start(bf16[256,1024]{1,0:T(8,128)(2,1)} %x_ref.1), channel_id=1, source_target_pairs={{0,1},{1,0},{2,3},{3,2},{4,5},{5,4},{6,7},{7,6},{8,9},{9,8},{10,11... | collective-permute-start | bytes 1572872 | tf_op jit(solution)/shard_map/ppermute | solution.py:780
  18.4 35.4 %collective-permute-start.9 = (bf16[256,1024]{1,0:T(8,128)(2,1)S(1)}, bf16[256,1024]{1,0:T(8,128)(2,1)S(1)}, u32[]{:S(2)}, u32[]{:S(2)}) collective-permute-start(bf16[256,1024]{1,0:T(8,128)(2,1)S(1)} %copy-done), channel_id=1, source_target_pairs={{0,2},{1,3},{2,0},{3,1},{4,6},{5,7},{6,4},{7,5},{8,10},{9,11},{10,... | collective-permute-start | bytes 1572872 | tf_op jit(solution)/shard_map/ppermute | solution.py:780
  19.3 4.5 %copy-start.30 = (s32[1,1024]{1,0:T(1,128)S(1)}, s32[1,1024]{1,0:T(1,128)}, u32[]{:S(2)}) copy-start(s32[1,1024]{1,0:T(1,128)} %param.15) | copy-start | bytes 12292
  27.2 41.8 %collective-permute-start.12 = (bf16[256,1024]{1,0:T(8,128)(2,1)S(1)}, bf16[256,1024]{1,0:T(8,128)(2,1)S(1)}, u32[]{:S(2)}, u32[]{:S(2)}) collective-permute-start(bf16[256,1024]{1,0:T(8,128)(2,1)S(1)} %copy-done), channel_id=1, source_target_pairs={{0,1},{1,0},{2,3},{3,2},{4,5},{5,4},{6,7},{7,6},{8,9},{9,8},{10,11... | collective-permute-start | bytes 1572872 | tf_op jit(solution)/shard_map/ppermute | solution.py:780
  31.6 19.2 %collective-permute-start.6 = (bf16[256,1024]{1,0:T(8,128)(2,1)}, bf16[256,1024]{1,0:T(8,128)(2,1)S(1)}, u32[]{:S(2)}, u32[]{:S(2)}) collective-permute-start(bf16[256,1024]{1,0:T(8,128)(2,1)} %collective-permute-done.2), channel_id=1, source_target_pairs={{0,1},{1,0},{2,3},{3,2},{4,5},{5,4},{6,7},{7,6},{8,9},{9,8},{10,11... | collective-permute-start | bytes 1572872 | tf_op jit(solution)/shard_map/ppermute | solution.py:780
  31.6 15.5 %collective-permute-start.4 = (bf16[128,1152]{1,0:T(8,128)(2,1)}, bf16[128,1152]{1,0:T(8,128)(2,1)S(1)}, u32[]{:S(2)}, u32[]{:S(2)}) collective-permute-start(bf16[128,1152]{1,0:T(8,128)(2,1)} %collective-permute-done), channel_id=1, source_target_pairs={{0,8},{8,16},{16,24},{24,28},{28,20},{20,12},{12,4},{4,0},{1,9},{9... | collective-permute-start | bytes 884744 | tf_op jit(solution)/shard_map/ppermute | solution.py:831
  33.6 17.2 %collective-permute-start.5 = (bf16[128,1152]{1,0:T(8,128)(2,1)}, bf16[128,1152]{1,0:T(8,128)(2,1)S(1)}, u32[]{:S(2)}, u32[]{:S(2)}) collective-permute-start(bf16[128,1152]{1,0:T(8,128)(2,1)} %collective-permute-done.1), channel_id=1, source_target_pairs={{8,0},{16,8},{24,16},{28,24},{20,28},{12,20},{4,12},{0,4},{9,1},{1... | collective-permute-start | bytes 884744 | tf_op jit(solution)/shard_map/ppermute | solution.py:833
  50.8 10.1 %collective-permute-start.7 = (bf16[128,1152]{1,0:T(8,128)(2,1)S(1)}, bf16[128,1152]{1,0:T(8,128)(2,1)S(1)}, u32[]{:S(2)}, u32[]{:S(2)}) collective-permute-start(bf16[128,1152]{1,0:T(8,128)(2,1)S(1)} %collective-permute-done.4), channel_id=1, source_target_pairs={{0,8},{8,16},{16,24},{24,28},{28,20},{20,12},{12,4},{4,0},{1,9},{9... | collective-permute-start | bytes 884744 | tf_op jit(solution)/shard_map/ppermute | solution.py:831
  52.4 12.2 %collective-permute-start.8 = (bf16[128,1152]{1,0:T(8,128)(2,1)S(1)}, bf16[128,1152]{1,0:T(8,128)(2,1)S(1)}, u32[]{:S(2)}, u32[]{:S(2)}) collective-permute-start(bf16[128,1152]{1,0:T(8,128)(2,1)S(1)} %collective-permute-done.5), channel_id=1, source_target_pairs={{8,0},{16,8},{24,16},{28,24},{20,28},{12,20},{4,12},{0,4},{9,1},{1... | collective-permute-start | bytes 884744 | tf_op jit(solution)/shard_map/ppermute | solution.py:833
  65.2 8.6 %collective-permute-start.10 = (bf16[64,1152]{1,0:T(8,128)(2,1)}, bf16[64,1152]{1,0:T(8,128)(2,1)}, u32[]{:S(2)}, u32[]{:S(2)}) collective-permute-start(bf16[64,1152]{1,0:T(8,128)(2,1)} %slice.48), channel_id=1, source_target_pairs={{0,8},{8,16},{16,24},{24,28},{28,20},{20,12},{12,4},{4,0},{1,9},{9... | collective-permute-start | bytes 442376 | tf_op jit(solution)/shard_map/ppermute | solution.py:828
  65.9 12.7 %collective-permute-start.11 = (bf16[64,1152]{1,0:T(8,128)(2,1)}, bf16[64,1152]{1,0:T(8,128)(2,1)S(1)}, u32[]{:S(2)}, u32[]{:S(2)}) collective-permute-start(bf16[64,1152]{1,0:T(8,128)(2,1)} %slice.49), channel_id=1, source_target_pairs={{8,0},{16,8},{24,16},{28,24},{20,28},{12,20},{4,12},{0,4},{9,1},{1... | collective-permute-start | bytes 442376 | tf_op jit(solution)/shard_map/ppermute | solution.py:829
  68.0 10.6 %collective-permute-start.13 = (bf16[256,1024]{1,0:T(8,128)(2,1)S(1)}, bf16[256,1024]{1,0:T(8,128)(2,1)}, u32[]{:S(2)}, u32[]{:S(2)}) collective-permute-start(bf16[256,1024]{1,0:T(8,128)(2,1)S(1)} %collective-permute-done.9.refs_4_.refs_6_), channel_id=1, source_target_pairs={{0,1},{1,0},{2,3},{3,2},{4,5},{5,4},{6,7},{7,6},{8,9},{9,8},{10,11... | collective-permute-start | bytes 1572872 | tf_op jit(solution)/shard_map/ppermute | solution.py:780
  80.9 14.9 %copy-start.16 = (bf16[1024,256]{1,0:T(8,128)(2,1)}, bf16[1024,256]{1,0:T(8,128)(2,1)S(1)}, u32[]{:S(2)}) copy-start(bf16[1024,256]{1,0:T(8,128)(2,1)S(1)} %slice.50.refs_4_.out_ref) | copy-start | bytes 1572868
  80.9 14.9 %collective-permute-start.14 = (bf16[1024,256]{1,0:T(8,128)(2,1)S(1)}, bf16[1024,256]{1,0:T(8,128)(2,1)}, u32[]{:S(2)}, u32[]{:S(2)}) collective-permute-start(bf16[1024,256]{1,0:T(8,128)(2,1)S(1)} %slice.50.refs_4_.out_ref), channel_id=1, source_target_pairs={{0,2},{1,3},{2,0},{3,1},{4,6},{5,7},{6,4},{7,5},{8,10},{9,11},{10,... | collective-permute-start | bytes 1572872 | tf_op jit(solution)/shard_map/ppermute | solution.py:780
  82.6 13.3 %collective-permute-start.15 = (bf16[1024,256]{1,0:T(8,128)(2,1)S(1)}, bf16[1024,256]{1,0:T(8,128)(2,1)}, u32[]{:S(2)}, u32[]{:S(2)}) collective-permute-start(bf16[1024,256]{1,0:T(8,128)(2,1)S(1)} %slice.50.refs_4_.out_ref), channel_id=1, source_target_pairs={{0,1},{1,0},{2,3},{3,2},{4,5},{5,4},{6,7},{7,6},{8,9},{9,8},{10,11... | collective-permute-start | bytes 1572872 | tf_op jit(solution)/shard_map/ppermute | solution.py:780
  95.9 15.0 %collective-permute-start.16 = (bf16[512,256]{1,0:T(8,128)(2,1)}, bf16[512,256]{1,0:T(8,128)(2,1)S(1)}, u32[]{:S(2)}, u32[]{:S(2)}) collective-permute-start(bf16[512,256]{1,0:T(8,128)(2,1)} %get-tuple-element.173.refs_0_), channel_id=1, source_target_pairs={{0,2},{1,3},{2,0},{3,1},{4,6},{5,7},{6,4},{7,5},{8,10},{9,11},{10,... | collective-permute-start | bytes 786440 | tf_op jit(solution)/shard_map/ppermute | solution.py:780
  96.4 14.5 %collective-permute-start.17 = (bf16[512,256]{1,0:T(8,128)(2,1)}, bf16[512,256]{1,0:T(8,128)(2,1)S(1)}, u32[]{:S(2)}, u32[]{:S(2)}) collective-permute-start(bf16[512,256]{1,0:T(8,128)(2,1)} %get-tuple-element.173.refs_0_), channel_id=1, source_target_pairs={{0,1},{1,0},{2,3},{3,2},{4,5},{5,4},{6,7},{7,6},{8,9},{9,8},{10,11... | collective-permute-start | bytes 786440 | tf_op jit(solution)/shard_map/ppermute | solution.py:780
  96.6 14.3 %collective-permute-start.18 = (bf16[1024,256]{1,0:T(8,128)(2,1)}, bf16[1024,256]{1,0:T(8,128)(2,1)S(1)}, u32[]{:S(2)}, u32[]{:S(2)}) collective-permute-start(bf16[1024,256]{1,0:T(8,128)(2,1)} %collective-permute-done.14.refs_5_), channel_id=1, source_target_pairs={{0,1},{1,0},{2,3},{3,2},{4,5},{5,4},{6,7},{7,6},{8,9},{9,8},{10,11... | collective-permute-start | bytes 1572872 | tf_op jit(solution)/shard_map/ppermute | solution.py:780
  111.0 1.9 collective-permute-start.21
  111.3 13.4 %collective-permute-start.19 = (bf16[512,256]{1,0:T(8,128)(2,1)}, bf16[512,256]{1,0:T(8,128)(2,1)S(1)}, u32[]{:S(2)}, u32[]{:S(2)}) collective-permute-start(bf16[512,256]{1,0:T(8,128)(2,1)} %get-tuple-element.191.refs_0_), channel_id=1, source_target_pairs={{0,2},{1,3},{2,0},{3,1},{4,6},{5,7},{6,4},{7,5},{8,10},{9,11},{10,... | collective-permute-start | bytes 786440 | tf_op jit(solution)/shard_map/ppermute | solution.py:780
  112.9 11.9 %collective-permute-start.20 = (bf16[512,256]{1,0:T(8,128)(2,1)}, bf16[512,256]{1,0:T(8,128)(2,1)S(1)}, u32[]{:S(2)}, u32[]{:S(2)}) collective-permute-start(bf16[512,256]{1,0:T(8,128)(2,1)} %get-tuple-element.191.refs_0_), channel_id=1, source_target_pairs={{0,1},{1,0},{2,3},{3,2},{4,5},{5,4},{6,7},{7,6},{8,9},{9,8},{10,11... | collective-permute-start | bytes 786440 | tf_op jit(solution)/shard_map/ppermute | solution.py:780
  124.7 5.0 %copy-start.36 = (bf16[512,256]{1,0:T(8,128)(2,1)}, bf16[512,256]{1,0:T(8,128)(2,1)S(1)}, u32[]{:S(2)}) copy-start(bf16[512,256]{1,0:T(8,128)(2,1)S(1)} %collective-permute-done.19.refs_1_) | copy-start | bytes 786436
  124.7 2.3 collective-permute-start.23
  125.3 3.1 %collective-permute-start.22 = (bf16[512,256]{1,0:T(8,128)(2,1)S(1)}, bf16[512,256]{1,0:T(8,128)(2,1)S(1)}, u32[]{:S(2)}, u32[]{:S(2)}) collective-permute-start(bf16[512,256]{1,0:T(8,128)(2,1)S(1)} %collective-permute-done.19.refs_1_), channel_id=1, source_target_pairs={{0,1},{1,0},{2,3},{3,2},{4,5},{5,4},{6,7},{7,6},{8,9},{9,8},{10,11... | collective-permute-start | bytes 786440 | tf_op jit(solution)/shard_map/ppermute | solution.py:780
  128.4 14.3 %copy-start.1 = (f32[256,1024]{1,0:T(8,128)S(1)}, f32[256,1024]{1,0:T(8,128)}, u32[]{:S(2)}) copy-start(f32[256,1024]{1,0:T(8,128)} %get-tuple-element.208.refs_2_.mid0) | copy-start | bytes 3145732
  128.4 14.3 %copy-start.7 = (f32[1,1024]{1,0:T(1,128)S(1)}, f32[1,1024]{1,0:T(1,128)}, u32[]{:S(2)}) copy-start(f32[1,1024]{1,0:T(1,128)} %refs_7_.5) | copy-start | bytes 12292
  128.5 14.3 %collective-permute-start.24 = (bf16[256,1024]{1,0:T(8,128)(2,1)S(1)}, bf16[256,1024]{1,0:T(8,128)(2,1)S(1)}, u32[]{:S(2)}, u32[]{:S(2)}) collective-permute-start(bf16[256,1024]{1,0:T(8,128)(2,1)S(1)} %add_convert_fusion.refs_0_), channel_id=1, source_target_pairs={{0,2},{1,3},{2,0},{3,1},{4,6},{5,7},{6,4},{7,5},{8,10},{9,11},{10,... | collective-permute-start | bytes 1572872 | tf_op jit(solution)/shard_map/ppermute | solution.py:780
  142.7 2.1 collective-permute-start.25
  144.3 11.2 %copy-start.8 = (bf16[256,1024]{1,0:T(8,128)(2,1)}, bf16[256,1024]{1,0:T(8,128)(2,1)S(1)}, u32[]{:S(2)}) copy-start(bf16[256,1024]{1,0:T(8,128)(2,1)S(1)} %get-tuple-element.215.ga0_ref) | copy-start | bytes 1572868
  145.0 10.4 %collective-permute-start.27 = (bf16[256,1024]{1,0:T(8,128)(2,1)S(1)}, bf16[256,1024]{1,0:T(8,128)(2,1)S(1)}, u32[]{:S(2)}, u32[]{:S(2)}) collective-permute-start(bf16[256,1024]{1,0:T(8,128)(2,1)S(1)} %get-tuple-element.215.ga0_ref), channel_id=1, source_target_pairs={{0,1},{1,0},{2,3},{3,2},{4,5},{5,4},{6,7},{7,6},{8,9},{9,8},{10,11... | collective-permute-start | bytes 1572872 | tf_op jit(solution)/shard_map/ppermute | solution.py:780
  145.2 10.2 %collective-permute-start.26 = (bf16[128,1024]{1,0:T(8,128)(2,1)S(1)}, bf16[128,1024]{1,0:T(8,128)(2,1)S(1)}, u32[]{:S(2)}, u32[]{:S(2)}) collective-permute-start(bf16[128,1024]{1,0:T(8,128)(2,1)S(1)} %get-tuple-element.213.refs_7_.refs_0_), channel_id=1, source_target_pairs={{0,2},{1,3},{2,0},{3,1},{4,6},{5,7},{6,4},{7,5},{8,10},{9,11},{10,... | collective-permute-start | bytes 786440 | tf_op jit(solution)/shard_map/ppermute | solution.py:780
  156.3 8.4 %copy-start.2 = (f32[256,1024]{1,0:T(8,128)S(1)}, f32[256,1024]{1,0:T(8,128)}, u32[]{:S(2)}) copy-start(f32[256,1024]{1,0:T(8,128)} %get-tuple-element.226.refs_4_.mid1) | copy-start | bytes 3145732
  156.3 8.4 %copy-start.6 = (bf16[128,1024]{1,0:T(8,128)(2,1)S(1)}, bf16[128,1024]{1,0:T(8,128)(2,1)}, u32[]{:S(2)}) copy-start(bf16[128,1024]{1,0:T(8,128)(2,1)} %copy-done.5) | copy-start | bytes 786436
  156.3 8.4 %collective-permute-start.28 = (bf16[128,1024]{1,0:T(8,128)(2,1)S(1)}, bf16[128,1024]{1,0:T(8,128)(2,1)S(1)}, u32[]{:S(2)}, u32[]{:S(2)}) collective-permute-start(bf16[128,1024]{1,0:T(8,128)(2,1)S(1)} %get-tuple-element.214.refs_1_), channel_id=1, source_target_pairs={{0,2},{1,3},{2,0},{3,1},{4,6},{5,7},{6,4},{7,5},{8,10},{9,11},{10,... | collective-permute-start | bytes 786440 | tf_op jit(solution)/shard_map/ppermute | solution.py:780
  166.2 2.6 collective-permute-start.29
  166.2 38.1 %collective-permute-start.30 = (bf16[2,256,1024]{2,1,0:T(8,128)(2,1)}, bf16[2,256,1024]{2,1,0:T(8,128)(2,1)S(1)}, u32[]{:S(2)}, u32[]{:S(2)}) collective-permute-start(bf16[2,256,1024]{2,1,0:T(8,128)(2,1)} %get-tuple-element.255), channel_id=1, source_target_pairs={{0,1},{1,0},{2,3},{3,2},{4,5},{5,4},{6,7},{7,6},{8,9},{9,8},{10,11... | collective-permute-start | bytes 3145736 | tf_op jit(solution)/shard_map/ppermute | solution.py:780
  204.3 10.2 %copy-start.11 = (bf16[2,256,1024]{2,1,0:T(8,128)(2,1)}, bf16[2,256,1024]{2,1,0:T(8,128)(2,1)S(1)}, u32[]{:S(2)}) copy-start(bf16[2,256,1024]{2,1,0:T(8,128)(2,1)S(1)} %collective-permute-done.30.got) | copy-start | bytes 3145732
  204.3 9.3 %collective-permute-start.31 = (bf16[2,256,1024]{2,1,0:T(8,128)(2,1)}, bf16[2,256,1024]{2,1,0:T(8,128)(2,1)S(1)}, u32[]{:S(2)}, u32[]{:S(2)}) collective-permute-start(bf16[2,256,1024]{2,1,0:T(8,128)(2,1)} %get-tuple-element.257), channel_id=1, source_target_pairs={{0,1},{1,0},{2,3},{3,2},{4,5},{5,4},{6,7},{7,6},{8,9},{9,8},{10,11... | collective-permute-start | bytes 3145736 | tf_op jit(solution)/shard_map/ppermute | solution.py:780
  204.5 23.2 %collective-permute-start.32 = (bf16[4,128,512]{2,1,0:T(8,128)(2,1)}, bf16[4,128,512]{2,1,0:T(8,128)(2,1)S(1)}, u32[]{:S(2)}, u32[]{:S(2)}) collective-permute-start(bf16[4,128,512]{2,1,0:T(8,128)(2,1)} %get-tuple-element.261), channel_id=1, source_target_pairs={{0,4},{4,0},{8,12},{12,8},{16,20},{20,16},{24,28},{28,24},{1,5},{5... | collective-permute-start | bytes 1572872 | tf_op jit(solution)/shard_map/ppermute | solution.py:780
  208.1 19.6 %collective-permute-start.33 = (bf16[4,128,512]{2,1,0:T(8,128)(2,1)}, bf16[4,128,512]{2,1,0:T(8,128)(2,1)S(1)}, u32[]{:S(2)}, u32[]{:S(2)}) collective-permute-start(bf16[4,128,512]{2,1,0:T(8,128)(2,1)} %get-tuple-element.262), channel_id=1, source_target_pairs={{0,8},{4,12},{8,0},{12,4},{16,24},{20,28},{24,16},{28,20},{1,9},{5... | collective-permute-start | bytes 1572872 | tf_op jit(solution)/shard_map/ppermute | solution.py:780
  212.6 8.3 %collective-permute-start.34 = (f32[8,1024]{1,0:T(8,128)}, f32[8,1024]{1,0:T(8,128)S(1)}, u32[]{:S(2)}, u32[]{:S(2)}) collective-permute-start(f32[8,1024]{1,0:T(8,128)} %get-tuple-element.258.wait_for), channel_id=1, source_target_pairs={{0,1},{1,0},{2,3},{3,2},{4,5},{5,4},{6,7},{7,6},{8,9},{9,8},{10,11... | collective-permute-start | bytes 98312 | tf_op jit(solution)/shard_map/ppermute | solution.py:780
  212.6 8.3 %collective-permute-start.35 = (f32[8,1024]{1,0:T(8,128)}, f32[8,1024]{1,0:T(8,128)S(1)}, u32[]{:S(2)}, u32[]{:S(2)}) collective-permute-start(f32[8,1024]{1,0:T(8,128)} %get-tuple-element.258.wait_for), channel_id=1, source_target_pairs={{0,2},{1,3},{2,0},{3,1},{4,6},{5,7},{6,4},{7,5},{8,10},{9,11},{10,... | collective-permute-start | bytes 98312 | tf_op jit(solution)/shard_map/ppermute | solution.py:780
  213.6 7.3 %collective-permute-start.36 = (f32[8,1024]{1,0:T(8,128)}, f32[8,1024]{1,0:T(8,128)S(1)}, u32[]{:S(2)}, u32[]{:S(2)}) collective-permute-start(f32[8,1024]{1,0:T(8,128)} %get-tuple-element.258.wait_for), channel_id=1, source_target_pairs={{0,3},{1,2},{2,1},{3,0},{4,7},{5,6},{6,5},{7,4},{8,11},{9,10},{10,... | collective-permute-start | bytes 98312 | tf_op jit(solution)/shard_map/ppermute | solution.py:780
  217.8 19.8 %copy-start.22 = (f32[8,1024]{1,0:T(8,128)S(1)}, f32[8,1024]{1,0:T(8,128)}, u32[]{:S(2)}) copy-start(f32[8,1024]{1,0:T(8,128)} %get-tuple-element.258.wait_for) | copy-start | bytes 98308
  217.8 19.8 %copy-start.29 = (f32[8,1024]{1,0:T(8,128)S(1)}, f32[8,1024]{1,0:T(8,128)}, u32[]{:S(2)}) copy-start(f32[8,1024]{1,0:T(8,128)} %get-tuple-element.273) | copy-start | bytes 98308
  227.7 23.0 %collective-permute-start.40 = (bf16[256,1024]{1,0:T(8,128)(2,1)}, bf16[256,1024]{1,0:T(8,128)(2,1)S(1)}, u32[]{:S(2)}, u32[]{:S(2)}) collective-permute-start(bf16[256,1024]{1,0:T(8,128)(2,1)} %get-tuple-element.277), channel_id=1, source_target_pairs={{0,2},{1,3},{2,0},{3,1},{4,6},{5,7},{6,4},{7,5},{8,10},{9,11},{10,... | collective-permute-start | bytes 1572872 | tf_op jit(solution)/shard_map/ppermute | solution.py:780
  229.2 32.0 %collective-permute-start.41 = (bf16[256,1024]{1,0:T(8,128)(2,1)}, bf16[256,1024]{1,0:T(8,128)(2,1)S(1)}, u32[]{:S(2)}, u32[]{:S(2)}) collective-permute-start(bf16[256,1024]{1,0:T(8,128)(2,1)} %get-tuple-element.280), channel_id=1, source_target_pairs={{0,2},{1,3},{2,0},{3,1},{4,6},{5,7},{6,4},{7,5},{8,10},{9,11},{10,... | collective-permute-start | bytes 1572872 | tf_op jit(solution)/shard_map/ppermute | solution.py:780
  232.4 18.3 %collective-permute-start.37 = (bf16[2,128,512]{2,1,0:T(8,128)(2,1)}, bf16[2,128,512]{2,1,0:T(8,128)(2,1)S(1)}, u32[]{:S(2)}, u32[]{:S(2)}) collective-permute-start(bf16[2,128,512]{2,1,0:T(8,128)(2,1)} %get-tuple-element.271), channel_id=1, source_target_pairs={{0,8},{4,12},{8,0},{12,4},{16,24},{20,28},{24,16},{28,20},{1,9},{5... | collective-permute-start | bytes 786440 | tf_op jit(solution)/shard_map/ppermute | solution.py:780
  235.8 14.9 %collective-permute-start.38 = (bf16[2,128,512]{2,1,0:T(8,128)(2,1)}, bf16[2,128,512]{2,1,0:T(8,128)(2,1)S(1)}, u32[]{:S(2)}, u32[]{:S(2)}) collective-permute-start(bf16[2,128,512]{2,1,0:T(8,128)(2,1)} %get-tuple-element.272), channel_id=1, source_target_pairs={{0,4},{4,0},{8,12},{12,8},{16,20},{20,16},{24,28},{28,24},{1,5},{5... | collective-permute-start | bytes 786440 | tf_op jit(solution)/shard_map/ppermute | solution.py:780
  237.6 12.2 %collective-permute-start.39 = (f32[8,1024]{1,0:T(8,128)S(1)}, f32[8,1024]{1,0:T(8,128)S(1)}, u32[]{:S(2)}, u32[]{:S(2)}) collective-permute-start(f32[8,1024]{1,0:T(8,128)S(1)} %add_add_fusion), channel_id=1, source_target_pairs={{0,4},{4,0},{8,12},{12,8},{16,20},{20,16},{24,28},{28,24},{1,5},{5... | collective-permute-start | bytes 98312 | tf_op jit(solution)/shard_map/ppermute | solution.py:780
  249.8 24.4 %copy-start.23 = (f32[8,1024]{1,0:T(8,128)}, f32[8,1024]{1,0:T(8,128)S(1)}, u32[]{:S(2)}) copy-start(f32[8,1024]{1,0:T(8,128)S(1)} %add.201.s_ref) | copy-start | bytes 98308
  250.7 10.5 %copy-start.14 = (bf16[256,1024]{1,0:T(8,128)(2,1)}, bf16[256,1024]{1,0:T(8,128)(2,1)S(1)}, u32[]{:S(2)}) copy-start(bf16[256,1024]{1,0:T(8,128)(2,1)S(1)} %collective-permute-done.40.na_y) | copy-start | bytes 1572868
  253.5 20.6 %collective-permute-start.42 = (bf16[1,128,512]{2,1,0:T(8,128)(2,1)}, bf16[1,128,512]{2,1,0:T(8,128)(2,1)S(1)}, u32[]{:S(2)}, u32[]{:S(2)}) collective-permute-start(bf16[1,128,512]{2,1,0:T(8,128)(2,1)} %get-tuple-element.288), channel_id=1, source_target_pairs={{0,16},{4,20},{8,24},{12,28},{16,0},{20,4},{24,8},{28,12},{1,17},{... | collective-permute-start | bytes 393224 | tf_op jit(solution)/shard_map/ppermute | solution.py:780
  255.5 18.6 %collective-permute-start.43 = (bf16[1,128,512]{2,1,0:T(8,128)(2,1)}, bf16[1,128,512]{2,1,0:T(8,128)(2,1)S(1)}, u32[]{:S(2)}, u32[]{:S(2)}) collective-permute-start(bf16[1,128,512]{2,1,0:T(8,128)(2,1)} %get-tuple-element.290), channel_id=1, source_target_pairs={{0,16},{4,20},{8,24},{12,28},{16,0},{20,4},{24,8},{28,12},{1,17},{... | collective-permute-start | bytes 393224 | tf_op jit(solution)/shard_map/ppermute | solution.py:780
  256.4 16.8 %collective-permute-start.44 = (f32[8,1024]{1,0:T(8,128)S(1)}, f32[8,1024]{1,0:T(8,128)S(1)}, u32[]{:S(2)}, u32[]{:S(2)}) collective-permute-start(f32[8,1024]{1,0:T(8,128)S(1)} %add.201.s_ref), channel_id=1, source_target_pairs={{0,8},{4,12},{8,0},{12,4},{16,24},{20,28},{24,16},{28,20},{1,9},{5... | collective-permute-start | bytes 98312 | tf_op jit(solution)/shard_map/ppermute | solution.py:780
  258.3 15.8 %collective-permute-start.45 = (f32[8,1024]{1,0:T(8,128)S(1)}, f32[8,1024]{1,0:T(8,128)S(1)}, u32[]{:S(2)}, u32[]{:S(2)}) collective-permute-start(f32[8,1024]{1,0:T(8,128)S(1)} %add.201.s_ref), channel_id=1, source_target_pairs={{0,16},{4,20},{8,24},{12,28},{16,0},{20,4},{24,8},{28,12},{1,17},{... | collective-permute-start | bytes 98312 | tf_op jit(solution)/shard_map/ppermute | solution.py:780
  261.2 12.9 %collective-permute-start.46 = (f32[8,1024]{1,0:T(8,128)S(1)}, f32[8,1024]{1,0:T(8,128)S(1)}, u32[]{:S(2)}, u32[]{:S(2)}) collective-permute-start(f32[8,1024]{1,0:T(8,128)S(1)} %add.201.s_ref), channel_id=1, source_target_pairs={{0,24},{4,28},{8,16},{12,20},{16,8},{20,12},{24,0},{28,4},{1,25},{... | collective-permute-start | bytes 98312 | tf_op jit(solution)/shard_map/ppermute | solution.py:780
  (25 other events, 39.6 us)
Sparse Core Ops, SparseCore 0:
  13.4 88.6 all-gather.1
  156.4 114.7 reduce-scatter.1

commit v5 on v4

--- a/solution.py
+++ b/solution.py
@@ -875,17 +875,17 @@
     x_cy = core_hop(x_y)
     c_y = y_hop(cotangent)
     c_c = core_hop(cotangent)
-    ring.a, ring.b, x_cy = fence(ring.a, ring.b, x_cy)
+    ring.a, ring.b, x_cy, c_y = fence(ring.a, ring.b, x_cy, c_y)
     ring.keep()
     ring.step()
+    c_cy = core_hop(c_y)
     x_full = in_order(layer_input, x_y, (x_c, x_cy))
-    ring.a, ring.b, x_full, cols, c_y = fence(ring.a, ring.b, x_full, cols, c_y)
+    ring.a, ring.b, x_full, cols, c_cy = fence(ring.a, ring.b, x_full, cols, c_cy)
     ring.keep()
+    g_f = in_order(cotangent, c_y, (c_c, c_cy))
     while 2 * ring.k < n_f:
         ring.step()
         ring.keep()
-    c_cy = core_hop(c_y)
-    g_f = in_order(cotangent, c_y, (c_c, c_cy))
     wide, g_f = fence(ring.full, g_f)
 
     out_own = wide[:, 3 * width + HEAD:]

time: 288 us -> 285 us (0.990)
    ppermute x39, waiting for transfers between devices: 31.9 us -> 36 us  [hop(): return lax.ppermute(value, axis, [(i, i ^ bit) for i in range(n)])]
    unnamed x81 -> x91, local copies, waits for them, and re-layouts: 7.97 us -> 8.06 us
  transfers between devices with their start and end apart: 49 -> 49, of which waited for: 17 -> 19; matrix products, arithmetic and copies ran while one was open for 9% -> 8% of each run, Pallas kernels for 42% -> 42%
where the time goes in v5:
time: 285 us; the launch traced here: 281 us
  Pallas kernels  122 us (43%)
  waiting for transfers between devices  65.3 us (23%)
  starting transfers between devices  45.2 us (16%)
  local copies, waits for them, and re-layouts  29.6 us (10%)
  between operations  15 us (5%)
  other arithmetic  4.04 us (1%)
    ppermute x39, waiting for transfers between devices, hop(): return lax.ppermute(value, axis, [(i, i ^ bit) for i in range(n)])  36 us
    ppermute x39, starting transfers between devices, hop(): return lax.ppermute(value, axis, [(i, i ^ bit) for i in range(n)])  35.8 us
    pallas_call x1, Pallas kernels, mixer_bwd(): pl.pallas_call(functools.partial(bwd_kernel, heads, cb, n_f, shard), grid...  34.6 us
    pallas_call x2, Pallas kernels, mixer_fwd(): pl.pallas_call(functools.partial(fwd_call_kernel, heads, cb, base, len(ol...  27.3 us
    pallas_call x2, Pallas kernels, ffn(): pl.pallas_call(functools.partial(ffn_kernel, ff), grid=(1,), in_specs=[wh...  22.3 us
    ppermute x3, waiting for transfers between devices, step(): self.a = lax.ppermute(self.a, 'fsdp', self.right)  13.7 us
    pallas_call x1, Pallas kernels, ffn_grads(): pl.pallas_call(functools.partial(ffn_grads_kernel, ff, len(pieces)), grid...  9.18 us
    dynamic_update_slice x8, local copies, waits for them, and re-layouts, in_order(): lax.dynamic_update_slice(full, block[None], (me ^ k,) + (0,) * own.ndim)  8.58 us
  transfers between devices with their start and end apart: 49, of which 19 were waited for; matrix products, arithmetic and copies ran while one was open for 8% of the time, Pallas kernels for 42%

profile of v5, /device:TPU:0, one launch (start us, length us, event | category | flops | bytes accessed | tf_op | source)
XLA Modules:
  0.0 281.5 jit_solution(14681181282214992082)
XLA Ops:
  7.2 1.4 copy.45
  8.7 1.8 pack.1
  10.4 1.0 slice_bitcast_fusion.1
  11.5 1.8 pad_maximum_fusion
  13.3 3.1 %collective-permute-start = (bf16[128,1152]{1,0:T(8,128)(2,1)}, bf16[128,1152]{1,0:T(8,128)(2,1)}, u32[]{:S(2)}, u32[]{:S(2)}) collective-permute-start(bf16[128,1152]{1,0:T(8,128)(2,1)} %pack.1), channel_id=1, source_target_pairs={{0,8},{8,16},{16,24},{24,28},{28,20},{20,12},{12,4},{4,0},{1,9},{9... | collective-permute-start | bytes 884744 | tf_op jit(solution)/shard_map/ppermute | solution.py:831
  16.4 2.0 collective-permute-start.2
  19.3 1.0 constant_dynamic-update-slice_fusion.8
  20.3 1.7 broadcast.20.clone
  22.0 1.9 bitcast_dynamic-update-slice_fusion.7
  25.6 5.9 %collective-permute-done.2 = bf16[256,1024]{1,0:T(8,128)(2,1)} collective-permute-done((bf16[256,1024]{1,0:T(8,128)(2,1)}, bf16[256,1024]{1,0:T(8,128)(2,1)}, u32[]{:S(2)}, u32[]{:S(2)}) %collective-permute-start.2) | collective-permute-done | bytes 524320 | tf_op jit(solution)/shard_map/ppermute | solution.py:780
  31.6 2.0 collective-permute-start.4
  33.6 1.9 bitcast_dynamic-update-slice_fusion.6
  35.5 1.0 constant_dynamic-update-slice_fusion.7
  36.5 1.0 constant_dynamic-update-slice_fusion.6
  37.5 1.9 bitcast_dynamic-update-slice_fusion.5
  39.4 1.8 collective-permute-done.7.refs_4_.refs_6_
  41.2 5.9 %collective-permute-done.4 = bf16[128,1152]{1,0:T(8,128)(2,1)S(1)} collective-permute-done((bf16[128,1152]{1,0:T(8,128)(2,1)}, bf16[128,1152]{1,0:T(8,128)(2,1)S(1)}, u32[]{:S(2)}, u32[]{:S(2)}) %collective-permute-start.4) | collective-permute-done | bytes 294944 | tf_op jit(solution)/shard_map/ppermute | solution.py:831
  47.1 3.7 %collective-permute-done.5 = bf16[128,1152]{1,0:T(8,128)(2,1)S(1)} collective-permute-done((bf16[128,1152]{1,0:T(8,128)(2,1)}, bf16[128,1152]{1,0:T(8,128)(2,1)S(1)}, u32[]{:S(2)}, u32[]{:S(2)}) %collective-permute-start.5) | collective-permute-done | bytes 294944 | tf_op jit(solution)/shard_map/ppermute | solution.py:833
  50.8 1.9 collective-permute-start.8
  53.9 7.8 %collective-permute-done.8 = bf16[128,1152]{1,0:T(8,128)(2,1)S(1)} collective-permute-done((bf16[128,1152]{1,0:T(8,128)(2,1)S(1)}, bf16[128,1152]{1,0:T(8,128)(2,1)S(1)}, u32[]{:S(2)}, u32[]{:S(2)}) %collective-permute-start.8) | collective-permute-done | bytes 294944 | tf_op jit(solution)/shard_map/ppermute | solution.py:831
  61.7 4.4 %collective-permute-done.9 = bf16[128,1152]{1,0:T(8,128)(2,1)S(1)} collective-permute-done((bf16[128,1152]{1,0:T(8,128)(2,1)S(1)}, bf16[128,1152]{1,0:T(8,128)(2,1)S(1)}, u32[]{:S(2)}, u32[]{:S(2)}) %collective-permute-start.9) | collective-permute-done | bytes 294944 | tf_op jit(solution)/shard_map/ppermute | solution.py:833
  67.5 2.2 collective-permute-start.12
  69.7 1.8 copy.46.refs_4_.cols_ref
  71.5 1.0 constant_dynamic-update-slice_fusion.3
  72.5 1.9 bitcast_dynamic-update-slice_fusion
  74.3 1.0 constant_dynamic-update-slice_fusion.2
  76.4 3.2 %collective-permute-done.12 = bf16[64,1152]{1,0:T(8,128)(2,1)S(1)} collective-permute-done((bf16[64,1152]{1,0:T(8,128)(2,1)}, bf16[64,1152]{1,0:T(8,128)(2,1)S(1)}, u32[]{:S(2)}, u32[]{:S(2)}) %collective-permute-start.12) | collective-permute-done | bytes 147488 | tf_op jit(solution)/shard_map/ppermute | solution.py:829
  79.6 1.4 collective-permute-start.14
  81.0 13.2 %mixer_fwd.2 = (bf16[512,256]{1,0:T(8,128)(2,1)}, bf16[1024,256]{1,0:T(8,128)(2,1)}, bf16[1024,1024]{1,0:T(8,128)(2,1)}, f32[1024,896]{1,0:T(8,128)}, f32[1024,7...) custom-call(s32[1024]{0:T(1024)} %bitcast.66, ...), custom_call_target="tpu_custom_call" | custom-call | flops 10000000000 | bytes 10000000 | tf_op jit(solution)/shard_map/mixer_fwd/pallas_call | solution.py:354
  94.3 1.3 collective-permute-start.16
  96.2 14.0 %mixer_fwd.3 = (bf16[512,256]{1,0:T(8,128)(2,1)}, bf16[1024,256]{1,0:T(8,128)(2,1)}, bf16[1024,1024]{1,0:T(8,128)(2,1)}, f32[1024,896]{1,0:T(8,128)}, f32[1024,7...) custom-call(s32[1024]{0:T(1024)} %bitcast.67, ...), custom_call_target="tpu_custom_call", output_to_operand_aliasing={{1}: (10, {}), {2}: (11, {}), {3}: (12, {}), {4}: (13, {}),... | custom-call | flops 10000000000 | bytes 10000000 | tf_op jit(solution)/shard_map/mixer_fwd/pallas_call | solution.py:354
  112.6 11.1 %ffn.2 = (f32[256,1024]{1,0:T(8,128)}, bf16[512,1024]{1,0:T(8,128)(2,1)}, bf16[704,512]{1,0:T(8,128)(2,1)}, bf16[1408,512]{1,0:T(8,128)(2,1)}, f32[256,1024]{1,0...) custom-call(bf16[512,256]{1,0:T(8,128)(2,1)} %get-tuple-element.175.refs_0_, bf16[512,256]{1,0:T(8,128)(2,1)} %copy-done.39, ...), custom_call_target="tpu_custom_call" | custom-call | flops 10000000000 | bytes 10000000 | tf_op jit(solution)/shard_map/ffn/pallas_call | solution.py:511
  124.3 1.6 collective-permute-done.23
  125.9 1.4 add_convert_fusion.refs_0_
  128.1 11.2 %ffn.3 = (f32[256,1024]{1,0:T(8,128)}, bf16[512,1024]{1,0:T(8,128)(2,1)}, bf16[704,512]{1,0:T(8,128)(2,1)}, bf16[1408,512]{1,0:T(8,128)(2,1)}, f32[256,1024]{1,0...) custom-call(bf16[512,256]{1,0:T(8,128)(2,1)} %get-tuple-element.193.refs_0_, bf16[512,256]{1,0:T(8,128)(2,1)} %copy-done.41, ...), custom_call_target="tpu_custom_call" | custom-call | flops 10000000000 | bytes 10000000 | tf_op jit(solution)/shard_map/ffn/pallas_call | solution.py:511
  139.4 2.0 collective-permute-done.24.refs_1_
  141.9 1.0 copy-done.3
  143.8 1.0 collective-permute-start.26
  144.8 9.2 %ffn_grads.1.refs_3_.wait_for = bf16[8,2112,128]{2,1,0:T(8,128)(2,1)} custom-call(bf16[1408,512]{1,0:T(8,128)(2,1)} %get-tuple-element.218.refs_0_, bf16[704,512]{1,0:T(8,128)(2,1)} %get-tuple-element.219.refs_1_.refs_0_, bf16[512,1024]{1,0:T(8,128)(2,1)} %get-tuple-element.220.refs_2_, bf16[1408,512]{1,0:T(8,128)(2,1)} %get-tuple-element.221.refs_3_, ...), custom_call_target="tpu_custom_call" | custom-call | flops 5000000000 | bytes 10000000 | tf_op jit(solution)/shard_map/ffn_grads/pallas_call | solution.py:600
  154.8 1.1 collective-permute-start.28
  156.0 5.8 %down.1 = (bf16[2,256,1024]{2,1,0:T(8,128)(2,1)}, f32[2,256,1024]{2,1,0:T(8,128)}) custom-call(bf16[704,512]{1,0:T(8,128)(2,1)} %get-tuple-element.219.refs_1_.refs_0_, bf16[704,512]{1,0:T(8,128)(2,1)} %get-tuple-element.222.refs_4_.refs_1_, bf16[2112,1024]{1,0:T(8,128)(2,1)} %all-gather.2.cloned.1.call-done.refs_9_.refs_2_, ...), custom_call_target="tpu_custom_call" | custom-call | flops 1 | bytes 1 | tf_op jit(solution)/shard_map/down/pallas_call | solution.py:564
  161.8 1.4 collective-permute-done.28.refs_3_
  163.8 1.0 copy-done.4
  165.3 2.1 collective-permute-done.29.ga1c_ref
  168.2 34.6 %mixer_bwd.1 = (bf16[4,128,512]{2,1,0:T(8,128)(2,1)}, bf16[4,128,512]{2,1,0:T(8,128)(2,1)}, bf16[4,128,512]{2,1,0:T(8,128)(2,1)}, bf16[4,128,512]{2,1,0:T(8,128)...) custom-call(s32[1024]{0:T(1024)} %bitcast.68, ...), custom_call_target="tpu_custom_call" | custom-call | flops 10000000000 | bytes 10000000 | tf_op jit(solution)/shard_map/mixer_bwd/pallas_call | solution.py:386
  203.0 2.2 collective-permute-start.32
  205.3 4.9 %collective-permute-start.33 = (bf16[4,128,512]{2,1,0:T(8,128)(2,1)}, bf16[4,128,512]{2,1,0:T(8,128)(2,1)S(1)}, u32[]{:S(2)}, u32[]{:S(2)}) collective-permute-start(bf16[4,128,512]{2,1,0:T(8,128)(2,1)} %get-tuple-element.264), channel_id=1, source_target_pairs={{0,8},{4,12},{8,0},{12,4},{16,24},{20,28},{24,16},{28,20},{1,9},{5... | collective-permute-start | bytes 1572872 | tf_op jit(solution)/shard_map/ppermute | solution.py:780
  210.2 1.1 collective-permute-start.35
  212.0 3.2 %to_chips.3 = (f32[256,1024]{1,0:T(8,128)}, bf16[256,1024]{1,0:T(8,128)(2,1)}) custom-call(f32[2,256,1024]{2,1,0:T(8,128)} %get-tuple-element.266.keep, bf16[2,256,1024]{2,1,0:T(8,128)(2,1)} %copy-done.12, bf16[8,2112,128]{2,1,0:T(8,128)(2,1)} %ffn_grads.1.refs_3_.wait_for), custom_call_target="tpu_custom_call" | custom-call | flops 1 | bytes 1 | tf_op jit(solution)/shard_map/to_chips/pallas_call | solution.py:620
  215.3 3.3 %to_chips.2 = (f32[256,1024]{1,0:T(8,128)}, bf16[256,1024]{1,0:T(8,128)(2,1)}) custom-call(f32[2,256,1024]{2,1,0:T(8,128)} %get-tuple-element.258.keep, bf16[2,256,1024]{2,1,0:T(8,128)(2,1)} %copy-done.13, f32[8,1024]{1,0:T(8,128)} %get-tuple-element.260.wait_for), custom_call_target="tpu_custom_call" | custom-call | flops 1 | bytes 1 | tf_op jit(solution)/shard_map/to_chips/pallas_call | solution.py:620
  218.5 6.8 %collective-permute-done.32.g1_ref = bf16[4,128,512]{2,1,0:T(8,128)(2,1)S(1)} collective-permute-done((bf16[4,128,512]{2,1,0:T(8,128)(2,1)}, bf16[4,128,512]{2,1,0:T(8,128)(2,1)S(1)}, u32[]{:S(2)}, u32[]{:S(2)}) %collective-permute-start.32) | collective-permute-done | bytes 524320 | tf_op jit(solution)/shard_map/ppermute | solution.py:780
  225.4 1.3 collective-permute-start.40
  227.5 2.7 fold.2
  230.1 3.2 %collective-permute-start.37 = (bf16[2,128,512]{2,1,0:T(8,128)(2,1)}, bf16[2,128,512]{2,1,0:T(8,128)(2,1)S(1)}, u32[]{:S(2)}, u32[]{:S(2)}) collective-permute-start(bf16[2,128,512]{2,1,0:T(8,128)(2,1)} %get-tuple-element.273), channel_id=1, source_target_pairs={{0,8},{4,12},{8,0},{12,4},{16,24},{20,28},{24,16},{28,20},{1,9},{5... | collective-permute-start | bytes 786440 | tf_op jit(solution)/shard_map/ppermute | solution.py:780
  233.4 1.7 collective-permute-start.38
  235.5 11.8 %collective-permute-done.39 = f32[8,1024]{1,0:T(8,128)S(1)} collective-permute-done((f32[8,1024]{1,0:T(8,128)S(1)}, f32[8,1024]{1,0:T(8,128)S(1)}, u32[]{:S(2)}, u32[]{:S(2)}) %collective-permute-start.39) | collective-permute-done | bytes 32800 | tf_op jit(solution)/shard_map/ppermute | solution.py:780
  248.7 2.0 fold.3
  250.8 2.2 collective-permute-start.42
  253.7 2.3 collective-permute-start.44
  256.0 2.9 %collective-permute-start.45 = (f32[8,1024]{1,0:T(8,128)S(1)}, f32[8,1024]{1,0:T(8,128)S(1)}, u32[]{:S(2)}, u32[]{:S(2)}) collective-permute-start(f32[8,1024]{1,0:T(8,128)S(1)} %add.201.s_ref), channel_id=1, source_target_pairs={{0,16},{4,20},{8,24},{12,28},{16,0},{20,4},{24,8},{28,12},{1,17},{... | collective-permute-start | bytes 98312 | tf_op jit(solution)/shard_map/ppermute | solution.py:780
  259.7 5.0 %last_rows.1 = (f32[256,1024]{1,0:T(8,128)}, bf16[256,1024]{1,0:T(8,128)(2,1)}) custom-call(f32[256,1024]{1,0:T(8,128)} %copy-done.3, f32[256,1024]{1,0:T(8,128)} %copy-done.4, f32[256,1024]{1,0:T(8,128)} %get-tuple-element.261.na, bf16[256,1024]{1,0:T(8,128)(2,1)} %copy-done.17, bf16[256,1024]{1,0:T(8,128)(2,1)} %x_ref.1, f32[1,1024]{1,0:T(1,128)} %gain_ref.3, ...), custom_call_target="tpu_custom_call" | custom-call | flops 1 | bytes 1 | tf_op jit(solution)/shard_map/last_rows/pallas_call | solution.py:640
  264.7 4.2 %reduce-scatter.2.cloned.1.call-done = bf16[1,2112,128]{2,1,0:T(8,128)(2,1)} async-done(((bf16[8,2112,128]{2,1,0:T(8,128)(2,1)}), bf16[1,2112,128]{2,1,0:T(8,128)(2,1)}) %reduce-scatter.2.cloned.1.call-update) | async-done | bytes 540688 | tf_op jit(solution)/shard_map/reduce_scatter | solution.py:937
  268.9 2.1 ffn_cast.1
  272.4 2.0 finish.1
  (182 shorter events, 21.3 us)
Async XLA Ops:
  7.2 11.2 %copy-start = (bf16[256,1024]{1,0:T(8,128)(2,1)S(1)}, bf16[256,1024]{1,0:T(8,128)(2,1)}, u32[]{:S(2)}) copy-start(bf16[256,1024]{1,0:T(8,128)(2,1)} %refs_5_.3) | copy-start | bytes 1572868
  7.2 11.3 %copy-start.25 = (s32[1,1024]{1,0:T(1,128)S(1)}, s32[1,1024]{1,0:T(1,128)}, u32[]{:S(2)}) copy-start(s32[1,1024]{1,0:T(1,128)} %param.14) | copy-start | bytes 12292
  7.2 104.6 %all-gather.2.cloned.1.call-start = ((), (), s32[]{:S(2)}) async-start(), calls=%async_computation.1 | async-start | bytes 4866048 | tf_op jit(solution)/shard_map/all_gather | solution.py:868
  13.3 255.6 %reduce-scatter.2.cloned.1.call-start = ((), (), s32[]{:S(2)}) async-start(), calls=%async_computation.2 | async-start | bytes 4866048 | tf_op jit(solution)/shard_map/reduce_scatter | solution.py:937
  13.3 11.7 %collective-permute-start = (bf16[128,1152]{1,0:T(8,128)(2,1)}, bf16[128,1152]{1,0:T(8,128)(2,1)}, u32[]{:S(2)}, u32[]{:S(2)}) collective-permute-start(bf16[128,1152]{1,0:T(8,128)(2,1)} %pack.1), channel_id=1, source_target_pairs={{0,8},{8,16},{16,24},{24,28},{28,20},{20,12},{12,4},{4,0},{1,9},{9... | collective-permute-start | bytes 884744 | tf_op jit(solution)/shard_map/ppermute | solution.py:831
  16.4 9.2 %collective-permute-start.1 = (bf16[128,1152]{1,0:T(8,128)(2,1)}, bf16[128,1152]{1,0:T(8,128)(2,1)}, u32[]{:S(2)}, u32[]{:S(2)}) collective-permute-start(bf16[128,1152]{1,0:T(8,128)(2,1)} %pack.1), channel_id=1, source_target_pairs={{8,0},{16,8},{24,16},{28,24},{20,28},{12,20},{4,12},{0,4},{9,1},{1... | collective-permute-start | bytes 884744 | tf_op jit(solution)/shard_map/ppermute | solution.py:833
  16.4 15.2 %collective-permute-start.2 = (bf16[256,1024]{1,0:T(8,128)(2,1)}, bf16[256,1024]{1,0:T(8,128)(2,1)}, u32[]{:S(2)}, u32[]{:S(2)}) collective-permute-start(bf16[256,1024]{1,0:T(8,128)(2,1)} %x_ref.1), channel_id=1, source_target_pairs={{0,2},{1,3},{2,0},{3,1},{4,6},{5,7},{6,4},{7,5},{8,10},{9,11},{10,... | collective-permute-start | bytes 1572872 | tf_op jit(solution)/shard_map/ppermute | solution.py:780
  18.4 13.2 %collective-permute-start.3 = (bf16[256,1024]{1,0:T(8,128)(2,1)}, bf16[256,1024]{1,0:T(8,128)(2,1)}, u32[]{:S(2)}, u32[]{:S(2)}) collective-permute-start(bf16[256,1024]{1,0:T(8,128)(2,1)} %x_ref.1), channel_id=1, source_target_pairs={{0,1},{1,0},{2,3},{3,2},{4,5},{5,4},{6,7},{7,6},{8,9},{9,8},{10,11... | collective-permute-start | bytes 1572872 | tf_op jit(solution)/shard_map/ppermute | solution.py:780
  18.4 22.9 %collective-permute-start.7 = (bf16[256,1024]{1,0:T(8,128)(2,1)S(1)}, bf16[256,1024]{1,0:T(8,128)(2,1)S(1)}, u32[]{:S(2)}, u32[]{:S(2)}) collective-permute-start(bf16[256,1024]{1,0:T(8,128)(2,1)S(1)} %copy-done), channel_id=1, source_target_pairs={{0,2},{1,3},{2,0},{3,1},{4,6},{5,7},{6,4},{7,5},{8,10},{9,11},{10,... | collective-permute-start | bytes 1572872 | tf_op jit(solution)/shard_map/ppermute | solution.py:780
  25.0 28.8 %collective-permute-start.13 = (bf16[256,1024]{1,0:T(8,128)(2,1)S(1)}, bf16[256,1024]{1,0:T(8,128)(2,1)S(1)}, u32[]{:S(2)}, u32[]{:S(2)}) collective-permute-start(bf16[256,1024]{1,0:T(8,128)(2,1)S(1)} %copy-done), channel_id=1, source_target_pairs={{0,1},{1,0},{2,3},{3,2},{4,5},{5,4},{6,7},{7,6},{8,9},{9,8},{10,11... | collective-permute-start | bytes 1572872 | tf_op jit(solution)/shard_map/ppermute | solution.py:780
  31.6 19.2 %collective-permute-start.6 = (bf16[256,1024]{1,0:T(8,128)(2,1)}, bf16[256,1024]{1,0:T(8,128)(2,1)S(1)}, u32[]{:S(2)}, u32[]{:S(2)}) collective-permute-start(bf16[256,1024]{1,0:T(8,128)(2,1)} %collective-permute-done.2), channel_id=1, source_target_pairs={{0,1},{1,0},{2,3},{3,2},{4,5},{5,4},{6,7},{7,6},{8,9},{9,8},{10,11... | collective-permute-start | bytes 1572872 | tf_op jit(solution)/shard_map/ppermute | solution.py:780
  31.6 15.5 %collective-permute-start.4 = (bf16[128,1152]{1,0:T(8,128)(2,1)}, bf16[128,1152]{1,0:T(8,128)(2,1)S(1)}, u32[]{:S(2)}, u32[]{:S(2)}) collective-permute-start(bf16[128,1152]{1,0:T(8,128)(2,1)} %collective-permute-done), channel_id=1, source_target_pairs={{0,8},{8,16},{16,24},{24,28},{28,20},{20,12},{12,4},{4,0},{1,9},{9... | collective-permute-start | bytes 884744 | tf_op jit(solution)/shard_map/ppermute | solution.py:831
  33.6 17.2 %collective-permute-start.5 = (bf16[128,1152]{1,0:T(8,128)(2,1)}, bf16[128,1152]{1,0:T(8,128)(2,1)S(1)}, u32[]{:S(2)}, u32[]{:S(2)}) collective-permute-start(bf16[128,1152]{1,0:T(8,128)(2,1)} %collective-permute-done.1), channel_id=1, source_target_pairs={{8,0},{16,8},{24,16},{28,24},{20,28},{12,20},{4,12},{0,4},{9,1},{1... | collective-permute-start | bytes 884744 | tf_op jit(solution)/shard_map/ppermute | solution.py:833
  50.8 15.3 %collective-permute-start.10 = (bf16[256,1024]{1,0:T(8,128)(2,1)S(1)}, bf16[256,1024]{1,0:T(8,128)(2,1)S(1)}, u32[]{:S(2)}, u32[]{:S(2)}) collective-permute-start(bf16[256,1024]{1,0:T(8,128)(2,1)S(1)} %collective-permute-done.7.refs_4_.refs_6_), channel_id=1, source_target_pairs={{0,1},{1,0},{2,3},{3,2},{4,5},{5,4},{6,7},{7,6},{8,9},{9,8},{10,11... | collective-permute-start | bytes 1572872 | tf_op jit(solution)/shard_map/ppermute | solution.py:780
  50.8 10.9 %collective-permute-start.8 = (bf16[128,1152]{1,0:T(8,128)(2,1)S(1)}, bf16[128,1152]{1,0:T(8,128)(2,1)S(1)}, u32[]{:S(2)}, u32[]{:S(2)}) collective-permute-start(bf16[128,1152]{1,0:T(8,128)(2,1)S(1)} %collective-permute-done.4), channel_id=1, source_target_pairs={{0,8},{8,16},{16,24},{24,28},{28,20},{20,12},{12,4},{4,0},{1,9},{9... | collective-permute-start | bytes 884744 | tf_op jit(solution)/shard_map/ppermute | solution.py:831
  52.7 13.4 %collective-permute-start.9 = (bf16[128,1152]{1,0:T(8,128)(2,1)S(1)}, bf16[128,1152]{1,0:T(8,128)(2,1)S(1)}, u32[]{:S(2)}, u32[]{:S(2)}) collective-permute-start(bf16[128,1152]{1,0:T(8,128)(2,1)S(1)} %collective-permute-done.5), channel_id=1, source_target_pairs={{8,0},{16,8},{24,16},{28,24},{20,28},{12,20},{4,12},{0,4},{9,1},{1... | collective-permute-start | bytes 884744 | tf_op jit(solution)/shard_map/ppermute | solution.py:833
  53.9 12.2 %copy-start.11 = (bf16[4,256,1024]{2,1,0:T(8,128)(2,1)}, bf16[4,256,1024]{2,1,0:T(8,128)(2,1)S(1)}, u32[]{:S(2)}) copy-start(bf16[4,256,1024]{2,1,0:T(8,128)(2,1)S(1)} %bitcast_dynamic-update-slice_fusion.1) | copy-start | bytes 6291460
  66.9 8.6 %collective-permute-start.11 = (bf16[64,1152]{1,0:T(8,128)(2,1)}, bf16[64,1152]{1,0:T(8,128)(2,1)}, u32[]{:S(2)}, u32[]{:S(2)}) collective-permute-start(bf16[64,1152]{1,0:T(8,128)(2,1)} %slice.48), channel_id=1, source_target_pairs={{0,8},{8,16},{16,24},{24,28},{28,20},{20,12},{12,4},{4,0},{1,9},{9... | collective-permute-start | bytes 442376 | tf_op jit(solution)/shard_map/ppermute | solution.py:828
  67.5 12.0 %collective-permute-start.12 = (bf16[64,1152]{1,0:T(8,128)(2,1)}, bf16[64,1152]{1,0:T(8,128)(2,1)S(1)}, u32[]{:S(2)}, u32[]{:S(2)}) collective-permute-start(bf16[64,1152]{1,0:T(8,128)(2,1)} %slice.49), channel_id=1, source_target_pairs={{8,0},{16,8},{24,16},{28,24},{20,28},{12,20},{4,12},{0,4},{9,1},{1... | collective-permute-start | bytes 442376 | tf_op jit(solution)/shard_map/ppermute | solution.py:829
  79.6 14.7 %copy-start.19 = (bf16[1024,256]{1,0:T(8,128)(2,1)}, bf16[1024,256]{1,0:T(8,128)(2,1)S(1)}, u32[]{:S(2)}) copy-start(bf16[1024,256]{1,0:T(8,128)(2,1)S(1)} %slice.50.refs_4_.out_ref) | copy-start | bytes 1572868
  79.6 14.7 %collective-permute-start.14 = (bf16[1024,256]{1,0:T(8,128)(2,1)S(1)}, bf16[1024,256]{1,0:T(8,128)(2,1)}, u32[]{:S(2)}, u32[]{:S(2)}) collective-permute-start(bf16[1024,256]{1,0:T(8,128)(2,1)S(1)} %slice.50.refs_4_.out_ref), channel_id=1, source_target_pairs={{0,2},{1,3},{2,0},{3,1},{4,6},{5,7},{6,4},{7,5},{8,10},{9,11},{10,... | collective-permute-start | bytes 1572872 | tf_op jit(solution)/shard_map/ppermute | solution.py:780
  81.0 13.3 %collective-permute-start.15 = (bf16[1024,256]{1,0:T(8,128)(2,1)S(1)}, bf16[1024,256]{1,0:T(8,128)(2,1)}, u32[]{:S(2)}, u32[]{:S(2)}) collective-permute-start(bf16[1024,256]{1,0:T(8,128)(2,1)S(1)} %slice.50.refs_4_.out_ref), channel_id=1, source_target_pairs={{0,1},{1,0},{2,3},{3,2},{4,5},{5,4},{6,7},{7,6},{8,9},{9,8},{10,11... | collective-permute-start | bytes 1572872 | tf_op jit(solution)/shard_map/ppermute | solution.py:780
  94.3 15.9 %collective-permute-start.16 = (bf16[512,256]{1,0:T(8,128)(2,1)}, bf16[512,256]{1,0:T(8,128)(2,1)S(1)}, u32[]{:S(2)}, u32[]{:S(2)}) collective-permute-start(bf16[512,256]{1,0:T(8,128)(2,1)} %get-tuple-element.175.refs_0_), channel_id=1, source_target_pairs={{0,2},{1,3},{2,0},{3,1},{4,6},{5,7},{6,4},{7,5},{8,10},{9,11},{10,... | collective-permute-start | bytes 786440 | tf_op jit(solution)/shard_map/ppermute | solution.py:780
  95.7 14.5 %collective-permute-start.17 = (bf16[512,256]{1,0:T(8,128)(2,1)}, bf16[512,256]{1,0:T(8,128)(2,1)S(1)}, u32[]{:S(2)}, u32[]{:S(2)}) collective-permute-start(bf16[512,256]{1,0:T(8,128)(2,1)} %get-tuple-element.175.refs_0_), channel_id=1, source_target_pairs={{0,1},{1,0},{2,3},{3,2},{4,5},{5,4},{6,7},{7,6},{8,9},{9,8},{10,11... | collective-permute-start | bytes 786440 | tf_op jit(solution)/shard_map/ppermute | solution.py:780
  95.7 14.6 %collective-permute-start.18 = (bf16[1024,256]{1,0:T(8,128)(2,1)}, bf16[1024,256]{1,0:T(8,128)(2,1)S(1)}, u32[]{:S(2)}, u32[]{:S(2)}) collective-permute-start(bf16[1024,256]{1,0:T(8,128)(2,1)} %collective-permute-done.14.refs_5_), channel_id=1, source_target_pairs={{0,1},{1,0},{2,3},{3,2},{4,5},{5,4},{6,7},{7,6},{8,9},{9,8},{10,11... | collective-permute-start | bytes 1572872 | tf_op jit(solution)/shard_map/ppermute | solution.py:780
  110.2 1.6 collective-permute-start.21
  110.3 13.3 %collective-permute-start.19 = (bf16[512,256]{1,0:T(8,128)(2,1)}, bf16[512,256]{1,0:T(8,128)(2,1)S(1)}, u32[]{:S(2)}, u32[]{:S(2)}) collective-permute-start(bf16[512,256]{1,0:T(8,128)(2,1)} %get-tuple-element.193.refs_0_), channel_id=1, source_target_pairs={{0,2},{1,3},{2,0},{3,1},{4,6},{5,7},{6,4},{7,5},{8,10},{9,11},{10,... | collective-permute-start | bytes 786440 | tf_op jit(solution)/shard_map/ppermute | solution.py:780
  111.3 12.4 %collective-permute-start.20 = (bf16[512,256]{1,0:T(8,128)(2,1)}, bf16[512,256]{1,0:T(8,128)(2,1)S(1)}, u32[]{:S(2)}, u32[]{:S(2)}) collective-permute-start(bf16[512,256]{1,0:T(8,128)(2,1)} %get-tuple-element.193.refs_0_), channel_id=1, source_target_pairs={{0,1},{1,0},{2,3},{3,2},{4,5},{5,4},{6,7},{7,6},{8,9},{9,8},{10,11... | collective-permute-start | bytes 786440 | tf_op jit(solution)/shard_map/ppermute | solution.py:780
  123.7 2.2 collective-permute-start.23
  123.9 3.4 %collective-permute-start.22 = (bf16[512,256]{1,0:T(8,128)(2,1)S(1)}, bf16[512,256]{1,0:T(8,128)(2,1)S(1)}, u32[]{:S(2)}, u32[]{:S(2)}) collective-permute-start(bf16[512,256]{1,0:T(8,128)(2,1)S(1)} %collective-permute-done.19.refs_1_), channel_id=1, source_target_pairs={{0,1},{1,0},{2,3},{3,2},{4,5},{5,4},{6,7},{7,6},{8,9},{9,8},{10,11... | collective-permute-start | bytes 786440 | tf_op jit(solution)/shard_map/ppermute | solution.py:780
  127.2 14.1 %copy-start.1 = (f32[256,1024]{1,0:T(8,128)S(1)}, f32[256,1024]{1,0:T(8,128)}, u32[]{:S(2)}) copy-start(f32[256,1024]{1,0:T(8,128)} %get-tuple-element.210.refs_2_.mid0) | copy-start | bytes 3145732
  127.3 14.1 %copy-start.7 = (f32[1,1024]{1,0:T(1,128)S(1)}, f32[1,1024]{1,0:T(1,128)}, u32[]{:S(2)}) copy-start(f32[1,1024]{1,0:T(1,128)} %refs_7_.5) | copy-start | bytes 12292
  127.3 14.0 %collective-permute-start.24 = (bf16[256,1024]{1,0:T(8,128)(2,1)S(1)}, bf16[256,1024]{1,0:T(8,128)(2,1)S(1)}, u32[]{:S(2)}, u32[]{:S(2)}) collective-permute-start(bf16[256,1024]{1,0:T(8,128)(2,1)S(1)} %add_convert_fusion.refs_0_), channel_id=1, source_target_pairs={{0,2},{1,3},{2,0},{3,1},{4,6},{5,7},{6,4},{7,5},{8,10},{9,11},{10,... | collective-permute-start | bytes 1572872 | tf_op jit(solution)/shard_map/ppermute | solution.py:780
  141.3 2.1 collective-permute-start.25
  142.9 11.1 %copy-start.8 = (bf16[256,1024]{1,0:T(8,128)(2,1)}, bf16[256,1024]{1,0:T(8,128)(2,1)S(1)}, u32[]{:S(2)}) copy-start(bf16[256,1024]{1,0:T(8,128)(2,1)S(1)} %get-tuple-element.217.ga0_ref) | copy-start | bytes 1572868
  143.6 10.4 %collective-permute-start.27 = (bf16[256,1024]{1,0:T(8,128)(2,1)S(1)}, bf16[256,1024]{1,0:T(8,128)(2,1)S(1)}, u32[]{:S(2)}, u32[]{:S(2)}) collective-permute-start(bf16[256,1024]{1,0:T(8,128)(2,1)S(1)} %get-tuple-element.217.ga0_ref), channel_id=1, source_target_pairs={{0,1},{1,0},{2,3},{3,2},{4,5},{5,4},{6,7},{7,6},{8,9},{9,8},{10,11... | collective-permute-start | bytes 1572872 | tf_op jit(solution)/shard_map/ppermute | solution.py:780
  143.8 10.1 %collective-permute-start.26 = (bf16[128,1024]{1,0:T(8,128)(2,1)S(1)}, bf16[128,1024]{1,0:T(8,128)(2,1)S(1)}, u32[]{:S(2)}, u32[]{:S(2)}) collective-permute-start(bf16[128,1024]{1,0:T(8,128)(2,1)S(1)} %get-tuple-element.215.refs_7_.refs_0_), channel_id=1, source_target_pairs={{0,2},{1,3},{2,0},{3,1},{4,6},{5,7},{6,4},{7,5},{8,10},{9,11},{10,... | collective-permute-start | bytes 786440 | tf_op jit(solution)/shard_map/ppermute | solution.py:780
  154.8 8.4 %copy-start.2 = (f32[256,1024]{1,0:T(8,128)S(1)}, f32[256,1024]{1,0:T(8,128)}, u32[]{:S(2)}) copy-start(f32[256,1024]{1,0:T(8,128)} %get-tuple-element.228.refs_4_.mid1) | copy-start | bytes 3145732
  154.8 8.4 %copy-start.6 = (bf16[128,1024]{1,0:T(8,128)(2,1)S(1)}, bf16[128,1024]{1,0:T(8,128)(2,1)}, u32[]{:S(2)}) copy-start(bf16[128,1024]{1,0:T(8,128)(2,1)} %copy-done.5) | copy-start | bytes 786436
  154.8 8.4 %collective-permute-start.28 = (bf16[128,1024]{1,0:T(8,128)(2,1)S(1)}, bf16[128,1024]{1,0:T(8,128)(2,1)S(1)}, u32[]{:S(2)}, u32[]{:S(2)}) collective-permute-start(bf16[128,1024]{1,0:T(8,128)(2,1)S(1)} %get-tuple-element.216.refs_1_), channel_id=1, source_target_pairs={{0,2},{1,3},{2,0},{3,1},{4,6},{5,7},{6,4},{7,5},{8,10},{9,11},{10,... | collective-permute-start | bytes 786440 | tf_op jit(solution)/shard_map/ppermute | solution.py:780
  164.7 2.6 collective-permute-start.29
  164.8 38.1 %collective-permute-start.30 = (bf16[2,256,1024]{2,1,0:T(8,128)(2,1)}, bf16[2,256,1024]{2,1,0:T(8,128)(2,1)S(1)}, u32[]{:S(2)}, u32[]{:S(2)}) collective-permute-start(bf16[2,256,1024]{2,1,0:T(8,128)(2,1)} %get-tuple-element.257), channel_id=1, source_target_pairs={{0,1},{1,0},{2,3},{3,2},{4,5},{5,4},{6,7},{7,6},{8,9},{9,8},{10,11... | collective-permute-start | bytes 3145736 | tf_op jit(solution)/shard_map/ppermute | solution.py:780
  202.8 9.2 %copy-start.12 = (bf16[2,256,1024]{2,1,0:T(8,128)(2,1)}, bf16[2,256,1024]{2,1,0:T(8,128)(2,1)S(1)}, u32[]{:S(2)}) copy-start(bf16[2,256,1024]{2,1,0:T(8,128)(2,1)S(1)} %collective-permute-done.30.got) | copy-start | bytes 3145732
  202.8 8.4 %collective-permute-start.31 = (bf16[2,256,1024]{2,1,0:T(8,128)(2,1)}, bf16[2,256,1024]{2,1,0:T(8,128)(2,1)S(1)}, u32[]{:S(2)}, u32[]{:S(2)}) collective-permute-start(bf16[2,256,1024]{2,1,0:T(8,128)(2,1)} %get-tuple-element.259), channel_id=1, source_target_pairs={{0,1},{1,0},{2,3},{3,2},{4,5},{5,4},{6,7},{7,6},{8,9},{9,8},{10,11... | collective-permute-start | bytes 3145736 | tf_op jit(solution)/shard_map/ppermute | solution.py:780
  203.0 22.3 %collective-permute-start.32 = (bf16[4,128,512]{2,1,0:T(8,128)(2,1)}, bf16[4,128,512]{2,1,0:T(8,128)(2,1)S(1)}, u32[]{:S(2)}, u32[]{:S(2)}) collective-permute-start(bf16[4,128,512]{2,1,0:T(8,128)(2,1)} %get-tuple-element.263), channel_id=1, source_target_pairs={{0,4},{4,0},{8,12},{12,8},{16,20},{20,16},{24,28},{28,24},{1,5},{5... | collective-permute-start | bytes 1572872 | tf_op jit(solution)/shard_map/ppermute | solution.py:780
  205.3 20.1 %collective-permute-start.33 = (bf16[4,128,512]{2,1,0:T(8,128)(2,1)}, bf16[4,128,512]{2,1,0:T(8,128)(2,1)S(1)}, u32[]{:S(2)}, u32[]{:S(2)}) collective-permute-start(bf16[4,128,512]{2,1,0:T(8,128)(2,1)} %get-tuple-element.264), channel_id=1, source_target_pairs={{0,8},{4,12},{8,0},{12,4},{16,24},{20,28},{24,16},{28,20},{1,9},{5... | collective-permute-start | bytes 1572872 | tf_op jit(solution)/shard_map/ppermute | solution.py:780
  210.2 8.4 %collective-permute-start.34 = (f32[8,1024]{1,0:T(8,128)}, f32[8,1024]{1,0:T(8,128)S(1)}, u32[]{:S(2)}, u32[]{:S(2)}) collective-permute-start(f32[8,1024]{1,0:T(8,128)} %get-tuple-element.260.wait_for), channel_id=1, source_target_pairs={{0,1},{1,0},{2,3},{3,2},{4,5},{5,4},{6,7},{7,6},{8,9},{9,8},{10,11... | collective-permute-start | bytes 98312 | tf_op jit(solution)/shard_map/ppermute | solution.py:780
  210.2 8.4 %collective-permute-start.35 = (f32[8,1024]{1,0:T(8,128)}, f32[8,1024]{1,0:T(8,128)S(1)}, u32[]{:S(2)}, u32[]{:S(2)}) collective-permute-start(f32[8,1024]{1,0:T(8,128)} %get-tuple-element.260.wait_for), channel_id=1, source_target_pairs={{0,2},{1,3},{2,0},{3,1},{4,6},{5,7},{6,4},{7,5},{8,10},{9,11},{10,... | collective-permute-start | bytes 98312 | tf_op jit(solution)/shard_map/ppermute | solution.py:780
  211.2 7.3 %collective-permute-start.36 = (f32[8,1024]{1,0:T(8,128)}, f32[8,1024]{1,0:T(8,128)S(1)}, u32[]{:S(2)}, u32[]{:S(2)}) collective-permute-start(f32[8,1024]{1,0:T(8,128)} %get-tuple-element.260.wait_for), channel_id=1, source_target_pairs={{0,3},{1,2},{2,1},{3,0},{4,7},{5,6},{6,5},{7,4},{8,11},{9,10},{10,... | collective-permute-start | bytes 98312 | tf_op jit(solution)/shard_map/ppermute | solution.py:780
  215.2 11.4 %copy-start.36 = (bf16[256,1024]{1,0:T(8,128)(2,1)S(1)}, bf16[256,1024]{1,0:T(8,128)(2,1)}, u32[]{:S(2)}) copy-start(bf16[256,1024]{1,0:T(8,128)(2,1)} %get-tuple-element.282) | copy-start | bytes 1572868
  215.2 19.9 %copy-start.26 = (f32[8,1024]{1,0:T(8,128)S(1)}, f32[8,1024]{1,0:T(8,128)}, u32[]{:S(2)}) copy-start(f32[8,1024]{1,0:T(8,128)} %get-tuple-element.260.wait_for) | copy-start | bytes 98308
  215.2 19.9 %copy-start.33 = (f32[8,1024]{1,0:T(8,128)S(1)}, f32[8,1024]{1,0:T(8,128)}, u32[]{:S(2)}) copy-start(f32[8,1024]{1,0:T(8,128)} %get-tuple-element.275) | copy-start | bytes 98308
  225.4 22.6 %collective-permute-start.40 = (bf16[256,1024]{1,0:T(8,128)(2,1)}, bf16[256,1024]{1,0:T(8,128)(2,1)S(1)}, u32[]{:S(2)}, u32[]{:S(2)}) collective-permute-start(bf16[256,1024]{1,0:T(8,128)(2,1)} %get-tuple-element.279), channel_id=1, source_target_pairs={{0,2},{1,3},{2,0},{3,1},{4,6},{5,7},{6,4},{7,5},{8,10},{9,11},{10,... | collective-permute-start | bytes 1572872 | tf_op jit(solution)/shard_map/ppermute | solution.py:780
  226.7 32.2 %collective-permute-start.41 = (bf16[256,1024]{1,0:T(8,128)(2,1)S(1)}, bf16[256,1024]{1,0:T(8,128)(2,1)S(1)}, u32[]{:S(2)}, u32[]{:S(2)}) collective-permute-start(bf16[256,1024]{1,0:T(8,128)(2,1)S(1)} %copy-done.36), channel_id=1, source_target_pairs={{0,2},{1,3},{2,0},{3,1},{4,6},{5,7},{6,4},{7,5},{8,10},{9,11},{10,... | collective-permute-start | bytes 1572872 | tf_op jit(solution)/shard_map/ppermute | solution.py:780
  230.1 17.8 %collective-permute-start.37 = (bf16[2,128,512]{2,1,0:T(8,128)(2,1)}, bf16[2,128,512]{2,1,0:T(8,128)(2,1)S(1)}, u32[]{:S(2)}, u32[]{:S(2)}) collective-permute-start(bf16[2,128,512]{2,1,0:T(8,128)(2,1)} %get-tuple-element.273), channel_id=1, source_target_pairs={{0,8},{4,12},{8,0},{12,4},{16,24},{20,28},{24,16},{28,20},{1,9},{5... | collective-permute-start | bytes 786440 | tf_op jit(solution)/shard_map/ppermute | solution.py:780
  233.4 14.6 %collective-permute-start.38 = (bf16[2,128,512]{2,1,0:T(8,128)(2,1)}, bf16[2,128,512]{2,1,0:T(8,128)(2,1)S(1)}, u32[]{:S(2)}, u32[]{:S(2)}) collective-permute-start(bf16[2,128,512]{2,1,0:T(8,128)(2,1)} %get-tuple-element.274), channel_id=1, source_target_pairs={{0,4},{4,0},{8,12},{12,8},{16,20},{20,16},{24,28},{28,24},{1,5},{5... | collective-permute-start | bytes 786440 | tf_op jit(solution)/shard_map/ppermute | solution.py:780
  235.1 12.1 %collective-permute-start.39 = (f32[8,1024]{1,0:T(8,128)S(1)}, f32[8,1024]{1,0:T(8,128)S(1)}, u32[]{:S(2)}, u32[]{:S(2)}) collective-permute-start(f32[8,1024]{1,0:T(8,128)S(1)} %add_add_fusion), channel_id=1, source_target_pairs={{0,4},{4,0},{8,12},{12,8},{16,20},{20,16},{24,28},{28,24},{1,5},{5... | collective-permute-start | bytes 98312 | tf_op jit(solution)/shard_map/ppermute | solution.py:780
  247.3 24.5 %copy-start.27 = (f32[8,1024]{1,0:T(8,128)}, f32[8,1024]{1,0:T(8,128)S(1)}, u32[]{:S(2)}) copy-start(f32[8,1024]{1,0:T(8,128)S(1)} %add.201.s_ref) | copy-start | bytes 98308
  248.0 10.9 %copy-start.17 = (bf16[256,1024]{1,0:T(8,128)(2,1)}, bf16[256,1024]{1,0:T(8,128)(2,1)S(1)}, u32[]{:S(2)}) copy-start(bf16[256,1024]{1,0:T(8,128)(2,1)S(1)} %collective-permute-done.40.na_y) | copy-start | bytes 1572868
  250.8 20.9 %collective-permute-start.42 = (bf16[1,128,512]{2,1,0:T(8,128)(2,1)}, bf16[1,128,512]{2,1,0:T(8,128)(2,1)S(1)}, u32[]{:S(2)}, u32[]{:S(2)}) collective-permute-start(bf16[1,128,512]{2,1,0:T(8,128)(2,1)} %get-tuple-element.290), channel_id=1, source_target_pairs={{0,16},{4,20},{8,24},{12,28},{16,0},{20,4},{24,8},{28,12},{1,17},{... | collective-permute-start | bytes 393224 | tf_op jit(solution)/shard_map/ppermute | solution.py:780
  253.0 18.7 %collective-permute-start.43 = (bf16[1,128,512]{2,1,0:T(8,128)(2,1)}, bf16[1,128,512]{2,1,0:T(8,128)(2,1)S(1)}, u32[]{:S(2)}, u32[]{:S(2)}) collective-permute-start(bf16[1,128,512]{2,1,0:T(8,128)(2,1)} %get-tuple-element.292), channel_id=1, source_target_pairs={{0,16},{4,20},{8,24},{12,28},{16,0},{20,4},{24,8},{28,12},{1,17},{... | collective-permute-start | bytes 393224 | tf_op jit(solution)/shard_map/ppermute | solution.py:780
  253.7 17.3 %collective-permute-start.44 = (f32[8,1024]{1,0:T(8,128)S(1)}, f32[8,1024]{1,0:T(8,128)S(1)}, u32[]{:S(2)}, u32[]{:S(2)}) collective-permute-start(f32[8,1024]{1,0:T(8,128)S(1)} %add.201.s_ref), channel_id=1, source_target_pairs={{0,8},{4,12},{8,0},{12,4},{16,24},{20,28},{24,16},{28,20},{1,9},{5... | collective-permute-start | bytes 98312 | tf_op jit(solution)/shard_map/ppermute | solution.py:780
  256.0 15.7 %collective-permute-start.45 = (f32[8,1024]{1,0:T(8,128)S(1)}, f32[8,1024]{1,0:T(8,128)S(1)}, u32[]{:S(2)}, u32[]{:S(2)}) collective-permute-start(f32[8,1024]{1,0:T(8,128)S(1)} %add.201.s_ref), channel_id=1, source_target_pairs={{0,16},{4,20},{8,24},{12,28},{16,0},{20,4},{24,8},{28,12},{1,17},{... | collective-permute-start | bytes 98312 | tf_op jit(solution)/shard_map/ppermute | solution.py:780
  258.9 12.8 %collective-permute-start.46 = (f32[8,1024]{1,0:T(8,128)S(1)}, f32[8,1024]{1,0:T(8,128)S(1)}, u32[]{:S(2)}, u32[]{:S(2)}) collective-permute-start(f32[8,1024]{1,0:T(8,128)S(1)} %add.201.s_ref), channel_id=1, source_target_pairs={{0,24},{4,28},{8,16},{12,20},{16,8},{20,12},{24,0},{28,4},{1,25},{... | collective-permute-start | bytes 98312 | tf_op jit(solution)/shard_map/ppermute | solution.py:780
  (30 other events, 52.5 us)
Sparse Core Ops, SparseCore 0:
  13.4 90.2 all-gather.1
  154.9 113.9 reduce-scatter.1

commit v6 on v5

--- a/solution.py
+++ b/solution.py
@@ -869,24 +869,24 @@
     seg = segment_ids[0]
     cols = columns(seg, pad_mask[0])
     segr = seg.astype(F32)[None]
-    ring.a, ring.b, x_y, x_c = fence(ring.a, ring.b, x_y, x_c)
+    ring.a, ring.b, x_c = fence(ring.a, ring.b, x_c)
+    ring.keep()
+    ring.step()
+    c_y = y_hop(cotangent)
+    c_c = core_hop(cotangent)
+    ring.a, ring.b, x_y, c_y = fence(ring.a, ring.b, x_y, c_y)
     ring.keep()
     ring.step()
     x_cy = core_hop(x_y)
-    c_y = y_hop(cotangent)
-    c_c = core_hop(cotangent)
-    ring.a, ring.b, x_cy, c_y = fence(ring.a, ring.b, x_cy, c_y)
+    c_cy = core_hop(c_y)
+    ring.a, ring.b, cols, x_cy, c_cy = fence(ring.a, ring.b, cols, x_cy, c_cy)
     ring.keep()
-    ring.step()
-    c_cy = core_hop(c_y)
     x_full = in_order(layer_input, x_y, (x_c, x_cy))
-    ring.a, ring.b, x_full, cols, c_cy = fence(ring.a, ring.b, x_full, cols, c_cy)
-    ring.keep()
     g_f = in_order(cotangent, c_y, (c_c, c_cy))
     while 2 * ring.k < n_f:
         ring.step()
         ring.keep()
-    wide, g_f = fence(ring.full, g_f)
+    wide, x_full, g_f = fence(ring.full, x_full, g_f)
 
     out_own = wide[:, 3 * width + HEAD:]
     tail = state = None

time: 285 us -> 275 us (0.965)
  waiting for transfers between devices: 65.3 us -> 55 us
  local copies, waits for them, and re-layouts: 29.6 us -> 32.7 us
  starting transfers between devices: 45.2 us -> 42.1 us
    ppermute x3, waiting for transfers between devices: 13.7 us -> 1.34 us  [step(): self.a = lax.ppermute(self.a, 'fsdp', self.right)]
    ppermute x39, waiting for transfers between devices: 36 us -> 43.3 us  [hop(): return lax.ppermute(value, axis, [(i, i ^ bit) for i in range(n)])]
    reduce_scatter x1, waiting for transfers between devices: 4.25 us -> 0.01 us  [on_device(): d_ffn = lax.psum_scatter(blocks, 'fsdp', scatter_dimension=0, tiled=False)]
    dynamic_update_slice x8, local copies, waits for them, and re-layouts: 8.58 us -> 12 us  [in_order(): lax.dynamic_update_slice(full, block[None], (me ^ k,) + (0,) * own.ndim)]
    ppermute x39, starting transfers between devices: 35.8 us -> 32.6 us  [hop(): return lax.ppermute(value, axis, [(i, i ^ bit) for i in range(n)])]
  transfers between devices with their start and end apart: 49 -> 49, of which waited for: 19 -> 16; matrix products, arithmetic and copies ran while one was open for 8% -> 10% of each run, Pallas kernels for 42% -> 44%
where the time goes in v6:
time: 275 us; the launch traced here: 271 us
  Pallas kernels  122 us (44%)
  waiting for transfers between devices  55 us (20%)
  starting transfers between devices  42.1 us (15%)
  local copies, waits for them, and re-layouts  32.7 us (12%)
  between operations  14.9 us (5%)
  other arithmetic  4.04 us (1%)
    ppermute x39, waiting for transfers between devices, hop(): return lax.ppermute(value, axis, [(i, i ^ bit) for i in range(n)])  43.3 us
    pallas_call x1, Pallas kernels, mixer_bwd(): pl.pallas_call(functools.partial(bwd_kernel, heads, cb, n_f, shard), grid...  34.6 us
    ppermute x39, starting transfers between devices, hop(): return lax.ppermute(value, axis, [(i, i ^ bit) for i in range(n)])  32.6 us
    pallas_call x2, Pallas kernels, mixer_fwd(): pl.pallas_call(functools.partial(fwd_call_kernel, heads, cb, base, len(ol...  27.3 us
    pallas_call x2, Pallas kernels, ffn(): pl.pallas_call(functools.partial(ffn_kernel, ff), grid=(1,), in_specs=[wh...  22.5 us
    dynamic_update_slice x8, local copies, waits for them, and re-layouts, in_order(): lax.dynamic_update_slice(full, block[None], (me ^ k,) + (0,) * own.ndim)  12 us
    pallas_call x1, Pallas kernels, ffn_grads(): pl.pallas_call(functools.partial(ffn_grads_kernel, ff, len(pieces)), grid...  9.19 us
    unnamed x91, local copies, waits for them, and re-layouts  7.32 us
  transfers between devices with their start and end apart: 49, of which 16 were waited for; matrix products, arithmetic and copies ran while one was open for 10% of the time, Pallas kernels for 44%

profile of v6, /device:TPU:0, one launch (start us, length us, event | category | flops | bytes accessed | tf_op | source)
XLA Modules:
  0.0 271.2 jit_solution(6673348783381931094)
XLA Ops:
  7.2 1.4 copy.45
  8.7 1.8 pack.1
  10.4 1.0 slice_bitcast_fusion.1
  11.5 1.8 pad_maximum_fusion
  13.3 3.1 %collective-permute-start = (bf16[128,1152]{1,0:T(8,128)(2,1)}, bf16[128,1152]{1,0:T(8,128)(2,1)}, u32[]{:S(2)}, u32[]{:S(2)}) collective-permute-start(bf16[128,1152]{1,0:T(8,128)(2,1)} %pack.1), channel_id=1, source_target_pairs={{0,8},{8,16},{16,24},{24,28},{28,20},{20,12},{12,4},{4,0},{1,9},{9... | collective-permute-start | bytes 884744 | tf_op jit(solution)/shard_map/ppermute | solution.py:831
  16.4 2.0 collective-permute-start.5
  19.3 1.0 constant_dynamic-update-slice_fusion.8
  20.3 1.7 broadcast.20.clone
  21.9 1.9 bitcast_dynamic-update-slice_fusion.7
  23.8 1.6 broadcast.20.clone.1
  27.4 1.9 collective-permute-start.3
  29.4 1.0 constant_dynamic-update-slice_fusion.7
  30.4 1.0 constant_dynamic-update-slice_fusion.6
  31.5 10.9 %collective-permute-done.6.refs_4_.refs_6_ = bf16[256,1024]{1,0:T(8,128)(2,1)S(1)} collective-permute-done((bf16[256,1024]{1,0:T(8,128)(2,1)S(1)}, bf16[256,1024]{1,0:T(8,128)(2,1)S(1)}, u32[]{:S(2)}, u32[]{:S(2)}) %collective-permute-start.6) | collective-permute-done | bytes 524320 | tf_op jit(solution)/shard_map/ppermute | solution.py:780
  42.4 4.5 %collective-permute-done.4 = bf16[128,1152]{1,0:T(8,128)(2,1)S(1)} collective-permute-done((bf16[128,1152]{1,0:T(8,128)(2,1)}, bf16[128,1152]{1,0:T(8,128)(2,1)S(1)}, u32[]{:S(2)}, u32[]{:S(2)}) %collective-permute-start.4) | collective-permute-done | bytes 294944 | tf_op jit(solution)/shard_map/ppermute | solution.py:833
  47.4 2.0 collective-permute-start.8
  49.4 1.9 bitcast_dynamic-update-slice_fusion.6
  52.2 1.9 bitcast_dynamic-update-slice_fusion.5
  55.0 1.3 collective-permute-done.7
  56.3 2.8 %collective-permute-done.8 = bf16[128,1152]{1,0:T(8,128)(2,1)S(1)} collective-permute-done((bf16[128,1152]{1,0:T(8,128)(2,1)S(1)}, bf16[128,1152]{1,0:T(8,128)(2,1)S(1)}, u32[]{:S(2)}, u32[]{:S(2)}) %collective-permute-start.8) | collective-permute-done | bytes 294944 | tf_op jit(solution)/shard_map/ppermute | solution.py:833
  59.9 1.2 collective-permute-start.11
  61.8 1.0 collective-permute-start.12
  62.8 1.8 copy.46.refs_4_.cols_ref
  64.6 1.0 constant_dynamic-update-slice_fusion.3
  65.7 1.9 bitcast_dynamic-update-slice_fusion.4
  67.6 1.9 bitcast_dynamic-update-slice_fusion
  70.4 3.1 %collective-permute-done.12 = bf16[64,1152]{1,0:T(8,128)(2,1)S(1)} collective-permute-done((bf16[64,1152]{1,0:T(8,128)(2,1)}, bf16[64,1152]{1,0:T(8,128)(2,1)S(1)}, u32[]{:S(2)}, u32[]{:S(2)}) %collective-permute-start.12) | collective-permute-done | bytes 147488 | tf_op jit(solution)/shard_map/ppermute | solution.py:829
  73.6 1.3 collective-permute-start.14
  75.0 13.3 %mixer_fwd.2 = (bf16[512,256]{1,0:T(8,128)(2,1)}, bf16[1024,256]{1,0:T(8,128)(2,1)}, bf16[1024,1024]{1,0:T(8,128)(2,1)}, f32[1024,896]{1,0:T(8,128)}, f32[1024,7...) custom-call(s32[1024]{0:T(1024)} %bitcast.63, ...), custom_call_target="tpu_custom_call" | custom-call | flops 10000000000 | bytes 10000000 | tf_op jit(solution)/shard_map/mixer_fwd/pallas_call | solution.py:354
  88.3 1.3 collective-permute-start.16
  90.1 14.0 %mixer_fwd.3 = (bf16[512,256]{1,0:T(8,128)(2,1)}, bf16[1024,256]{1,0:T(8,128)(2,1)}, bf16[1024,1024]{1,0:T(8,128)(2,1)}, f32[1024,896]{1,0:T(8,128)}, f32[1024,7...) custom-call(s32[1024]{0:T(1024)} %bitcast.64, ...), custom_call_target="tpu_custom_call", output_to_operand_aliasing={{1}: (10, {}), {2}: (11, {}), {3}: (12, {}), {4}: (13, {}),... | custom-call | flops 10000000000 | bytes 10000000 | tf_op jit(solution)/shard_map/mixer_fwd/pallas_call | solution.py:354
  104.2 1.0 collective-permute-start.19
  106.5 11.1 %ffn.2 = (f32[256,1024]{1,0:T(8,128)}, bf16[512,1024]{1,0:T(8,128)(2,1)}, bf16[704,512]{1,0:T(8,128)(2,1)}, bf16[1408,512]{1,0:T(8,128)(2,1)}, f32[256,1024]{1,0...) custom-call(bf16[512,256]{1,0:T(8,128)(2,1)} %get-tuple-element.175.refs_0_, bf16[512,256]{1,0:T(8,128)(2,1)} %copy-done.39, ...), custom_call_target="tpu_custom_call" | custom-call | flops 10000000000 | bytes 10000000 | tf_op jit(solution)/shard_map/ffn/pallas_call | solution.py:511
  118.2 1.6 collective-permute-done.23
  119.8 1.4 add_convert_fusion.refs_0_
  122.1 11.4 %ffn.3 = (f32[256,1024]{1,0:T(8,128)}, bf16[512,1024]{1,0:T(8,128)(2,1)}, bf16[704,512]{1,0:T(8,128)(2,1)}, bf16[1408,512]{1,0:T(8,128)(2,1)}, f32[256,1024]{1,0...) custom-call(bf16[512,256]{1,0:T(8,128)(2,1)} %get-tuple-element.193.refs_0_, bf16[512,256]{1,0:T(8,128)(2,1)} %copy-done.41, ...), custom_call_target="tpu_custom_call" | custom-call | flops 10000000000 | bytes 10000000 | tf_op jit(solution)/shard_map/ffn/pallas_call | solution.py:511
  133.5 1.8 collective-permute-done.24.refs_1_
  135.9 1.0 copy-done.3
  137.7 1.0 collective-permute-start.26
  138.7 9.2 %ffn_grads.1.refs_3_.wait_for = bf16[8,2112,128]{2,1,0:T(8,128)(2,1)} custom-call(bf16[1408,512]{1,0:T(8,128)(2,1)} %get-tuple-element.218.refs_0_, bf16[704,512]{1,0:T(8,128)(2,1)} %get-tuple-element.219.refs_1_.refs_0_, bf16[512,1024]{1,0:T(8,128)(2,1)} %get-tuple-element.220.refs_2_, bf16[1408,512]{1,0:T(8,128)(2,1)} %get-tuple-element.221.refs_3_, ...), custom_call_target="tpu_custom_call" | custom-call | flops 5000000000 | bytes 10000000 | tf_op jit(solution)/shard_map/ffn_grads/pallas_call | solution.py:600
  148.7 1.1 collective-permute-start.28
  149.9 5.8 %down.1 = (bf16[2,256,1024]{2,1,0:T(8,128)(2,1)}, f32[2,256,1024]{2,1,0:T(8,128)}) custom-call(bf16[704,512]{1,0:T(8,128)(2,1)} %get-tuple-element.219.refs_1_.refs_0_, bf16[704,512]{1,0:T(8,128)(2,1)} %get-tuple-element.222.refs_4_.refs_1_, bf16[2112,1024]{1,0:T(8,128)(2,1)} %all-gather.2.cloned.1.call-done.refs_9_.refs_2_, ...), custom_call_target="tpu_custom_call" | custom-call | flops 1 | bytes 1 | tf_op jit(solution)/shard_map/down/pallas_call | solution.py:564
  155.7 1.4 collective-permute-done.28.refs_3_
  157.7 1.0 copy-done.4
  159.2 2.1 collective-permute-done.29.ga1c_ref
  162.1 34.6 %mixer_bwd.1 = (bf16[4,128,512]{2,1,0:T(8,128)(2,1)}, bf16[4,128,512]{2,1,0:T(8,128)(2,1)}, bf16[4,128,512]{2,1,0:T(8,128)(2,1)}, bf16[4,128,512]{2,1,0:T(8,128)...) custom-call(s32[1024]{0:T(1024)} %bitcast.65, ...), custom_call_target="tpu_custom_call" | custom-call | flops 10000000000 | bytes 10000000 | tf_op jit(solution)/shard_map/mixer_bwd/pallas_call | solution.py:386
  196.9 4.9 %collective-permute-start.33 = (bf16[4,128,512]{2,1,0:T(8,128)(2,1)}, bf16[4,128,512]{2,1,0:T(8,128)(2,1)S(1)}, u32[]{:S(2)}, u32[]{:S(2)}) collective-permute-start(bf16[4,128,512]{2,1,0:T(8,128)(2,1)} %get-tuple-element.264), channel_id=1, source_target_pairs={{0,8},{4,12},{8,0},{12,4},{16,24},{20,28},{24,16},{28,20},{1,9},{5... | collective-permute-start | bytes 1572872 | tf_op jit(solution)/shard_map/ppermute | solution.py:780
  201.8 1.1 collective-permute-start.35
  203.7 3.3 %to_chips.3 = (f32[256,1024]{1,0:T(8,128)}, bf16[256,1024]{1,0:T(8,128)(2,1)}) custom-call(f32[2,256,1024]{2,1,0:T(8,128)} %get-tuple-element.266.keep, bf16[2,256,1024]{2,1,0:T(8,128)(2,1)} %copy-done.11, bf16[8,2112,128]{2,1,0:T(8,128)(2,1)} %ffn_grads.1.refs_3_.wait_for), custom_call_target="tpu_custom_call" | custom-call | flops 1 | bytes 1 | tf_op jit(solution)/shard_map/to_chips/pallas_call | solution.py:620
  206.9 3.2 %to_chips.2 = (f32[256,1024]{1,0:T(8,128)}, bf16[256,1024]{1,0:T(8,128)(2,1)}) custom-call(f32[2,256,1024]{2,1,0:T(8,128)} %get-tuple-element.258.keep, bf16[2,256,1024]{2,1,0:T(8,128)(2,1)} %copy-done.12, f32[8,1024]{1,0:T(8,128)} %get-tuple-element.260.wait_for), custom_call_target="tpu_custom_call" | custom-call | flops 1 | bytes 1 | tf_op jit(solution)/shard_map/to_chips/pallas_call | solution.py:620
  210.1 7.1 %collective-permute-done.32.g1_ref = bf16[4,128,512]{2,1,0:T(8,128)(2,1)S(1)} collective-permute-done((bf16[4,128,512]{2,1,0:T(8,128)(2,1)}, bf16[4,128,512]{2,1,0:T(8,128)(2,1)S(1)}, u32[]{:S(2)}, u32[]{:S(2)}) %collective-permute-start.32) | collective-permute-done | bytes 524320 | tf_op jit(solution)/shard_map/ppermute | solution.py:780
  217.2 1.1 collective-permute-start.40
  218.3 1.0 collective-permute-start.41
  219.3 2.6 fold.2
  221.9 3.0 %collective-permute-start.37 = (bf16[2,128,512]{2,1,0:T(8,128)(2,1)}, bf16[2,128,512]{2,1,0:T(8,128)(2,1)S(1)}, u32[]{:S(2)}, u32[]{:S(2)}) collective-permute-start(bf16[2,128,512]{2,1,0:T(8,128)(2,1)} %get-tuple-element.273), channel_id=1, source_target_pairs={{0,8},{4,12},{8,0},{12,4},{16,24},{20,28},{24,16},{28,20},{1,9},{5... | collective-permute-start | bytes 786440 | tf_op jit(solution)/shard_map/ppermute | solution.py:780
  225.0 1.8 collective-permute-start.38
  227.1 11.7 %collective-permute-done.39 = f32[8,1024]{1,0:T(8,128)S(1)} collective-permute-done((f32[8,1024]{1,0:T(8,128)S(1)}, f32[8,1024]{1,0:T(8,128)S(1)}, u32[]{:S(2)}, u32[]{:S(2)}) %collective-permute-start.39) | collective-permute-done | bytes 32800 | tf_op jit(solution)/shard_map/ppermute | solution.py:780
  238.8 4.5 %collective-permute-done.37.g1_ref = bf16[2,128,512]{2,1,0:T(8,128)(2,1)S(1)} collective-permute-done((bf16[2,128,512]{2,1,0:T(8,128)(2,1)}, bf16[2,128,512]{2,1,0:T(8,128)(2,1)S(1)}, u32[]{:S(2)}, u32[]{:S(2)}) %collective-permute-start.37) | collective-permute-done | bytes 262176 | tf_op jit(solution)/shard_map/ppermute | solution.py:780
  244.1 2.0 fold.3
  246.2 2.9 %collective-permute-start.43 = (bf16[1,128,512]{2,1,0:T(8,128)(2,1)}, bf16[1,128,512]{2,1,0:T(8,128)(2,1)S(1)}, u32[]{:S(2)}, u32[]{:S(2)}) collective-permute-start(bf16[1,128,512]{2,1,0:T(8,128)(2,1)} %get-tuple-element.292), channel_id=1, source_target_pairs={{0,16},{4,20},{8,24},{12,28},{16,0},{20,4},{24,8},{28,12},{1,17},{... | collective-permute-start | bytes 393224 | tf_op jit(solution)/shard_map/ppermute | solution.py:780
  249.1 4.3 %collective-permute-start.46 = (f32[8,1024]{1,0:T(8,128)S(1)}, f32[8,1024]{1,0:T(8,128)S(1)}, u32[]{:S(2)}, u32[]{:S(2)}) collective-permute-start(f32[8,1024]{1,0:T(8,128)S(1)} %add.201.s_ref), channel_id=1, source_target_pairs={{0,24},{4,28},{8,16},{12,20},{16,8},{20,12},{24,0},{28,4},{1,25},{... | collective-permute-start | bytes 98312 | tf_op jit(solution)/shard_map/ppermute | solution.py:780
  253.5 5.0 %last_rows.1 = (f32[256,1024]{1,0:T(8,128)}, bf16[256,1024]{1,0:T(8,128)(2,1)}) custom-call(f32[256,1024]{1,0:T(8,128)} %copy-done.3, f32[256,1024]{1,0:T(8,128)} %copy-done.4, f32[256,1024]{1,0:T(8,128)} %get-tuple-element.261.na, bf16[256,1024]{1,0:T(8,128)(2,1)} %copy-done.17, bf16[256,1024]{1,0:T(8,128)(2,1)} %x_ref.1, f32[1,1024]{1,0:T(1,128)} %gain_ref.3, ...), custom_call_target="tpu_custom_call" | custom-call | flops 1 | bytes 1 | tf_op jit(solution)/shard_map/last_rows/pallas_call | solution.py:640
  258.5 2.1 ffn_cast.1
  262.1 2.0 finish.1
  (182 shorter events, 19.2 us)
Async XLA Ops:
  7.2 11.2 %copy-start = (bf16[256,1024]{1,0:T(8,128)(2,1)S(1)}, bf16[256,1024]{1,0:T(8,128)(2,1)}, u32[]{:S(2)}) copy-start(bf16[256,1024]{1,0:T(8,128)(2,1)} %refs_5_.3) | copy-start | bytes 1572868
  7.2 11.3 %copy-start.26 = (s32[1,1024]{1,0:T(1,128)S(1)}, s32[1,1024]{1,0:T(1,128)}, u32[]{:S(2)}) copy-start(s32[1,1024]{1,0:T(1,128)} %param.14) | copy-start | bytes 12292
  7.2 98.6 %all-gather.2.cloned.1.call-start = ((), (), s32[]{:S(2)}) async-start(), calls=%async_computation.1 | async-start | bytes 4866048 | tf_op jit(solution)/shard_map/all_gather | solution.py:868
  13.3 245.2 %reduce-scatter.2.cloned.1.call-start = ((), (), s32[]{:S(2)}) async-start(), calls=%async_computation.2 | async-start | bytes 4866048 | tf_op jit(solution)/shard_map/reduce_scatter | solution.py:937
  13.3 13.8 %collective-permute-start = (bf16[128,1152]{1,0:T(8,128)(2,1)}, bf16[128,1152]{1,0:T(8,128)(2,1)}, u32[]{:S(2)}, u32[]{:S(2)}) collective-permute-start(bf16[128,1152]{1,0:T(8,128)(2,1)} %pack.1), channel_id=1, source_target_pairs={{0,8},{8,16},{16,24},{24,28},{28,20},{20,12},{12,4},{4,0},{1,9},{9... | collective-permute-start | bytes 884744 | tf_op jit(solution)/shard_map/ppermute | solution.py:831
  16.4 11.0 %collective-permute-start.1 = (bf16[128,1152]{1,0:T(8,128)(2,1)}, bf16[128,1152]{1,0:T(8,128)(2,1)}, u32[]{:S(2)}, u32[]{:S(2)}) collective-permute-start(bf16[128,1152]{1,0:T(8,128)(2,1)} %pack.1), channel_id=1, source_target_pairs={{8,0},{16,8},{24,16},{28,24},{20,28},{12,20},{4,12},{0,4},{9,1},{1... | collective-permute-start | bytes 884744 | tf_op jit(solution)/shard_map/ppermute | solution.py:833
  16.4 11.0 %collective-permute-start.2 = (bf16[256,1024]{1,0:T(8,128)(2,1)}, bf16[256,1024]{1,0:T(8,128)(2,1)}, u32[]{:S(2)}, u32[]{:S(2)}) collective-permute-start(bf16[256,1024]{1,0:T(8,128)(2,1)} %x_ref.1), channel_id=1, source_target_pairs={{0,1},{1,0},{2,3},{3,2},{4,5},{5,4},{6,7},{7,6},{8,9},{9,8},{10,11... | collective-permute-start | bytes 1572872 | tf_op jit(solution)/shard_map/ppermute | solution.py:780
  16.4 15.1 %collective-permute-start.5 = (bf16[256,1024]{1,0:T(8,128)(2,1)}, bf16[256,1024]{1,0:T(8,128)(2,1)}, u32[]{:S(2)}, u32[]{:S(2)}) collective-permute-start(bf16[256,1024]{1,0:T(8,128)(2,1)} %x_ref.1), channel_id=1, source_target_pairs={{0,2},{1,3},{2,0},{3,1},{4,6},{5,7},{6,4},{7,5},{8,10},{9,11},{10,... | collective-permute-start | bytes 1572872 | tf_op jit(solution)/shard_map/ppermute | solution.py:780
  18.4 24.0 %collective-permute-start.6 = (bf16[256,1024]{1,0:T(8,128)(2,1)S(1)}, bf16[256,1024]{1,0:T(8,128)(2,1)S(1)}, u32[]{:S(2)}, u32[]{:S(2)}) collective-permute-start(bf16[256,1024]{1,0:T(8,128)(2,1)S(1)} %copy-done), channel_id=1, source_target_pairs={{0,2},{1,3},{2,0},{3,1},{4,6},{5,7},{6,4},{7,5},{8,10},{9,11},{10,... | collective-permute-start | bytes 1572872 | tf_op jit(solution)/shard_map/ppermute | solution.py:780
  27.2 27.0 %collective-permute-start.13 = (bf16[256,1024]{1,0:T(8,128)(2,1)S(1)}, bf16[256,1024]{1,0:T(8,128)(2,1)S(1)}, u32[]{:S(2)}, u32[]{:S(2)}) collective-permute-start(bf16[256,1024]{1,0:T(8,128)(2,1)S(1)} %copy-done), channel_id=1, source_target_pairs={{0,1},{1,0},{2,3},{3,2},{4,5},{5,4},{6,7},{7,6},{8,9},{9,8},{10,11... | collective-permute-start | bytes 1572872 | tf_op jit(solution)/shard_map/ppermute | solution.py:780
  27.4 15.0 %collective-permute-start.3 = (bf16[128,1152]{1,0:T(8,128)(2,1)}, bf16[128,1152]{1,0:T(8,128)(2,1)S(1)}, u32[]{:S(2)}, u32[]{:S(2)}) collective-permute-start(bf16[128,1152]{1,0:T(8,128)(2,1)} %collective-permute-done), channel_id=1, source_target_pairs={{0,8},{8,16},{16,24},{24,28},{28,20},{20,12},{12,4},{4,0},{1,9},{9... | collective-permute-start | bytes 884744 | tf_op jit(solution)/shard_map/ppermute | solution.py:831
  29.3 17.6 %collective-permute-start.4 = (bf16[128,1152]{1,0:T(8,128)(2,1)}, bf16[128,1152]{1,0:T(8,128)(2,1)S(1)}, u32[]{:S(2)}, u32[]{:S(2)}) collective-permute-start(bf16[128,1152]{1,0:T(8,128)(2,1)} %collective-permute-done.1), channel_id=1, source_target_pairs={{8,0},{16,8},{24,16},{28,24},{20,28},{12,20},{4,12},{0,4},{9,1},{1... | collective-permute-start | bytes 884744 | tf_op jit(solution)/shard_map/ppermute | solution.py:833
  46.9 12.2 %collective-permute-start.10 = (bf16[256,1024]{1,0:T(8,128)(2,1)S(1)}, bf16[256,1024]{1,0:T(8,128)(2,1)S(1)}, u32[]{:S(2)}, u32[]{:S(2)}) collective-permute-start(bf16[256,1024]{1,0:T(8,128)(2,1)S(1)} %collective-permute-done.6.refs_4_.refs_6_), channel_id=1, source_target_pairs={{0,1},{1,0},{2,3},{3,2},{4,5},{5,4},{6,7},{7,6},{8,9},{9,8},{10,11... | collective-permute-start | bytes 1572872 | tf_op jit(solution)/shard_map/ppermute | solution.py:780
  46.9 12.2 %collective-permute-start.9 = (bf16[256,1024]{1,0:T(8,128)(2,1)}, bf16[256,1024]{1,0:T(8,128)(2,1)S(1)}, u32[]{:S(2)}, u32[]{:S(2)}) collective-permute-start(bf16[256,1024]{1,0:T(8,128)(2,1)} %collective-permute-done.5), channel_id=1, source_target_pairs={{0,1},{1,0},{2,3},{3,2},{4,5},{5,4},{6,7},{7,6},{8,9},{9,8},{10,11... | collective-permute-start | bytes 1572872 | tf_op jit(solution)/shard_map/ppermute | solution.py:780
  47.4 8.9 %collective-permute-start.7 = (bf16[128,1152]{1,0:T(8,128)(2,1)S(1)}, bf16[128,1152]{1,0:T(8,128)(2,1)S(1)}, u32[]{:S(2)}, u32[]{:S(2)}) collective-permute-start(bf16[128,1152]{1,0:T(8,128)(2,1)S(1)} %collective-permute-done.3), channel_id=1, source_target_pairs={{0,8},{8,16},{16,24},{24,28},{28,20},{20,12},{12,4},{4,0},{1,9},{9... | collective-permute-start | bytes 884744 | tf_op jit(solution)/shard_map/ppermute | solution.py:831
  47.4 11.7 %collective-permute-start.8 = (bf16[128,1152]{1,0:T(8,128)(2,1)S(1)}, bf16[128,1152]{1,0:T(8,128)(2,1)S(1)}, u32[]{:S(2)}, u32[]{:S(2)}) collective-permute-start(bf16[128,1152]{1,0:T(8,128)(2,1)S(1)} %collective-permute-done.4), channel_id=1, source_target_pairs={{8,0},{16,8},{24,16},{28,24},{20,28},{12,20},{4,12},{0,4},{9,1},{1... | collective-permute-start | bytes 884744 | tf_op jit(solution)/shard_map/ppermute | solution.py:833
  56.3 5.5 %copy-start.16 = (bf16[128,1152]{1,0:T(8,128)(2,1)}, bf16[128,1152]{1,0:T(8,128)(2,1)S(1)}, u32[]{:S(2)}) copy-start(bf16[128,1152]{1,0:T(8,128)(2,1)S(1)} %collective-permute-done.7) | copy-start | bytes 884740
  59.9 9.6 %collective-permute-start.11 = (bf16[64,1152]{1,0:T(8,128)(2,1)}, bf16[64,1152]{1,0:T(8,128)(2,1)}, u32[]{:S(2)}, u32[]{:S(2)}) collective-permute-start(bf16[64,1152]{1,0:T(8,128)(2,1)} %slice.48), channel_id=1, source_target_pairs={{0,8},{8,16},{16,24},{24,28},{28,20},{20,12},{12,4},{4,0},{1,9},{9... | collective-permute-start | bytes 442376 | tf_op jit(solution)/shard_map/ppermute | solution.py:828
  61.8 11.8 %collective-permute-start.12 = (bf16[64,1152]{1,0:T(8,128)(2,1)}, bf16[64,1152]{1,0:T(8,128)(2,1)S(1)}, u32[]{:S(2)}, u32[]{:S(2)}) collective-permute-start(bf16[64,1152]{1,0:T(8,128)(2,1)} %slice.49), channel_id=1, source_target_pairs={{8,0},{16,8},{24,16},{28,24},{20,28},{12,20},{4,12},{0,4},{9,1},{1... | collective-permute-start | bytes 442376 | tf_op jit(solution)/shard_map/ppermute | solution.py:829
  64.6 4.8 %copy-start.15 = (bf16[128,1152]{1,0:T(8,128)(2,1)S(1)}, bf16[128,1152]{1,0:T(8,128)(2,1)}, u32[]{:S(2)}) copy-start(bf16[128,1152]{1,0:T(8,128)(2,1)} %copy-done.14) | copy-start | bytes 884740
  73.6 14.6 %copy-start.19 = (bf16[1024,256]{1,0:T(8,128)(2,1)}, bf16[1024,256]{1,0:T(8,128)(2,1)S(1)}, u32[]{:S(2)}) copy-start(bf16[1024,256]{1,0:T(8,128)(2,1)S(1)} %slice.50.refs_4_.out_ref) | copy-start | bytes 1572868
  73.6 14.6 %collective-permute-start.14 = (bf16[1024,256]{1,0:T(8,128)(2,1)S(1)}, bf16[1024,256]{1,0:T(8,128)(2,1)}, u32[]{:S(2)}, u32[]{:S(2)}) collective-permute-start(bf16[1024,256]{1,0:T(8,128)(2,1)S(1)} %slice.50.refs_4_.out_ref), channel_id=1, source_target_pairs={{0,2},{1,3},{2,0},{3,1},{4,6},{5,7},{6,4},{7,5},{8,10},{9,11},{10,... | collective-permute-start | bytes 1572872 | tf_op jit(solution)/shard_map/ppermute | solution.py:780
  74.9 13.4 %collective-permute-start.15 = (bf16[1024,256]{1,0:T(8,128)(2,1)S(1)}, bf16[1024,256]{1,0:T(8,128)(2,1)}, u32[]{:S(2)}, u32[]{:S(2)}) collective-permute-start(bf16[1024,256]{1,0:T(8,128)(2,1)S(1)} %slice.50.refs_4_.out_ref), channel_id=1, source_target_pairs={{0,1},{1,0},{2,3},{3,2},{4,5},{5,4},{6,7},{7,6},{8,9},{9,8},{10,11... | collective-permute-start | bytes 1572872 | tf_op jit(solution)/shard_map/ppermute | solution.py:780
  88.3 15.8 %collective-permute-start.16 = (bf16[512,256]{1,0:T(8,128)(2,1)}, bf16[512,256]{1,0:T(8,128)(2,1)S(1)}, u32[]{:S(2)}, u32[]{:S(2)}) collective-permute-start(bf16[512,256]{1,0:T(8,128)(2,1)} %get-tuple-element.175.refs_0_), channel_id=1, source_target_pairs={{0,2},{1,3},{2,0},{3,1},{4,6},{5,7},{6,4},{7,5},{8,10},{9,11},{10,... | collective-permute-start | bytes 786440 | tf_op jit(solution)/shard_map/ppermute | solution.py:780
  89.6 14.6 %collective-permute-start.17 = (bf16[512,256]{1,0:T(8,128)(2,1)}, bf16[512,256]{1,0:T(8,128)(2,1)S(1)}, u32[]{:S(2)}, u32[]{:S(2)}) collective-permute-start(bf16[512,256]{1,0:T(8,128)(2,1)} %get-tuple-element.175.refs_0_), channel_id=1, source_target_pairs={{0,1},{1,0},{2,3},{3,2},{4,5},{5,4},{6,7},{7,6},{8,9},{9,8},{10,11... | collective-permute-start | bytes 786440 | tf_op jit(solution)/shard_map/ppermute | solution.py:780
  89.6 14.6 %collective-permute-start.18 = (bf16[1024,256]{1,0:T(8,128)(2,1)}, bf16[1024,256]{1,0:T(8,128)(2,1)S(1)}, u32[]{:S(2)}, u32[]{:S(2)}) collective-permute-start(bf16[1024,256]{1,0:T(8,128)(2,1)} %collective-permute-done.14.refs_5_), channel_id=1, source_target_pairs={{0,1},{1,0},{2,3},{3,2},{4,5},{5,4},{6,7},{7,6},{8,9},{9,8},{10,11... | collective-permute-start | bytes 1572872 | tf_op jit(solution)/shard_map/ppermute | solution.py:780
  104.2 1.6 collective-permute-start.21
  104.2 13.3 %collective-permute-start.19 = (bf16[512,256]{1,0:T(8,128)(2,1)}, bf16[512,256]{1,0:T(8,128)(2,1)S(1)}, u32[]{:S(2)}, u32[]{:S(2)}) collective-permute-start(bf16[512,256]{1,0:T(8,128)(2,1)} %get-tuple-element.193.refs_0_), channel_id=1, source_target_pairs={{0,2},{1,3},{2,0},{3,1},{4,6},{5,7},{6,4},{7,5},{8,10},{9,11},{10,... | collective-permute-start | bytes 786440 | tf_op jit(solution)/shard_map/ppermute | solution.py:780
  105.2 12.4 %collective-permute-start.20 = (bf16[512,256]{1,0:T(8,128)(2,1)}, bf16[512,256]{1,0:T(8,128)(2,1)S(1)}, u32[]{:S(2)}, u32[]{:S(2)}) collective-permute-start(bf16[512,256]{1,0:T(8,128)(2,1)} %get-tuple-element.193.refs_0_), channel_id=1, source_target_pairs={{0,1},{1,0},{2,3},{3,2},{4,5},{5,4},{6,7},{7,6},{8,9},{9,8},{10,11... | collective-permute-start | bytes 786440 | tf_op jit(solution)/shard_map/ppermute | solution.py:780
  117.6 2.2 collective-permute-start.23
  117.8 3.4 %collective-permute-start.22 = (bf16[512,256]{1,0:T(8,128)(2,1)S(1)}, bf16[512,256]{1,0:T(8,128)(2,1)S(1)}, u32[]{:S(2)}, u32[]{:S(2)}) collective-permute-start(bf16[512,256]{1,0:T(8,128)(2,1)S(1)} %collective-permute-done.19.refs_1_), channel_id=1, source_target_pairs={{0,1},{1,0},{2,3},{3,2},{4,5},{5,4},{6,7},{7,6},{8,9},{9,8},{10,11... | collective-permute-start | bytes 786440 | tf_op jit(solution)/shard_map/ppermute | solution.py:780
  121.2 14.1 %copy-start.1 = (f32[256,1024]{1,0:T(8,128)S(1)}, f32[256,1024]{1,0:T(8,128)}, u32[]{:S(2)}) copy-start(f32[256,1024]{1,0:T(8,128)} %get-tuple-element.210.refs_2_.mid0) | copy-start | bytes 3145732
  121.2 14.1 %copy-start.7 = (f32[1,1024]{1,0:T(1,128)S(1)}, f32[1,1024]{1,0:T(1,128)}, u32[]{:S(2)}) copy-start(f32[1,1024]{1,0:T(1,128)} %refs_7_.5) | copy-start | bytes 12292
  121.2 14.0 %collective-permute-start.24 = (bf16[256,1024]{1,0:T(8,128)(2,1)S(1)}, bf16[256,1024]{1,0:T(8,128)(2,1)S(1)}, u32[]{:S(2)}, u32[]{:S(2)}) collective-permute-start(bf16[256,1024]{1,0:T(8,128)(2,1)S(1)} %add_convert_fusion.refs_0_), channel_id=1, source_target_pairs={{0,2},{1,3},{2,0},{3,1},{4,6},{5,7},{6,4},{7,5},{8,10},{9,11},{10,... | collective-permute-start | bytes 1572872 | tf_op jit(solution)/shard_map/ppermute | solution.py:780
  135.3 2.1 collective-permute-start.25
  136.8 11.1 %copy-start.8 = (bf16[256,1024]{1,0:T(8,128)(2,1)}, bf16[256,1024]{1,0:T(8,128)(2,1)S(1)}, u32[]{:S(2)}) copy-start(bf16[256,1024]{1,0:T(8,128)(2,1)S(1)} %get-tuple-element.217.ga0_ref) | copy-start | bytes 1572868
  137.5 10.4 %collective-permute-start.27 = (bf16[256,1024]{1,0:T(8,128)(2,1)S(1)}, bf16[256,1024]{1,0:T(8,128)(2,1)S(1)}, u32[]{:S(2)}, u32[]{:S(2)}) collective-permute-start(bf16[256,1024]{1,0:T(8,128)(2,1)S(1)} %get-tuple-element.217.ga0_ref), channel_id=1, source_target_pairs={{0,1},{1,0},{2,3},{3,2},{4,5},{5,4},{6,7},{7,6},{8,9},{9,8},{10,11... | collective-permute-start | bytes 1572872 | tf_op jit(solution)/shard_map/ppermute | solution.py:780
  137.7 10.2 %collective-permute-start.26 = (bf16[128,1024]{1,0:T(8,128)(2,1)S(1)}, bf16[128,1024]{1,0:T(8,128)(2,1)S(1)}, u32[]{:S(2)}, u32[]{:S(2)}) collective-permute-start(bf16[128,1024]{1,0:T(8,128)(2,1)S(1)} %get-tuple-element.215.refs_7_.refs_0_), channel_id=1, source_target_pairs={{0,2},{1,3},{2,0},{3,1},{4,6},{5,7},{6,4},{7,5},{8,10},{9,11},{10,... | collective-permute-start | bytes 786440 | tf_op jit(solution)/shard_map/ppermute | solution.py:780
  148.7 8.4 %copy-start.2 = (f32[256,1024]{1,0:T(8,128)S(1)}, f32[256,1024]{1,0:T(8,128)}, u32[]{:S(2)}) copy-start(f32[256,1024]{1,0:T(8,128)} %get-tuple-element.228.refs_4_.mid1) | copy-start | bytes 3145732
  148.7 8.4 %copy-start.6 = (bf16[128,1024]{1,0:T(8,128)(2,1)S(1)}, bf16[128,1024]{1,0:T(8,128)(2,1)}, u32[]{:S(2)}) copy-start(bf16[128,1024]{1,0:T(8,128)(2,1)} %copy-done.5) | copy-start | bytes 786436
  148.7 8.4 %collective-permute-start.28 = (bf16[128,1024]{1,0:T(8,128)(2,1)S(1)}, bf16[128,1024]{1,0:T(8,128)(2,1)S(1)}, u32[]{:S(2)}, u32[]{:S(2)}) collective-permute-start(bf16[128,1024]{1,0:T(8,128)(2,1)S(1)} %get-tuple-element.216.refs_1_), channel_id=1, source_target_pairs={{0,2},{1,3},{2,0},{3,1},{4,6},{5,7},{6,4},{7,5},{8,10},{9,11},{10,... | collective-permute-start | bytes 786440 | tf_op jit(solution)/shard_map/ppermute | solution.py:780
  158.7 2.6 collective-permute-start.29
  158.7 38.1 %collective-permute-start.30 = (bf16[2,256,1024]{2,1,0:T(8,128)(2,1)}, bf16[2,256,1024]{2,1,0:T(8,128)(2,1)S(1)}, u32[]{:S(2)}, u32[]{:S(2)}) collective-permute-start(bf16[2,256,1024]{2,1,0:T(8,128)(2,1)} %get-tuple-element.257), channel_id=1, source_target_pairs={{0,1},{1,0},{2,3},{3,2},{4,5},{5,4},{6,7},{7,6},{8,9},{9,8},{10,11... | collective-permute-start | bytes 3145736 | tf_op jit(solution)/shard_map/ppermute | solution.py:780
  196.7 6.9 %copy-start.11 = (bf16[2,256,1024]{2,1,0:T(8,128)(2,1)}, bf16[2,256,1024]{2,1,0:T(8,128)(2,1)S(1)}, u32[]{:S(2)}) copy-start(bf16[2,256,1024]{2,1,0:T(8,128)(2,1)S(1)} %collective-permute-done.30.got) | copy-start | bytes 3145732
  196.8 6.1 %collective-permute-start.31 = (bf16[2,256,1024]{2,1,0:T(8,128)(2,1)}, bf16[2,256,1024]{2,1,0:T(8,128)(2,1)S(1)}, u32[]{:S(2)}, u32[]{:S(2)}) collective-permute-start(bf16[2,256,1024]{2,1,0:T(8,128)(2,1)} %get-tuple-element.259), channel_id=1, source_target_pairs={{0,1},{1,0},{2,3},{3,2},{4,5},{5,4},{6,7},{7,6},{8,9},{9,8},{10,11... | collective-permute-start | bytes 3145736 | tf_op jit(solution)/shard_map/ppermute | solution.py:780
  196.9 20.3 %collective-permute-start.32 = (bf16[4,128,512]{2,1,0:T(8,128)(2,1)}, bf16[4,128,512]{2,1,0:T(8,128)(2,1)S(1)}, u32[]{:S(2)}, u32[]{:S(2)}) collective-permute-start(bf16[4,128,512]{2,1,0:T(8,128)(2,1)} %get-tuple-element.263), channel_id=1, source_target_pairs={{0,4},{4,0},{8,12},{12,8},{16,20},{20,16},{24,28},{28,24},{1,5},{5... | collective-permute-start | bytes 1572872 | tf_op jit(solution)/shard_map/ppermute | solution.py:780
  196.9 20.3 %collective-permute-start.33 = (bf16[4,128,512]{2,1,0:T(8,128)(2,1)}, bf16[4,128,512]{2,1,0:T(8,128)(2,1)S(1)}, u32[]{:S(2)}, u32[]{:S(2)}) collective-permute-start(bf16[4,128,512]{2,1,0:T(8,128)(2,1)} %get-tuple-element.264), channel_id=1, source_target_pairs={{0,8},{4,12},{8,0},{12,4},{16,24},{20,28},{24,16},{28,20},{1,9},{5... | collective-permute-start | bytes 1572872 | tf_op jit(solution)/shard_map/ppermute | solution.py:780
  201.8 8.3 %collective-permute-start.34 = (f32[8,1024]{1,0:T(8,128)}, f32[8,1024]{1,0:T(8,128)S(1)}, u32[]{:S(2)}, u32[]{:S(2)}) collective-permute-start(f32[8,1024]{1,0:T(8,128)} %get-tuple-element.260.wait_for), channel_id=1, source_target_pairs={{0,1},{1,0},{2,3},{3,2},{4,5},{5,4},{6,7},{7,6},{8,9},{9,8},{10,11... | collective-permute-start | bytes 98312 | tf_op jit(solution)/shard_map/ppermute | solution.py:780
  201.8 8.3 %collective-permute-start.35 = (f32[8,1024]{1,0:T(8,128)}, f32[8,1024]{1,0:T(8,128)S(1)}, u32[]{:S(2)}, u32[]{:S(2)}) collective-permute-start(f32[8,1024]{1,0:T(8,128)} %get-tuple-element.260.wait_for), channel_id=1, source_target_pairs={{0,2},{1,3},{2,0},{3,1},{4,6},{5,7},{6,4},{7,5},{8,10},{9,11},{10,... | collective-permute-start | bytes 98312 | tf_op jit(solution)/shard_map/ppermute | solution.py:780
  202.9 7.2 %collective-permute-start.36 = (f32[8,1024]{1,0:T(8,128)}, f32[8,1024]{1,0:T(8,128)S(1)}, u32[]{:S(2)}, u32[]{:S(2)}) collective-permute-start(f32[8,1024]{1,0:T(8,128)} %get-tuple-element.260.wait_for), channel_id=1, source_target_pairs={{0,3},{1,2},{2,1},{3,0},{4,7},{5,6},{6,5},{7,4},{8,11},{9,10},{10,... | collective-permute-start | bytes 98312 | tf_op jit(solution)/shard_map/ppermute | solution.py:780
  206.9 19.8 %copy-start.27 = (f32[8,1024]{1,0:T(8,128)S(1)}, f32[8,1024]{1,0:T(8,128)}, u32[]{:S(2)}) copy-start(f32[8,1024]{1,0:T(8,128)} %get-tuple-element.260.wait_for) | copy-start | bytes 98308
  206.9 19.8 %copy-start.34 = (f32[8,1024]{1,0:T(8,128)S(1)}, f32[8,1024]{1,0:T(8,128)}, u32[]{:S(2)}) copy-start(f32[8,1024]{1,0:T(8,128)} %get-tuple-element.275) | copy-start | bytes 98308
  217.2 26.2 %collective-permute-start.40 = (bf16[256,1024]{1,0:T(8,128)(2,1)}, bf16[256,1024]{1,0:T(8,128)(2,1)S(1)}, u32[]{:S(2)}, u32[]{:S(2)}) collective-permute-start(bf16[256,1024]{1,0:T(8,128)(2,1)} %get-tuple-element.279), channel_id=1, source_target_pairs={{0,2},{1,3},{2,0},{3,1},{4,6},{5,7},{6,4},{7,5},{8,10},{9,11},{10,... | collective-permute-start | bytes 1572872 | tf_op jit(solution)/shard_map/ppermute | solution.py:780
  218.3 30.8 %collective-permute-start.41 = (bf16[256,1024]{1,0:T(8,128)(2,1)}, bf16[256,1024]{1,0:T(8,128)(2,1)S(1)}, u32[]{:S(2)}, u32[]{:S(2)}) collective-permute-start(bf16[256,1024]{1,0:T(8,128)(2,1)} %get-tuple-element.282), channel_id=1, source_target_pairs={{0,2},{1,3},{2,0},{3,1},{4,6},{5,7},{6,4},{7,5},{8,10},{9,11},{10,... | collective-permute-start | bytes 1572872 | tf_op jit(solution)/shard_map/ppermute | solution.py:780
  221.9 21.4 %collective-permute-start.37 = (bf16[2,128,512]{2,1,0:T(8,128)(2,1)}, bf16[2,128,512]{2,1,0:T(8,128)(2,1)S(1)}, u32[]{:S(2)}, u32[]{:S(2)}) collective-permute-start(bf16[2,128,512]{2,1,0:T(8,128)(2,1)} %get-tuple-element.273), channel_id=1, source_target_pairs={{0,8},{4,12},{8,0},{12,4},{16,24},{20,28},{24,16},{28,20},{1,9},{5... | collective-permute-start | bytes 786440 | tf_op jit(solution)/shard_map/ppermute | solution.py:780
  225.0 18.4 %collective-permute-start.38 = (bf16[2,128,512]{2,1,0:T(8,128)(2,1)}, bf16[2,128,512]{2,1,0:T(8,128)(2,1)S(1)}, u32[]{:S(2)}, u32[]{:S(2)}) collective-permute-start(bf16[2,128,512]{2,1,0:T(8,128)(2,1)} %get-tuple-element.274), channel_id=1, source_target_pairs={{0,4},{4,0},{8,12},{12,8},{16,20},{20,16},{24,28},{28,24},{1,5},{5... | collective-permute-start | bytes 786440 | tf_op jit(solution)/shard_map/ppermute | solution.py:780
  226.7 12.1 %collective-permute-start.39 = (f32[8,1024]{1,0:T(8,128)S(1)}, f32[8,1024]{1,0:T(8,128)S(1)}, u32[]{:S(2)}, u32[]{:S(2)}) collective-permute-start(f32[8,1024]{1,0:T(8,128)S(1)} %add_add_fusion), channel_id=1, source_target_pairs={{0,4},{4,0},{8,12},{12,8},{16,20},{20,16},{24,28},{28,24},{1,5},{5... | collective-permute-start | bytes 98312 | tf_op jit(solution)/shard_map/ppermute | solution.py:780
  238.8 22.7 %copy-start.28 = (f32[8,1024]{1,0:T(8,128)}, f32[8,1024]{1,0:T(8,128)S(1)}, u32[]{:S(2)}) copy-start(f32[8,1024]{1,0:T(8,128)S(1)} %add.201.s_ref) | copy-start | bytes 98308
  243.3 10.1 %copy-start.17 = (bf16[256,1024]{1,0:T(8,128)(2,1)}, bf16[256,1024]{1,0:T(8,128)(2,1)S(1)}, u32[]{:S(2)}) copy-start(bf16[256,1024]{1,0:T(8,128)(2,1)S(1)} %collective-permute-done.40.na_y) | copy-start | bytes 1572868
  246.1 15.3 %collective-permute-start.42 = (bf16[1,128,512]{2,1,0:T(8,128)(2,1)}, bf16[1,128,512]{2,1,0:T(8,128)(2,1)S(1)}, u32[]{:S(2)}, u32[]{:S(2)}) collective-permute-start(bf16[1,128,512]{2,1,0:T(8,128)(2,1)} %get-tuple-element.290), channel_id=1, source_target_pairs={{0,16},{4,20},{8,24},{12,28},{16,0},{20,4},{24,8},{28,12},{1,17},{... | collective-permute-start | bytes 393224 | tf_op jit(solution)/shard_map/ppermute | solution.py:780
  246.2 15.3 %collective-permute-start.43 = (bf16[1,128,512]{2,1,0:T(8,128)(2,1)}, bf16[1,128,512]{2,1,0:T(8,128)(2,1)S(1)}, u32[]{:S(2)}, u32[]{:S(2)}) collective-permute-start(bf16[1,128,512]{2,1,0:T(8,128)(2,1)} %get-tuple-element.292), channel_id=1, source_target_pairs={{0,16},{4,20},{8,24},{12,28},{16,0},{20,4},{24,8},{28,12},{1,17},{... | collective-permute-start | bytes 393224 | tf_op jit(solution)/shard_map/ppermute | solution.py:780
  249.1 11.4 %collective-permute-start.44 = (f32[8,1024]{1,0:T(8,128)S(1)}, f32[8,1024]{1,0:T(8,128)S(1)}, u32[]{:S(2)}, u32[]{:S(2)}) collective-permute-start(f32[8,1024]{1,0:T(8,128)S(1)} %add.201.s_ref), channel_id=1, source_target_pairs={{0,8},{4,12},{8,0},{12,4},{16,24},{20,28},{24,16},{28,20},{1,9},{5... | collective-permute-start | bytes 98312 | tf_op jit(solution)/shard_map/ppermute | solution.py:780
  249.1 12.4 %collective-permute-start.45 = (f32[8,1024]{1,0:T(8,128)S(1)}, f32[8,1024]{1,0:T(8,128)S(1)}, u32[]{:S(2)}, u32[]{:S(2)}) collective-permute-start(f32[8,1024]{1,0:T(8,128)S(1)} %add.201.s_ref), channel_id=1, source_target_pairs={{0,16},{4,20},{8,24},{12,28},{16,0},{20,4},{24,8},{28,12},{1,17},{... | collective-permute-start | bytes 98312 | tf_op jit(solution)/shard_map/ppermute | solution.py:780
  249.1 12.3 %collective-permute-start.46 = (f32[8,1024]{1,0:T(8,128)S(1)}, f32[8,1024]{1,0:T(8,128)S(1)}, u32[]{:S(2)}, u32[]{:S(2)}) collective-permute-start(f32[8,1024]{1,0:T(8,128)S(1)} %add.201.s_ref), channel_id=1, source_target_pairs={{0,24},{4,28},{8,16},{12,20},{16,8},{20,12},{24,0},{28,4},{1,25},{... | collective-permute-start | bytes 98312 | tf_op jit(solution)/shard_map/ppermute | solution.py:780
  (30 other events, 55.2 us)
Sparse Core Ops, SparseCore 0:
  13.4 89.7 all-gather.1
  148.8 103.3 reduce-scatter.1

commit v7 on v6

--- a/solution.py
+++ b/solution.py
@@ -961,7 +961,7 @@
         g2 = hop(away2, "fsdp", second_bits[stage])
         if stage < count - 1:
             small = hop_sum(small, "fsdp", first_bits[stage - 1])
-            g1, g2, small, na_y = fence(g1, g2, small, na_y)
+            g1, g2, small = fence(g1, g2, small)
     if n_f == 8:
         got = [hop(small, "fsdp", k) for k in (2, 4, 6)]
     else:

time: 275 us -> 275 us (level)
  no operation moved by 1% of the time
where the time goes in v7:
time: 275 us; the launch traced here: 271 us
  Pallas kernels  122 us (44%)
  waiting for transfers between devices  55 us (20%)
  starting transfers between devices  42.1 us (15%)
  local copies, waits for them, and re-layouts  32.8 us (12%)
  between operations  14.9 us (5%)
  other arithmetic  4.04 us (1%)
    ppermute x39, waiting for transfers between devices, hop(): return lax.ppermute(value, axis, [(i, i ^ bit) for i in range(n)])  43.3 us
    pallas_call x1, Pallas kernels, mixer_bwd(): pl.pallas_call(functools.partial(bwd_kernel, heads, cb, n_f, shard), grid...  34.6 us
    ppermute x39, starting transfers between devices, hop(): return lax.ppermute(value, axis, [(i, i ^ bit) for i in range(n)])  32.6 us
    pallas_call x2, Pallas kernels, mixer_fwd(): pl.pallas_call(functools.partial(fwd_call_kernel, heads, cb, base, len(ol...  27.3 us
    pallas_call x2, Pallas kernels, ffn(): pl.pallas_call(functools.partial(ffn_kernel, ff), grid=(1,), in_specs=[wh...  22.5 us
    dynamic_update_slice x8, local copies, waits for them, and re-layouts, in_order(): lax.dynamic_update_slice(full, block[None], (me ^ k,) + (0,) * own.ndim)  12 us
    pallas_call x1, Pallas kernels, ffn_grads(): pl.pallas_call(functools.partial(ffn_grads_kernel, ff, len(pieces)), grid...  9.19 us
    unnamed x91, local copies, waits for them, and re-layouts  7.34 us
  transfers between devices with their start and end apart: 49, of which 16 were waited for; matrix products, arithmetic and copies ran while one was open for 10% of the time, Pallas kernels for 44%

profile of v7, /device:TPU:0, one launch (start us, length us, event | category | flops | bytes accessed | tf_op | source)
XLA Modules:
  0.0 271.2 jit_solution(15261717525627201555)
XLA Ops:
  7.2 1.4 copy.45
  8.7 1.8 pack.1
  10.4 1.0 slice_bitcast_fusion.1
  11.5 1.8 pad_maximum_fusion
  13.3 3.1 %collective-permute-start = (bf16[128,1152]{1,0:T(8,128)(2,1)}, bf16[128,1152]{1,0:T(8,128)(2,1)}, u32[]{:S(2)}, u32[]{:S(2)}) collective-permute-start(bf16[128,1152]{1,0:T(8,128)(2,1)} %pack.1), channel_id=1, source_target_pairs={{0,8},{8,16},{16,24},{24,28},{28,20},{20,12},{12,4},{4,0},{1,9},{9... | collective-permute-start | bytes 884744 | tf_op jit(solution)/shard_map/ppermute | solution.py:831
  16.4 2.0 collective-permute-start.5
  19.3 1.0 constant_dynamic-update-slice_fusion.8
  20.3 1.7 broadcast.20.clone
  21.9 1.9 bitcast_dynamic-update-slice_fusion.7
  23.8 1.6 broadcast.20.clone.1
  27.4 1.9 collective-permute-start.3
  29.4 1.0 constant_dynamic-update-slice_fusion.7
  30.4 1.0 constant_dynamic-update-slice_fusion.6
  31.5 10.9 %collective-permute-done.6.refs_4_.refs_6_ = bf16[256,1024]{1,0:T(8,128)(2,1)S(1)} collective-permute-done((bf16[256,1024]{1,0:T(8,128)(2,1)S(1)}, bf16[256,1024]{1,0:T(8,128)(2,1)S(1)}, u32[]{:S(2)}, u32[]{:S(2)}) %collective-permute-start.6) | collective-permute-done | bytes 524320 | tf_op jit(solution)/shard_map/ppermute | solution.py:780
  42.4 4.5 %collective-permute-done.4 = bf16[128,1152]{1,0:T(8,128)(2,1)S(1)} collective-permute-done((bf16[128,1152]{1,0:T(8,128)(2,1)}, bf16[128,1152]{1,0:T(8,128)(2,1)S(1)}, u32[]{:S(2)}, u32[]{:S(2)}) %collective-permute-start.4) | collective-permute-done | bytes 294944 | tf_op jit(solution)/shard_map/ppermute | solution.py:833
  47.4 2.0 collective-permute-start.8
  49.4 1.9 bitcast_dynamic-update-slice_fusion.6
  52.2 1.9 bitcast_dynamic-update-slice_fusion.5
  55.0 1.3 collective-permute-done.7
  56.3 2.8 %collective-permute-done.8 = bf16[128,1152]{1,0:T(8,128)(2,1)S(1)} collective-permute-done((bf16[128,1152]{1,0:T(8,128)(2,1)S(1)}, bf16[128,1152]{1,0:T(8,128)(2,1)S(1)}, u32[]{:S(2)}, u32[]{:S(2)}) %collective-permute-start.8) | collective-permute-done | bytes 294944 | tf_op jit(solution)/shard_map/ppermute | solution.py:833
  59.9 1.2 collective-permute-start.11
  61.8 1.0 collective-permute-start.12
  62.8 1.8 copy.46.refs_4_.cols_ref
  64.6 1.0 constant_dynamic-update-slice_fusion.3
  65.7 1.9 bitcast_dynamic-update-slice_fusion.4
  67.6 1.9 bitcast_dynamic-update-slice_fusion
  70.4 3.1 %collective-permute-done.12 = bf16[64,1152]{1,0:T(8,128)(2,1)S(1)} collective-permute-done((bf16[64,1152]{1,0:T(8,128)(2,1)}, bf16[64,1152]{1,0:T(8,128)(2,1)S(1)}, u32[]{:S(2)}, u32[]{:S(2)}) %collective-permute-start.12) | collective-permute-done | bytes 147488 | tf_op jit(solution)/shard_map/ppermute | solution.py:829
  73.6 1.3 collective-permute-start.14
  75.0 13.3 %mixer_fwd.2 = (bf16[512,256]{1,0:T(8,128)(2,1)}, bf16[1024,256]{1,0:T(8,128)(2,1)}, bf16[1024,1024]{1,0:T(8,128)(2,1)}, f32[1024,896]{1,0:T(8,128)}, f32[1024,7...) custom-call(s32[1024]{0:T(1024)} %bitcast.63, ...), custom_call_target="tpu_custom_call" | custom-call | flops 10000000000 | bytes 10000000 | tf_op jit(solution)/shard_map/mixer_fwd/pallas_call | solution.py:354
  88.3 1.3 collective-permute-start.16
  90.1 14.0 %mixer_fwd.3 = (bf16[512,256]{1,0:T(8,128)(2,1)}, bf16[1024,256]{1,0:T(8,128)(2,1)}, bf16[1024,1024]{1,0:T(8,128)(2,1)}, f32[1024,896]{1,0:T(8,128)}, f32[1024,7...) custom-call(s32[1024]{0:T(1024)} %bitcast.64, ...), custom_call_target="tpu_custom_call", output_to_operand_aliasing={{1}: (10, {}), {2}: (11, {}), {3}: (12, {}), {4}: (13, {}),... | custom-call | flops 10000000000 | bytes 10000000 | tf_op jit(solution)/shard_map/mixer_fwd/pallas_call | solution.py:354
  104.2 1.0 collective-permute-start.19
  106.5 11.1 %ffn.2 = (f32[256,1024]{1,0:T(8,128)}, bf16[512,1024]{1,0:T(8,128)(2,1)}, bf16[704,512]{1,0:T(8,128)(2,1)}, bf16[1408,512]{1,0:T(8,128)(2,1)}, f32[256,1024]{1,0...) custom-call(bf16[512,256]{1,0:T(8,128)(2,1)} %get-tuple-element.174.refs_0_, bf16[512,256]{1,0:T(8,128)(2,1)} %copy-done.39, ...), custom_call_target="tpu_custom_call" | custom-call | flops 10000000000 | bytes 10000000 | tf_op jit(solution)/shard_map/ffn/pallas_call | solution.py:511
  118.2 1.6 collective-permute-done.23
  119.8 1.4 add_convert_fusion.refs_0_
  122.1 11.4 %ffn.3 = (f32[256,1024]{1,0:T(8,128)}, bf16[512,1024]{1,0:T(8,128)(2,1)}, bf16[704,512]{1,0:T(8,128)(2,1)}, bf16[1408,512]{1,0:T(8,128)(2,1)}, f32[256,1024]{1,0...) custom-call(bf16[512,256]{1,0:T(8,128)(2,1)} %get-tuple-element.192.refs_0_, bf16[512,256]{1,0:T(8,128)(2,1)} %copy-done.41, ...), custom_call_target="tpu_custom_call" | custom-call | flops 10000000000 | bytes 10000000 | tf_op jit(solution)/shard_map/ffn/pallas_call | solution.py:511
  133.5 1.8 collective-permute-done.24.refs_1_
  135.9 1.0 copy-done.3
  137.7 1.0 collective-permute-start.26
  138.7 9.2 %ffn_grads.1.refs_3_.wait_for = bf16[8,2112,128]{2,1,0:T(8,128)(2,1)} custom-call(bf16[1408,512]{1,0:T(8,128)(2,1)} %get-tuple-element.217.refs_0_, bf16[704,512]{1,0:T(8,128)(2,1)} %get-tuple-element.218.refs_1_.refs_0_, bf16[512,1024]{1,0:T(8,128)(2,1)} %get-tuple-element.219.refs_2_, bf16[1408,512]{1,0:T(8,128)(2,1)} %get-tuple-element.220.refs_3_, ...), custom_call_target="tpu_custom_call" | custom-call | flops 5000000000 | bytes 10000000 | tf_op jit(solution)/shard_map/ffn_grads/pallas_call | solution.py:600
  148.7 1.1 collective-permute-start.28
  149.9 5.8 %down.1 = (bf16[2,256,1024]{2,1,0:T(8,128)(2,1)}, f32[2,256,1024]{2,1,0:T(8,128)}) custom-call(bf16[704,512]{1,0:T(8,128)(2,1)} %get-tuple-element.218.refs_1_.refs_0_, bf16[704,512]{1,0:T(8,128)(2,1)} %get-tuple-element.221.refs_4_.refs_1_, bf16[2112,1024]{1,0:T(8,128)(2,1)} %all-gather.2.cloned.1.call-done.refs_9_.refs_2_, ...), custom_call_target="tpu_custom_call" | custom-call | flops 1 | bytes 1 | tf_op jit(solution)/shard_map/down/pallas_call | solution.py:564
  155.7 1.4 collective-permute-done.28.refs_3_
  157.7 1.0 copy-done.4
  159.2 2.1 collective-permute-done.29.ga1c_ref
  162.1 34.6 %mixer_bwd.1 = (bf16[4,128,512]{2,1,0:T(8,128)(2,1)}, bf16[4,128,512]{2,1,0:T(8,128)(2,1)}, bf16[4,128,512]{2,1,0:T(8,128)(2,1)}, bf16[4,128,512]{2,1,0:T(8,128)...) custom-call(s32[1024]{0:T(1024)} %bitcast.65, ...), custom_call_target="tpu_custom_call" | custom-call | flops 10000000000 | bytes 10000000 | tf_op jit(solution)/shard_map/mixer_bwd/pallas_call | solution.py:386
  196.9 4.9 %collective-permute-start.33 = (bf16[4,128,512]{2,1,0:T(8,128)(2,1)}, bf16[4,128,512]{2,1,0:T(8,128)(2,1)S(1)}, u32[]{:S(2)}, u32[]{:S(2)}) collective-permute-start(bf16[4,128,512]{2,1,0:T(8,128)(2,1)} %get-tuple-element.262), channel_id=1, source_target_pairs={{0,8},{4,12},{8,0},{12,4},{16,24},{20,28},{24,16},{28,20},{1,9},{5... | collective-permute-start | bytes 1572872 | tf_op jit(solution)/shard_map/ppermute | solution.py:780
  201.8 1.1 collective-permute-start.35
  203.7 3.3 %to_chips.3 = (f32[256,1024]{1,0:T(8,128)}, bf16[256,1024]{1,0:T(8,128)(2,1)}) custom-call(f32[2,256,1024]{2,1,0:T(8,128)} %get-tuple-element.264.keep, bf16[2,256,1024]{2,1,0:T(8,128)(2,1)} %copy-done.11, bf16[8,2112,128]{2,1,0:T(8,128)(2,1)} %ffn_grads.1.refs_3_.wait_for), custom_call_target="tpu_custom_call" | custom-call | flops 1 | bytes 1 | tf_op jit(solution)/shard_map/to_chips/pallas_call | solution.py:620
  206.9 3.2 %to_chips.2 = (f32[256,1024]{1,0:T(8,128)}, bf16[256,1024]{1,0:T(8,128)(2,1)}) custom-call(f32[2,256,1024]{2,1,0:T(8,128)} %get-tuple-element.257.keep, bf16[2,256,1024]{2,1,0:T(8,128)(2,1)} %copy-done.12, f32[8,1024]{1,0:T(8,128)} %get-tuple-element.259.wait_for), custom_call_target="tpu_custom_call" | custom-call | flops 1 | bytes 1 | tf_op jit(solution)/shard_map/to_chips/pallas_call | solution.py:620
  210.1 7.1 %collective-permute-done.32.g1_ref = bf16[4,128,512]{2,1,0:T(8,128)(2,1)S(1)} collective-permute-done((bf16[4,128,512]{2,1,0:T(8,128)(2,1)}, bf16[4,128,512]{2,1,0:T(8,128)(2,1)S(1)}, u32[]{:S(2)}, u32[]{:S(2)}) %collective-permute-start.32) | collective-permute-done | bytes 524320 | tf_op jit(solution)/shard_map/ppermute | solution.py:780
  217.2 1.1 collective-permute-start.37
  218.3 1.0 collective-permute-start.38
  219.3 2.6 fold.2
  221.9 3.0 %collective-permute-start.39 = (bf16[2,128,512]{2,1,0:T(8,128)(2,1)}, bf16[2,128,512]{2,1,0:T(8,128)(2,1)S(1)}, u32[]{:S(2)}, u32[]{:S(2)}) collective-permute-start(bf16[2,128,512]{2,1,0:T(8,128)(2,1)} %get-tuple-element.278), channel_id=1, source_target_pairs={{0,8},{4,12},{8,0},{12,4},{16,24},{20,28},{24,16},{28,20},{1,9},{5... | collective-permute-start | bytes 786440 | tf_op jit(solution)/shard_map/ppermute | solution.py:780
  225.0 1.8 collective-permute-start.40
  227.1 11.7 %collective-permute-done.41 = f32[8,1024]{1,0:T(8,128)S(1)} collective-permute-done((f32[8,1024]{1,0:T(8,128)S(1)}, f32[8,1024]{1,0:T(8,128)S(1)}, u32[]{:S(2)}, u32[]{:S(2)}) %collective-permute-start.41) | collective-permute-done | bytes 32800 | tf_op jit(solution)/shard_map/ppermute | solution.py:780
  238.8 4.5 %collective-permute-done.39.g1_ref = bf16[2,128,512]{2,1,0:T(8,128)(2,1)S(1)} collective-permute-done((bf16[2,128,512]{2,1,0:T(8,128)(2,1)}, bf16[2,128,512]{2,1,0:T(8,128)(2,1)S(1)}, u32[]{:S(2)}, u32[]{:S(2)}) %collective-permute-start.39) | collective-permute-done | bytes 262176 | tf_op jit(solution)/shard_map/ppermute | solution.py:780
  244.1 2.0 fold.3
  246.2 2.9 %collective-permute-start.43 = (bf16[1,128,512]{2,1,0:T(8,128)(2,1)}, bf16[1,128,512]{2,1,0:T(8,128)(2,1)S(1)}, u32[]{:S(2)}, u32[]{:S(2)}) collective-permute-start(bf16[1,128,512]{2,1,0:T(8,128)(2,1)} %get-tuple-element.290), channel_id=1, source_target_pairs={{0,16},{4,20},{8,24},{12,28},{16,0},{20,4},{24,8},{28,12},{1,17},{... | collective-permute-start | bytes 393224 | tf_op jit(solution)/shard_map/ppermute | solution.py:780
  249.2 4.3 %collective-permute-start.46 = (f32[8,1024]{1,0:T(8,128)S(1)}, f32[8,1024]{1,0:T(8,128)S(1)}, u32[]{:S(2)}, u32[]{:S(2)}) collective-permute-start(f32[8,1024]{1,0:T(8,128)S(1)} %add.201.s_ref), channel_id=1, source_target_pairs={{0,24},{4,28},{8,16},{12,20},{16,8},{20,12},{24,0},{28,4},{1,25},{... | collective-permute-start | bytes 98312 | tf_op jit(solution)/shard_map/ppermute | solution.py:780
  253.5 5.0 %last_rows.1 = (f32[256,1024]{1,0:T(8,128)}, bf16[256,1024]{1,0:T(8,128)(2,1)}) custom-call(f32[256,1024]{1,0:T(8,128)} %copy-done.3, f32[256,1024]{1,0:T(8,128)} %copy-done.4, f32[256,1024]{1,0:T(8,128)} %get-tuple-element.260.na, bf16[256,1024]{1,0:T(8,128)(2,1)} %copy-done.17, bf16[256,1024]{1,0:T(8,128)(2,1)} %x_ref.1, f32[1,1024]{1,0:T(1,128)} %gain_ref.3, ...), custom_call_target="tpu_custom_call" | custom-call | flops 1 | bytes 1 | tf_op jit(solution)/shard_map/last_rows/pallas_call | solution.py:640
  258.5 2.1 ffn_cast.1
  262.1 2.0 finish.1
  (182 shorter events, 19.3 us)
Async XLA Ops:
  7.2 11.2 %copy-start = (bf16[256,1024]{1,0:T(8,128)(2,1)S(1)}, bf16[256,1024]{1,0:T(8,128)(2,1)}, u32[]{:S(2)}) copy-start(bf16[256,1024]{1,0:T(8,128)(2,1)} %refs_5_.3) | copy-start | bytes 1572868
  7.2 11.3 %copy-start.26 = (s32[1,1024]{1,0:T(1,128)S(1)}, s32[1,1024]{1,0:T(1,128)}, u32[]{:S(2)}) copy-start(s32[1,1024]{1,0:T(1,128)} %param.14) | copy-start | bytes 12292
  7.2 98.6 %all-gather.2.cloned.1.call-start = ((), (), s32[]{:S(2)}) async-start(), calls=%async_computation.1 | async-start | bytes 4866048 | tf_op jit(solution)/shard_map/all_gather | solution.py:868
  13.3 245.2 %reduce-scatter.2.cloned.1.call-start = ((), (), s32[]{:S(2)}) async-start(), calls=%async_computation.2 | async-start | bytes 4866048 | tf_op jit(solution)/shard_map/reduce_scatter | solution.py:937
  13.3 13.8 %collective-permute-start = (bf16[128,1152]{1,0:T(8,128)(2,1)}, bf16[128,1152]{1,0:T(8,128)(2,1)}, u32[]{:S(2)}, u32[]{:S(2)}) collective-permute-start(bf16[128,1152]{1,0:T(8,128)(2,1)} %pack.1), channel_id=1, source_target_pairs={{0,8},{8,16},{16,24},{24,28},{28,20},{20,12},{12,4},{4,0},{1,9},{9... | collective-permute-start | bytes 884744 | tf_op jit(solution)/shard_map/ppermute | solution.py:831
  16.4 11.0 %collective-permute-start.1 = (bf16[128,1152]{1,0:T(8,128)(2,1)}, bf16[128,1152]{1,0:T(8,128)(2,1)}, u32[]{:S(2)}, u32[]{:S(2)}) collective-permute-start(bf16[128,1152]{1,0:T(8,128)(2,1)} %pack.1), channel_id=1, source_target_pairs={{8,0},{16,8},{24,16},{28,24},{20,28},{12,20},{4,12},{0,4},{9,1},{1... | collective-permute-start | bytes 884744 | tf_op jit(solution)/shard_map/ppermute | solution.py:833
  16.4 11.0 %collective-permute-start.2 = (bf16[256,1024]{1,0:T(8,128)(2,1)}, bf16[256,1024]{1,0:T(8,128)(2,1)}, u32[]{:S(2)}, u32[]{:S(2)}) collective-permute-start(bf16[256,1024]{1,0:T(8,128)(2,1)} %x_ref.1), channel_id=1, source_target_pairs={{0,1},{1,0},{2,3},{3,2},{4,5},{5,4},{6,7},{7,6},{8,9},{9,8},{10,11... | collective-permute-start | bytes 1572872 | tf_op jit(solution)/shard_map/ppermute | solution.py:780
  16.4 15.1 %collective-permute-start.5 = (bf16[256,1024]{1,0:T(8,128)(2,1)}, bf16[256,1024]{1,0:T(8,128)(2,1)}, u32[]{:S(2)}, u32[]{:S(2)}) collective-permute-start(bf16[256,1024]{1,0:T(8,128)(2,1)} %x_ref.1), channel_id=1, source_target_pairs={{0,2},{1,3},{2,0},{3,1},{4,6},{5,7},{6,4},{7,5},{8,10},{9,11},{10,... | collective-permute-start | bytes 1572872 | tf_op jit(solution)/shard_map/ppermute | solution.py:780
  18.4 24.0 %collective-permute-start.6 = (bf16[256,1024]{1,0:T(8,128)(2,1)S(1)}, bf16[256,1024]{1,0:T(8,128)(2,1)S(1)}, u32[]{:S(2)}, u32[]{:S(2)}) collective-permute-start(bf16[256,1024]{1,0:T(8,128)(2,1)S(1)} %copy-done), channel_id=1, source_target_pairs={{0,2},{1,3},{2,0},{3,1},{4,6},{5,7},{6,4},{7,5},{8,10},{9,11},{10,... | collective-permute-start | bytes 1572872 | tf_op jit(solution)/shard_map/ppermute | solution.py:780
  27.2 27.0 %collective-permute-start.13 = (bf16[256,1024]{1,0:T(8,128)(2,1)S(1)}, bf16[256,1024]{1,0:T(8,128)(2,1)S(1)}, u32[]{:S(2)}, u32[]{:S(2)}) collective-permute-start(bf16[256,1024]{1,0:T(8,128)(2,1)S(1)} %copy-done), channel_id=1, source_target_pairs={{0,1},{1,0},{2,3},{3,2},{4,5},{5,4},{6,7},{7,6},{8,9},{9,8},{10,11... | collective-permute-start | bytes 1572872 | tf_op jit(solution)/shard_map/ppermute | solution.py:780
  27.4 15.0 %collective-permute-start.3 = (bf16[128,1152]{1,0:T(8,128)(2,1)}, bf16[128,1152]{1,0:T(8,128)(2,1)S(1)}, u32[]{:S(2)}, u32[]{:S(2)}) collective-permute-start(bf16[128,1152]{1,0:T(8,128)(2,1)} %collective-permute-done), channel_id=1, source_target_pairs={{0,8},{8,16},{16,24},{24,28},{28,20},{20,12},{12,4},{4,0},{1,9},{9... | collective-permute-start | bytes 884744 | tf_op jit(solution)/shard_map/ppermute | solution.py:831
  29.3 17.6 %collective-permute-start.4 = (bf16[128,1152]{1,0:T(8,128)(2,1)}, bf16[128,1152]{1,0:T(8,128)(2,1)S(1)}, u32[]{:S(2)}, u32[]{:S(2)}) collective-permute-start(bf16[128,1152]{1,0:T(8,128)(2,1)} %collective-permute-done.1), channel_id=1, source_target_pairs={{8,0},{16,8},{24,16},{28,24},{20,28},{12,20},{4,12},{0,4},{9,1},{1... | collective-permute-start | bytes 884744 | tf_op jit(solution)/shard_map/ppermute | solution.py:833
  46.9 12.2 %collective-permute-start.10 = (bf16[256,1024]{1,0:T(8,128)(2,1)S(1)}, bf16[256,1024]{1,0:T(8,128)(2,1)S(1)}, u32[]{:S(2)}, u32[]{:S(2)}) collective-permute-start(bf16[256,1024]{1,0:T(8,128)(2,1)S(1)} %collective-permute-done.6.refs_4_.refs_6_), channel_id=1, source_target_pairs={{0,1},{1,0},{2,3},{3,2},{4,5},{5,4},{6,7},{7,6},{8,9},{9,8},{10,11... | collective-permute-start | bytes 1572872 | tf_op jit(solution)/shard_map/ppermute | solution.py:780
  46.9 12.2 %collective-permute-start.9 = (bf16[256,1024]{1,0:T(8,128)(2,1)}, bf16[256,1024]{1,0:T(8,128)(2,1)S(1)}, u32[]{:S(2)}, u32[]{:S(2)}) collective-permute-start(bf16[256,1024]{1,0:T(8,128)(2,1)} %collective-permute-done.5), channel_id=1, source_target_pairs={{0,1},{1,0},{2,3},{3,2},{4,5},{5,4},{6,7},{7,6},{8,9},{9,8},{10,11... | collective-permute-start | bytes 1572872 | tf_op jit(solution)/shard_map/ppermute | solution.py:780
  47.4 8.9 %collective-permute-start.7 = (bf16[128,1152]{1,0:T(8,128)(2,1)S(1)}, bf16[128,1152]{1,0:T(8,128)(2,1)S(1)}, u32[]{:S(2)}, u32[]{:S(2)}) collective-permute-start(bf16[128,1152]{1,0:T(8,128)(2,1)S(1)} %collective-permute-done.3), channel_id=1, source_target_pairs={{0,8},{8,16},{16,24},{24,28},{28,20},{20,12},{12,4},{4,0},{1,9},{9... | collective-permute-start | bytes 884744 | tf_op jit(solution)/shard_map/ppermute | solution.py:831
  47.4 11.7 %collective-permute-start.8 = (bf16[128,1152]{1,0:T(8,128)(2,1)S(1)}, bf16[128,1152]{1,0:T(8,128)(2,1)S(1)}, u32[]{:S(2)}, u32[]{:S(2)}) collective-permute-start(bf16[128,1152]{1,0:T(8,128)(2,1)S(1)} %collective-permute-done.4), channel_id=1, source_target_pairs={{8,0},{16,8},{24,16},{28,24},{20,28},{12,20},{4,12},{0,4},{9,1},{1... | collective-permute-start | bytes 884744 | tf_op jit(solution)/shard_map/ppermute | solution.py:833
  56.3 5.5 %copy-start.16 = (bf16[128,1152]{1,0:T(8,128)(2,1)}, bf16[128,1152]{1,0:T(8,128)(2,1)S(1)}, u32[]{:S(2)}) copy-start(bf16[128,1152]{1,0:T(8,128)(2,1)S(1)} %collective-permute-done.7) | copy-start | bytes 884740
  59.9 9.6 %collective-permute-start.11 = (bf16[64,1152]{1,0:T(8,128)(2,1)}, bf16[64,1152]{1,0:T(8,128)(2,1)}, u32[]{:S(2)}, u32[]{:S(2)}) collective-permute-start(bf16[64,1152]{1,0:T(8,128)(2,1)} %slice.48), channel_id=1, source_target_pairs={{0,8},{8,16},{16,24},{24,28},{28,20},{20,12},{12,4},{4,0},{1,9},{9... | collective-permute-start | bytes 442376 | tf_op jit(solution)/shard_map/ppermute | solution.py:828
  61.8 11.8 %collective-permute-start.12 = (bf16[64,1152]{1,0:T(8,128)(2,1)}, bf16[64,1152]{1,0:T(8,128)(2,1)S(1)}, u32[]{:S(2)}, u32[]{:S(2)}) collective-permute-start(bf16[64,1152]{1,0:T(8,128)(2,1)} %slice.49), channel_id=1, source_target_pairs={{8,0},{16,8},{24,16},{28,24},{20,28},{12,20},{4,12},{0,4},{9,1},{1... | collective-permute-start | bytes 442376 | tf_op jit(solution)/shard_map/ppermute | solution.py:829
  64.6 4.8 %copy-start.15 = (bf16[128,1152]{1,0:T(8,128)(2,1)S(1)}, bf16[128,1152]{1,0:T(8,128)(2,1)}, u32[]{:S(2)}) copy-start(bf16[128,1152]{1,0:T(8,128)(2,1)} %copy-done.14) | copy-start | bytes 884740
  73.6 14.6 %copy-start.19 = (bf16[1024,256]{1,0:T(8,128)(2,1)}, bf16[1024,256]{1,0:T(8,128)(2,1)S(1)}, u32[]{:S(2)}) copy-start(bf16[1024,256]{1,0:T(8,128)(2,1)S(1)} %slice.50.refs_4_.out_ref) | copy-start | bytes 1572868
  73.6 14.6 %collective-permute-start.14 = (bf16[1024,256]{1,0:T(8,128)(2,1)S(1)}, bf16[1024,256]{1,0:T(8,128)(2,1)}, u32[]{:S(2)}, u32[]{:S(2)}) collective-permute-start(bf16[1024,256]{1,0:T(8,128)(2,1)S(1)} %slice.50.refs_4_.out_ref), channel_id=1, source_target_pairs={{0,2},{1,3},{2,0},{3,1},{4,6},{5,7},{6,4},{7,5},{8,10},{9,11},{10,... | collective-permute-start | bytes 1572872 | tf_op jit(solution)/shard_map/ppermute | solution.py:780
  74.9 13.4 %collective-permute-start.15 = (bf16[1024,256]{1,0:T(8,128)(2,1)S(1)}, bf16[1024,256]{1,0:T(8,128)(2,1)}, u32[]{:S(2)}, u32[]{:S(2)}) collective-permute-start(bf16[1024,256]{1,0:T(8,128)(2,1)S(1)} %slice.50.refs_4_.out_ref), channel_id=1, source_target_pairs={{0,1},{1,0},{2,3},{3,2},{4,5},{5,4},{6,7},{7,6},{8,9},{9,8},{10,11... | collective-permute-start | bytes 1572872 | tf_op jit(solution)/shard_map/ppermute | solution.py:780
  88.3 15.8 %collective-permute-start.16 = (bf16[512,256]{1,0:T(8,128)(2,1)}, bf16[512,256]{1,0:T(8,128)(2,1)S(1)}, u32[]{:S(2)}, u32[]{:S(2)}) collective-permute-start(bf16[512,256]{1,0:T(8,128)(2,1)} %get-tuple-element.174.refs_0_), channel_id=1, source_target_pairs={{0,2},{1,3},{2,0},{3,1},{4,6},{5,7},{6,4},{7,5},{8,10},{9,11},{10,... | collective-permute-start | bytes 786440 | tf_op jit(solution)/shard_map/ppermute | solution.py:780
  89.6 14.6 %collective-permute-start.17 = (bf16[512,256]{1,0:T(8,128)(2,1)}, bf16[512,256]{1,0:T(8,128)(2,1)S(1)}, u32[]{:S(2)}, u32[]{:S(2)}) collective-permute-start(bf16[512,256]{1,0:T(8,128)(2,1)} %get-tuple-element.174.refs_0_), channel_id=1, source_target_pairs={{0,1},{1,0},{2,3},{3,2},{4,5},{5,4},{6,7},{7,6},{8,9},{9,8},{10,11... | collective-permute-start | bytes 786440 | tf_op jit(solution)/shard_map/ppermute | solution.py:780
  89.6 14.6 %collective-permute-start.18 = (bf16[1024,256]{1,0:T(8,128)(2,1)}, bf16[1024,256]{1,0:T(8,128)(2,1)S(1)}, u32[]{:S(2)}, u32[]{:S(2)}) collective-permute-start(bf16[1024,256]{1,0:T(8,128)(2,1)} %collective-permute-done.14.refs_5_), channel_id=1, source_target_pairs={{0,1},{1,0},{2,3},{3,2},{4,5},{5,4},{6,7},{7,6},{8,9},{9,8},{10,11... | collective-permute-start | bytes 1572872 | tf_op jit(solution)/shard_map/ppermute | solution.py:780
  104.2 1.6 collective-permute-start.21
  104.2 13.3 %collective-permute-start.19 = (bf16[512,256]{1,0:T(8,128)(2,1)}, bf16[512,256]{1,0:T(8,128)(2,1)S(1)}, u32[]{:S(2)}, u32[]{:S(2)}) collective-permute-start(bf16[512,256]{1,0:T(8,128)(2,1)} %get-tuple-element.192.refs_0_), channel_id=1, source_target_pairs={{0,2},{1,3},{2,0},{3,1},{4,6},{5,7},{6,4},{7,5},{8,10},{9,11},{10,... | collective-permute-start | bytes 786440 | tf_op jit(solution)/shard_map/ppermute | solution.py:780
  105.2 12.4 %collective-permute-start.20 = (bf16[512,256]{1,0:T(8,128)(2,1)}, bf16[512,256]{1,0:T(8,128)(2,1)S(1)}, u32[]{:S(2)}, u32[]{:S(2)}) collective-permute-start(bf16[512,256]{1,0:T(8,128)(2,1)} %get-tuple-element.192.refs_0_), channel_id=1, source_target_pairs={{0,1},{1,0},{2,3},{3,2},{4,5},{5,4},{6,7},{7,6},{8,9},{9,8},{10,11... | collective-permute-start | bytes 786440 | tf_op jit(solution)/shard_map/ppermute | solution.py:780
  117.6 4.5 %copy-start.41 = (bf16[512,256]{1,0:T(8,128)(2,1)}, bf16[512,256]{1,0:T(8,128)(2,1)S(1)}, u32[]{:S(2)}) copy-start(bf16[512,256]{1,0:T(8,128)(2,1)S(1)} %collective-permute-done.19.refs_1_) | copy-start | bytes 786436
  117.6 2.2 collective-permute-start.23
  117.8 3.4 %collective-permute-start.22 = (bf16[512,256]{1,0:T(8,128)(2,1)S(1)}, bf16[512,256]{1,0:T(8,128)(2,1)S(1)}, u32[]{:S(2)}, u32[]{:S(2)}) collective-permute-start(bf16[512,256]{1,0:T(8,128)(2,1)S(1)} %collective-permute-done.19.refs_1_), channel_id=1, source_target_pairs={{0,1},{1,0},{2,3},{3,2},{4,5},{5,4},{6,7},{7,6},{8,9},{9,8},{10,11... | collective-permute-start | bytes 786440 | tf_op jit(solution)/shard_map/ppermute | solution.py:780
  121.2 14.1 %copy-start.1 = (f32[256,1024]{1,0:T(8,128)S(1)}, f32[256,1024]{1,0:T(8,128)}, u32[]{:S(2)}) copy-start(f32[256,1024]{1,0:T(8,128)} %get-tuple-element.209.refs_2_.mid0) | copy-start | bytes 3145732
  121.2 14.1 %copy-start.7 = (f32[1,1024]{1,0:T(1,128)S(1)}, f32[1,1024]{1,0:T(1,128)}, u32[]{:S(2)}) copy-start(f32[1,1024]{1,0:T(1,128)} %refs_7_.5) | copy-start | bytes 12292
  121.2 14.0 %collective-permute-start.24 = (bf16[256,1024]{1,0:T(8,128)(2,1)S(1)}, bf16[256,1024]{1,0:T(8,128)(2,1)S(1)}, u32[]{:S(2)}, u32[]{:S(2)}) collective-permute-start(bf16[256,1024]{1,0:T(8,128)(2,1)S(1)} %add_convert_fusion.refs_0_), channel_id=1, source_target_pairs={{0,2},{1,3},{2,0},{3,1},{4,6},{5,7},{6,4},{7,5},{8,10},{9,11},{10,... | collective-permute-start | bytes 1572872 | tf_op jit(solution)/shard_map/ppermute | solution.py:780
  135.3 2.1 collective-permute-start.25
  136.8 11.1 %copy-start.8 = (bf16[256,1024]{1,0:T(8,128)(2,1)}, bf16[256,1024]{1,0:T(8,128)(2,1)S(1)}, u32[]{:S(2)}) copy-start(bf16[256,1024]{1,0:T(8,128)(2,1)S(1)} %get-tuple-element.216.ga0_ref) | copy-start | bytes 1572868
  137.5 10.4 %collective-permute-start.27 = (bf16[256,1024]{1,0:T(8,128)(2,1)S(1)}, bf16[256,1024]{1,0:T(8,128)(2,1)S(1)}, u32[]{:S(2)}, u32[]{:S(2)}) collective-permute-start(bf16[256,1024]{1,0:T(8,128)(2,1)S(1)} %get-tuple-element.216.ga0_ref), channel_id=1, source_target_pairs={{0,1},{1,0},{2,3},{3,2},{4,5},{5,4},{6,7},{7,6},{8,9},{9,8},{10,11... | collective-permute-start | bytes 1572872 | tf_op jit(solution)/shard_map/ppermute | solution.py:780
  137.7 10.2 %collective-permute-start.26 = (bf16[128,1024]{1,0:T(8,128)(2,1)S(1)}, bf16[128,1024]{1,0:T(8,128)(2,1)S(1)}, u32[]{:S(2)}, u32[]{:S(2)}) collective-permute-start(bf16[128,1024]{1,0:T(8,128)(2,1)S(1)} %get-tuple-element.214.refs_7_.refs_0_), channel_id=1, source_target_pairs={{0,2},{1,3},{2,0},{3,1},{4,6},{5,7},{6,4},{7,5},{8,10},{9,11},{10,... | collective-permute-start | bytes 786440 | tf_op jit(solution)/shard_map/ppermute | solution.py:780
  148.7 8.4 %copy-start.2 = (f32[256,1024]{1,0:T(8,128)S(1)}, f32[256,1024]{1,0:T(8,128)}, u32[]{:S(2)}) copy-start(f32[256,1024]{1,0:T(8,128)} %get-tuple-element.227.refs_4_.mid1) | copy-start | bytes 3145732
  148.7 8.4 %copy-start.6 = (bf16[128,1024]{1,0:T(8,128)(2,1)S(1)}, bf16[128,1024]{1,0:T(8,128)(2,1)}, u32[]{:S(2)}) copy-start(bf16[128,1024]{1,0:T(8,128)(2,1)} %copy-done.5) | copy-start | bytes 786436
  148.7 8.4 %collective-permute-start.28 = (bf16[128,1024]{1,0:T(8,128)(2,1)S(1)}, bf16[128,1024]{1,0:T(8,128)(2,1)S(1)}, u32[]{:S(2)}, u32[]{:S(2)}) collective-permute-start(bf16[128,1024]{1,0:T(8,128)(2,1)S(1)} %get-tuple-element.215.refs_1_), channel_id=1, source_target_pairs={{0,2},{1,3},{2,0},{3,1},{4,6},{5,7},{6,4},{7,5},{8,10},{9,11},{10,... | collective-permute-start | bytes 786440 | tf_op jit(solution)/shard_map/ppermute | solution.py:780
  158.7 2.6 collective-permute-start.29
  158.7 38.1 %collective-permute-start.30 = (bf16[2,256,1024]{2,1,0:T(8,128)(2,1)}, bf16[2,256,1024]{2,1,0:T(8,128)(2,1)S(1)}, u32[]{:S(2)}, u32[]{:S(2)}) collective-permute-start(bf16[2,256,1024]{2,1,0:T(8,128)(2,1)} %get-tuple-element.256), channel_id=1, source_target_pairs={{0,1},{1,0},{2,3},{3,2},{4,5},{5,4},{6,7},{7,6},{8,9},{9,8},{10,11... | collective-permute-start | bytes 3145736 | tf_op jit(solution)/shard_map/ppermute | solution.py:780
  196.7 6.9 %copy-start.11 = (bf16[2,256,1024]{2,1,0:T(8,128)(2,1)}, bf16[2,256,1024]{2,1,0:T(8,128)(2,1)S(1)}, u32[]{:S(2)}) copy-start(bf16[2,256,1024]{2,1,0:T(8,128)(2,1)S(1)} %collective-permute-done.30.got) | copy-start | bytes 3145732
  196.8 6.1 %collective-permute-start.31 = (bf16[2,256,1024]{2,1,0:T(8,128)(2,1)}, bf16[2,256,1024]{2,1,0:T(8,128)(2,1)S(1)}, u32[]{:S(2)}, u32[]{:S(2)}) collective-permute-start(bf16[2,256,1024]{2,1,0:T(8,128)(2,1)} %get-tuple-element.258), channel_id=1, source_target_pairs={{0,1},{1,0},{2,3},{3,2},{4,5},{5,4},{6,7},{7,6},{8,9},{9,8},{10,11... | collective-permute-start | bytes 3145736 | tf_op jit(solution)/shard_map/ppermute | solution.py:780
  196.9 20.3 %collective-permute-start.32 = (bf16[4,128,512]{2,1,0:T(8,128)(2,1)}, bf16[4,128,512]{2,1,0:T(8,128)(2,1)S(1)}, u32[]{:S(2)}, u32[]{:S(2)}) collective-permute-start(bf16[4,128,512]{2,1,0:T(8,128)(2,1)} %get-tuple-element.261), channel_id=1, source_target_pairs={{0,4},{4,0},{8,12},{12,8},{16,20},{20,16},{24,28},{28,24},{1,5},{5... | collective-permute-start | bytes 1572872 | tf_op jit(solution)/shard_map/ppermute | solution.py:780
  196.9 20.3 %collective-permute-start.33 = (bf16[4,128,512]{2,1,0:T(8,128)(2,1)}, bf16[4,128,512]{2,1,0:T(8,128)(2,1)S(1)}, u32[]{:S(2)}, u32[]{:S(2)}) collective-permute-start(bf16[4,128,512]{2,1,0:T(8,128)(2,1)} %get-tuple-element.262), channel_id=1, source_target_pairs={{0,8},{4,12},{8,0},{12,4},{16,24},{20,28},{24,16},{28,20},{1,9},{5... | collective-permute-start | bytes 1572872 | tf_op jit(solution)/shard_map/ppermute | solution.py:780
  201.8 8.3 %collective-permute-start.34 = (f32[8,1024]{1,0:T(8,128)}, f32[8,1024]{1,0:T(8,128)S(1)}, u32[]{:S(2)}, u32[]{:S(2)}) collective-permute-start(f32[8,1024]{1,0:T(8,128)} %get-tuple-element.259.wait_for), channel_id=1, source_target_pairs={{0,1},{1,0},{2,3},{3,2},{4,5},{5,4},{6,7},{7,6},{8,9},{9,8},{10,11... | collective-permute-start | bytes 98312 | tf_op jit(solution)/shard_map/ppermute | solution.py:780
  201.8 8.3 %collective-permute-start.35 = (f32[8,1024]{1,0:T(8,128)}, f32[8,1024]{1,0:T(8,128)S(1)}, u32[]{:S(2)}, u32[]{:S(2)}) collective-permute-start(f32[8,1024]{1,0:T(8,128)} %get-tuple-element.259.wait_for), channel_id=1, source_target_pairs={{0,2},{1,3},{2,0},{3,1},{4,6},{5,7},{6,4},{7,5},{8,10},{9,11},{10,... | collective-permute-start | bytes 98312 | tf_op jit(solution)/shard_map/ppermute | solution.py:780
  202.9 7.2 %collective-permute-start.36 = (f32[8,1024]{1,0:T(8,128)}, f32[8,1024]{1,0:T(8,128)S(1)}, u32[]{:S(2)}, u32[]{:S(2)}) collective-permute-start(f32[8,1024]{1,0:T(8,128)} %get-tuple-element.259.wait_for), channel_id=1, source_target_pairs={{0,3},{1,2},{2,1},{3,0},{4,7},{5,6},{6,5},{7,4},{8,11},{9,10},{10,... | collective-permute-start | bytes 98312 | tf_op jit(solution)/shard_map/ppermute | solution.py:780
  206.9 19.8 %copy-start.27 = (f32[8,1024]{1,0:T(8,128)S(1)}, f32[8,1024]{1,0:T(8,128)}, u32[]{:S(2)}) copy-start(f32[8,1024]{1,0:T(8,128)} %get-tuple-element.259.wait_for) | copy-start | bytes 98308
  206.9 19.8 %copy-start.34 = (f32[8,1024]{1,0:T(8,128)S(1)}, f32[8,1024]{1,0:T(8,128)}, u32[]{:S(2)}) copy-start(f32[8,1024]{1,0:T(8,128)} %get-tuple-element.280) | copy-start | bytes 98308
  217.2 31.9 %collective-permute-start.37 = (bf16[256,1024]{1,0:T(8,128)(2,1)}, bf16[256,1024]{1,0:T(8,128)(2,1)S(1)}, u32[]{:S(2)}, u32[]{:S(2)}) collective-permute-start(bf16[256,1024]{1,0:T(8,128)(2,1)} %get-tuple-element.268), channel_id=1, source_target_pairs={{0,2},{1,3},{2,0},{3,1},{4,6},{5,7},{6,4},{7,5},{8,10},{9,11},{10,... | collective-permute-start | bytes 1572872 | tf_op jit(solution)/shard_map/ppermute | solution.py:780
  218.3 30.9 %collective-permute-start.38 = (bf16[256,1024]{1,0:T(8,128)(2,1)}, bf16[256,1024]{1,0:T(8,128)(2,1)S(1)}, u32[]{:S(2)}, u32[]{:S(2)}) collective-permute-start(bf16[256,1024]{1,0:T(8,128)(2,1)} %get-tuple-element.270), channel_id=1, source_target_pairs={{0,2},{1,3},{2,0},{3,1},{4,6},{5,7},{6,4},{7,5},{8,10},{9,11},{10,... | collective-permute-start | bytes 1572872 | tf_op jit(solution)/shard_map/ppermute | solution.py:780
  221.9 21.4 %collective-permute-start.39 = (bf16[2,128,512]{2,1,0:T(8,128)(2,1)}, bf16[2,128,512]{2,1,0:T(8,128)(2,1)S(1)}, u32[]{:S(2)}, u32[]{:S(2)}) collective-permute-start(bf16[2,128,512]{2,1,0:T(8,128)(2,1)} %get-tuple-element.278), channel_id=1, source_target_pairs={{0,8},{4,12},{8,0},{12,4},{16,24},{20,28},{24,16},{28,20},{1,9},{5... | collective-permute-start | bytes 786440 | tf_op jit(solution)/shard_map/ppermute | solution.py:780
  225.0 18.4 %collective-permute-start.40 = (bf16[2,128,512]{2,1,0:T(8,128)(2,1)}, bf16[2,128,512]{2,1,0:T(8,128)(2,1)S(1)}, u32[]{:S(2)}, u32[]{:S(2)}) collective-permute-start(bf16[2,128,512]{2,1,0:T(8,128)(2,1)} %get-tuple-element.279), channel_id=1, source_target_pairs={{0,4},{4,0},{8,12},{12,8},{16,20},{20,16},{24,28},{28,24},{1,5},{5... | collective-permute-start | bytes 786440 | tf_op jit(solution)/shard_map/ppermute | solution.py:780
  226.7 12.1 %collective-permute-start.41 = (f32[8,1024]{1,0:T(8,128)S(1)}, f32[8,1024]{1,0:T(8,128)S(1)}, u32[]{:S(2)}, u32[]{:S(2)}) collective-permute-start(f32[8,1024]{1,0:T(8,128)S(1)} %add_add_fusion), channel_id=1, source_target_pairs={{0,4},{4,0},{8,12},{12,8},{16,20},{20,16},{24,28},{28,24},{1,5},{5... | collective-permute-start | bytes 98312 | tf_op jit(solution)/shard_map/ppermute | solution.py:780
  238.8 22.7 %copy-start.28 = (f32[8,1024]{1,0:T(8,128)}, f32[8,1024]{1,0:T(8,128)S(1)}, u32[]{:S(2)}) copy-start(f32[8,1024]{1,0:T(8,128)S(1)} %add.201.s_ref) | copy-start | bytes 98308
  246.1 15.3 %collective-permute-start.42 = (bf16[1,128,512]{2,1,0:T(8,128)(2,1)}, bf16[1,128,512]{2,1,0:T(8,128)(2,1)S(1)}, u32[]{:S(2)}, u32[]{:S(2)}) collective-permute-start(bf16[1,128,512]{2,1,0:T(8,128)(2,1)} %get-tuple-element.288), channel_id=1, source_target_pairs={{0,16},{4,20},{8,24},{12,28},{16,0},{20,4},{24,8},{28,12},{1,17},{... | collective-permute-start | bytes 393224 | tf_op jit(solution)/shard_map/ppermute | solution.py:780
  246.2 15.3 %collective-permute-start.43 = (bf16[1,128,512]{2,1,0:T(8,128)(2,1)}, bf16[1,128,512]{2,1,0:T(8,128)(2,1)S(1)}, u32[]{:S(2)}, u32[]{:S(2)}) collective-permute-start(bf16[1,128,512]{2,1,0:T(8,128)(2,1)} %get-tuple-element.290), channel_id=1, source_target_pairs={{0,16},{4,20},{8,24},{12,28},{16,0},{20,4},{24,8},{28,12},{1,17},{... | collective-permute-start | bytes 393224 | tf_op jit(solution)/shard_map/ppermute | solution.py:780
  249.1 11.5 %collective-permute-start.44 = (f32[8,1024]{1,0:T(8,128)S(1)}, f32[8,1024]{1,0:T(8,128)S(1)}, u32[]{:S(2)}, u32[]{:S(2)}) collective-permute-start(f32[8,1024]{1,0:T(8,128)S(1)} %add.201.s_ref), channel_id=1, source_target_pairs={{0,8},{4,12},{8,0},{12,4},{16,24},{20,28},{24,16},{28,20},{1,9},{5... | collective-permute-start | bytes 98312 | tf_op jit(solution)/shard_map/ppermute | solution.py:780
  249.1 12.3 %collective-permute-start.45 = (f32[8,1024]{1,0:T(8,128)S(1)}, f32[8,1024]{1,0:T(8,128)S(1)}, u32[]{:S(2)}, u32[]{:S(2)}) collective-permute-start(f32[8,1024]{1,0:T(8,128)S(1)} %add.201.s_ref), channel_id=1, source_target_pairs={{0,16},{4,20},{8,24},{12,28},{16,0},{20,4},{24,8},{28,12},{1,17},{... | collective-permute-start | bytes 98312 | tf_op jit(solution)/shard_map/ppermute | solution.py:780
  249.2 12.2 %collective-permute-start.46 = (f32[8,1024]{1,0:T(8,128)S(1)}, f32[8,1024]{1,0:T(8,128)S(1)}, u32[]{:S(2)}, u32[]{:S(2)}) collective-permute-start(f32[8,1024]{1,0:T(8,128)S(1)} %add.201.s_ref), channel_id=1, source_target_pairs={{0,24},{4,28},{8,16},{12,20},{16,8},{20,12},{24,0},{28,4},{1,25},{... | collective-permute-start | bytes 98312 | tf_op jit(solution)/shard_map/ppermute | solution.py:780
  (30 other events, 55.0 us)
Sparse Core Ops, SparseCore 0:
  13.4 89.7 all-gather.1
  148.8 103.4 reduce-scatter.1
